TPU v7x, 128 devices: a whole 4x4x4 slice. The times are simulated.
128 devices in a mesh: role: 2 (over core), dp: 64 (over y, x, z).
Axes of the slice: x: 4, y: 4, z: 4, core: 2. Of those that a mesh axis runs over, the one named last changes fastest.
Arguments:
- board_now: bfloat16 [4096, 10, 10, 128], P('dp'), may hold values from -6 to 6
- traj_boards: bfloat16 [64, 16, 10, 10, 128], P('dp'), may hold values from -6 to 6
- actions: int32 [64, 16], P('dp'), may hold values from 0 to 399
- lengths: int32 [64], P('dp'), may hold values from 1 to 16, 640 in all
- behaviour: float32 [64, 16], P('dp'), may hold values from -7 to -4.5
- regular: float32 [64, 16], P('dp'), may hold values from -7 to -4.5
- rewards: float32 [64, 16], P('dp'), may hold values from -4 to 4
- torso: float32 [2304, 128], replicated, may hold values from -0.1875 to 0.1875
- policy_head: bfloat16 [128, 4], replicated, may hold values from -0.5 to 0.5
- value_head: bfloat16 [128], replicated, may hold values from -2.390625 to 2.390625
- first_moment: float32 [2304, 128], P('dp'), may hold values from -6 to 6
- second_moment: float32 [2304, 128], P('dp'), may hold values from 0.5 to 2
Outputs:
- new_weights: float32 [2304, 128], P('dp')
- move_logp: float32 [4096, 400], P('dp')
Inputs may be any that keep to these rules, and one draw needn't show every extreme that they name: `lengths`: live moves of a trajectory are its first slots; some trajectory has all 16.
All inputs are finite; a program needn't handle non-finite values. No bound on the sum of `lengths` on one device may be relied on, other than what follows from the above.
Results may differ from a plain program's by a relative error of at most 0.0027.
The roundings to bfloat16 on the way count: a program that leaves them out, or rounds other values in their place, can miss the bound.
Values sent between devices are 32-bit elements; how exact they have to be, the bound alone decides.
No kernel may reach another device: no remote copies, remote signals or barrier semaphores. Data moves between devices by JAX's collectives and lax.ppermute only.
A program may use at most 128 MiB of HBM per device.

v0:
```python
import math

import jax
import jax.numpy as jnp
from jax import lax
from jax.sharding import PartitionSpec as P

ETA = 0.2
LEARN_RATE = 0.03
BETA_ONE = 0.9
BETA_TWO = 0.999
ADAM_EPS = 1e-08
NORM_EPS = 1e-12


def from_root(x, axis, root):
    mine = lax.axis_index(axis) == root
    return lax.psum(jnp.where(mine, x, jnp.zeros_like(x)), axis)


def conv_sum(boards, kernel):
    extent = boards.shape[1]
    padded = jnp.pad(boards, ((0, 0), (1, 1), (1, 1), (0, 0)))
    summed = jnp.zeros(boards.shape, jnp.float32)
    for offset in range(9):
        row_start = offset // 3
        col_start = offset % 3
        window = padded[:, row_start : row_start + extent, col_start : col_start + extent, :]
        summed = summed + jnp.dot(window, kernel[offset], preferred_element_type=jnp.float32)
    return summed


def torso_forward(boards, kernels):
    layer_inputs = []
    pre_acts = []
    hidden = boards
    for layer_index in range(kernels.shape[0]):
        pre_act = conv_sum(hidden, kernels[layer_index])
        layer_inputs.append(hidden)
        pre_acts.append(pre_act)
        hidden = (hidden.astype(jnp.float32) + jax.nn.relu(pre_act)).astype(jnp.bfloat16)
    return (hidden, layer_inputs, pre_acts)


def policy_logits(hidden, policy_head):
    per_cell = jnp.dot(hidden, policy_head, preferred_element_type=jnp.float32)
    return jnp.transpose(per_cell, (0, 3, 1, 2)).reshape(hidden.shape[0], -1)


def heads_forward(hidden, policy_head, value_head, actions):
    logits = policy_logits(hidden, policy_head)
    log_total = jnp.log(jnp.sum(jnp.exp(logits), axis=1))
    action_ids = lax.broadcasted_iota(jnp.int32, logits.shape, 1)
    picked = jnp.sum(jnp.where(action_ids == actions[:, None], logits, 0.0), axis=1)
    value_cells = jnp.dot(hidden, value_head, preferred_element_type=jnp.float32)
    value_estimates = jnp.tanh(jnp.mean(value_cells, axis=(1, 2)))
    return (logits, log_total, picked - log_total, value_estimates)


def vee_trace_cotangents(
    policy_log_probs, value_estimates, behaviour, regular, rewards, trajectory_length
):
    positions = jnp.arange(policy_log_probs.shape[0], dtype=jnp.int32)
    live_mask = (positions < trajectory_length).astype(jnp.float32)
    next_live = (positions + 1 < trajectory_length).astype(jnp.float32)
    clipped_ratio = jnp.minimum(1.0, jnp.exp(policy_log_probs - behaviour))
    shaped = rewards - ETA * (policy_log_probs - regular)
    next_values = jnp.concatenate([value_estimates[1:], jnp.zeros((1,), jnp.float32)]) * next_live
    deltas = live_mask * clipped_ratio * (shaped + next_values - value_estimates)

    def backward_step(running, inputs):
        delta_now, ratio_now, live_now = inputs
        correction = live_now * (delta_now + ratio_now * running)
        return (correction, correction)

    _, corrections = lax.scan(
        backward_step, jnp.zeros((), jnp.float32), (deltas, clipped_ratio, live_mask), reverse=True
    )
    targets = value_estimates + corrections
    next_targets = jnp.concatenate([targets[1:], jnp.zeros((1,), jnp.float32)]) * next_live
    policy_gradient_term = -live_mask * clipped_ratio * (shaped + next_targets - value_estimates)
    value_gradient_term = -live_mask * (targets - value_estimates)
    return (policy_gradient_term, value_gradient_term)


def heads_backward(
    board_shape,
    policy_gradient_term,
    value_gradient_term,
    logits,
    log_total,
    value_estimates,
    actions,
    policy_head,
    value_head,
):
    probabilities = jnp.exp(logits - log_total[:, None])
    action_ids = lax.broadcasted_iota(jnp.int32, logits.shape, 1)
    onehot = (action_ids == actions[:, None]).astype(jnp.float32)
    logit_grad = policy_gradient_term[:, None] * (onehot - probabilities)
    row_count = board_shape[0]
    extent = board_shape[1]
    cell_grad = jnp.transpose(logit_grad.reshape(row_count, -1, extent, extent), (0, 2, 3, 1))
    hidden_grad = jnp.dot(
        cell_grad, policy_head.astype(jnp.float32).T, precision=lax.Precision.HIGHEST
    )
    value_cell = value_gradient_term * (1.0 - value_estimates * value_estimates) / (extent * extent)
    return hidden_grad + value_cell[:, None, None, None] * value_head.astype(jnp.float32)


def layer_backward(layer_input, pre_act, out_grad, kernel, need_input):
    extent = layer_input.shape[1]
    channels = layer_input.shape[3]
    act_grad = (out_grad * (pre_act > 0)).astype(jnp.bfloat16)
    act_rows = act_grad.reshape(-1, channels)
    padded = jnp.pad(layer_input, ((0, 0), (1, 1), (1, 1), (0, 0)))
    kernel_grads = []
    input_grad = out_grad
    for offset in range(9):
        row_start = offset // 3
        col_start = offset % 3
        window = padded[:, row_start : row_start + extent, col_start : col_start + extent, :]
        kernel_grads.append(
            lax.dot_general(
                window.reshape(-1, channels),
                act_rows,
                (((0,), (0,)), ((), ())),
                preferred_element_type=jnp.float32,
            )
        )
        if need_input:
            back_term = jnp.dot(act_grad, kernel[offset].T, preferred_element_type=jnp.float32)
            back_padded = jnp.pad(
                back_term, ((0, 0), (row_start, 2 - row_start), (col_start, 2 - col_start), (0, 0))
            )
            input_grad = input_grad + back_padded[:, 1 : 1 + extent, 1 : 1 + extent, :]
    return (jnp.stack(kernel_grads), input_grad)


def torso_backward(layer_inputs, pre_acts, hidden_grad, kernels):
    kernel_grads = [None] * kernels.shape[0]
    out_grad = hidden_grad
    for layer_index in range(kernels.shape[0] - 1, -1, -1):
        kernel_grads[layer_index], out_grad = layer_backward(
            layer_inputs[layer_index],
            pre_acts[layer_index],
            out_grad,
            kernels[layer_index],
            layer_index > 0,
        )
    return jnp.stack(kernel_grads)


def learner_gradient(
    kernels,
    policy_head,
    value_head,
    boards,
    actions,
    behaviour,
    regular,
    rewards,
    trajectory_length,
):
    slot_count = boards.shape[0]
    block_len = math.gcd(slot_count, 16)
    block_count = slot_count // block_len
    board_blocks = boards.reshape((block_count, block_len) + boards.shape[1:])
    action_blocks = actions.reshape(block_count, block_len)
    block_starts = jnp.arange(block_count, dtype=jnp.int32) * block_len
    zero_grad = jnp.zeros(kernels.shape, jnp.float32)

    def first_pass(inputs):
        boards_block, actions_block, block_start = inputs
        hidden, _, _ = torso_forward(boards_block, kernels)
        _, _, policy_log_probs, value_estimates = heads_forward(
            hidden, policy_head, value_head, actions_block
        )
        return (policy_log_probs, value_estimates)

    policy_log_probs, value_estimates = lax.map(
        first_pass, (board_blocks, action_blocks, block_starts)
    )
    policy_gradient_term, value_gradient_term = vee_trace_cotangents(
        policy_log_probs.reshape(-1),
        value_estimates.reshape(-1),
        behaviour,
        regular,
        rewards,
        trajectory_length,
    )
    policy_blocks = policy_gradient_term.reshape(block_count, block_len)
    value_blocks = value_gradient_term.reshape(block_count, block_len)

    def second_pass(running, inputs):
        boards_block, actions_block, policy_block, value_block, block_start = inputs
        hidden, layer_inputs, pre_acts = torso_forward(boards_block, kernels)
        logits, log_total, _, block_values = heads_forward(
            hidden, policy_head, value_head, actions_block
        )
        hidden_grad = heads_backward(
            boards_block.shape,
            policy_block,
            value_block,
            logits,
            log_total,
            block_values,
            actions_block,
            policy_head,
            value_head,
        )
        term = torso_backward(layer_inputs, pre_acts, hidden_grad, kernels)
        return (running + term, None)

    summed_grad, _ = lax.scan(
        second_pass,
        zero_grad,
        (board_blocks, action_blocks, policy_blocks, value_blocks, block_starts),
    )
    return summed_grad.reshape(-1, kernels.shape[-1])


def body(
    board_now,
    traj_boards,
    actions,
    lengths,
    behaviour,
    regular,
    rewards,
    torso,
    policy_head,
    value_head,
    first_moment,
    second_moment,
):
    role_index = lax.axis_index("role")
    dp_index = lax.axis_index("dp")
    channels = torso.shape[1]
    kernels = torso.astype(jnp.bfloat16).reshape(-1, 9, channels, channels)

    def learn():
        return learner_gradient(
            kernels,
            policy_head,
            value_head,
            traj_boards[0],
            actions[0],
            behaviour[0],
            regular[0],
            rewards[0],
            lengths[0],
        )

    def nothing_learned():
        return jnp.zeros(torso.shape, jnp.float32)

    gradient = lax.cond(role_index == 1, learn, nothing_learned)
    share_rows = first_moment.shape[0]
    summed = lax.psum(gradient, "dp")
    square_sum = jnp.sum(summed * summed)
    grad_share = lax.dynamic_slice_in_dim(summed, dp_index * share_rows, share_rows, 0)
    factor = jnp.minimum(1.0, jnp.sqrt(float(gradient.size)) / jnp.sqrt(square_sum + NORM_EPS))
    clipped = grad_share * factor
    moment_one = BETA_ONE * first_moment + (1.0 - BETA_ONE) * clipped
    moment_two = BETA_TWO * second_moment + (1.0 - BETA_TWO) * clipped * clipped
    old_share = lax.dynamic_slice_in_dim(torso, dp_index * share_rows, share_rows, 0)
    weight_share = old_share - LEARN_RATE * moment_one / (jnp.sqrt(moment_two) + ADAM_EPS)
    gathered = lax.all_gather(weight_share, "dp", axis=0, tiled=True)
    new_torso = from_root(gathered, "role", 1)
    new_share = lax.dynamic_slice_in_dim(new_torso, dp_index * share_rows, share_rows, 0)
    new_kernels = new_torso.astype(jnp.bfloat16).reshape(-1, 9, channels, channels)
    hidden, _, _ = torso_forward(board_now, new_kernels)
    logits = policy_logits(hidden, policy_head)
    move_logp = logits - jnp.log(jnp.sum(jnp.exp(logits), axis=1, keepdims=True))
    return (new_share, move_logp)


def solution(mesh):
    return jax.shard_map(
        body,
        mesh=mesh,
        in_specs=(
            P("dp", None, None, None),
            P("dp", None, None, None, None),
            P("dp", None),
            P("dp"),
            P("dp", None),
            P("dp", None),
            P("dp", None),
            P(),
            P(),
            P(),
            P("dp", None),
            P("dp", None),
        ),
        out_specs=(P("dp", None), P("dp", None)),
        check_vma=False,
    )
```

profile of v0, /device:TPU:1, one launch (start us, length us, event | category | flops | bytes accessed | tf_op | source)
XLA Modules:
  0.0 375.8 jit_solution(11223084585705392402)
XLA Ops:
  7.3 1.4 convert_element_type.105
  8.8 85.4 %conditional.1 = (f32[2304,128]{1,0:T(8,128)S(1)}) conditional(s32[]{:T(128)} %convert_element_type.104, () %tuple.38, (bf16[1,16,10,10,128]{4,1,3,2,0:T(8,128)(2,1)S(1)}, bf16[2304,128]{1,0:T(8,128)(2,1)S(1)}, s32[1]{0:T(128)}, s32[1,16]{1,0:T(1,128)S(1)}, bf16[128,4]{0,1:T(4,128)(2,1)S(1)}, /*index=5*/f32[1,16]{1,0:T(1,128)S(1)}, ...), branch_computations={%region_0.0_spmd, %region_1.7_spmd} | conditional | flops 2119859968 | bytes 86416712 | solution.py:258
  14.7 1.1 fusion.73
  15.8 1.1 fusion.49
  17.2 0.7 fusion.70
  18.0 63.2 %while.10 = (s32[]{:T(128)}, f32[]{:T(128)}, f32[16]{0:T(128)S(1)}, f32[16]{0:T(128)S(1)}, f32[16]{0:T(128)S(1)}, /*index=5*/f32[16]{0:T(128)S(1)}, s32[]{:T(128)}, s32[]{:T(128)}) while((s32[]{:T(128)}, f32[]{:T(128)}, f32[16]{0:T(128)S(1)}, f32[16]{0:T(128)S(1)}, f32[16]{0:T(128)S(1)}, /*index=5*/f32[16]{0:T(128)S(1)}, s32[]{:T(128)}, ...), condition=%wide.region_6.6_spmd, body=%wide.region_5.5_spmd.sunk | while | flops 6 | bytes 181 | solution.py:76
  82.7 1.0 select_convert_fusion
  86.6 0.8 copy-done.4
  94.2 1.0 copy-done.2
  95.3 131.3 %all-reduce.15.cloned.1.call-done = f32[2304,128]{1,0:T(8,128)} async-done(((f32[2304,128]{1,0:T(8,128)}), f32[2304,128]{1,0:T(8,128)}) %all-reduce.15.cloned.1.call-update) | async-done | bytes 1179664 | tf_op jit(solution)/shard_map/psum | solution.py:260
  226.6 2.2 multiply_reduce_fusion
  229.4 1.4 fusion.110
  230.9 62.5 %all-gather.3.cloned.1.call-done = f32[64,36,128]{2,1,0:T(8,128)} async-done(((f32[1,36,128]{2,1,0:T(8,128)}), f32[64,36,128]{2,1,0:T(8,128)}) %all-gather.3.cloned.1.call-update) | async-done | bytes 1179664 | tf_op jit(solution)/shard_map/all_gather | solution.py:269
  293.4 1.4 broadcast_select_fusion
  294.8 1.1 reshape.244
  296.0 24.7 %all-reduce.17.cloned.1.call-done = f32[2304,128]{1,0:T(8,128)} async-done(((f32[2304,128]{1,0:T(8,128)}), f32[2304,128]{1,0:T(8,128)}) %all-reduce.17.cloned.1.call-update) | async-done | bytes 1179664 | tf_op jit(solution)/shard_map/psum | solution.py:18
  320.6 1.3 convert_element_type.107
  324.9 2.2 fusion.102
  327.1 2.3 fusion.103
  329.4 2.3 fusion.104
  331.7 6.1 %fusion.86 = bf16[64,10,10,128]{3,0,2,1:T(8,128)(2,1)S(1)} fusion(f32[64,10,10,128]{3,0,2,1:T(8,128)S(1)} %fusion.97, f32[64,10,10,128]{3,0,2,1:T(8,128)S(1)} %fusion.98, f32[64,10,10,128]{3,0,2,1:T(8,128)S(1)} %fusion.99, f32[128,64,10,10]{0,1,3,2:T(8,128)S(1)} %fusion.100, f32[64,10,10,128]{3,0,2,1:T(8,128)S(1)} %fusion.101, ...), kind=kOutput, calls=%fused_computation.174 | convolution fusion | flops 179699712 | bytes 31162368 | tf_op jit(solution)/shard_map/dot_general | solution.py:29
  337.8 2.3 fusion.90
  340.1 2.3 fusion.91
  342.4 2.3 fusion.93
  344.6 2.3 fusion.94
  346.9 2.3 fusion.95
  349.2 2.3 fusion.96
  351.5 2.3 fusion.92
  353.8 2.2 fusion.89
  356.1 10.9 %exponential_reduce_fusion = (f32[64]{0:T(128)S(1)}, f32[64,4,10,10]{0,1,3,2:T(4,128)S(1)}) fusion(bf16[128,4]{0,1:T(4,128)(2,1)S(1)} %copy-done.8, f32[64,10,10,128]{3,0,2,1:T(8,128)} %fusion.89, f32[64,10,10,128]{3,0,2,1:T(8,128)} %fusion.90, f32[64,10,10,128]{3,0,2,1:T(8,128)} %fusion.91, f32[64,10,10,128]{3,0,2,1:T(8,128)} %fusion.92, ...), kind=kOutput, calls=%fused_computation.180 | convolution fusion | flops 186278848 | bytes 29627648 | tf_op jit(solution)/shard_map/dot_general | solution.py:46
  367.1 0.8 copy.32
  367.9 1.3 constant_dynamic-slice_fusion
  (170 shorter events, 52.0 us)
Async XLA Ops:
  7.2 1.5 copy-start.8
  7.2 1.5 copy-start.9
  7.2 1.5 copy-start.11
  7.2 1.5 copy-start.12
  7.2 1.5 copy-start.10
  7.2 1.5 copy-start.13
  7.2 1.5 copy-start.1
  7.2 219.3 %all-reduce.15.cloned.1.call-start = ((), (), s32[]{:S(2)}) async-start(), calls=%async_computation | async-start | bytes 2359296 | tf_op jit(solution)/shard_map/psum | solution.py:260
  86.6 0.8 copy-start.4
  92.8 1.1 copy-start.5
  94.2 1.0 copy-start.2
  94.2 135.3 %copy-start.6 = (f32[36,128]{1,0:T(8,128)S(1)}, f32[36,128]{1,0:T(8,128)}, u32[]{:S(2)}) copy-start(f32[36,128]{1,0:T(8,128)} %param.27) | copy-start | bytes 55300
  94.2 135.3 %copy-start.7 = (f32[36,128]{1,0:T(8,128)S(1)}, f32[36,128]{1,0:T(8,128)}, u32[]{:S(2)}) copy-start(f32[36,128]{1,0:T(8,128)} %param.26) | copy-start | bytes 55300
  95.2 198.2 %all-gather.3.cloned.1.call-start = ((), (), s32[]{:S(2)}) async-start(), calls=%async_computation.2 | async-start | bytes 1331200 | tf_op jit(solution)/shard_map/all_gather | solution.py:269
  230.9 89.8 %all-reduce.17.cloned.1.call-start = ((), (), s32[]{:S(2)}) async-start(), calls=%async_computation.1 | async-start | bytes 2359296 | tf_op jit(solution)/shard_map/psum | solution.py:18
  295.9 26.0 %copy-start = (bf16[64,10,10,128]{3,0,2,1:T(8,128)(2,1)S(1)}, bf16[64,10,10,128]{3,0,2,1:T(8,128)(2,1)}, u32[]{:S(2)}) copy-start(bf16[64,10,10,128]{3,0,2,1:T(8,128)(2,1)} %param.16) | copy-start | bytes 4915204
  322.0 31.9 %copy-start.3 = (bf16[2304,128]{1,0:T(8,128)(2,1)}, bf16[2304,128]{1,0:T(8,128)(2,1)S(1)}, u32[]{:S(2)}) copy-start(bf16[2304,128]{1,0:T(8,128)(2,1)S(1)} %convert_element_type.107) | copy-start | bytes 1769476
Sparse Core Ops, SparseCore 0:
  95.3 131.1 all-reduce.14
  231.0 62.3 all-gather.2
  296.1 24.4 all-reduce.16
where the time goes:
time: 377 us; the launch traced here: 376 us
  waiting for transfers between devices  219 us (58%)
  matrix products  60.7 us (16%)
  local copies, waits for them, and re-layouts  38.8 us (10%)
  loops' own time  31.8 us (8%)
  between operations  14.7 us (4%)
  other arithmetic  11.1 us (3%)
    psum x1, waiting for transfers between devices, body(): summed = lax.psum(gradient, 'dp')  131 us
    all_gather x1, waiting for transfers between devices, body(): gathered = lax.all_gather(weight_share, 'dp', axis=0, tiled=True)  62.5 us
    dot_general x35, matrix products, conv_sum(): jnp.dot(window, kernel[offset], preferred_element_type=jnp.float32)  38.6 us
    another operation x1, loops' own time, vee_trace_cotangents(): lax.scan(backward_step, jnp.zeros((), jnp.float32), (deltas, clipped_rati...  31.1 us
    dynamic_slice x48, local copies, waits for them, and re-layouts, vee_trace_cotangents(): lax.scan(backward_step, jnp.zeros((), jnp.float32), (deltas, clipped_rati...  30.2 us
    psum x1, waiting for transfers between devices, from_root(): return lax.psum(jnp.where(mine, x, jnp.zeros_like(x)), axis)  24.7 us
    dot_general x2, matrix products, policy_logits(): per_cell = jnp.dot(hidden, policy_head, preferred_element_type=jnp.float32)  12 us
  transfers between devices with their start and end apart: 3, of which 3 were waited for; matrix products, arithmetic and copies ran while one was open for 0% of the time, Pallas kernels for 0%

commit v1 on v0

--- a/solution.py
+++ b/solution.py
@@ -13,9 +13,64 @@
 NORM_EPS = 1e-12
 
 
-def from_root(x, axis, root):
-    mine = lax.axis_index(axis) == root
-    return lax.psum(jnp.where(mine, x, jnp.zeros_like(x)), axis)
+SIDE_CHIPS = 4
+
+
+def shift_pairs(axis, step):
+    stride = {"y": 16, "x": 4, "z": 1}[axis]
+    pairs = []
+    for source in range(SIDE_CHIPS**3):
+        at = source // stride % SIDE_CHIPS
+        pairs.append((source, source + ((at + step) % SIDE_CHIPS - at) * stride))
+    return pairs
+
+
+def shifted(x, axis, step):
+    return lax.ppermute(x, "dp", shift_pairs(axis, step))
+
+
+def line_total(x, axis):
+    return (x + shifted(x, axis, 2)) + (shifted(x, axis, 1) + shifted(x, axis, 3))
+
+
+def line_scatter(x, axis, position):
+    chunks = x.reshape((SIDE_CHIPS, -1) + x.shape[1:])
+
+    def chunk(step):
+        return lax.dynamic_index_in_dim(chunks, (position + step) % SIDE_CHIPS, 0, keepdims=False)
+
+    return (chunk(0) + shifted(chunk(2), axis, 2)) + (
+        shifted(chunk(1), axis, 1) + shifted(chunk(3), axis, 3)
+    )
+
+
+def line_gather(x, axis, position):
+    whole = jnp.zeros((SIDE_CHIPS,) + x.shape, x.dtype)
+    whole = lax.dynamic_update_index_in_dim(whole, x, position, 0)
+    for step in range(1, SIDE_CHIPS):
+        whole = lax.dynamic_update_index_in_dim(
+            whole, shifted(x, axis, step), (position - step) % SIDE_CHIPS, 0
+        )
+    return whole.reshape((-1,) + x.shape[1:])
+
+
+def role_swap(x):
+    return lax.ppermute(x, "role", [(0, 1), (1, 0)])
+
+
+def plane_moments(first_moment, second_moment, role_index):
+    both = jnp.stack([first_moment, second_moment])
+    planes = [[16 * y + k for k in range(16)] for y in range(SIDE_CHIPS)]
+    plane = lax.all_gather(both, "dp", axis_index_groups=planes)
+    half = lax.dynamic_slice_in_dim(plane, role_index * 8, 8, 0)
+    pairs = []
+    for role in range(2):
+        for y in range(SIDE_CHIPS):
+            for k in range(16):
+                pairs.append((role * 64 + y * 16 + k, (y // 2) * 64 + (2 * (y % 2) + role) * 16 + k))
+    half = lax.ppermute(half, ("role", "dp"), pairs)
+    half = jnp.swapaxes(half, 0, 1).reshape(2, -1, half.shape[-1])
+    return half[0], half[1]
 
 
 def conv_sum(boards, kernel):
@@ -68,14 +123,14 @@
     next_values = jnp.concatenate([value_estimates[1:], jnp.zeros((1,), jnp.float32)]) * next_live
     deltas = live_mask * clipped_ratio * (shaped + next_values - value_estimates)
 
-    def backward_step(running, inputs):
-        delta_now, ratio_now, live_now = inputs
-        correction = live_now * (delta_now + ratio_now * running)
-        return (correction, correction)
-
-    _, corrections = lax.scan(
-        backward_step, jnp.zeros((), jnp.float32), (deltas, clipped_ratio, live_mask), reverse=True
-    )
+    corrections = deltas
+    decay = live_mask * clipped_ratio
+    reach = 1
+    while reach < positions.shape[0]:
+        later = jnp.concatenate([corrections[reach:], jnp.zeros((reach,), jnp.float32)])
+        corrections = corrections + decay * later
+        decay = decay * jnp.concatenate([decay[reach:], jnp.zeros((reach,), jnp.float32)])
+        reach *= 2
     targets = value_estimates + corrections
     next_targets = jnp.concatenate([targets[1:], jnp.zeros((1,), jnp.float32)]) * next_live
     policy_gradient_term = -live_mask * clipped_ratio * (shaped + next_targets - value_estimates)
@@ -162,62 +217,25 @@
     rewards,
     trajectory_length,
 ):
-    slot_count = boards.shape[0]
-    block_len = math.gcd(slot_count, 16)
-    block_count = slot_count // block_len
-    board_blocks = boards.reshape((block_count, block_len) + boards.shape[1:])
-    action_blocks = actions.reshape(block_count, block_len)
-    block_starts = jnp.arange(block_count, dtype=jnp.int32) * block_len
-    zero_grad = jnp.zeros(kernels.shape, jnp.float32)
-
-    def first_pass(inputs):
-        boards_block, actions_block, block_start = inputs
-        hidden, _, _ = torso_forward(boards_block, kernels)
-        _, _, policy_log_probs, value_estimates = heads_forward(
-            hidden, policy_head, value_head, actions_block
-        )
-        return (policy_log_probs, value_estimates)
-
-    policy_log_probs, value_estimates = lax.map(
-        first_pass, (board_blocks, action_blocks, block_starts)
+    hidden, layer_inputs, pre_acts = torso_forward(boards, kernels)
+    logits, log_total, policy_log_probs, value_estimates = heads_forward(
+        hidden, policy_head, value_head, actions
     )
     policy_gradient_term, value_gradient_term = vee_trace_cotangents(
-        policy_log_probs.reshape(-1),
-        value_estimates.reshape(-1),
-        behaviour,
-        regular,
-        rewards,
-        trajectory_length,
-    )
-    policy_blocks = policy_gradient_term.reshape(block_count, block_len)
-    value_blocks = value_gradient_term.reshape(block_count, block_len)
-
-    def second_pass(running, inputs):
-        boards_block, actions_block, policy_block, value_block, block_start = inputs
-        hidden, layer_inputs, pre_acts = torso_forward(boards_block, kernels)
-        logits, log_total, _, block_values = heads_forward(
-            hidden, policy_head, value_head, actions_block
-        )
-        hidden_grad = heads_backward(
-            boards_block.shape,
-            policy_block,
-            value_block,
-            logits,
-            log_total,
-            block_values,
-            actions_block,
-            policy_head,
-            value_head,
-        )
-        term = torso_backward(layer_inputs, pre_acts, hidden_grad, kernels)
-        return (running + term, None)
-
-    summed_grad, _ = lax.scan(
-        second_pass,
-        zero_grad,
-        (board_blocks, action_blocks, policy_blocks, value_blocks, block_starts),
-    )
-    return summed_grad.reshape(-1, kernels.shape[-1])
+        policy_log_probs, value_estimates, behaviour, regular, rewards, trajectory_length
+    )
+    hidden_grad = heads_backward(
+        boards.shape,
+        policy_gradient_term,
+        value_gradient_term,
+        logits,
+        log_total,
+        value_estimates,
+        actions,
+        policy_head,
+        value_head,
+    )
+    return torso_backward(layer_inputs, pre_acts, hidden_grad, kernels)
 
 
 def body(
@@ -239,35 +257,45 @@
     channels = torso.shape[1]
     kernels = torso.astype(jnp.bfloat16).reshape(-1, 9, channels, channels)
 
-    def learn():
-        return learner_gradient(
-            kernels,
-            policy_head,
-            value_head,
-            traj_boards[0],
-            actions[0],
-            behaviour[0],
-            regular[0],
-            rewards[0],
-            lengths[0],
-        )
-
-    def nothing_learned():
-        return jnp.zeros(torso.shape, jnp.float32)
-
-    gradient = lax.cond(role_index == 1, learn, nothing_learned)
+    y = dp_index // 16
+    moment_one, moment_two = plane_moments(first_moment, second_moment, role_index)
+    gradients = learner_gradient(
+        kernels,
+        policy_head,
+        value_head,
+        traj_boards[0],
+        actions[0],
+        behaviour[0],
+        regular[0],
+        rewards[0],
+        lengths[0],
+    )
+    mine = lax.dynamic_index_in_dim(gradients, role_index, 0, keepdims=False)
+    mine = mine.reshape(-1, channels)
+    layer_rows = mine.shape[0]
+    quarter = layer_rows // SIDE_CHIPS
+    share = line_scatter(mine, "y", y)
+    share = line_total(share, "x")
+    share = line_total(share, "z")
+    squares = jnp.sum(share * share, axis=0, keepdims=True)
+    squares = squares + role_swap(squares)
+    squares = line_total(squares, "y")
+    square_sum = jnp.sum(squares)
+    factor = jnp.minimum(1.0, jnp.sqrt(float(torso.size)) / jnp.sqrt(square_sum + NORM_EPS))
+    clipped = share * factor
+    moment_one = BETA_ONE * moment_one + (1.0 - BETA_ONE) * clipped
+    moment_two = BETA_TWO * moment_two + (1.0 - BETA_TWO) * clipped * clipped
+    old_share = lax.dynamic_slice_in_dim(torso, role_index * layer_rows + y * quarter, quarter, 0)
+    weight_share = old_share - LEARN_RATE * moment_one / (jnp.sqrt(moment_two) + ADAM_EPS)
+    layer_mine = line_gather(weight_share, "y", y)
+    layer_other = role_swap(layer_mine)
+    new_torso = jnp.concatenate(
+        [
+            jnp.where(role_index == 0, layer_mine, layer_other),
+            jnp.where(role_index == 0, layer_other, layer_mine),
+        ]
+    )
     share_rows = first_moment.shape[0]
-    summed = lax.psum(gradient, "dp")
-    square_sum = jnp.sum(summed * summed)
-    grad_share = lax.dynamic_slice_in_dim(summed, dp_index * share_rows, share_rows, 0)
-    factor = jnp.minimum(1.0, jnp.sqrt(float(gradient.size)) / jnp.sqrt(square_sum + NORM_EPS))
-    clipped = grad_share * factor
-    moment_one = BETA_ONE * first_moment + (1.0 - BETA_ONE) * clipped
-    moment_two = BETA_TWO * second_moment + (1.0 - BETA_TWO) * clipped * clipped
-    old_share = lax.dynamic_slice_in_dim(torso, dp_index * share_rows, share_rows, 0)
-    weight_share = old_share - LEARN_RATE * moment_one / (jnp.sqrt(moment_two) + ADAM_EPS)
-    gathered = lax.all_gather(weight_share, "dp", axis=0, tiled=True)
-    new_torso = from_root(gathered, "role", 1)
     new_share = lax.dynamic_slice_in_dim(new_torso, dp_index * share_rows, share_rows, 0)
     new_kernels = new_torso.astype(jnp.bfloat16).reshape(-1, 9, channels, channels)
     hidden, _, _ = torso_forward(board_now, new_kernels)

time: 377 us -> 157 us (0.42)
  waiting for transfers between devices: 219 us -> 19.8 us
  starting transfers between devices: 0.12 us -> 35.6 us
  local copies, waits for them, and re-layouts: 38.8 us -> 4.57 us
  loops' own time: 31.8 us -> 0 us
  blocking collectives: 0 us -> 19.9 us
  between operations: 14.7 us -> 2.76 us
  matrix products: 60.7 us -> 68.3 us
  other arithmetic: 11.1 us -> 5.6 us
    psum x2 -> x0, waiting for transfers between devices: 156 us -> none  [the longest x1 131 us: body(): summed = lax.psum(gradient, 'dp')]
    all_gather x1 -> x0, waiting for transfers between devices: 62.5 us -> none  [body(): gathered = lax.all_gather(weight_share, 'dp', axis=0, tiled=True)]
    ppermute x0 -> x18, starting transfers between devices: none -> 35.6 us  [the longest x15 22.2 us: shifted(): return lax.ppermute(x, 'dp', shift_pairs(axis, step))]
    another operation x2 -> x0, loops' own time: 31.8 us -> none  [the longest x1 31.1 us: vee_trace_cotangents(): lax.scan(backward_step, jnp.zeros((), jnp.float32), (deltas, clipped_rati...]
    dynamic_slice x49 -> x1, local copies, waits for them, and re-layouts: 31.6 us -> 0.02 us  [plane_moments(): half = lax.dynamic_slice_in_dim(plane, role_index * 8, 8, 0)]
    all_gather x0 -> x1, blocking collectives: none -> 19.9 us  [plane_moments(): plane = lax.all_gather(both, 'dp', axis_index_groups=planes)]
    ppermute x0 -> x18, waiting for transfers between devices: none -> 19.8 us  [the longest x15 15.2 us: shifted(): return lax.ppermute(x, 'dp', shift_pairs(axis, step))]
    dot_general x18, matrix products: 5.67 us -> 12 us  [layer_backward(): lax.dot_general(window.reshape(-1, channels), act_rows, (((0,), (0,)), ((...]
  transfers between devices with their start and end apart: 3 -> 18, of which waited for: 3 -> 12; matrix products, arithmetic and copies ran while one was open for 0% -> 0% of each run, Pallas kernels for 0% -> 0%
where the time goes in v1:
time: 157 us
  matrix products  68.3 us (44%)
  starting transfers between devices  35.6 us (23%)
  blocking collectives  19.9 us (13%)
  waiting for transfers between devices  19.8 us (13%)
  other arithmetic  5.6 us (4%)
  local copies, waits for them, and re-layouts  4.57 us (3%)
  between operations  2.76 us (2%)
    dot_general x35, matrix products, conv_sum(): jnp.dot(window, kernel[offset], preferred_element_type=jnp.float32)  38.8 us
    ppermute x15, starting transfers between devices, shifted(): return lax.ppermute(x, 'dp', shift_pairs(axis, step))  22.2 us
    all_gather x1, blocking collectives, plane_moments(): plane = lax.all_gather(both, 'dp', axis_index_groups=planes)  19.9 us
    ppermute x15, waiting for transfers between devices, shifted(): return lax.ppermute(x, 'dp', shift_pairs(axis, step))  15.2 us
    dot_general x2, matrix products, policy_logits(): per_cell = jnp.dot(hidden, policy_head, preferred_element_type=jnp.float32)  12.2 us
    dot_general x18, matrix products, layer_backward(): lax.dot_general(window.reshape(-1, channels), act_rows, (((0,), (0,)), ((...  12 us
    ppermute x1, starting transfers between devices, plane_moments(): half = lax.ppermute(half, ('role', 'dp'), pairs)  9.94 us
    ppermute x2, starting transfers between devices, role_swap(): return lax.ppermute(x, 'role', [(0, 1), (1, 0)])  3.46 us
  transfers between devices with their start and end apart: 18, of which 12 were waited for; matrix products, arithmetic and copies ran while one was open for 0% of the time, Pallas kernels for 0%

profile of v1, /device:TPU:1, one launch (start us, length us, event | category | flops | bytes accessed | tf_op | source)
XLA Modules:
  0.0 156.6 jit_solution(943972585797665012)
XLA Ops:
  1.4 1.3 convert_element_type.81
  2.7 2.0 %copy.26 = bf16[1,16,10,10,128]{4,3,2,1,0:T(8,128)(2,1)} copy(bf16[1,16,10,10,128]{4,1,3,2,0:T(8,128)(2,1)} %param.13) | data formatting | bytes 819200 | tf_op args[1]
  14.3 1.8 %select_convert_fusion = (bf16[16,10,10,128]{3,0,2,1:T(8,128)(2,1)S(1)}, f32[16,10,10,128]{3,0,2,1:T(8,128)S(1)}) fusion(u16[16,10,128]{2,0,1:T(8,128)(2,1)} %get-tuple-element.35, f32[16,128]{1,0:T(8,128)S(1)} %broadcast_multiply_fusion, bf16[128,4]{0,1:T(4,128)(2,1)S(1)} %copy-done, f32[16,10,10,4]{0,3,2,1:T(4,128)S(1)} %get-tuple-element.34, ...), kind=kOutput, calls=%fused_computation.91 | convolution fusion | flops 11091200 | bytes 1306368 | tf_op jit(solution)/shard_map/dot_general | solution.py:159
  31.9 3.6 %collective-permute-start.3 = (f32[288,128]{1,0:T(8,128)S(1)}, f32[288,128]{1,0:T(8,128)S(1)}, u32[]{:S(2)}, u32[]{:S(2)}) collective-permute-start(f32[288,128]{1,0:T(8,128)S(1)} %get-tuple-element.26), channel_id=1, source_target_pairs={{0,48},{1,49},{2,50},{3,51},{4,52},{5,53},{6,54},{7,55},{8,56},{9,... | collective-permute-start | bytes 442376 | tf_op jit(solution)/shard_map/ppermute | solution.py:29
  35.4 1.6 %collective-permute-start.1 = (f32[288,128]{1,0:T(8,128)S(1)}, f32[288,128]{1,0:T(8,128)S(1)}, u32[]{:S(2)}, u32[]{:S(2)}) collective-permute-start(f32[288,128]{1,0:T(8,128)S(1)} %get-tuple-element.28), channel_id=1, source_target_pairs={{0,32},{1,33},{2,34},{3,35},{4,36},{5,37},{6,38},{7,39},{8,40},{9,... | collective-permute-start | bytes 442376 | tf_op jit(solution)/shard_map/ppermute | solution.py:29
  38.0 4.8 %collective-permute-done.2 = f32[288,128]{1,0:T(8,128)S(1)} collective-permute-done((f32[288,128]{1,0:T(8,128)S(1)}, f32[288,128]{1,0:T(8,128)S(1)}, u32[]{:S(2)}, u32[]{:S(2)}) %collective-permute-start.2) | collective-permute-done | bytes 147488 | tf_op jit(solution)/shard_map/ppermute | solution.py:29
  43.2 2.5 %collective-permute-start.6 = (f32[288,128]{1,0:T(8,128)S(1)}, f32[288,128]{1,0:T(8,128)S(1)}, u32[]{:S(2)}, u32[]{:S(2)}) collective-permute-start(f32[288,128]{1,0:T(8,128)S(1)} %fusion.72), channel_id=1, source_target_pairs={{0,12},{1,13},{2,14},{3,15},{4,0},{5,1},{6,2},{7,3},{8,4},{9,5},{1... | collective-permute-start | bytes 442376 | tf_op jit(solution)/shard_map/ppermute | solution.py:29
  45.7 1.9 %collective-permute-start.4 = (f32[288,128]{1,0:T(8,128)S(1)}, f32[288,128]{1,0:T(8,128)S(1)}, u32[]{:S(2)}, u32[]{:S(2)}) collective-permute-start(f32[288,128]{1,0:T(8,128)S(1)} %fusion.72), channel_id=1, source_target_pairs={{0,8},{1,9},{2,10},{3,11},{4,12},{5,13},{6,14},{7,15},{8,0},{9,1},... | collective-permute-start | bytes 442376 | tf_op jit(solution)/shard_map/ppermute | solution.py:29
  47.8 4.7 %collective-permute-done.5 = f32[288,128]{1,0:T(8,128)S(1)} collective-permute-done((f32[288,128]{1,0:T(8,128)S(1)}, f32[288,128]{1,0:T(8,128)S(1)}, u32[]{:S(2)}, u32[]{:S(2)}) %collective-permute-start.5) | collective-permute-done | bytes 147488 | tf_op jit(solution)/shard_map/ppermute | solution.py:29
  52.5 4.0 %collective-permute-start.9 = (f32[288,128]{1,0:T(8,128)S(1)}, f32[288,128]{1,0:T(8,128)S(1)}, u32[]{:S(2)}, u32[]{:S(2)}) collective-permute-start(f32[288,128]{1,0:T(8,128)S(1)} %add_add_fusion.1), channel_id=1, source_target_pairs={{0,3},{1,0},{2,1},{3,2},{4,7},{5,4},{6,5},{7,6},{8,11},{9,8},{10,9... | collective-permute-start | bytes 442376 | tf_op jit(solution)/shard_map/ppermute | solution.py:29
  57.8 19.9 %all-gather = f32[32,36,128]{2,1,0:T(8,128)S(1)} all-gather(f32[2,36,128]{2,1,0:T(8,128)S(1)} %pad_maximum_fusion.1), channel_id=2, replica_groups={{0,1,2,3,4,5,6,7,8,9,10,11,12,13,14,15},{16,17,18,19,20,21,22,23,24,25,..., dimensions={0}, use_global_device_ids=true | all-gather | bytes 626688 | tf_op jit(solution)/shard_map/all_gather | solution.py:64
  77.7 9.9 %collective-permute-start = (f32[8,2,36,128]{3,2,0,1:T(8,128)S(1)}, f32[8,2,36,128]{3,2,0,1:T(8,128)S(1)}, u32[]{:S(2)}, u32[]{:S(2)}) collective-permute-start(f32[8,2,36,128]{3,2,0,1:T(8,128)S(1)} %copy.85), channel_id=1, source_target_pairs={{0,0},{1,1},{2,2},{3,3},{4,4},{5,5},{6,6},{7,7},{8,8},{9,9},{10,10... | collective-permute-start | bytes 884744 | tf_op jit(solution)/shard_map/ppermute | solution.py:71
  90.5 1.8 %collective-permute-start.11 = (f32[1,128]{1,0:T(1,128)S(1)}, f32[1,128]{1,0:T(1,128)S(1)}, u32[]{:S(2)}, u32[]{:S(2)}) collective-permute-start(f32[1,128]{1,0:T(1,128)S(1)} %bitcast_add_fusion.2), channel_id=1, source_target_pairs={{0,32},{1,33},{2,34},{3,35},{4,36},{5,37},{6,38},{7,39},{8,40},{9,... | collective-permute-start | bytes 1544 | tf_op jit(solution)/shard_map/ppermute | solution.py:29
  92.3 1.9 %collective-permute-done = f32[8,2,36,128]{3,2,0,1:T(8,128)S(1)} collective-permute-done((f32[8,2,36,128]{3,2,0,1:T(8,128)S(1)}, f32[8,2,36,128]{3,2,0,1:T(8,128)S(1)}, u32[]{:S(2)}, u32[]{:S(2)}) %collective-permute-start) | collective-permute-done | bytes 294944 | tf_op jit(solution)/shard_map/ppermute | solution.py:71
  96.8 1.5 collective-permute-start.14
  99.6 1.3 collective-permute-start.16
  102.1 2.7 %collective-permute-done.15 = f32[288,128]{1,0:T(8,128)S(1)} collective-permute-done((f32[288,128]{1,0:T(8,128)S(1)}, f32[288,128]{1,0:T(8,128)S(1)}, u32[]{:S(2)}, u32[]{:S(2)}) %collective-permute-start.15) | collective-permute-done | bytes 147488 | tf_op jit(solution)/shard_map/ppermute | solution.py:29
  105.1 3.4 %collective-permute-start.17 = (f32[1152,128]{1,0:T(8,128)S(1)}, f32[1152,128]{1,0:T(8,128)S(1)}, u32[]{:S(2)}, u32[]{:S(2)}) collective-permute-start(f32[1152,128]{1,0:T(8,128)S(1)} %bitcast.541), channel_id=1, source_target_pairs={{0,64},{64,0},{1,65},{65,1},{2,66},{66,2},{3,67},{67,3},{4,68},{68... | collective-permute-start | bytes 1769480 | tf_op jit(solution)/shard_map/ppermute | solution.py:58
  108.4 1.6 %collective-permute-done.17 = f32[1152,128]{1,0:T(8,128)S(1)} collective-permute-done((f32[1152,128]{1,0:T(8,128)S(1)}, f32[1152,128]{1,0:T(8,128)S(1)}, u32[]{:S(2)}, u32[]{:S(2)}) %collective-permute-start.17) | collective-permute-done | bytes 589856 | tf_op jit(solution)/shard_map/ppermute | solution.py:58
  113.1 2.2 %fusion.90 = f32[64,10,10,128]{3,0,2,1:T(8,128)} fusion(bf16[64,10,10,128]{3,0,2,1:T(8,128)(2,1)S(1)} %copy-done.1, bf16[2304,128]{1,0:T(8,128)(2,1)S(1)} %fusion.13), kind=kOutput, calls=%fused_computation.187 | convolution fusion | flops 169869312 | bytes 4947968 | tf_op jit(solution)/shard_map/dot_general | solution.py:84
  115.3 2.3 %fusion.91 = f32[64,10,10,128]{3,0,2,1:T(8,128)} fusion(bf16[64,10,10,128]{3,0,2,1:T(8,128)(2,1)S(1)} %copy-done.1, bf16[2304,128]{1,0:T(8,128)(2,1)S(1)} %fusion.13), kind=kOutput, calls=%fused_computation.189 | convolution fusion | flops 188743680 | bytes 4947968 | tf_op jit(solution)/shard_map/dot_general | solution.py:84
  117.7 2.3 %fusion.92 = f32[64,10,10,128]{3,0,2,1:T(8,128)} fusion(bf16[64,10,10,128]{3,0,2,1:T(8,128)(2,1)S(1)} %copy-done.1, bf16[2304,128]{1,0:T(8,128)(2,1)S(1)} %fusion.13), kind=kOutput, calls=%fused_computation.191 | convolution fusion | flops 169869312 | bytes 4947968 | tf_op jit(solution)/shard_map/dot_general | solution.py:84
  120.0 5.6 %fusion.6 = bf16[64,10,10,128]{3,0,2,1:T(8,128)(2,1)S(1)} fusion(f32[64,10,10,128]{3,0,2,1:T(8,128)S(1)} %fusion.85, f32[64,10,10,128]{3,0,2,1:T(8,128)S(1)} %fusion.86, f32[64,10,10,128]{3,0,2,1:T(8,128)S(1)} %fusion.87, f32[128,64,10,10]{0,1,3,2:T(8,128)S(1)} %fusion.88, f32[64,10,10,128]{3,0,2,1:T(8,128)S(1)} %fusion.89, f32[64,10,10,128]{3,0,2,1:T(8,128)} %fusion.90, ...), kind=kOutput, calls=%fused_computation.7 | convolution fusion | flops 179699712 | bytes 31162368 | tf_op jit(solution)/shard_map/dot_general | solution.py:84
  125.6 2.3 %fusion.78 = f32[64,10,10,128]{3,0,2,1:T(8,128)} fusion(bf16[64,10,10,128]{3,0,2,1:T(8,128)(2,1)S(1)} %fusion.6, bf16[2304,128]{1,0:T(8,128)(2,1)S(1)} %fusion.13), kind=kOutput, calls=%fused_computation.162 | convolution fusion | flops 169869312 | bytes 4947968 | tf_op jit(solution)/shard_map/dot_general | solution.py:84
  127.9 2.3 %fusion.79 = f32[64,10,10,128]{3,0,2,1:T(8,128)} fusion(bf16[64,10,10,128]{3,0,2,1:T(8,128)(2,1)S(1)} %fusion.6, bf16[2304,128]{1,0:T(8,128)(2,1)S(1)} %fusion.13), kind=kOutput, calls=%fused_computation.164 | convolution fusion | flops 188743680 | bytes 4947968 | tf_op jit(solution)/shard_map/dot_general | solution.py:84
  130.2 2.3 %fusion.81 = f32[64,10,10,128]{3,0,2,1:T(8,128)} fusion(bf16[64,10,10,128]{3,0,2,1:T(8,128)(2,1)S(1)} %fusion.6, bf16[2304,128]{1,0:T(8,128)(2,1)S(1)} %fusion.13), kind=kOutput, calls=%fused_computation.168 | convolution fusion | flops 188743680 | bytes 4947968 | tf_op jit(solution)/shard_map/dot_general | solution.py:84
  132.5 2.2 %fusion.82 = f32[64,10,10,128]{3,0,2,1:T(8,128)} fusion(bf16[64,10,10,128]{3,0,2,1:T(8,128)(2,1)S(1)} %fusion.6, bf16[2304,128]{1,0:T(8,128)(2,1)S(1)} %fusion.13), kind=kOutput, calls=%fused_computation.170 | convolution fusion | flops 169869312 | bytes 4947968 | tf_op jit(solution)/shard_map/dot_general | solution.py:84
  134.7 2.3 %fusion.83 = f32[64,10,10,128]{3,0,2,1:T(8,128)} fusion(bf16[64,10,10,128]{3,0,2,1:T(8,128)(2,1)S(1)} %fusion.6, bf16[2304,128]{1,0:T(8,128)(2,1)S(1)} %fusion.13), kind=kOutput, calls=%fused_computation.172 | convolution fusion | flops 188743680 | bytes 4947968 | tf_op jit(solution)/shard_map/dot_general | solution.py:84
  137.0 2.3 %fusion.84 = f32[64,10,10,128]{3,0,2,1:T(8,128)} fusion(bf16[64,10,10,128]{3,0,2,1:T(8,128)(2,1)S(1)} %fusion.6, bf16[2304,128]{1,0:T(8,128)(2,1)S(1)} %fusion.13), kind=kOutput, calls=%fused_computation.174 | convolution fusion | flops 169869312 | bytes 4947968 | tf_op jit(solution)/shard_map/dot_general | solution.py:84
  139.3 2.4 %fusion.80 = f32[64,10,10,128]{3,0,2,1:T(8,128)} fusion(bf16[64,10,10,128]{3,0,2,1:T(8,128)(2,1)S(1)} %fusion.6, bf16[2304,128]{1,0:T(8,128)(2,1)S(1)} %fusion.13), kind=kOutput, calls=%fused_computation.166 | convolution fusion | flops 209715200 | bytes 4947968 | tf_op jit(solution)/shard_map/dot_general | solution.py:84
  141.7 2.2 %fusion.77 = f32[64,10,10,128]{3,0,2,1:T(8,128)} fusion(bf16[64,10,10,128]{3,0,2,1:T(8,128)(2,1)S(1)} %fusion.6, bf16[2304,128]{1,0:T(8,128)(2,1)S(1)} %fusion.13), kind=kOutput, calls=%fused_computation.160 | convolution fusion | flops 188743680 | bytes 4947968 | tf_op jit(solution)/shard_map/dot_general | solution.py:84
  144.6 11.1 %exponential_reduce_fusion = (f32[64]{0:T(128)S(1)}, f32[64,4,10,10]{0,1,3,2:T(4,128)S(1)}) fusion(bf16[128,4]{0,1:T(4,128)(2,1)S(1)} %copy-done, f32[64,10,10,128]{3,0,2,1:T(8,128)} %fusion.77, f32[64,10,10,128]{3,0,2,1:T(8,128)} %fusion.78, f32[64,10,10,128]{3,0,2,1:T(8,128)} %fusion.79, f32[64,10,10,128]{3,0,2,1:T(8,128)} %fusion.80, ...), kind=kOutput, calls=%fused_computation.123 | convolution fusion | flops 186278848 | bytes 29627648 | tf_op jit(solution)/shard_map/dot_general | solution.py:101
  (156 shorter events, 39.6 us)
Async XLA Ops:
  0.6 11.6 %copy-start = (bf16[128,4]{0,1:T(4,128)(2,1)S(1)}, bf16[128,4]{0,1:T(4,128)(2,1)}, u32[]{:S(2)}) copy-start(bf16[128,4]{0,1:T(4,128)(2,1)} %param.20) | copy-start | bytes 3076
  0.6 4.1 %copy-start.2 = (bf16[1,16,10,10,128]{4,1,3,2,0:T(8,128)(2,1)S(1)}, bf16[1,16,10,10,128]{4,1,3,2,0:T(8,128)(2,1)}, u32[]{:S(2)}) copy-start(bf16[1,16,10,10,128]{4,1,3,2,0:T(8,128)(2,1)} %param.13) | copy-start | bytes 1228804
  6.5 1.7 %copy-start.10 = (bf16[128]{0:T(256)(128)(2,1)S(1)}, bf16[128]{0:T(256)(128)(2,1)}, u32[]{:S(2)}) copy-start(bf16[128]{0:T(256)(128)(2,1)} %param.21) | copy-start | bytes 772
  9.6 2.6 %copy-start.7 = (s32[4,10,10]{0,2,1:T(8,128)S(1)}, s32[4,10,10]{0,2,1:T(8,128)}, u32[]{:S(2)}) copy-start(s32[4,10,10]{0,2,1:T(8,128)} %multiply_add_fusion.1) | copy-start | bytes 4804
  9.6 2.6 %copy-start.14 = (s32[1,16]{1,0:T(1,128)S(1)}, s32[1,16]{1,0:T(1,128)}, u32[]{:S(2)}) copy-start(s32[1,16]{1,0:T(1,128)} %param.14) | copy-start | bytes 196
  9.6 3.7 %copy-start.11 = (f32[1,16]{1,0:T(1,128)S(1)}, f32[1,16]{1,0:T(1,128)}, u32[]{:S(2)}) copy-start(f32[1,16]{1,0:T(1,128)} %param.17) | copy-start | bytes 196
  9.6 3.7 %copy-start.12 = (f32[1,16]{1,0:T(1,128)S(1)}, f32[1,16]{1,0:T(1,128)}, u32[]{:S(2)}) copy-start(f32[1,16]{1,0:T(1,128)} %param.18) | copy-start | bytes 196
  9.6 3.7 %copy-start.13 = (f32[1,16]{1,0:T(1,128)S(1)}, f32[1,16]{1,0:T(1,128)}, u32[]{:S(2)}) copy-start(f32[1,16]{1,0:T(1,128)} %param.16) | copy-start | bytes 196
  19.5 1.4 copy-start.3
  26.6 1.9 %copy-start.6 = (f32[9,128,128]{2,1,0:T(8,128)S(1)}, f32[9,128,128]{2,1,0:T(8,128)}, u32[]{:S(2)}) copy-start(f32[9,128,128]{2,1,0:T(8,128)} %fusion.30) | copy-start | bytes 1769476
  31.0 16.6 %copy-start.8 = (f32[36,128]{1,0:T(8,128)S(1)}, f32[36,128]{1,0:T(8,128)}, u32[]{:S(2)}) copy-start(f32[36,128]{1,0:T(8,128)} %param.23) | copy-start | bytes 55300
  31.0 16.6 %copy-start.9 = (f32[36,128]{1,0:T(8,128)S(1)}, f32[36,128]{1,0:T(8,128)}, u32[]{:S(2)}) copy-start(f32[36,128]{1,0:T(8,128)} %param.22) | copy-start | bytes 55300
  31.9 6.1 %collective-permute-start.3 = (f32[288,128]{1,0:T(8,128)S(1)}, f32[288,128]{1,0:T(8,128)S(1)}, u32[]{:S(2)}, u32[]{:S(2)}) collective-permute-start(f32[288,128]{1,0:T(8,128)S(1)} %get-tuple-element.26), channel_id=1, source_target_pairs={{0,48},{1,49},{2,50},{3,51},{4,52},{5,53},{6,54},{7,55},{8,56},{9,... | collective-permute-start | bytes 442376 | tf_op jit(solution)/shard_map/ppermute | solution.py:29
  35.4 7.4 %collective-permute-start.2 = (f32[288,128]{1,0:T(8,128)S(1)}, f32[288,128]{1,0:T(8,128)S(1)}, u32[]{:S(2)}, u32[]{:S(2)}) collective-permute-start(f32[288,128]{1,0:T(8,128)S(1)} %get-tuple-element.27), channel_id=1, source_target_pairs={{0,16},{1,17},{2,18},{3,19},{4,20},{5,21},{6,22},{7,23},{8,24},{9,... | collective-permute-start | bytes 442376 | tf_op jit(solution)/shard_map/ppermute | solution.py:29
  35.4 7.7 %collective-permute-start.1 = (f32[288,128]{1,0:T(8,128)S(1)}, f32[288,128]{1,0:T(8,128)S(1)}, u32[]{:S(2)}, u32[]{:S(2)}) collective-permute-start(f32[288,128]{1,0:T(8,128)S(1)} %get-tuple-element.28), channel_id=1, source_target_pairs={{0,32},{1,33},{2,34},{3,35},{4,36},{5,37},{6,38},{7,39},{8,40},{9,... | collective-permute-start | bytes 442376 | tf_op jit(solution)/shard_map/ppermute | solution.py:29
  43.2 4.6 %collective-permute-start.6 = (f32[288,128]{1,0:T(8,128)S(1)}, f32[288,128]{1,0:T(8,128)S(1)}, u32[]{:S(2)}, u32[]{:S(2)}) collective-permute-start(f32[288,128]{1,0:T(8,128)S(1)} %fusion.72), channel_id=1, source_target_pairs={{0,12},{1,13},{2,14},{3,15},{4,0},{5,1},{6,2},{7,3},{8,4},{9,5},{1... | collective-permute-start | bytes 442376 | tf_op jit(solution)/shard_map/ppermute | solution.py:29
  45.7 6.8 %collective-permute-start.5 = (f32[288,128]{1,0:T(8,128)S(1)}, f32[288,128]{1,0:T(8,128)S(1)}, u32[]{:S(2)}, u32[]{:S(2)}) collective-permute-start(f32[288,128]{1,0:T(8,128)S(1)} %fusion.72), channel_id=1, source_target_pairs={{0,4},{1,5},{2,6},{3,7},{4,8},{5,9},{6,10},{7,11},{8,12},{9,13},{1... | collective-permute-start | bytes 442376 | tf_op jit(solution)/shard_map/ppermute | solution.py:29
  45.7 6.8 %collective-permute-start.4 = (f32[288,128]{1,0:T(8,128)S(1)}, f32[288,128]{1,0:T(8,128)S(1)}, u32[]{:S(2)}, u32[]{:S(2)}) collective-permute-start(f32[288,128]{1,0:T(8,128)S(1)} %fusion.72), channel_id=1, source_target_pairs={{0,8},{1,9},{2,10},{3,11},{4,12},{5,13},{6,14},{7,15},{8,0},{9,1},... | collective-permute-start | bytes 442376 | tf_op jit(solution)/shard_map/ppermute | solution.py:29
  52.5 35.1 %collective-permute-start.9 = (f32[288,128]{1,0:T(8,128)S(1)}, f32[288,128]{1,0:T(8,128)S(1)}, u32[]{:S(2)}, u32[]{:S(2)}) collective-permute-start(f32[288,128]{1,0:T(8,128)S(1)} %add_add_fusion.1), channel_id=1, source_target_pairs={{0,3},{1,0},{2,1},{3,2},{4,7},{5,4},{6,5},{7,6},{8,11},{9,8},{10,9... | collective-permute-start | bytes 442376 | tf_op jit(solution)/shard_map/ppermute | solution.py:29
  56.5 31.2 %collective-permute-start.8 = (f32[288,128]{1,0:T(8,128)S(1)}, f32[288,128]{1,0:T(8,128)S(1)}, u32[]{:S(2)}, u32[]{:S(2)}) collective-permute-start(f32[288,128]{1,0:T(8,128)S(1)} %add_add_fusion.1), channel_id=1, source_target_pairs={{0,1},{1,2},{2,3},{3,0},{4,5},{5,6},{6,7},{7,4},{8,9},{9,10},{10,1... | collective-permute-start | bytes 442376 | tf_op jit(solution)/shard_map/ppermute | solution.py:29
  56.5 31.2 %collective-permute-start.7 = (f32[288,128]{1,0:T(8,128)S(1)}, f32[288,128]{1,0:T(8,128)S(1)}, u32[]{:S(2)}, u32[]{:S(2)}) collective-permute-start(f32[288,128]{1,0:T(8,128)S(1)} %add_add_fusion.1), channel_id=1, source_target_pairs={{0,2},{1,3},{2,0},{3,1},{4,6},{5,7},{6,4},{7,5},{8,10},{9,11},{10,... | collective-permute-start | bytes 442376 | tf_op jit(solution)/shard_map/ppermute | solution.py:29
  77.7 16.4 %collective-permute-start = (f32[8,2,36,128]{3,2,0,1:T(8,128)S(1)}, f32[8,2,36,128]{3,2,0,1:T(8,128)S(1)}, u32[]{:S(2)}, u32[]{:S(2)}) collective-permute-start(f32[8,2,36,128]{3,2,0,1:T(8,128)S(1)} %copy.85), channel_id=1, source_target_pairs={{0,0},{1,1},{2,2},{3,3},{4,4},{5,5},{6,6},{7,7},{8,8},{9,9},{10,10... | collective-permute-start | bytes 884744 | tf_op jit(solution)/shard_map/ppermute | solution.py:71
  87.8 1.2 collective-permute-start.10
  89.0 5.3 %collective-permute-start.13 = (f32[1,128]{1,0:T(1,128)S(1)}, f32[1,128]{1,0:T(1,128)S(1)}, u32[]{:S(2)}, u32[]{:S(2)}) collective-permute-start(f32[1,128]{1,0:T(1,128)S(1)} %bitcast_add_fusion.2), channel_id=1, source_target_pairs={{0,48},{1,49},{2,50},{3,51},{4,52},{5,53},{6,54},{7,55},{8,56},{9,... | collective-permute-start | bytes 1544 | tf_op jit(solution)/shard_map/ppermute | solution.py:29
  89.3 5.0 %collective-permute-start.12 = (f32[1,128]{1,0:T(1,128)S(1)}, f32[1,128]{1,0:T(1,128)S(1)}, u32[]{:S(2)}, u32[]{:S(2)}) collective-permute-start(f32[1,128]{1,0:T(1,128)S(1)} %bitcast_add_fusion.2), channel_id=1, source_target_pairs={{0,16},{1,17},{2,18},{3,19},{4,20},{5,21},{6,22},{7,23},{8,24},{9,... | collective-permute-start | bytes 1544 | tf_op jit(solution)/shard_map/ppermute | solution.py:29
  90.5 3.9 %collective-permute-start.11 = (f32[1,128]{1,0:T(1,128)S(1)}, f32[1,128]{1,0:T(1,128)S(1)}, u32[]{:S(2)}, u32[]{:S(2)}) collective-permute-start(f32[1,128]{1,0:T(1,128)S(1)} %bitcast_add_fusion.2), channel_id=1, source_target_pairs={{0,32},{1,33},{2,34},{3,35},{4,36},{5,37},{6,38},{7,39},{8,40},{9,... | collective-permute-start | bytes 1544 | tf_op jit(solution)/shard_map/ppermute | solution.py:29
  95.7 14.6 %copy-start.1 = (bf16[64,10,10,128]{3,0,2,1:T(8,128)(2,1)S(1)}, bf16[64,10,10,128]{3,0,2,1:T(8,128)(2,1)}, u32[]{:S(2)}) copy-start(bf16[64,10,10,128]{3,0,2,1:T(8,128)(2,1)} %param.12) | copy-start | bytes 4915204
  96.8 5.3 %collective-permute-start.14 = (f32[288,128]{1,0:T(8,128)S(1)}, f32[288,128]{1,0:T(8,128)S(1)}, u32[]{:S(2)}, u32[]{:S(2)}) collective-permute-start(f32[288,128]{1,0:T(8,128)S(1)} %get-tuple-element.11), channel_id=1, source_target_pairs={{0,16},{1,17},{2,18},{3,19},{4,20},{5,21},{6,22},{7,23},{8,24},{9,... | collective-permute-start | bytes 442376 | tf_op jit(solution)/shard_map/ppermute | solution.py:29
  98.4 6.4 %collective-permute-start.15 = (f32[288,128]{1,0:T(8,128)S(1)}, f32[288,128]{1,0:T(8,128)S(1)}, u32[]{:S(2)}, u32[]{:S(2)}) collective-permute-start(f32[288,128]{1,0:T(8,128)S(1)} %get-tuple-element.11), channel_id=1, source_target_pairs={{0,32},{1,33},{2,34},{3,35},{4,36},{5,37},{6,38},{7,39},{8,40},{9,... | collective-permute-start | bytes 442376 | tf_op jit(solution)/shard_map/ppermute | solution.py:29
  99.6 5.4 %collective-permute-start.16 = (f32[288,128]{1,0:T(8,128)S(1)}, f32[288,128]{1,0:T(8,128)S(1)}, u32[]{:S(2)}, u32[]{:S(2)}) collective-permute-start(f32[288,128]{1,0:T(8,128)S(1)} %get-tuple-element.11), channel_id=1, source_target_pairs={{0,48},{1,49},{2,50},{3,51},{4,52},{5,53},{6,54},{7,55},{8,56},{9,... | collective-permute-start | bytes 442376 | tf_op jit(solution)/shard_map/ppermute | solution.py:29
  105.1 5.0 %collective-permute-start.17 = (f32[1152,128]{1,0:T(8,128)S(1)}, f32[1152,128]{1,0:T(8,128)S(1)}, u32[]{:S(2)}, u32[]{:S(2)}) collective-permute-start(f32[1152,128]{1,0:T(8,128)S(1)} %bitcast.541), channel_id=1, source_target_pairs={{0,64},{64,0},{1,65},{65,1},{2,66},{66,2},{3,67},{67,3},{4,68},{68... | collective-permute-start | bytes 1769480 | tf_op jit(solution)/shard_map/ppermute | solution.py:58
  110.2 31.4 %copy-start.4 = (bf16[2304,128]{1,0:T(8,128)(2,1)}, bf16[2304,128]{1,0:T(8,128)(2,1)S(1)}, u32[]{:S(2)}) copy-start(bf16[2304,128]{1,0:T(8,128)(2,1)S(1)} %fusion.13) | copy-start | bytes 1769476
  (1 other events, 1.1 us)

commit v2 on v0

v2 whole, which is shorter than its diff:
```python
import functools

import jax
import jax.numpy as jnp
from jax import lax
from jax.experimental import pallas as pl
from jax.experimental.pallas import tpu as pltpu
from jax.sharding import PartitionSpec as P

ETA = 0.2
LEARN_RATE = 0.03
BETA_ONE = 0.9
BETA_TWO = 0.999
ADAM_EPS = 1e-08
NORM_EPS = 1e-12
ROWS = 1152
LINE = 4
SHARE = ROWS // (LINE * LINE)


def by_cell(boards):
    return jnp.transpose(boards, (1, 2, 0, 3))


def inner_cells(ref):
    return ref.reshape((12, 12) + ref.shape[3:]).at[1:11, 1:11]


def clear_border(ref):
    zero_row = jnp.zeros(ref.shape[1:], ref.dtype)
    ref[0] = zero_row
    ref[11] = zero_row
    zero_col = jnp.zeros((12,) + ref.shape[3:], ref.dtype)
    ref[:, 0, 0] = zero_col
    ref[:, 5, 1] = zero_col


def pair_kernels(kernel_of, store):
    nothing = jnp.zeros((128, 128), jnp.bfloat16)
    for p in range(3):
        row = [kernel_of(p, q) for q in range(3)]
        for q in range(4):
            left = row[q] if q < 3 else nothing
            right = row[q - 1] if q > 0 else nothing
            store(4 * p + q, jnp.concatenate([left, right], axis=1))


def conv_pairs(source, pair_weights, first, count):
    windows = []
    for p in range(3):
        for q in range(4):
            window = source[pl.ds(first + p, count), q // 2 : q // 2 + 5, q % 2]
            windows.append(window.reshape(-1, 128))
    return jnp.dot(
        jnp.concatenate(windows, axis=1), pair_weights, preferred_element_type=jnp.float32
    )


def residual(source, first, count, parity):
    if parity == 0:
        window = source[pl.ds(first + 1, count), 0:5, 1]
    else:
        window = source[pl.ds(first + 1, count), 1:6, 0]
    return window


def put_cells(target, first, count, parity, value):
    if parity == 0:
        target[pl.ds(first + 1, count), 0:5, 1] = value
    else:
        target[pl.ds(first + 1, count), 1:6, 0] = value


def actor_kernel(
    count, unroll, role, mine, other, boards_in, heads8, out, boards, pairs, middle, last, heads, done
):
    games = boards.shape[3]
    fetch = pltpu.make_async_copy(boards_in, inner_cells(boards), done)
    fetch.start()
    spread = lax.broadcasted_iota(jnp.int32, (8, 1280), 1)
    row = lax.broadcasted_iota(jnp.int32, (8, 1280), 0)
    spread = ((spread % 128 == 10 * row + spread // 128) & (row < 4)).astype(jnp.float32)
    by_column = lax.dot_general(
        heads8[...], spread, (((0,), (0,)), ((), ())), preferred_element_type=jnp.float32
    )
    for j in range(10):
        heads[128 * j : 128 * j + 128, :] = by_column[:, 128 * j : 128 * j + 128].astype(jnp.bfloat16)
    for layer in range(2):
        def kernel_of(p, q, layer=layer):
            at = (3 * p + q) * 128
            block = jnp.where(role[0] == layer, mine[at : at + 128, :], other[at : at + 128, :])
            return block.astype(jnp.bfloat16)

        def store(block, value, layer=layer):
            pairs[layer, block * 128 : (block + 1) * 128, :] = value

        pair_kernels(kernel_of, store)
    clear_border(middle)
    clear_border(boards)
    fetch.wait()

    def run_layer(layer, source, emit):
        def step(at, carry):
            first = at * count
            pre = conv_pairs(source, pairs[layer], first, count)
            for parity in range(2):
                part = pre[:, parity * 128 : (parity + 1) * 128].reshape(count, 5, games, 128)
                before = residual(source, first, count, parity).astype(jnp.float32)
                emit(first, parity, (before + jnp.maximum(part, 0.0)).astype(jnp.bfloat16))
            return carry

        lax.fori_loop(0, 10 // count, step, 0, unroll=unroll)

    run_layer(0, boards, lambda first, parity, value: put_cells(middle, first, count, parity, value))

    def to_last(first, parity, value):
        last[pl.ds(first, count), :, parity] = value

    run_layer(1, middle, to_last)
    cells = [last[:, j // 2, j % 2].reshape(-1, 128) for j in range(10)]
    logits = jnp.dot(jnp.concatenate(cells, axis=1), heads[...], preferred_element_type=jnp.float32)
    logits = logits.reshape(10, games, 128)
    lanes = lax.broadcasted_iota(jnp.int32, (games, 128), 1)
    moves = []
    total = jnp.zeros((games, 1), jnp.float32)
    for d in range(4):
        gathered = jnp.zeros((games, 128), jnp.float32)
        for i in range(10):
            turned = pltpu.roll(logits[i], (10 * i - 10 * d) % 128, 1)
            gathered = jnp.where((lanes >= 10 * i) & (lanes < 10 * i + 10), turned, gathered)
        moves.append(gathered)
        total = total + jnp.sum(
            jnp.where(lanes < 100, jnp.exp(gathered), 0.0), axis=1, keepdims=True
        )
    log_total = jnp.log(total)
    for d in range(4):
        out[:, 100 * d : 100 * d + 100] = (moves[d] - log_total)[:, :100]


def act(role, mine, other, boards, heads8, count=2, unroll=1):
    games = boards.shape[2]
    vmem = pl.BlockSpec(memory_space=pltpu.VMEM)
    return pl.pallas_call(
        functools.partial(actor_kernel, count, unroll),
        out_shape=jax.ShapeDtypeStruct((games, 400), jnp.float32),
        in_specs=[
            pl.BlockSpec(memory_space=pltpu.SMEM), vmem, vmem, pl.BlockSpec(memory_space=pltpu.HBM), vmem
        ],
        out_specs=vmem,
        scratch_shapes=[
            pltpu.VMEM((12, 6, 2, games, 128), jnp.bfloat16),
            pltpu.VMEM((2, 1536, 256), jnp.bfloat16),
            pltpu.VMEM((12, 6, 2, games, 128), jnp.bfloat16),
            pltpu.VMEM((10, 5, 2, games, 128), jnp.bfloat16),
            pltpu.VMEM((1280, 128), jnp.bfloat16),
            pltpu.SemaphoreType.DMA,
        ],
        compiler_params=pltpu.CompilerParams(vmem_limit_bytes=32 * 1024 * 1024),
        cost_estimate=pl.CostEstimate(
            flops=8 * 10**9, bytes_accessed=4 * 10**6, transcendentals=30000
        ),
        name="act",
    )(role, mine, other, boards, heads8)


def column_of(row):
    size = row.shape[1]
    across = lax.broadcasted_iota(jnp.int32, (size, size), 1)
    down = lax.broadcasted_iota(jnp.int32, (size, size), 0)
    spread = jnp.broadcast_to(row, (size, size))
    return jnp.sum(jnp.where(across == down, spread, jnp.zeros_like(spread)), axis=1, keepdims=True)


def later(x, reach):
    return jnp.concatenate([x[reach:], jnp.zeros((reach, x.shape[1]), x.dtype)], axis=0)


def learner_kernel(
    count, role, length, boards_in, actions_in, behaviour_in, regular_in, rewards_in, weights_in,
    heads8, grad,
    boards, weights, actions, behaviour, regular, rewards, pairs, back_pairs, middle, last, masks,
    slope, done,
):
    slots = boards.shape[3]
    moves = [
        (weights_in.at[0:ROWS], weights.at[0:ROWS]),
        (boards_in, inner_cells(boards)),
        (weights_in.at[ROWS : 2 * ROWS], weights.at[ROWS : 2 * ROWS]),
        (actions_in, actions),
        (behaviour_in, behaviour),
        (regular_in, regular),
        (rewards_in, rewards),
    ]
    copies = [pltpu.make_async_copy(a, b, done.at[k]) for k, (a, b) in enumerate(moves)]
    for copy in copies:
        copy.start()
    eight = heads8[...].astype(jnp.bfloat16).astype(jnp.float32)
    heads_t = jnp.concatenate(
        [eight, eight, eight, jnp.zeros((104, 128), jnp.float32)], axis=0
    ).astype(jnp.bfloat16)
    clear_border(boards)
    copies[0].wait()

    for layer in range(2):
        if layer == 1:
            copies[2].wait()

        def kernel_of(p, q, layer=layer):
            at = layer * ROWS + (3 * p + q) * 128
            return weights[at : at + 128, :].astype(jnp.bfloat16)

        def store(block, value, layer=layer):
            pairs[layer, block * 128 : (block + 1) * 128, :] = value

        pair_kernels(kernel_of, store)
    clear_border(middle)
    clear_border(slope)
    copies[1].wait()

    def run_layer(layer, source, emit):
        for first in range(0, 10, count):
            pre = conv_pairs(source, pairs[layer], first, count)
            for parity in range(2):
                part = pre[:, parity * 128 : (parity + 1) * 128].reshape(count, 5, slots, 128)
                before = residual(source, first, count, parity).astype(jnp.float32)
                emit(first, parity, (before + jnp.maximum(part, 0.0)).astype(jnp.bfloat16))
                masks[layer, first : first + count, :, parity] = (part > 0).astype(jnp.bfloat16)

    run_layer(0, boards, lambda first, parity, value: put_cells(middle, first, count, parity, value))

    def to_last(first, parity, value):
        last[pl.ds(first, count), :, parity] = value

    run_layer(1, middle, to_last)

    for copy in copies[3:]:
        copy.wait()

    scores = lax.dot_general(
        last[...].reshape(-1, 128), heads_t, (((1,), (1,)), ((), ())),
        preferred_element_type=jnp.float32,
    ).reshape(100, slots, 128)
    lane = lax.broadcasted_iota(jnp.int32, (slots, 128), 1)
    weights_sum = jnp.sum(jnp.where(lane < 4, jnp.exp(scores), 0.0), axis=0)
    log_total = jnp.log(jnp.sum(weights_sum, axis=1, keepdims=True))
    action = column_of(actions[...])
    direction = action // 100
    cell = action - 100 * direction
    cells = lax.broadcasted_iota(jnp.int32, (100, slots, 128), 0)
    taken = (cells == cell[None]) & (lane % 8 == direction)[None]
    picked = jnp.sum(
        jnp.sum(jnp.where(taken & (lane < 4)[None], scores, 0.0), axis=0), axis=1, keepdims=True
    )
    value_sum = jnp.sum(scores, axis=0)
    value = jnp.tanh(
        jnp.sum(jnp.where(lane == 4, value_sum, 0.0), axis=1, keepdims=True) / 100.0
    )
    log_policy = picked - log_total

    positions = lax.broadcasted_iota(jnp.int32, (slots, 1), 0)
    live = (positions < length[0]).astype(jnp.float32)
    next_live = (positions + 1 < length[0]).astype(jnp.float32)
    ratio = jnp.minimum(1.0, jnp.exp(log_policy - column_of(behaviour[...])))
    shaped = column_of(rewards[...]) - ETA * (log_policy - column_of(regular[...]))
    next_values = later(value, 1) * next_live
    correction = live * ratio * (shaped + next_values - value)
    decay = live * ratio
    reach = 1
    while reach < slots:
        correction = correction + decay * later(correction, reach)
        decay = decay * later(decay, reach)
        reach *= 2
    targets = value + correction
    next_targets = later(targets, 1) * next_live
    policy_grad = -live * ratio * (shaped + next_targets - value)
    value_grad = -live * (targets - value)

    value_cell = value_grad * (1.0 - value * value) / 100.0
    by_policy = policy_grad[None] * (taken.astype(jnp.float32) - jnp.exp(scores - log_total[None]))
    in_policy = (lane % 8 < 4) & (lane < 24)
    in_value = (lane % 8 == 4) & (lane < 24)
    by_score = jnp.where(
        in_policy[None], by_policy, jnp.where(in_value, value_cell, 0.0)[None]
    )
    high = by_score.astype(jnp.bfloat16)
    rest = by_score - high.astype(jnp.float32)
    mid = rest.astype(jnp.bfloat16)
    low = rest - mid.astype(jnp.float32)
    parts = jnp.where(
        (lane < 8)[None],
        high.astype(jnp.float32),
        jnp.where((lane < 16)[None], mid.astype(jnp.float32), low),
    ).astype(jnp.bfloat16)
    out_grad = jnp.dot(
        parts.reshape(-1, 128), heads_t, preferred_element_type=jnp.float32
    )
    act_grad = (out_grad * masks[1].reshape(-1, 128).astype(jnp.float32)).astype(jnp.bfloat16)

    def kernel_gradients(source, act_grad):
        turned = act_grad.T
        windows = []
        for p in range(3):
            for q in range(3):
                cols = [source[p : p + 10, (j + q) // 2, (j + q) % 2] for j in range(10)]
                windows.append(jnp.stack(cols, axis=1).reshape(-1, 128))
        for offset in range(9):
            block = jnp.dot(turned, windows[offset], preferred_element_type=jnp.float32)
            grad[offset * 128 : (offset + 1) * 128, :] = block.T

    @pl.when(role[0] == 1)
    def _():
        kernel_gradients(middle, act_grad)

    @pl.when(role[0] == 0)
    def _():
        def kernel_of(p, q):
            at = ROWS + (8 - (3 * p + q)) * 128
            return weights[at : at + 128, :].T.astype(jnp.bfloat16)

        def store(block, value):
            back_pairs[block * 128 : (block + 1) * 128, :] = value

        pair_kernels(kernel_of, store)
        act_cells = act_grad.reshape(10, 5, 2, slots, 128)
        put_cells(slope, 0, 10, 0, act_cells[:, :, 0])
        put_cells(slope, 0, 10, 1, act_cells[:, :, 1])
        out_cells = out_grad.reshape(10, 5, 2, slots, 128)
        for first in range(0, 10, count):
            back = conv_pairs(slope, back_pairs[...], first, count)
            for parity in range(2):
                part = back[:, parity * 128 : (parity + 1) * 128].reshape(count, 5, slots, 128)
                total = out_cells[first : first + count, :, parity] + part
                gate = masks[0, first : first + count, :, parity].astype(jnp.float32)
                last[pl.ds(first, count), :, parity] = (total * gate).astype(jnp.bfloat16)
        kernel_gradients(boards, last[...].reshape(-1, 128))


def head_rows(policy_head, value_head):
    five = jnp.concatenate([policy_head.T, value_head[None]]).astype(jnp.float32)
    return jnp.pad(five, ((0, 3), (0, 0)))


def learn(role, length, boards, actions, behaviour, regular, rewards, weights, heads8, count=5):
    slots = boards.shape[2]
    smem = pl.BlockSpec(memory_space=pltpu.SMEM)
    vmem = pl.BlockSpec(memory_space=pltpu.VMEM)
    anywhere = pl.BlockSpec(memory_space=pltpu.HBM)
    cells = (10, 5, 2, slots, 128)
    around = (12, 6, 2, slots, 128)
    return pl.pallas_call(
        functools.partial(learner_kernel, count),
        out_shape=jax.ShapeDtypeStruct((ROWS, 128), jnp.float32),
        in_specs=[smem, smem] + [anywhere] * 6 + [vmem],
        out_specs=vmem,
        scratch_shapes=[
            pltpu.VMEM(around, jnp.bfloat16),
            pltpu.VMEM((2 * ROWS, 128), jnp.float32),
            pltpu.VMEM((1, slots), jnp.int32),
            pltpu.VMEM((1, slots), jnp.float32),
            pltpu.VMEM((1, slots), jnp.float32),
            pltpu.VMEM((1, slots), jnp.float32),
            pltpu.VMEM((2, 1536, 256), jnp.bfloat16),
            pltpu.VMEM((1536, 256), jnp.bfloat16),
            pltpu.VMEM(around, jnp.bfloat16),
            pltpu.VMEM(cells, jnp.bfloat16),
            pltpu.VMEM((2,) + cells, jnp.bfloat16),
            pltpu.VMEM(around, jnp.bfloat16),
            pltpu.SemaphoreType.DMA((7,)),
        ],
        compiler_params=pltpu.CompilerParams(vmem_limit_bytes=60 * 1024 * 1024),
        cost_estimate=pl.CostEstimate(
            flops=4 * 10**9, bytes_accessed=3 * 10**6, transcendentals=10000
        ),
        name="learn",
    )(role, length, boards, actions, behaviour, regular, rewards, weights, heads8)


PLANES = [[LINE * k + z for k in range(LINE * LINE)] for z in range(LINE)]


def shifted_z(x, step):
    pairs = [(d, d - d % LINE + (d + step) % LINE) for d in range(LINE**3)]
    return lax.ppermute(x, "dp", pairs)


def line_total(x):
    return (x + shifted_z(x, 2)) + (shifted_z(x, 1) + shifted_z(x, 3))


def plane_exchange(x):
    return lax.all_to_all(x, "dp", 0, 0, axis_index_groups=PLANES)


def plane_gather(x):
    return plane_exchange(jnp.broadcast_to(x, (LINE * LINE,) + x.shape))


def role_swap(x):
    return lax.ppermute(x, "role", [(0, 1), (1, 0)])


def share_moments(first_moment, second_moment, z):
    both = jnp.stack([first_moment, second_moment])
    got = []
    for k in range(2):
        pairs = []
        for role in range(2):
            for d in range(LINE**3):
                z_of = d % LINE
                owner = 32 * role + 2 * (d // LINE) + (k + z_of) % 2
                pairs.append(((z_of // 2) * LINE**3 + owner, role * LINE**3 + d))
        got.append(lax.ppermute(both, ("role", "dp"), pairs))
    even = z % 2 == 0
    low = jnp.where(even, got[0], got[1])
    high = jnp.where(even, got[1], got[0])
    return jnp.concatenate([low, high], axis=1)


def body(
    board_now,
    traj_boards,
    actions,
    lengths,
    behaviour,
    regular,
    rewards,
    torso,
    policy_head,
    value_head,
    first_moment,
    second_moment,
):
    role = lax.axis_index("role")
    dp = lax.axis_index("dp")
    role_box = jnp.full((1,), role, jnp.int32)
    heads8 = head_rows(policy_head, value_head)
    moments = share_moments(first_moment, second_moment, dp % LINE)
    gradient = learn(
        role_box,
        lengths,
        by_cell(traj_boards[0]),
        actions,
        behaviour,
        regular,
        rewards,
        torso,
        heads8,
    )
    share = jnp.sum(plane_exchange(gradient.reshape(LINE * LINE, SHARE, 128)), axis=0)
    share = line_total(share)
    squares = jnp.sum(share * share, axis=0, keepdims=True)
    squares = plane_gather(squares + role_swap(squares))
    square_sum = jnp.sum(squares)
    factor = jnp.minimum(1.0, jnp.sqrt(float(torso.size)) / jnp.sqrt(square_sum + NORM_EPS))
    clipped = share * factor
    moment_one = BETA_ONE * moments[0] + (1.0 - BETA_ONE) * clipped
    moment_two = BETA_TWO * moments[1] + (1.0 - BETA_TWO) * clipped * clipped
    old_share = lax.dynamic_slice_in_dim(torso, role * ROWS + dp // LINE * SHARE, SHARE, 0)
    weight_share = old_share - LEARN_RATE * moment_one / (jnp.sqrt(moment_two) + ADAM_EPS)
    mine = plane_gather(weight_share).reshape(ROWS, 128)
    other = role_swap(mine)
    move_logp = act(role_box, mine, other, by_cell(board_now), heads8)
    out_rows = first_moment.shape[0]
    layer = dp // (LINE**3 // 2)
    at = dp % (LINE**3 // 2) * out_rows
    new_share = jnp.where(
        role == layer,
        lax.dynamic_slice_in_dim(mine, at, out_rows, 0),
        lax.dynamic_slice_in_dim(other, at, out_rows, 0),
    )
    return (new_share, move_logp)


def solution(mesh):
    return jax.shard_map(
        body,
        mesh=mesh,
        in_specs=(
            P("dp", None, None, None),
            P("dp", None, None, None, None),
            P("dp", None),
            P("dp"),
            P("dp", None),
            P("dp", None),
            P("dp", None),
            P(),
            P(),
            P(),
            P("dp", None),
            P("dp", None),
        ),
        out_specs=(P("dp", None), P("dp", None)),
        check_vma=False,
    )
```

time: 377 us -> 84.7 us (0.22)
  waiting for transfers between devices: 219 us -> 9.02 us
  matrix products: 60.7 us -> 0 us
  local copies, waits for them, and re-layouts: 38.8 us -> 0.67 us
  loops' own time: 31.8 us -> 0 us
  blocking collectives: 0 us -> 31.2 us
  starting transfers between devices: 0.12 us -> 21.6 us
  Pallas kernels: 0 us -> 16.2 us
  between operations: 14.7 us -> 2.12 us
  other arithmetic: 11.1 us -> 3.42 us
    psum x2 -> x0, waiting for transfers between devices: 156 us -> none  [the longest x1 131 us: body(): summed = lax.psum(gradient, 'dp')]
    all_gather x1 -> x0, waiting for transfers between devices: 62.5 us -> none  [body(): gathered = lax.all_gather(weight_share, 'dp', axis=0, tiled=True)]
    dot_general x63 -> x0, matrix products: 59.9 us -> none  [the longest x35 38.6 us: conv_sum(): jnp.dot(window, kernel[offset], preferred_element_type=jnp.float32)]
    another operation x2 -> x0, loops' own time: 31.8 us -> none  [the longest x1 31.1 us: vee_trace_cotangents(): lax.scan(backward_step, jnp.zeros((), jnp.float32), (deltas, clipped_rati...]
    dynamic_slice x49 -> x0, local copies, waits for them, and re-layouts: 31.6 us -> none  [the longest x48 30.2 us: vee_trace_cotangents(): lax.scan(backward_step, jnp.zeros((), jnp.float32), (deltas, clipped_rati...]
    all_to_all x0 -> x2, blocking collectives: none -> 31.2 us  [plane_exchange(): return lax.all_to_all(x, 'dp', 0, 0, axis_index_groups=PLANES)]
    ppermute x0 -> x7, starting transfers between devices: none -> 17 us  [the longest x2 7.63 us: share_moments(): got.append(lax.ppermute(both, ('role', 'dp'), pairs))]
    pallas_call x0 -> x2, Pallas kernels: none -> 16.2 us  [the longest x1 9.07 us: act(): pl.pallas_call(functools.partial(actor_kernel, count, unroll), out_shape=...]
  transfers between devices with their start and end apart: 3 -> 8, of which waited for: 3 -> 3; matrix products, arithmetic and copies ran while one was open for 0% -> 1% of each run, Pallas kernels for 0% -> 0%
where the time goes in v2:
time: 84.7 us; the launch traced here: 84.2 us
  blocking collectives  31.2 us (37%)
  starting transfers between devices  21.6 us (26%)
  Pallas kernels  16.2 us (19%)
  waiting for transfers between devices  9.02 us (11%)
  other arithmetic  3.42 us (4%)
  between operations  2.12 us (3%)
    all_to_all x2, blocking collectives, plane_exchange(): return lax.all_to_all(x, 'dp', 0, 0, axis_index_groups=PLANES)  31.2 us
    pallas_call x1, Pallas kernels, act(): pl.pallas_call(functools.partial(actor_kernel, count, unroll), out_shape=...  9.07 us
    ppermute x2, starting transfers between devices, share_moments(): got.append(lax.ppermute(both, ('role', 'dp'), pairs))  7.63 us
    pallas_call x1, Pallas kernels, learn(): pl.pallas_call(functools.partial(learner_kernel, count), out_shape=jax.Sh...  7.14 us
    ppermute x3, starting transfers between devices, shifted_z(): return lax.ppermute(x, 'dp', pairs)  6.35 us
    all_to_all x1, waiting for transfers between devices, plane_exchange(): return lax.all_to_all(x, 'dp', 0, 0, axis_index_groups=PLANES)  6.29 us
    all_to_all x1, starting transfers between devices, plane_exchange(): return lax.all_to_all(x, 'dp', 0, 0, axis_index_groups=PLANES)  4.61 us
    ppermute x2, starting transfers between devices, role_swap(): return lax.ppermute(x, 'role', [(0, 1), (1, 0)])  2.97 us
  transfers between devices with their start and end apart: 8, of which 3 were waited for; matrix products, arithmetic and copies ran while one was open for 1% of the time, Pallas kernels for 0%

profile of v2, /device:TPU:1, one launch (start us, length us, event | category | flops | bytes accessed | tf_op | source)
XLA Modules:
  0.0 84.2 jit_solution(4659979338005887073)
XLA Ops:
  1.3 1.3 %fusion.15.heads8 = f32[8,128]{1,0:T(8,128)} fusion(bf16[1,128]{1,0:T(2,128)(2,1)} %bitcast.38, bf16[4,128]{1,0:T(4,128)(2,1)} %bitcast.36), kind=kLoop, calls=%fused_computation.26 | loop fusion | flops 7168 | bytes 5376 | tf_op jit(solution)/shard_map/jit(_pad)/pad | solution.py:340
  2.6 7.1 %learn.1 = f32[1152,128]{1,0:T(8,128)} custom-call(s32[1]{0:T(128)} %bitcast.3.role, s32[1]{0:T(128)S(6)} %copy.15.length, bf16[10,10,16,128]{3,2,1,0:T(8,128)(2,1)} %bitcast.39, s32[1,16]{1,0:T(1,128)} %actions_in.1, f32[1,16]{1,0:T(1,128)} %behaviour_in.1, f32[1,16]{1,0:T(1,128)} %regular_in.1, f32[1,16]{1,0:T(1,128)} %rewards_in.1, ...), custom_call_target="tpu_custom_call" | custom-call | flops 4000000000 | bytes 3000000 | tf_op jit(solution)/shard_map/learn/pallas_call | solution.py:350
  9.7 0.0 copy-start.2
  9.7 0.0 copy-start.3
  9.7 18.1 %all_to_all.15 = f32[16,72,128]{2,1,0:T(8,128)S(1)} all-to-all(f32[16,72,128]{2,1,0:T(8,128)} %bitcast.32), channel_id=1, replica_groups={{0,4,8,12,16,20,24,28,32,36,40,44,48,52,56,60},{1,5,9,13,17,21,25,29,33..., dimensions={0} | all-to-all | bytes 1179648 | tf_op jit(solution)/shard_map/all_to_all | solution.py:391
  27.9 3.7 %collective-permute-start.2 = (f32[72,128]{1,0:T(8,128)S(1)}, f32[72,128]{1,0:T(8,128)S(1)}, u32[]{:S(2)}, u32[]{:S(2)}) collective-permute-start(f32[72,128]{1,0:T(8,128)S(1)} %reduce_sum.27), channel_id=1, source_target_pairs={{0,2},{1,3},{2,0},{3,1},{4,6},{5,7},{6,4},{7,5},{8,10},{9,11},{10,... | collective-permute-start | bytes 110600 | tf_op jit(solution)/shard_map/ppermute | solution.py:383
  31.6 0.7 collective-permute-start.3
  32.3 1.9 %collective-permute-start.4 = (f32[72,128]{1,0:T(8,128)S(1)}, f32[72,128]{1,0:T(8,128)S(1)}, u32[]{:S(2)}, u32[]{:S(2)}) collective-permute-start(f32[72,128]{1,0:T(8,128)S(1)} %reduce_sum.27), channel_id=1, source_target_pairs={{0,3},{1,0},{2,1},{3,2},{4,7},{5,4},{6,5},{7,6},{8,11},{9,8},{10,9... | collective-permute-start | bytes 110600 | tf_op jit(solution)/shard_map/ppermute | solution.py:383
  34.3 0.0 copy-done.2
  34.3 0.0 copy-done.3
  34.3 4.9 %collective-permute-start = (f32[2,36,128]{2,1,0:T(8,128)S(1)}, f32[2,36,128]{2,1,0:T(8,128)S(1)}, u32[]{:S(2)}, u32[]{:S(2)}) collective-permute-start(f32[2,36,128]{2,1,0:T(8,128)S(1)} %pad_maximum_fusion), channel_id=1, source_target_pairs={{0,0},{1,1},{64,2},{65,3},{2,4},{3,5},{66,6},{67,7},{4,8},{5,9},{6... | collective-permute-start | bytes 110600 | tf_op jit(solution)/shard_map/ppermute | solution.py:412
  39.2 2.7 %collective-permute-start.1 = (f32[2,36,128]{2,1,0:T(8,128)S(1)}, f32[2,36,128]{2,1,0:T(8,128)S(1)}, u32[]{:S(2)}, u32[]{:S(2)}) collective-permute-start(f32[2,36,128]{2,1,0:T(8,128)S(1)} %pad_maximum_fusion), channel_id=1, source_target_pairs={{1,0},{0,1},{65,2},{64,3},{3,4},{2,5},{67,6},{66,7},{5,8},{4,9},{6... | collective-permute-start | bytes 110600 | tf_op jit(solution)/shard_map/ppermute | solution.py:412
  41.9 0.0 collective-permute-done.2
  41.9 0.0 collective-permute-done.3
  41.9 0.0 collective-permute-done.4
  42.0 0.0 copy-start.1
  42.0 0.1 collective-permute-start.5
  42.1 1.1 %collective-permute-done.5 = f32[1,128]{1,0:T(1,128)S(1)} collective-permute-done((f32[1,128]{1,0:T(1,128)S(1)}, f32[1,128]{1,0:T(1,128)S(1)}, u32[]{:S(2)}, u32[]{:S(2)}) %collective-permute-start.5) | collective-permute-done | bytes 544 | tf_op jit(solution)/shard_map/ppermute | solution.py:399
  43.2 0.6 broadcast_in_dim.18
  43.8 4.6 %all-to-all-start.1 = ((f32[16,1,128]{2,1,0:T(1,128)}), f32[16,1,128]{2,1,0:T(1,128)S(1)}, u32[]{:S(2)}, u32[]{:S(2)}) async-start(f32[16,1,128]{2,1,0:T(1,128)} %broadcast_in_dim.18), calls=%async_computation.1 | async-start | bytes 16384 | tf_op jit(solution)/shard_map/all_to_all | solution.py:391
  48.4 0.0 collective-permute-done
  48.4 0.0 collective-permute-done.1
  48.5 6.3 %all-to-all-done.1 = f32[16,1,128]{2,1,0:T(1,128)S(1)} async-done(((f32[16,1,128]{2,1,0:T(1,128)}), f32[16,1,128]{2,1,0:T(1,128)S(1)}, u32[]{:S(2)}, u32[]{:S(2)}) %all-to-all-start.1) | async-done | bytes 8224 | tf_op jit(solution)/shard_map/all_to_all | solution.py:391
  54.8 0.6 reduce_sum.29
  56.1 0.8 fusion.4
  56.9 13.0 %all_to_all.16 = f32[16,72,128]{2,1,0:T(8,128)S(1)} all-to-all(f32[16,72,128]{2,1,0:T(8,128)S(1)} %broadcast_in_dim.19), channel_id=1, replica_groups={{0,4,8,12,16,20,24,28,32,36,40,44,48,52,56,60},{1,5,9,13,17,21,25,29,33..., dimensions={0} | all-to-all | bytes 1179648 | tf_op jit(solution)/shard_map/all_to_all | solution.py:391
  70.0 2.9 %collective-permute-start.6 = (f32[1152,128]{1,0:T(8,128)S(1)}, f32[1152,128]{1,0:T(8,128)S(1)}, u32[]{:S(2)}, u32[]{:S(2)}) collective-permute-start(f32[1152,128]{1,0:T(8,128)S(1)} %bitcast.28), channel_id=1, source_target_pairs={{0,64},{64,0},{1,65},{65,1},{2,66},{66,2},{3,67},{67,3},{4,68},{68... | collective-permute-start | bytes 1769480 | tf_op jit(solution)/shard_map/ppermute | solution.py:399
  72.8 1.6 %collective-permute-done.6.other = f32[1152,128]{1,0:T(8,128)S(1)} collective-permute-done((f32[1152,128]{1,0:T(8,128)S(1)}, f32[1152,128]{1,0:T(8,128)S(1)}, u32[]{:S(2)}, u32[]{:S(2)}) %collective-permute-start.6) | collective-permute-done | bytes 589856 | tf_op jit(solution)/shard_map/ppermute | solution.py:399
  74.5 0.0 copy-done
  74.5 0.0 copy-done.1
  74.5 9.1 %act.1 = f32[64,400]{1,0:T(8,128)} custom-call(s32[1]{0:T(128)} %bitcast.3.role, f32[1152,128]{1,0:T(8,128)S(1)} %bitcast.29, f32[1152,128]{1,0:T(8,128)S(1)} %collective-permute-done.6.other, bf16[10,10,64,128]{3,2,1,0:T(8,128)(2,1)S(1)} %bitcast.31, f32[8,128]{1,0:T(8,128)S(1)} %copy-done), custom_call_target="tpu_custom_call" | custom-call | flops 8000000000 | bytes 4000000 | tf_op jit(solution)/shard_map/act/pallas_call | solution.py:143
  83.6 0.6 dynamic-slice_select_fusion
  (7 shorter events, 0.1 us)
Async XLA Ops:
  9.7 24.6 %copy-start.2 = (f32[36,128]{1,0:T(8,128)S(1)}, f32[36,128]{1,0:T(8,128)}, u32[]{:S(2)}) copy-start(f32[36,128]{1,0:T(8,128)} %param.23) | copy-start | bytes 55300
  9.7 24.6 %copy-start.3 = (f32[36,128]{1,0:T(8,128)S(1)}, f32[36,128]{1,0:T(8,128)}, u32[]{:S(2)}) copy-start(f32[36,128]{1,0:T(8,128)} %param.22) | copy-start | bytes 55300
  27.9 14.0 %collective-permute-start.2 = (f32[72,128]{1,0:T(8,128)S(1)}, f32[72,128]{1,0:T(8,128)S(1)}, u32[]{:S(2)}, u32[]{:S(2)}) collective-permute-start(f32[72,128]{1,0:T(8,128)S(1)} %reduce_sum.27), channel_id=1, source_target_pairs={{0,2},{1,3},{2,0},{3,1},{4,6},{5,7},{6,4},{7,5},{8,10},{9,11},{10,... | collective-permute-start | bytes 110600 | tf_op jit(solution)/shard_map/ppermute | solution.py:383
  31.6 10.3 %collective-permute-start.3 = (f32[72,128]{1,0:T(8,128)S(1)}, f32[72,128]{1,0:T(8,128)S(1)}, u32[]{:S(2)}, u32[]{:S(2)}) collective-permute-start(f32[72,128]{1,0:T(8,128)S(1)} %reduce_sum.27), channel_id=1, source_target_pairs={{0,1},{1,2},{2,3},{3,0},{4,5},{5,6},{6,7},{7,4},{8,9},{9,10},{10,1... | collective-permute-start | bytes 110600 | tf_op jit(solution)/shard_map/ppermute | solution.py:383
  32.3 9.6 %collective-permute-start.4 = (f32[72,128]{1,0:T(8,128)S(1)}, f32[72,128]{1,0:T(8,128)S(1)}, u32[]{:S(2)}, u32[]{:S(2)}) collective-permute-start(f32[72,128]{1,0:T(8,128)S(1)} %reduce_sum.27), channel_id=1, source_target_pairs={{0,3},{1,0},{2,1},{3,2},{4,7},{5,4},{6,5},{7,6},{8,11},{9,8},{10,9... | collective-permute-start | bytes 110600 | tf_op jit(solution)/shard_map/ppermute | solution.py:383
  34.3 14.1 %collective-permute-start = (f32[2,36,128]{2,1,0:T(8,128)S(1)}, f32[2,36,128]{2,1,0:T(8,128)S(1)}, u32[]{:S(2)}, u32[]{:S(2)}) collective-permute-start(f32[2,36,128]{2,1,0:T(8,128)S(1)} %pad_maximum_fusion), channel_id=1, source_target_pairs={{0,0},{1,1},{64,2},{65,3},{2,4},{3,5},{66,6},{67,7},{4,8},{5,9},{6... | collective-permute-start | bytes 110600 | tf_op jit(solution)/shard_map/ppermute | solution.py:412
  39.2 9.2 %collective-permute-start.1 = (f32[2,36,128]{2,1,0:T(8,128)S(1)}, f32[2,36,128]{2,1,0:T(8,128)S(1)}, u32[]{:S(2)}, u32[]{:S(2)}) collective-permute-start(f32[2,36,128]{2,1,0:T(8,128)S(1)} %pad_maximum_fusion), channel_id=1, source_target_pairs={{1,0},{0,1},{65,2},{64,3},{3,4},{2,5},{67,6},{66,7},{5,8},{4,9},{6... | collective-permute-start | bytes 110600 | tf_op jit(solution)/shard_map/ppermute | solution.py:412
  42.0 32.5 %copy-start = (f32[8,128]{1,0:T(8,128)S(1)}, f32[8,128]{1,0:T(8,128)}, u32[]{:S(2)}) copy-start(f32[8,128]{1,0:T(8,128)} %fusion.15.heads8) | copy-start | bytes 12292
  42.0 32.5 %copy-start.1 = (bf16[64,10,10,128]{3,0,2,1:T(8,128)(2,1)S(1)}, bf16[64,10,10,128]{3,0,2,1:T(8,128)(2,1)}, u32[]{:S(2)}) copy-start(bf16[64,10,10,128]{3,0,2,1:T(8,128)(2,1)} %param.12) | copy-start | bytes 4915204
  42.0 1.2 %collective-permute-start.5 = (f32[1,128]{1,0:T(1,128)S(1)}, f32[1,128]{1,0:T(1,128)S(1)}, u32[]{:S(2)}, u32[]{:S(2)}) collective-permute-start(f32[1,128]{1,0:T(1,128)S(1)} %bitcast.37), channel_id=1, source_target_pairs={{0,64},{64,0},{1,65},{65,1},{2,66},{66,2},{3,67},{67,3},{4,68},{68... | collective-permute-start | bytes 1544 | tf_op jit(solution)/shard_map/ppermute | solution.py:399
  43.8 10.9 %all-to-all-start.1 = ((f32[16,1,128]{2,1,0:T(1,128)}), f32[16,1,128]{2,1,0:T(1,128)S(1)}, u32[]{:S(2)}, u32[]{:S(2)}) async-start(f32[16,1,128]{2,1,0:T(1,128)} %broadcast_in_dim.18), calls=%async_computation.1 | async-start | bytes 16384 | tf_op jit(solution)/shard_map/all_to_all | solution.py:391
  70.0 4.5 %collective-permute-start.6 = (f32[1152,128]{1,0:T(8,128)S(1)}, f32[1152,128]{1,0:T(8,128)S(1)}, u32[]{:S(2)}, u32[]{:S(2)}) collective-permute-start(f32[1152,128]{1,0:T(8,128)S(1)} %bitcast.28), channel_id=1, source_target_pairs={{0,64},{64,0},{1,65},{65,1},{2,66},{66,2},{3,67},{67,3},{4,68},{68... | collective-permute-start | bytes 1769480 | tf_op jit(solution)/shard_map/ppermute | solution.py:399

commit v3 on v2

--- a/solution.py
+++ b/solution.py
@@ -446,18 +446,22 @@
         torso,
         heads8,
     )
+    moments = lax.all_gather(moments, "dp", axis_index_groups=PLANES)
     share = jnp.sum(plane_exchange(gradient.reshape(LINE * LINE, SHARE, 128)), axis=0)
     share = line_total(share)
     squares = jnp.sum(share * share, axis=0, keepdims=True)
-    squares = plane_gather(squares + role_swap(squares))
-    square_sum = jnp.sum(squares)
+    squares = squares + role_swap(squares)
+    gathered = plane_gather(jnp.concatenate([share, jnp.pad(squares, ((0, 7), (0, 0)))]))
+    summed = gathered[:, :SHARE].reshape(ROWS, 128)
+    square_sum = jnp.sum(gathered[:, SHARE])
     factor = jnp.minimum(1.0, jnp.sqrt(float(torso.size)) / jnp.sqrt(square_sum + NORM_EPS))
-    clipped = share * factor
-    moment_one = BETA_ONE * moments[0] + (1.0 - BETA_ONE) * clipped
-    moment_two = BETA_TWO * moments[1] + (1.0 - BETA_TWO) * clipped * clipped
-    old_share = lax.dynamic_slice_in_dim(torso, role * ROWS + dp // LINE * SHARE, SHARE, 0)
-    weight_share = old_share - LEARN_RATE * moment_one / (jnp.sqrt(moment_two) + ADAM_EPS)
-    mine = plane_gather(weight_share).reshape(ROWS, 128)
+    clipped = summed * factor
+    first = moments[:, 0].reshape(ROWS, 128)
+    second = moments[:, 1].reshape(ROWS, 128)
+    moment_one = BETA_ONE * first + (1.0 - BETA_ONE) * clipped
+    moment_two = BETA_TWO * second + (1.0 - BETA_TWO) * clipped * clipped
+    old = lax.dynamic_slice_in_dim(torso, role * ROWS, ROWS, 0)
+    mine = old - LEARN_RATE * moment_one / (jnp.sqrt(moment_two) + ADAM_EPS)
     other = role_swap(mine)
     move_logp = act(role_box, mine, other, by_cell(board_now), heads8)
     out_rows = first_moment.shape[0]

time: 84.7 us -> 100 us (1.18)
  between operations: 2.12 us -> 15.5 us
  waiting for transfers between devices: 9.02 us -> 21.3 us
  blocking collectives: 31.2 us -> 22.8 us
  starting transfers between devices: 21.6 us -> 17.1 us
  other arithmetic: 3.42 us -> 5.91 us
    all_to_all x2 -> x1, blocking collectives: 31.2 us -> 22.8 us  [plane_exchange(): return lax.all_to_all(x, 'dp', 0, 0, axis_index_groups=PLANES)]
    all_to_all x1, waiting for transfers between devices: 6.29 us -> 12.4 us  [plane_exchange(): return lax.all_to_all(x, 'dp', 0, 0, axis_index_groups=PLANES)]
    ppermute x3, starting transfers between devices: 6.35 us -> 1.53 us  [shifted_z(): return lax.ppermute(x, 'dp', pairs)]
    ppermute x3, waiting for transfers between devices: 0.01 us -> 4.31 us  [shifted_z(): return lax.ppermute(x, 'dp', pairs)]
    ppermute x2, waiting for transfers between devices: 0.01 us -> 2.08 us  [share_moments(): got.append(lax.ppermute(both, ('role', 'dp'), pairs))]
    mul x0 -> x2, other arithmetic: none -> 1.49 us  [the longest x1 1.45 us: body(): moment_one = BETA_ONE * first + (1.0 - BETA_ONE) * clipped]
    ppermute x2, starting transfers between devices: 2.97 us -> 4.02 us  [role_swap(): return lax.ppermute(x, 'role', [(0, 1), (1, 0)])]
    all_to_all x1, starting transfers between devices: 4.61 us -> 3.59 us  [plane_exchange(): return lax.all_to_all(x, 'dp', 0, 0, axis_index_groups=PLANES)]
  transfers between devices with their start and end apart: 8 -> 9, of which waited for: 3 -> 7; matrix products, arithmetic and copies ran while one was open for 1% -> 3% of each run, Pallas kernels for 0% -> 7%
where the time goes in v3:
time: 100 us
  blocking collectives  22.8 us (23%)
  waiting for transfers between devices  21.3 us (21%)
  starting transfers between devices  17.1 us (17%)
  Pallas kernels  16.2 us (16%)
  between operations  15.5 us (16%)
  other arithmetic  5.91 us (6%)
  local copies, waits for them, and re-layouts  1.1 us (1%)
    all_to_all x1, blocking collectives, plane_exchange(): return lax.all_to_all(x, 'dp', 0, 0, axis_index_groups=PLANES)  22.8 us
    all_to_all x1, waiting for transfers between devices, plane_exchange(): return lax.all_to_all(x, 'dp', 0, 0, axis_index_groups=PLANES)  12.4 us
    pallas_call x1, Pallas kernels, act(): pl.pallas_call(functools.partial(actor_kernel, count, unroll), out_shape=...  9.08 us
    ppermute x2, starting transfers between devices, share_moments(): got.append(lax.ppermute(both, ('role', 'dp'), pairs))  7.92 us
    pallas_call x1, Pallas kernels, learn(): pl.pallas_call(functools.partial(learner_kernel, count), out_shape=jax.Sh...  7.16 us
    ppermute x3, waiting for transfers between devices, shifted_z(): return lax.ppermute(x, 'dp', pairs)  4.31 us
    ppermute x2, starting transfers between devices, role_swap(): return lax.ppermute(x, 'role', [(0, 1), (1, 0)])  4.02 us
    all_to_all x1, starting transfers between devices, plane_exchange(): return lax.all_to_all(x, 'dp', 0, 0, axis_index_groups=PLANES)  3.59 us
  transfers between devices with their start and end apart: 9, of which 7 were waited for; matrix products, arithmetic and copies ran while one was open for 3% of the time, Pallas kernels for 7%

profile of v3, /device:TPU:1, one launch (start us, length us, event | category | flops | bytes accessed | tf_op | source)
XLA Modules:
  0.0 100.0 jit_solution(18410929274113475917)
XLA Ops:
  7.2 0.0 all-gather.3.cloned.1.call-start
  7.2 0.8 pad_maximum_fusion.1
  8.0 5.1 %collective-permute-start.1 = (f32[2,36,128]{2,1,0:T(8,128)S(1)}, f32[2,36,128]{2,1,0:T(8,128)S(1)}, u32[]{:S(2)}, u32[]{:S(2)}) collective-permute-start(f32[2,36,128]{2,1,0:T(8,128)S(1)} %pad_maximum_fusion.1), channel_id=1, source_target_pairs={{1,0},{0,1},{65,2},{64,3},{3,4},{2,5},{67,6},{66,7},{5,8},{4,9},{6... | collective-permute-start | bytes 110600 | tf_op jit(solution)/shard_map/ppermute | solution.py:412
  13.1 2.8 %collective-permute-start = (f32[2,36,128]{2,1,0:T(8,128)S(1)}, f32[2,36,128]{2,1,0:T(8,128)S(1)}, u32[]{:S(2)}, u32[]{:S(2)}) collective-permute-start(f32[2,36,128]{2,1,0:T(8,128)S(1)} %pad_maximum_fusion.1), channel_id=1, source_target_pairs={{0,0},{1,1},{64,2},{65,3},{2,4},{3,5},{66,6},{67,7},{4,8},{5,9},{6... | collective-permute-start | bytes 110600 | tf_op jit(solution)/shard_map/ppermute | solution.py:412
  15.9 1.3 %fusion.12.heads8 = f32[8,128]{1,0:T(8,128)} fusion(bf16[1,128]{1,0:T(2,128)(2,1)} %bitcast.41, bf16[4,128]{1,0:T(4,128)(2,1)} %bitcast.39), kind=kLoop, calls=%fused_computation.28 | loop fusion | flops 7168 | bytes 5376 | tf_op jit(solution)/shard_map/jit(_pad)/pad | solution.py:340
  17.8 0.0 collective-permute-done.1
  17.8 2.1 %collective-permute-done = f32[2,36,128]{2,1,0:T(8,128)S(1)} collective-permute-done((f32[2,36,128]{2,1,0:T(8,128)S(1)}, f32[2,36,128]{2,1,0:T(8,128)S(1)}, u32[]{:S(2)}, u32[]{:S(2)}) %collective-permute-start) | collective-permute-done | bytes 36896 | tf_op jit(solution)/shard_map/ppermute | solution.py:412
  19.9 0.6 pad_maximum_fusion
  20.6 0.0 all-gather.3.cloned.1.call-update
  20.6 7.2 %learn.1 = f32[1152,128]{1,0:T(8,128)} custom-call(s32[1]{0:T(128)} %bitcast.4.role, s32[1]{0:T(128)S(6)} %copy.20.length, bf16[10,10,16,128]{3,2,1,0:T(8,128)(2,1)} %bitcast.42, s32[1,16]{1,0:T(1,128)} %actions_in.1, f32[1,16]{1,0:T(1,128)} %behaviour_in.1, f32[1,16]{1,0:T(1,128)} %regular_in.1, f32[1,16]{1,0:T(1,128)} %rewards_in.1, ...), custom_call_target="tpu_custom_call" | custom-call | flops 4000000000 | bytes 3000000 | tf_op jit(solution)/shard_map/learn/pallas_call | solution.py:350
  27.8 22.8 %all_to_all.10 = f32[16,72,128]{2,1,0:T(8,128)S(1)} all-to-all(f32[16,72,128]{2,1,0:T(8,128)} %bitcast.36), channel_id=1, replica_groups={{0,4,8,12,16,20,24,28,32,36,40,44,48,52,56,60},{1,5,9,13,17,21,25,29,33..., dimensions={0} | all-to-all | bytes 1179648 | tf_op jit(solution)/shard_map/all_to_all | solution.py:391
  50.6 0.1 collective-permute-start.4
  50.7 1.5 %collective-permute-start.3 = (f32[72,128]{1,0:T(8,128)S(1)}, f32[72,128]{1,0:T(8,128)S(1)}, u32[]{:S(2)}, u32[]{:S(2)}) collective-permute-start(f32[72,128]{1,0:T(8,128)S(1)} %reduce_sum.27), channel_id=1, source_target_pairs={{0,1},{1,2},{2,3},{3,0},{4,5},{5,6},{6,7},{7,4},{8,9},{9,10},{10,1... | collective-permute-start | bytes 110600 | tf_op jit(solution)/shard_map/ppermute | solution.py:383
  52.2 0.0 collective-permute-start.2
  52.2 1.3 %collective-permute-done.4 = f32[72,128]{1,0:T(8,128)S(1)} collective-permute-done((f32[72,128]{1,0:T(8,128)S(1)}, f32[72,128]{1,0:T(8,128)S(1)}, u32[]{:S(2)}, u32[]{:S(2)}) %collective-permute-start.4) | collective-permute-done | bytes 36896 | tf_op jit(solution)/shard_map/ppermute | solution.py:383
  53.5 1.3 %collective-permute-done.3 = f32[72,128]{1,0:T(8,128)S(1)} collective-permute-done((f32[72,128]{1,0:T(8,128)S(1)}, f32[72,128]{1,0:T(8,128)S(1)}, u32[]{:S(2)}, u32[]{:S(2)}) %collective-permute-start.3) | collective-permute-done | bytes 36896 | tf_op jit(solution)/shard_map/ppermute | solution.py:383
  54.8 1.7 %collective-permute-done.2 = f32[72,128]{1,0:T(8,128)S(1)} collective-permute-done((f32[72,128]{1,0:T(8,128)S(1)}, f32[72,128]{1,0:T(8,128)S(1)}, u32[]{:S(2)}, u32[]{:S(2)}) %collective-permute-start.2) | collective-permute-done | bytes 36896 | tf_op jit(solution)/shard_map/ppermute | solution.py:383
  56.5 2.5 %collective-permute-start.5 = (f32[1,128]{1,0:T(1,128)S(1)}, f32[1,128]{1,0:T(1,128)S(1)}, u32[]{:S(2)}, u32[]{:S(2)}) collective-permute-start(f32[1,128]{1,0:T(1,128)S(1)} %bitcast.40), channel_id=1, source_target_pairs={{0,64},{64,0},{1,65},{65,1},{2,66},{66,2},{3,67},{67,3},{4,68},{68... | collective-permute-start | bytes 1544 | tf_op jit(solution)/shard_map/ppermute | solution.py:399
  59.0 0.8 collective-permute-done.5
  59.9 0.9 broadcast_in_dim.15
  60.8 3.6 %all-to-all-start.1 = ((f32[16,80,128]{2,1,0:T(8,128)}), f32[16,80,128]{2,1,0:T(8,128)S(1)}, u32[]{:S(2)}, u32[]{:S(2)}) async-start(f32[16,80,128]{2,1,0:T(8,128)} %broadcast_in_dim.15), calls=%async_computation.1 | async-start | bytes 1310720 | tf_op jit(solution)/shard_map/all_to_all | solution.py:391
  64.4 12.4 %all-to-all-done.1 = f32[16,80,128]{2,1,0:T(8,128)S(1)} async-done(((f32[16,80,128]{2,1,0:T(8,128)}), f32[16,80,128]{2,1,0:T(8,128)S(1)}, u32[]{:S(2)}, u32[]{:S(2)}) %all-to-all-start.1) | async-done | bytes 655392 | tf_op jit(solution)/shard_map/all_to_all | solution.py:391
  76.8 0.7 slice_reduce_fusion
  78.3 0.0 all-gather.3.cloned.1.call-done
  78.3 0.0 copy-start.2
  78.3 1.4 %fusion.6 = (f32[16,1,72,128]{3,2,0,1:T(8,128)S(1)}, f32[16,1,72,128]{3,2,0,1:T(8,128)S(1)}) fusion(f32[16,2,72,128]{3,2,1,0:T(8,128)} %bitcast.35), kind=kLoop, calls=%fused_computation.10 | loop fusion | flops 294912 | bytes 2359296 | tf_op jit(solution)/shard_map/mul | solution.py:461
  79.8 0.2 copy-done.2
  80.0 0.3 fusion.4.mine
  80.3 1.5 %collective-permute-start.6 = (f32[1152,128]{1,0:T(8,128)S(1)}, f32[1152,128]{1,0:T(8,128)S(1)}, u32[]{:S(2)}, u32[]{:S(2)}) collective-permute-start(f32[1152,128]{1,0:T(8,128)S(1)} %fusion.4.mine), channel_id=1, source_target_pairs={{0,64},{64,0},{1,65},{65,1},{2,66},{66,2},{3,67},{67,3},{4,68},{68... | collective-permute-start | bytes 1769480 | tf_op jit(solution)/shard_map/ppermute | solution.py:399
  81.8 1.6 %collective-permute-done.6.other = f32[1152,128]{1,0:T(8,128)S(1)} collective-permute-done((f32[1152,128]{1,0:T(8,128)S(1)}, f32[1152,128]{1,0:T(8,128)S(1)}, u32[]{:S(2)}, u32[]{:S(2)}) %collective-permute-start.6) | collective-permute-done | bytes 589856 | tf_op jit(solution)/shard_map/ppermute | solution.py:399
  83.4 9.1 %act.1 = f32[64,400]{1,0:T(8,128)} custom-call(s32[1]{0:T(128)} %bitcast.4.role, f32[1152,128]{1,0:T(8,128)S(1)} %fusion.4.mine, f32[1152,128]{1,0:T(8,128)S(1)} %collective-permute-done.6.other, bf16[10,10,64,128]{3,2,1,0:T(8,128)(2,1)S(1)} %bitcast.34, f32[8,128]{1,0:T(8,128)S(1)} %copy-done), custom_call_target="tpu_custom_call" | custom-call | flops 8000000000 | bytes 4000000 | tf_op jit(solution)/shard_map/act/pallas_call | solution.py:143
  92.5 0.6 dynamic-slice_select_fusion
  (10 shorter events, 0.1 us)
Async XLA Ops:
  7.2 71.2 %all-gather.3.cloned.1.call-start = ((), (), s32[]{:S(2)}) async-start(), calls=%async_computation.2 | async-start | bytes 1253376 | tf_op jit(solution)/shard_map/all_gather | solution.py:449
  8.0 9.9 %collective-permute-start.1 = (f32[2,36,128]{2,1,0:T(8,128)S(1)}, f32[2,36,128]{2,1,0:T(8,128)S(1)}, u32[]{:S(2)}, u32[]{:S(2)}) collective-permute-start(f32[2,36,128]{2,1,0:T(8,128)S(1)} %pad_maximum_fusion.1), channel_id=1, source_target_pairs={{1,0},{0,1},{65,2},{64,3},{3,4},{2,5},{67,6},{66,7},{5,8},{4,9},{6... | collective-permute-start | bytes 110600 | tf_op jit(solution)/shard_map/ppermute | solution.py:412
  13.1 6.8 %collective-permute-start = (f32[2,36,128]{2,1,0:T(8,128)S(1)}, f32[2,36,128]{2,1,0:T(8,128)S(1)}, u32[]{:S(2)}, u32[]{:S(2)}) collective-permute-start(f32[2,36,128]{2,1,0:T(8,128)S(1)} %pad_maximum_fusion.1), channel_id=1, source_target_pairs={{0,0},{1,1},{64,2},{65,3},{2,4},{3,5},{66,6},{67,7},{4,8},{5,9},{6... | collective-permute-start | bytes 110600 | tf_op jit(solution)/shard_map/ppermute | solution.py:412
  50.6 2.9 %collective-permute-start.4 = (f32[72,128]{1,0:T(8,128)S(1)}, f32[72,128]{1,0:T(8,128)S(1)}, u32[]{:S(2)}, u32[]{:S(2)}) collective-permute-start(f32[72,128]{1,0:T(8,128)S(1)} %reduce_sum.27), channel_id=1, source_target_pairs={{0,3},{1,0},{2,1},{3,2},{4,7},{5,4},{6,5},{7,6},{8,11},{9,8},{10,9... | collective-permute-start | bytes 110600 | tf_op jit(solution)/shard_map/ppermute | solution.py:383
  50.7 4.1 %collective-permute-start.3 = (f32[72,128]{1,0:T(8,128)S(1)}, f32[72,128]{1,0:T(8,128)S(1)}, u32[]{:S(2)}, u32[]{:S(2)}) collective-permute-start(f32[72,128]{1,0:T(8,128)S(1)} %reduce_sum.27), channel_id=1, source_target_pairs={{0,1},{1,2},{2,3},{3,0},{4,5},{5,6},{6,7},{7,4},{8,9},{9,10},{10,1... | collective-permute-start | bytes 110600 | tf_op jit(solution)/shard_map/ppermute | solution.py:383
  52.2 4.3 %collective-permute-start.2 = (f32[72,128]{1,0:T(8,128)S(1)}, f32[72,128]{1,0:T(8,128)S(1)}, u32[]{:S(2)}, u32[]{:S(2)}) collective-permute-start(f32[72,128]{1,0:T(8,128)S(1)} %reduce_sum.27), channel_id=1, source_target_pairs={{0,2},{1,3},{2,0},{3,1},{4,6},{5,7},{6,4},{7,5},{8,10},{9,11},{10,... | collective-permute-start | bytes 110600 | tf_op jit(solution)/shard_map/ppermute | solution.py:383
  56.5 3.4 %collective-permute-start.5 = (f32[1,128]{1,0:T(1,128)S(1)}, f32[1,128]{1,0:T(1,128)S(1)}, u32[]{:S(2)}, u32[]{:S(2)}) collective-permute-start(f32[1,128]{1,0:T(1,128)S(1)} %bitcast.40), channel_id=1, source_target_pairs={{0,64},{64,0},{1,65},{65,1},{2,66},{66,2},{3,67},{67,3},{4,68},{68... | collective-permute-start | bytes 1544 | tf_op jit(solution)/shard_map/ppermute | solution.py:399
  60.8 16.0 %all-to-all-start.1 = ((f32[16,80,128]{2,1,0:T(8,128)}), f32[16,80,128]{2,1,0:T(8,128)S(1)}, u32[]{:S(2)}, u32[]{:S(2)}) async-start(f32[16,80,128]{2,1,0:T(8,128)} %broadcast_in_dim.15), calls=%async_computation.1 | async-start | bytes 1310720 | tf_op jit(solution)/shard_map/all_to_all | solution.py:391
  78.3 1.6 %copy-start.2 = (f32[2304,128]{1,0:T(8,128)S(1)}, f32[2304,128]{1,0:T(8,128)}, u32[]{:S(2)}) copy-start(f32[2304,128]{1,0:T(8,128)} %weights_in.1) | copy-start | bytes 3538948
  80.0 3.5 %copy-start = (f32[8,128]{1,0:T(8,128)S(1)}, f32[8,128]{1,0:T(8,128)}, u32[]{:S(2)}) copy-start(f32[8,128]{1,0:T(8,128)} %fusion.12.heads8) | copy-start | bytes 12292
  80.0 3.5 %copy-start.1 = (bf16[64,10,10,128]{3,0,2,1:T(8,128)(2,1)S(1)}, bf16[64,10,10,128]{3,0,2,1:T(8,128)(2,1)}, u32[]{:S(2)}) copy-start(bf16[64,10,10,128]{3,0,2,1:T(8,128)(2,1)} %param.12) | copy-start | bytes 4915204
  80.3 3.1 %collective-permute-start.6 = (f32[1152,128]{1,0:T(8,128)S(1)}, f32[1152,128]{1,0:T(8,128)S(1)}, u32[]{:S(2)}, u32[]{:S(2)}) collective-permute-start(f32[1152,128]{1,0:T(8,128)S(1)} %fusion.4.mine), channel_id=1, source_target_pairs={{0,64},{64,0},{1,65},{65,1},{2,66},{66,2},{3,67},{67,3},{4,68},{68... | collective-permute-start | bytes 1769480 | tf_op jit(solution)/shard_map/ppermute | solution.py:399
Sparse Core Ops, SparseCore 0:
  20.7 46.5 all-gather.2

commit v4 on v2

--- a/solution.py
+++ b/solution.py
@@ -75,7 +75,8 @@
     count, unroll, role, mine, other, boards_in, heads8, out, boards, pairs, middle, last, heads, done
 ):
     games = boards.shape[3]
-    fetch = pltpu.make_async_copy(boards_in, inner_cells(boards), done)
+    half = pl.ds(pl.multiple_of(role[0] * games, games), games)
+    fetch = pltpu.make_async_copy(boards_in.at[:, :, half], inner_cells(boards), done)
     fetch.start()
     spread = lax.broadcasted_iota(jnp.int32, (8, 1280), 1)
     row = lax.broadcasted_iota(jnp.int32, (8, 1280), 0)
@@ -138,7 +139,7 @@
 
 
 def act(role, mine, other, boards, heads8, count=2, unroll=1):
-    games = boards.shape[2]
+    games = boards.shape[2] // 2
     vmem = pl.BlockSpec(memory_space=pltpu.VMEM)
     return pl.pallas_call(
         functools.partial(actor_kernel, count, unroll),
@@ -378,13 +379,17 @@
 PLANES = [[LINE * k + z for k in range(LINE * LINE)] for z in range(LINE)]
 
 
-def shifted_z(x, step):
-    pairs = [(d, d - d % LINE + (d + step) % LINE) for d in range(LINE**3)]
+def shifted(x, axis, step):
+    stride = {"y": LINE * LINE, "x": LINE, "z": 1}[axis]
+    pairs = []
+    for d in range(LINE**3):
+        at = d // stride % LINE
+        pairs.append((d, d + ((at + step) % LINE - at) * stride))
     return lax.ppermute(x, "dp", pairs)
 
 
-def line_total(x):
-    return (x + shifted_z(x, 2)) + (shifted_z(x, 1) + shifted_z(x, 3))
+def line_total(x, axis):
+    return (x + shifted(x, axis, 2)) + (shifted(x, axis, 1) + shifted(x, axis, 3))
 
 
 def plane_exchange(x):
@@ -399,21 +404,28 @@
     return lax.ppermute(x, "role", [(0, 1), (1, 0)])
 
 
-def share_moments(first_moment, second_moment, z):
-    both = jnp.stack([first_moment, second_moment])
-    got = []
-    for k in range(2):
-        pairs = []
-        for role in range(2):
-            for d in range(LINE**3):
-                z_of = d % LINE
-                owner = 32 * role + 2 * (d // LINE) + (k + z_of) % 2
-                pairs.append(((z_of // 2) * LINE**3 + owner, role * LINE**3 + d))
-        got.append(lax.ppermute(both, ("role", "dp"), pairs))
-    even = z % 2 == 0
-    low = jnp.where(even, got[0], got[1])
-    high = jnp.where(even, got[1], got[0])
-    return jnp.concatenate([low, high], axis=1)
+def half_moments(first_moment, second_moment):
+    pairs = []
+    for role in range(2):
+        for d in range(LINE**3):
+            z = d % LINE
+            owner = 32 * role + 2 * (d // LINE) + z % 2
+            pairs.append(((z // 2) * LINE**3 + owner, role * LINE**3 + d))
+    both = jnp.concatenate([first_moment, second_moment])
+    return lax.ppermute(both, ("role", "dp"), pairs)
+
+
+def line_exchange(share, half, z):
+    near = shifted(jnp.concatenate([share, half]), "z", 1)
+    total = (share + shifted(share, "z", 2)) + (near[:SHARE] + shifted(share, "z", 3))
+    rows = SHARE // 2
+    low = jnp.where(z % 2 == 0, half, near[SHARE:])
+    high = jnp.where(z % 2 == 0, near[SHARE:], half)
+    return (
+        total,
+        jnp.concatenate([low[:rows], high[:rows]]),
+        jnp.concatenate([low[rows:], high[rows:]]),
+    )
 
 
 def body(
@@ -434,7 +446,7 @@
     dp = lax.axis_index("dp")
     role_box = jnp.full((1,), role, jnp.int32)
     heads8 = head_rows(policy_head, value_head)
-    moments = share_moments(first_moment, second_moment, dp % LINE)
+    half = half_moments(first_moment, second_moment)
     gradient = learn(
         role_box,
         lengths,
@@ -447,19 +459,21 @@
         heads8,
     )
     share = jnp.sum(plane_exchange(gradient.reshape(LINE * LINE, SHARE, 128)), axis=0)
-    share = line_total(share)
+    share, first, second = line_exchange(share, half, dp % LINE)
     squares = jnp.sum(share * share, axis=0, keepdims=True)
-    squares = plane_gather(squares + role_swap(squares))
+    squares = squares + role_swap(squares)
+    squares = line_total(line_total(squares, "x"), "y")
     square_sum = jnp.sum(squares)
     factor = jnp.minimum(1.0, jnp.sqrt(float(torso.size)) / jnp.sqrt(square_sum + NORM_EPS))
     clipped = share * factor
-    moment_one = BETA_ONE * moments[0] + (1.0 - BETA_ONE) * clipped
-    moment_two = BETA_TWO * moments[1] + (1.0 - BETA_TWO) * clipped * clipped
+    moment_one = BETA_ONE * first + (1.0 - BETA_ONE) * clipped
+    moment_two = BETA_TWO * second + (1.0 - BETA_TWO) * clipped * clipped
     old_share = lax.dynamic_slice_in_dim(torso, role * ROWS + dp // LINE * SHARE, SHARE, 0)
     weight_share = old_share - LEARN_RATE * moment_one / (jnp.sqrt(moment_two) + ADAM_EPS)
     mine = plane_gather(weight_share).reshape(ROWS, 128)
     other = role_swap(mine)
-    move_logp = act(role_box, mine, other, by_cell(board_now), heads8)
+    here = act(role_box, mine, other, by_cell(board_now), heads8)
+    there = role_swap(here)
     out_rows = first_moment.shape[0]
     layer = dp // (LINE**3 // 2)
     at = dp % (LINE**3 // 2) * out_rows
@@ -468,6 +482,7 @@
         lax.dynamic_slice_in_dim(mine, at, out_rows, 0),
         lax.dynamic_slice_in_dim(other, at, out_rows, 0),
     )
+    move_logp = jnp.concatenate([jnp.where(role == 0, here, there), jnp.where(role == 0, there, here)])
     return (new_share, move_logp)
 
 

time: 84.7 us -> 83.7 us (0.988)
  blocking collectives: 31.2 us -> 12.1 us
  starting transfers between devices: 21.6 us -> 35.6 us
  waiting for transfers between devices: 9.02 us -> 16.8 us
  Pallas kernels: 16.2 us -> 12.7 us
    all_to_all x2 -> x1, blocking collectives: 31.2 us -> 12.1 us  [plane_exchange(): return lax.all_to_all(x, 'dp', 0, 0, axis_index_groups=PLANES)]
    ppermute x5 -> x10, waiting for transfers between devices: 0.01 us -> 10.7 us  [the longest x9 9 us: shifted(): return lax.ppermute(x, 'dp', pairs)]
    ppermute x2 -> x3, starting transfers between devices: 2.97 us -> 9.18 us  [role_swap(): return lax.ppermute(x, 'role', [(0, 1), (1, 0)])]
    ppermute x5 -> x10, starting transfers between devices: 14 us -> 18.8 us  [the longest x9 11.6 us: shifted(): return lax.ppermute(x, 'dp', pairs)]
    pallas_call x1, Pallas kernels: 9.07 us -> 5.54 us  [act(): pl.pallas_call(functools.partial(actor_kernel, count, unroll), out_shape=...]
    all_to_all x1, starting transfers between devices: 4.61 us -> 7.59 us  [plane_exchange(): return lax.all_to_all(x, 'dp', 0, 0, axis_index_groups=PLANES)]
    all_to_all x1, waiting for transfers between devices: 6.29 us -> 3.33 us  [plane_exchange(): return lax.all_to_all(x, 'dp', 0, 0, axis_index_groups=PLANES)]
    ppermute x2 -> x3, waiting for transfers between devices: 2.72 us -> 2.74 us  [role_swap(): return lax.ppermute(x, 'role', [(0, 1), (1, 0)])]
  transfers between devices with their start and end apart: 8 -> 14, of which waited for: 3 -> 10; matrix products, arithmetic and copies ran while one was open for 1% -> 1% of each run, Pallas kernels for 0% -> 0%
where the time goes in v4:
time: 83.7 us; the launch traced here: 83.3 us
  starting transfers between devices  35.6 us (43%)
  waiting for transfers between devices  16.8 us (20%)
  Pallas kernels  12.7 us (15%)
  blocking collectives  12.1 us (14%)
  other arithmetic  4.11 us (5%)
  between operations  2.01 us (2%)
    all_to_all x1, blocking collectives, plane_exchange(): return lax.all_to_all(x, 'dp', 0, 0, axis_index_groups=PLANES)  12.1 us
    ppermute x9, starting transfers between devices, shifted(): return lax.ppermute(x, 'dp', pairs)  11.6 us
    ppermute x3, starting transfers between devices, role_swap(): return lax.ppermute(x, 'role', [(0, 1), (1, 0)])  9.18 us
    ppermute x9, waiting for transfers between devices, shifted(): return lax.ppermute(x, 'dp', pairs)  9 us
    all_to_all x1, starting transfers between devices, plane_exchange(): return lax.all_to_all(x, 'dp', 0, 0, axis_index_groups=PLANES)  7.59 us
    ppermute x1, starting transfers between devices, half_moments(): return lax.ppermute(both, ('role', 'dp'), pairs)  7.23 us
    pallas_call x1, Pallas kernels, learn(): pl.pallas_call(functools.partial(learner_kernel, count), out_shape=jax.Sh...  7.13 us
    pallas_call x1, Pallas kernels, act(): pl.pallas_call(functools.partial(actor_kernel, count, unroll), out_shape=...  5.54 us
  transfers between devices with their start and end apart: 14, of which 10 were waited for; matrix products, arithmetic and copies ran while one was open for 1% of the time, Pallas kernels for 0%

profile of v4, /device:TPU:1, one launch (start us, length us, event | category | flops | bytes accessed | tf_op | source)
XLA Modules:
  0.0 83.3 jit_solution(8678065815065023295)
XLA Ops:
  1.3 1.3 %fusion.11.heads8 = f32[8,128]{1,0:T(8,128)} fusion(bf16[1,128]{1,0:T(2,128)(2,1)} %bitcast.18, bf16[4,128]{1,0:T(4,128)(2,1)} %bitcast.16), kind=kLoop, calls=%fused_computation.25 | loop fusion | flops 7168 | bytes 5376 | tf_op jit(solution)/shard_map/jit(_pad)/pad | solution.py:341
  2.6 7.1 %learn.1 = f32[1152,128]{1,0:T(8,128)} custom-call(s32[1]{0:T(128)} %bitcast.role, s32[1]{0:T(128)S(6)} %copy.14.length, bf16[10,10,16,128]{3,2,1,0:T(8,128)(2,1)} %bitcast.19, s32[1,16]{1,0:T(1,128)} %actions_in.1, f32[1,16]{1,0:T(1,128)} %behaviour_in.1, f32[1,16]{1,0:T(1,128)} %regular_in.1, f32[1,16]{1,0:T(1,128)} %rewards_in.1, f32[2304,128]{1,0:T(8,128)} %weights_in.1, ...), custom_call_target="tpu_custom_call" | custom-call | flops 4000000000 | bytes 3000000 | tf_op jit(solution)/shard_map/learn/pallas_call | solution.py:351
  9.7 7.6 %all-to-all-start = ((f32[16,72,128]{2,1,0:T(8,128)}), f32[16,72,128]{2,1,0:T(8,128)S(1)}, u32[]{:S(2)}, u32[]{:S(2)}) async-start(f32[16,72,128]{2,1,0:T(8,128)} %bitcast.15), calls=%async_computation | async-start | bytes 1179648 | tf_op jit(solution)/shard_map/all_to_all | solution.py:396
  17.4 7.2 %collective-permute-start = (f32[72,128]{1,0:T(8,128)S(1)}, f32[72,128]{1,0:T(8,128)S(1)}, u32[]{:S(2)}, u32[]{:S(2)}) collective-permute-start(f32[72,128]{1,0:T(8,128)S(1)} %pad_maximum_fusion.2), channel_id=1, source_target_pairs={{0,0},{1,1},{64,2},{65,3},{2,4},{3,5},{66,6},{67,7},{4,8},{5,9},{6... | collective-permute-start | bytes 110600 | tf_op jit(solution)/shard_map/ppermute | solution.py:415
  24.6 3.3 %all-to-all-done = f32[16,72,128]{2,1,0:T(8,128)S(1)} async-done(((f32[16,72,128]{2,1,0:T(8,128)}), f32[16,72,128]{2,1,0:T(8,128)S(1)}, u32[]{:S(2)}, u32[]{:S(2)}) %all-to-all-start) | async-done | bytes 589856 | tf_op jit(solution)/shard_map/all_to_all | solution.py:396
  28.0 1.7 %collective-permute-done = f32[72,128]{1,0:T(8,128)S(1)} collective-permute-done((f32[72,128]{1,0:T(8,128)S(1)}, f32[72,128]{1,0:T(8,128)S(1)}, u32[]{:S(2)}, u32[]{:S(2)}) %collective-permute-start) | collective-permute-done | bytes 36896 | tf_op jit(solution)/shard_map/ppermute | solution.py:415
  29.7 1.6 %collective-permute-start.1 = (f32[144,128]{1,0:T(8,128)S(1)}, f32[144,128]{1,0:T(8,128)S(1)}, u32[]{:S(2)}, u32[]{:S(2)}) collective-permute-start(f32[144,128]{1,0:T(8,128)S(1)} %pad_maximum_fusion.1), channel_id=1, source_target_pairs={{0,1},{1,2},{2,3},{3,0},{4,5},{5,6},{6,7},{7,4},{8,9},{9,10},{10,1... | collective-permute-start | bytes 221192 | tf_op jit(solution)/shard_map/ppermute | solution.py:388
  31.3 1.0 %collective-permute-start.3 = (f32[72,128]{1,0:T(8,128)S(1)}, f32[72,128]{1,0:T(8,128)S(1)}, u32[]{:S(2)}, u32[]{:S(2)}) collective-permute-start(f32[72,128]{1,0:T(8,128)S(1)} %reduce_sum.27), channel_id=1, source_target_pairs={{0,3},{1,0},{2,1},{3,2},{4,7},{5,4},{6,5},{7,6},{8,11},{9,8},{10,9... | collective-permute-start | bytes 110600 | tf_op jit(solution)/shard_map/ppermute | solution.py:388
  32.4 1.4 %collective-permute-start.2 = (f32[72,128]{1,0:T(8,128)S(1)}, f32[72,128]{1,0:T(8,128)S(1)}, u32[]{:S(2)}, u32[]{:S(2)}) collective-permute-start(f32[72,128]{1,0:T(8,128)S(1)} %reduce_sum.27), channel_id=1, source_target_pairs={{0,2},{1,3},{2,0},{3,1},{4,6},{5,7},{6,4},{7,5},{8,10},{9,11},{10,... | collective-permute-start | bytes 110600 | tf_op jit(solution)/shard_map/ppermute | solution.py:388
  33.8 0.4 collective-permute-done.3
  34.2 2.6 %collective-permute-done.2 = f32[72,128]{1,0:T(8,128)S(1)} collective-permute-done((f32[72,128]{1,0:T(8,128)S(1)}, f32[72,128]{1,0:T(8,128)S(1)}, u32[]{:S(2)}, u32[]{:S(2)}) %collective-permute-start.2) | collective-permute-done | bytes 36896 | tf_op jit(solution)/shard_map/ppermute | solution.py:388
  36.9 3.6 %collective-permute-start.4 = (f32[1,128]{1,0:T(1,128)S(1)}, f32[1,128]{1,0:T(1,128)S(1)}, u32[]{:S(2)}, u32[]{:S(2)}) collective-permute-start(f32[1,128]{1,0:T(1,128)S(1)} %bitcast.17), channel_id=1, source_target_pairs={{0,64},{64,0},{1,65},{65,1},{2,66},{66,2},{3,67},{67,3},{4,68},{68... | collective-permute-start | bytes 1544 | tf_op jit(solution)/shard_map/ppermute | solution.py:404
  40.4 0.8 collective-permute-done.4
  41.3 0.8 collective-permute-start.6
  42.0 1.9 %collective-permute-start.7 = (f32[1,128]{1,0:T(1,128)S(1)}, f32[1,128]{1,0:T(1,128)S(1)}, u32[]{:S(2)}, u32[]{:S(2)}) collective-permute-start(f32[1,128]{1,0:T(1,128)S(1)} %bitcast_add_fusion), channel_id=1, source_target_pairs={{0,12},{1,13},{2,14},{3,15},{4,0},{5,1},{6,2},{7,3},{8,4},{9,5},{1... | collective-permute-start | bytes 1544 | tf_op jit(solution)/shard_map/ppermute | solution.py:388
  43.9 0.7 collective-permute-start.5
  44.6 0.2 collective-permute-done.6
  44.9 3.0 %collective-permute-done.5 = f32[1,128]{1,0:T(1,128)S(1)} collective-permute-done((f32[1,128]{1,0:T(1,128)S(1)}, f32[1,128]{1,0:T(1,128)S(1)}, u32[]{:S(2)}, u32[]{:S(2)}) %collective-permute-start.5) | collective-permute-done | bytes 544 | tf_op jit(solution)/shard_map/ppermute | solution.py:388
  47.8 0.2 collective-permute-start.9
  48.1 2.8 %collective-permute-start.10 = (f32[1,128]{1,0:T(1,128)S(1)}, f32[1,128]{1,0:T(1,128)S(1)}, u32[]{:S(2)}, u32[]{:S(2)}) collective-permute-start(f32[1,128]{1,0:T(1,128)S(1)} %add_add_fusion), channel_id=1, source_target_pairs={{0,48},{1,49},{2,50},{3,51},{4,52},{5,53},{6,54},{7,55},{8,56},{9,... | collective-permute-start | bytes 1544 | tf_op jit(solution)/shard_map/ppermute | solution.py:388
  50.9 1.1 %collective-permute-start.8 = (f32[1,128]{1,0:T(1,128)S(1)}, f32[1,128]{1,0:T(1,128)S(1)}, u32[]{:S(2)}, u32[]{:S(2)}) collective-permute-start(f32[1,128]{1,0:T(1,128)S(1)} %add_add_fusion), channel_id=1, source_target_pairs={{0,32},{1,33},{2,34},{3,35},{4,36},{5,37},{6,38},{7,39},{8,40},{9,... | collective-permute-start | bytes 1544 | tf_op jit(solution)/shard_map/ppermute | solution.py:388
  52.0 2.8 %collective-permute-done.8 = f32[1,128]{1,0:T(1,128)S(1)} collective-permute-done((f32[1,128]{1,0:T(1,128)S(1)}, f32[1,128]{1,0:T(1,128)S(1)}, u32[]{:S(2)}, u32[]{:S(2)}) %collective-permute-start.8) | collective-permute-done | bytes 544 | tf_op jit(solution)/shard_map/ppermute | solution.py:388
  54.8 0.6 add_reduce_fusion
  56.0 0.8 fusion.4
  56.8 12.1 %all_to_all.10 = f32[16,72,128]{2,1,0:T(8,128)S(1)} all-to-all(f32[16,72,128]{2,1,0:T(8,128)S(1)} %broadcast_in_dim.15), channel_id=1, replica_groups={{0,4,8,12,16,20,24,28,32,36,40,44,48,52,56,60},{1,5,9,13,17,21,25,29,33..., dimensions={0} | all-to-all | bytes 1179648 | tf_op jit(solution)/shard_map/all_to_all | solution.py:396
  68.9 5.1 %collective-permute-start.11 = (f32[1152,128]{1,0:T(8,128)S(1)}, f32[1152,128]{1,0:T(8,128)S(1)}, u32[]{:S(2)}, u32[]{:S(2)}) collective-permute-start(f32[1152,128]{1,0:T(8,128)S(1)} %bitcast.11), channel_id=1, source_target_pairs={{0,64},{64,0},{1,65},{65,1},{2,66},{66,2},{3,67},{67,3},{4,68},{68... | collective-permute-start | bytes 1769480 | tf_op jit(solution)/shard_map/ppermute | solution.py:404
  74.1 1.6 %collective-permute-done.11.other = f32[1152,128]{1,0:T(8,128)S(1)} collective-permute-done((f32[1152,128]{1,0:T(8,128)S(1)}, f32[1152,128]{1,0:T(8,128)S(1)}, u32[]{:S(2)}, u32[]{:S(2)}) %collective-permute-start.11) | collective-permute-done | bytes 589856 | tf_op jit(solution)/shard_map/ppermute | solution.py:404
  75.7 5.5 %act.1 = f32[32,400]{1,0:T(8,128)S(1)} custom-call(s32[1]{0:T(128)} %bitcast.role, f32[1152,128]{1,0:T(8,128)S(1)} %bitcast.12, f32[1152,128]{1,0:T(8,128)S(1)} %collective-permute-done.11.other, bf16[10,10,64,128]{3,2,1,0:T(8,128)(2,1)S(1)} %bitcast.14, f32[8,128]{1,0:T(8,128)S(1)} %copy-done), custom_call_target="tpu_custom_call" | custom-call | flops 8000000000 | bytes 4000000 | tf_op jit(solution)/shard_map/act/pallas_call | solution.py:144
  81.2 0.5 collective-permute-start.12
  81.7 0.6 dynamic-slice_select_fusion
  82.3 0.3 collective-permute-done.12
  82.6 0.7 pad_maximum_fusion
  (21 shorter events, 0.2 us)
Async XLA Ops:
  9.7 7.6 %copy-start.2 = (f32[36,128]{1,0:T(8,128)S(1)}, f32[36,128]{1,0:T(8,128)}, u32[]{:S(2)}) copy-start(f32[36,128]{1,0:T(8,128)} %param.23) | copy-start | bytes 55300
  9.7 7.6 %copy-start.3 = (f32[36,128]{1,0:T(8,128)S(1)}, f32[36,128]{1,0:T(8,128)}, u32[]{:S(2)}) copy-start(f32[36,128]{1,0:T(8,128)} %param.22) | copy-start | bytes 55300
  9.7 18.2 %all-to-all-start = ((f32[16,72,128]{2,1,0:T(8,128)}), f32[16,72,128]{2,1,0:T(8,128)S(1)}, u32[]{:S(2)}, u32[]{:S(2)}) async-start(f32[16,72,128]{2,1,0:T(8,128)} %bitcast.15), calls=%async_computation | async-start | bytes 1179648 | tf_op jit(solution)/shard_map/all_to_all | solution.py:396
  17.4 12.3 %collective-permute-start = (f32[72,128]{1,0:T(8,128)S(1)}, f32[72,128]{1,0:T(8,128)S(1)}, u32[]{:S(2)}, u32[]{:S(2)}) collective-permute-start(f32[72,128]{1,0:T(8,128)S(1)} %pad_maximum_fusion.2), channel_id=1, source_target_pairs={{0,0},{1,1},{64,2},{65,3},{2,4},{3,5},{66,6},{67,7},{4,8},{5,9},{6... | collective-permute-start | bytes 110600 | tf_op jit(solution)/shard_map/ppermute | solution.py:415
  29.7 7.1 %collective-permute-start.1 = (f32[144,128]{1,0:T(8,128)S(1)}, f32[144,128]{1,0:T(8,128)S(1)}, u32[]{:S(2)}, u32[]{:S(2)}) collective-permute-start(f32[144,128]{1,0:T(8,128)S(1)} %pad_maximum_fusion.1), channel_id=1, source_target_pairs={{0,1},{1,2},{2,3},{3,0},{4,5},{5,6},{6,7},{7,4},{8,9},{9,10},{10,1... | collective-permute-start | bytes 221192 | tf_op jit(solution)/shard_map/ppermute | solution.py:388
  31.3 2.8 %collective-permute-start.3 = (f32[72,128]{1,0:T(8,128)S(1)}, f32[72,128]{1,0:T(8,128)S(1)}, u32[]{:S(2)}, u32[]{:S(2)}) collective-permute-start(f32[72,128]{1,0:T(8,128)S(1)} %reduce_sum.27), channel_id=1, source_target_pairs={{0,3},{1,0},{2,1},{3,2},{4,7},{5,4},{6,5},{7,6},{8,11},{9,8},{10,9... | collective-permute-start | bytes 110600 | tf_op jit(solution)/shard_map/ppermute | solution.py:388
  32.4 4.4 %collective-permute-start.2 = (f32[72,128]{1,0:T(8,128)S(1)}, f32[72,128]{1,0:T(8,128)S(1)}, u32[]{:S(2)}, u32[]{:S(2)}) collective-permute-start(f32[72,128]{1,0:T(8,128)S(1)} %reduce_sum.27), channel_id=1, source_target_pairs={{0,2},{1,3},{2,0},{3,1},{4,6},{5,7},{6,4},{7,5},{8,10},{9,11},{10,... | collective-permute-start | bytes 110600 | tf_op jit(solution)/shard_map/ppermute | solution.py:388
  36.8 38.9 %copy-start = (f32[8,128]{1,0:T(8,128)S(1)}, f32[8,128]{1,0:T(8,128)}, u32[]{:S(2)}) copy-start(f32[8,128]{1,0:T(8,128)} %fusion.11.heads8) | copy-start | bytes 12292
  36.8 38.9 %copy-start.1 = (bf16[64,10,10,128]{3,0,2,1:T(8,128)(2,1)S(1)}, bf16[64,10,10,128]{3,0,2,1:T(8,128)(2,1)}, u32[]{:S(2)}) copy-start(bf16[64,10,10,128]{3,0,2,1:T(8,128)(2,1)} %param.12) | copy-start | bytes 4915204
  36.9 4.4 %collective-permute-start.4 = (f32[1,128]{1,0:T(1,128)S(1)}, f32[1,128]{1,0:T(1,128)S(1)}, u32[]{:S(2)}, u32[]{:S(2)}) collective-permute-start(f32[1,128]{1,0:T(1,128)S(1)} %bitcast.17), channel_id=1, source_target_pairs={{0,64},{64,0},{1,65},{65,1},{2,66},{66,2},{3,67},{67,3},{4,68},{68... | collective-permute-start | bytes 1544 | tf_op jit(solution)/shard_map/ppermute | solution.py:404
  41.3 3.6 %collective-permute-start.6 = (f32[1,128]{1,0:T(1,128)S(1)}, f32[1,128]{1,0:T(1,128)S(1)}, u32[]{:S(2)}, u32[]{:S(2)}) collective-permute-start(f32[1,128]{1,0:T(1,128)S(1)} %bitcast_add_fusion), channel_id=1, source_target_pairs={{0,4},{1,5},{2,6},{3,7},{4,8},{5,9},{6,10},{7,11},{8,12},{9,13},{1... | collective-permute-start | bytes 1544 | tf_op jit(solution)/shard_map/ppermute | solution.py:388
  42.0 2.8 %collective-permute-start.7 = (f32[1,128]{1,0:T(1,128)S(1)}, f32[1,128]{1,0:T(1,128)S(1)}, u32[]{:S(2)}, u32[]{:S(2)}) collective-permute-start(f32[1,128]{1,0:T(1,128)S(1)} %bitcast_add_fusion), channel_id=1, source_target_pairs={{0,12},{1,13},{2,14},{3,15},{4,0},{5,1},{6,2},{7,3},{8,4},{9,5},{1... | collective-permute-start | bytes 1544 | tf_op jit(solution)/shard_map/ppermute | solution.py:388
  43.9 3.9 %collective-permute-start.5 = (f32[1,128]{1,0:T(1,128)S(1)}, f32[1,128]{1,0:T(1,128)S(1)}, u32[]{:S(2)}, u32[]{:S(2)}) collective-permute-start(f32[1,128]{1,0:T(1,128)S(1)} %bitcast_add_fusion), channel_id=1, source_target_pairs={{0,8},{1,9},{2,10},{3,11},{4,12},{5,13},{6,14},{7,15},{8,0},{9,1},... | collective-permute-start | bytes 1544 | tf_op jit(solution)/shard_map/ppermute | solution.py:388
  47.8 4.2 %collective-permute-start.9 = (f32[1,128]{1,0:T(1,128)S(1)}, f32[1,128]{1,0:T(1,128)S(1)}, u32[]{:S(2)}, u32[]{:S(2)}) collective-permute-start(f32[1,128]{1,0:T(1,128)S(1)} %add_add_fusion), channel_id=1, source_target_pairs={{0,16},{1,17},{2,18},{3,19},{4,20},{5,21},{6,22},{7,23},{8,24},{9,... | collective-permute-start | bytes 1544 | tf_op jit(solution)/shard_map/ppermute | solution.py:388
  48.1 3.9 %collective-permute-start.10 = (f32[1,128]{1,0:T(1,128)S(1)}, f32[1,128]{1,0:T(1,128)S(1)}, u32[]{:S(2)}, u32[]{:S(2)}) collective-permute-start(f32[1,128]{1,0:T(1,128)S(1)} %add_add_fusion), channel_id=1, source_target_pairs={{0,48},{1,49},{2,50},{3,51},{4,52},{5,53},{6,54},{7,55},{8,56},{9,... | collective-permute-start | bytes 1544 | tf_op jit(solution)/shard_map/ppermute | solution.py:388
  50.9 3.9 %collective-permute-start.8 = (f32[1,128]{1,0:T(1,128)S(1)}, f32[1,128]{1,0:T(1,128)S(1)}, u32[]{:S(2)}, u32[]{:S(2)}) collective-permute-start(f32[1,128]{1,0:T(1,128)S(1)} %add_add_fusion), channel_id=1, source_target_pairs={{0,32},{1,33},{2,34},{3,35},{4,36},{5,37},{6,38},{7,39},{8,40},{9,... | collective-permute-start | bytes 1544 | tf_op jit(solution)/shard_map/ppermute | solution.py:388
  68.9 6.8 %collective-permute-start.11 = (f32[1152,128]{1,0:T(8,128)S(1)}, f32[1152,128]{1,0:T(8,128)S(1)}, u32[]{:S(2)}, u32[]{:S(2)}) collective-permute-start(f32[1152,128]{1,0:T(8,128)S(1)} %bitcast.11), channel_id=1, source_target_pairs={{0,64},{64,0},{1,65},{65,1},{2,66},{66,2},{3,67},{67,3},{4,68},{68... | collective-permute-start | bytes 1769480 | tf_op jit(solution)/shard_map/ppermute | solution.py:404
  81.2 1.4 %collective-permute-start.12 = (f32[32,400]{1,0:T(8,128)S(1)}, f32[32,400]{1,0:T(8,128)S(1)}, u32[]{:S(2)}, u32[]{:S(2)}) collective-permute-start(f32[32,400]{1,0:T(8,128)S(1)} %act.1), channel_id=1, source_target_pairs={{0,64},{64,0},{1,65},{65,1},{2,66},{66,2},{3,67},{67,3},{4,68},{68... | collective-permute-start | bytes 153608 | tf_op jit(solution)/shard_map/ppermute | solution.py:404

commit v5 on v4

--- a/solution.py
+++ b/solution.py
@@ -72,17 +72,17 @@
 
 
 def actor_kernel(
-    count, unroll, role, mine, other, boards_in, heads8, out, boards, pairs, middle, last, heads, done
+    count, unroll, role, mine, other, boards_in, policy_t, out, boards, pairs, middle, last, heads, done
 ):
     games = boards.shape[3]
     half = pl.ds(pl.multiple_of(role[0] * games, games), games)
     fetch = pltpu.make_async_copy(boards_in.at[:, :, half], inner_cells(boards), done)
     fetch.start()
-    spread = lax.broadcasted_iota(jnp.int32, (8, 1280), 1)
-    row = lax.broadcasted_iota(jnp.int32, (8, 1280), 0)
-    spread = ((spread % 128 == 10 * row + spread // 128) & (row < 4)).astype(jnp.float32)
+    spread = lax.broadcasted_iota(jnp.int32, (4, 1280), 1)
+    row = lax.broadcasted_iota(jnp.int32, (4, 1280), 0)
+    spread = (spread % 128 == 10 * row + spread // 128).astype(jnp.float32)
     by_column = lax.dot_general(
-        heads8[...], spread, (((0,), (0,)), ((), ())), preferred_element_type=jnp.float32
+        policy_t[...], spread, (((0,), (0,)), ((), ())), preferred_element_type=jnp.float32
     )
     for j in range(10):
         heads[128 * j : 128 * j + 128, :] = by_column[:, 128 * j : 128 * j + 128].astype(jnp.bfloat16)
@@ -138,7 +138,7 @@
         out[:, 100 * d : 100 * d + 100] = (moves[d] - log_total)[:, :100]
 
 
-def act(role, mine, other, boards, heads8, count=2, unroll=1):
+def act(role, mine, other, boards, policy_t, count=2, unroll=1):
     games = boards.shape[2] // 2
     vmem = pl.BlockSpec(memory_space=pltpu.VMEM)
     return pl.pallas_call(
@@ -161,7 +161,7 @@
             flops=8 * 10**9, bytes_accessed=4 * 10**6, transcendentals=30000
         ),
         name="act",
-    )(role, mine, other, boards, heads8)
+    )(role, mine, other, boards, policy_t)
 
 
 def column_of(row):
@@ -178,9 +178,9 @@
 
 def learner_kernel(
     count, role, length, boards_in, actions_in, behaviour_in, regular_in, rewards_in, weights_in,
-    heads8, grad,
-    boards, weights, actions, behaviour, regular, rewards, pairs, back_pairs, middle, last, masks,
-    slope, done,
+    policy_in, value_in, grad,
+    boards, weights, actions, behaviour, regular, rewards, policy_t, value_t, pairs, back_pairs,
+    middle, last, masks, slope, done,
 ):
     slots = boards.shape[3]
     moves = [
@@ -191,14 +191,12 @@
         (behaviour_in, behaviour),
         (regular_in, regular),
         (rewards_in, rewards),
+        (policy_in, policy_t),
+        (value_in, value_t),
     ]
     copies = [pltpu.make_async_copy(a, b, done.at[k]) for k, (a, b) in enumerate(moves)]
     for copy in copies:
         copy.start()
-    eight = heads8[...].astype(jnp.bfloat16).astype(jnp.float32)
-    heads_t = jnp.concatenate(
-        [eight, eight, eight, jnp.zeros((104, 128), jnp.float32)], axis=0
-    ).astype(jnp.bfloat16)
     clear_border(boards)
     copies[0].wait()
 
@@ -236,6 +234,18 @@
 
     for copy in copies[3:]:
         copy.wait()
+
+    eight = jnp.concatenate(
+        [
+            policy_t[...].astype(jnp.float32),
+            value_t[...].astype(jnp.float32),
+            jnp.zeros((3, 128), jnp.float32),
+        ],
+        axis=0,
+    )
+    heads_t = jnp.concatenate(
+        [eight, eight, eight, jnp.zeros((104, 128), jnp.float32)], axis=0
+    ).astype(jnp.bfloat16)
 
     scores = lax.dot_general(
         last[...].reshape(-1, 128), heads_t, (((1,), (1,)), ((), ())),
@@ -336,12 +346,9 @@
         kernel_gradients(boards, last[...].reshape(-1, 128))
 
 
-def head_rows(policy_head, value_head):
-    five = jnp.concatenate([policy_head.T, value_head[None]]).astype(jnp.float32)
-    return jnp.pad(five, ((0, 3), (0, 0)))
-
-
-def learn(role, length, boards, actions, behaviour, regular, rewards, weights, heads8, count=5):
+def learn(
+    role, length, boards, actions, behaviour, regular, rewards, weights, policy_t, value_t, count=5
+):
     slots = boards.shape[2]
     smem = pl.BlockSpec(memory_space=pltpu.SMEM)
     vmem = pl.BlockSpec(memory_space=pltpu.VMEM)
@@ -351,7 +358,7 @@
     return pl.pallas_call(
         functools.partial(learner_kernel, count),
         out_shape=jax.ShapeDtypeStruct((ROWS, 128), jnp.float32),
-        in_specs=[smem, smem] + [anywhere] * 6 + [vmem],
+        in_specs=[smem, smem] + [anywhere] * 8,
         out_specs=vmem,
         scratch_shapes=[
             pltpu.VMEM(around, jnp.bfloat16),
@@ -360,20 +367,57 @@
             pltpu.VMEM((1, slots), jnp.float32),
             pltpu.VMEM((1, slots), jnp.float32),
             pltpu.VMEM((1, slots), jnp.float32),
+            pltpu.VMEM(policy_t.shape, policy_t.dtype),
+            pltpu.VMEM(value_t.shape, value_t.dtype),
             pltpu.VMEM((2, 1536, 256), jnp.bfloat16),
             pltpu.VMEM((1536, 256), jnp.bfloat16),
             pltpu.VMEM(around, jnp.bfloat16),
             pltpu.VMEM(cells, jnp.bfloat16),
             pltpu.VMEM((2,) + cells, jnp.bfloat16),
             pltpu.VMEM(around, jnp.bfloat16),
-            pltpu.SemaphoreType.DMA((7,)),
+            pltpu.SemaphoreType.DMA((9,)),
         ],
         compiler_params=pltpu.CompilerParams(vmem_limit_bytes=60 * 1024 * 1024),
         cost_estimate=pl.CostEstimate(
             flops=4 * 10**9, bytes_accessed=3 * 10**6, transcendentals=10000
         ),
         name="learn",
-    )(role, length, boards, actions, behaviour, regular, rewards, weights, heads8)
+    )(role, length, boards, actions, behaviour, regular, rewards, weights, policy_t, value_t)
+
+
+def update_kernel(role, gathered, torso_in, mine, old, done):
+    fetch = pltpu.make_async_copy(
+        torso_in.at[pl.ds(pl.multiple_of(role[0] * ROWS, ROWS), ROWS)], old, done
+    )
+    fetch.start()
+    squares = jnp.sum(gathered[:, 3 * SHARE], axis=0, keepdims=True)
+    square_sum = jnp.sum(squares, axis=1, keepdims=True)
+    factor = jnp.minimum(1.0, jnp.sqrt(256.0 * ROWS) / jnp.sqrt(square_sum + NORM_EPS))
+    fetch.wait()
+
+    for k in range(LINE * LINE):
+        clipped = gathered[k, 0:SHARE] * factor
+        first = gathered[k, SHARE : 2 * SHARE]
+        second = gathered[k, 2 * SHARE : 3 * SHARE]
+        first = BETA_ONE * first + (1.0 - BETA_ONE) * clipped
+        second = BETA_TWO * second + (1.0 - BETA_TWO) * clipped * clipped
+        rows = slice(k * SHARE, (k + 1) * SHARE)
+        mine[rows] = old[rows] - LEARN_RATE * first / (jnp.sqrt(second) + ADAM_EPS)
+
+
+def update(role, gathered, torso):
+    vmem = pl.BlockSpec(memory_space=pltpu.VMEM)
+    return pl.pallas_call(
+        update_kernel,
+        out_shape=jax.ShapeDtypeStruct((ROWS, 128), jnp.float32),
+        in_specs=[
+            pl.BlockSpec(memory_space=pltpu.SMEM), vmem, pl.BlockSpec(memory_space=pltpu.HBM)
+        ],
+        out_specs=vmem,
+        scratch_shapes=[pltpu.VMEM((ROWS, 128), jnp.float32), pltpu.SemaphoreType.DMA],
+        compiler_params=pltpu.CompilerParams(vmem_limit_bytes=16 * 1024 * 1024),
+        name="update",
+    )(role, gathered, torso)
 
 
 PLANES = [[LINE * k + z for k in range(LINE * LINE)] for z in range(LINE)]
@@ -445,7 +489,6 @@
     role = lax.axis_index("role")
     dp = lax.axis_index("dp")
     role_box = jnp.full((1,), role, jnp.int32)
-    heads8 = head_rows(policy_head, value_head)
     half = half_moments(first_moment, second_moment)
     gradient = learn(
         role_box,
@@ -456,23 +499,18 @@
         regular,
         rewards,
         torso,
-        heads8,
+        policy_head.T,
+        value_head[None],
     )
     share = jnp.sum(plane_exchange(gradient.reshape(LINE * LINE, SHARE, 128)), axis=0)
     share, first, second = line_exchange(share, half, dp % LINE)
     squares = jnp.sum(share * share, axis=0, keepdims=True)
     squares = squares + role_swap(squares)
-    squares = line_total(line_total(squares, "x"), "y")
-    square_sum = jnp.sum(squares)
-    factor = jnp.minimum(1.0, jnp.sqrt(float(torso.size)) / jnp.sqrt(square_sum + NORM_EPS))
-    clipped = share * factor
-    moment_one = BETA_ONE * first + (1.0 - BETA_ONE) * clipped
-    moment_two = BETA_TWO * second + (1.0 - BETA_TWO) * clipped * clipped
-    old_share = lax.dynamic_slice_in_dim(torso, role * ROWS + dp // LINE * SHARE, SHARE, 0)
-    weight_share = old_share - LEARN_RATE * moment_one / (jnp.sqrt(moment_two) + ADAM_EPS)
-    mine = plane_gather(weight_share).reshape(ROWS, 128)
+    squares = jnp.pad(squares, ((0, 7), (0, 0)))
+    gathered = plane_gather(jnp.concatenate([share, first, second, squares]))
+    mine = update(role_box, gathered, torso)
     other = role_swap(mine)
-    here = act(role_box, mine, other, by_cell(board_now), heads8)
+    here = act(role_box, mine, other, by_cell(board_now), policy_head.T.astype(jnp.float32))
     there = role_swap(here)
     out_rows = first_moment.shape[0]
     layer = dp // (LINE**3 // 2)

time: 83.7 us -> 81.6 us (0.975)
  blocking collectives: 12.1 us -> 30.3 us
  starting transfers between devices: 35.6 us -> 25.1 us
  waiting for transfers between devices: 16.8 us -> 10 us
  other arithmetic: 4.11 us -> 1.39 us
    all_to_all x1, blocking collectives: 12.1 us -> 30.3 us  [plane_exchange(): return lax.all_to_all(x, 'dp', 0, 0, axis_index_groups=PLANES)]
    ppermute x9 -> x3, starting transfers between devices: 11.6 us -> 4.65 us  [shifted(): return lax.ppermute(x, 'dp', pairs)]
    ppermute x9 -> x3, waiting for transfers between devices: 9 us -> 2.23 us  [shifted(): return lax.ppermute(x, 'dp', pairs)]
    ppermute x3, starting transfers between devices: 9.18 us -> 5.59 us  [role_swap(): return lax.ppermute(x, 'role', [(0, 1), (1, 0)])]
    pad x1 -> x0, other arithmetic: 1.3 us -> none  [head_rows(): return jnp.pad(five, ((0, 3), (0, 0)))]
  transfers between devices with their start and end apart: 14 -> 8, of which waited for: 10 -> 7; matrix products, arithmetic and copies ran while one was open for 1% -> 1% of each run, Pallas kernels for 0% -> 0%
where the time goes in v5:
time: 81.6 us; the launch traced here: 81.3 us
  blocking collectives  30.3 us (37%)
  starting transfers between devices  25.1 us (31%)
  Pallas kernels  12.6 us (15%)
  waiting for transfers between devices  10 us (12%)
  between operations  1.4 us (2%)
  other arithmetic  1.39 us (2%)
    all_to_all x1, blocking collectives, plane_exchange(): return lax.all_to_all(x, 'dp', 0, 0, axis_index_groups=PLANES)  30.3 us
    all_to_all x1, starting transfers between devices, plane_exchange(): return lax.all_to_all(x, 'dp', 0, 0, axis_index_groups=PLANES)  7.6 us
    ppermute x1, starting transfers between devices, half_moments(): return lax.ppermute(both, ('role', 'dp'), pairs)  7.23 us
    pallas_call x1, Pallas kernels, learn(): pl.pallas_call(functools.partial(learner_kernel, count), out_shape=jax.Sh...  6.46 us
    ppermute x3, starting transfers between devices, role_swap(): return lax.ppermute(x, 'role', [(0, 1), (1, 0)])  5.59 us
    pallas_call x1, Pallas kernels, act(): pl.pallas_call(functools.partial(actor_kernel, count, unroll), out_shape=...  5.54 us
    ppermute x3, starting transfers between devices, shifted(): return lax.ppermute(x, 'dp', pairs)  4.65 us
    all_to_all x1, waiting for transfers between devices, plane_exchange(): return lax.all_to_all(x, 'dp', 0, 0, axis_index_groups=PLANES)  3.33 us
  transfers between devices with their start and end apart: 8, of which 7 were waited for; matrix products, arithmetic and copies ran while one was open for 1% of the time, Pallas kernels for 0%

profile of v5, /device:TPU:1, one launch (start us, length us, event | category | flops | bytes accessed | tf_op | source)
XLA Modules:
  0.0 81.3 jit_solution(5271818541690674389)
XLA Ops:
  1.3 0.0 copy-start.2
  1.3 0.0 copy-start.3
  1.3 6.5 %learn.1 = f32[1152,128]{1,0:T(8,128)} custom-call(s32[1]{0:T(128)} %bitcast.role, s32[1]{0:T(128)S(6)} %copy.14.length, bf16[10,10,16,128]{3,2,1,0:T(8,128)(2,1)} %bitcast.15, s32[1,16]{1,0:T(1,128)} %actions_in.1, f32[1,16]{1,0:T(1,128)} %behaviour_in.1, f32[1,16]{1,0:T(1,128)} %regular_in.1, f32[1,16]{1,0:T(1,128)} %rewards_in.1, f32[2304,128]{1,0:T(8,128)} %torso_in.1, ...), custom_call_target="tpu_custom_call" | custom-call | flops 4000000000 | bytes 3000000 | tf_op jit(solution)/shard_map/learn/pallas_call | solution.py:358
  7.8 7.6 %all-to-all-start = ((f32[16,72,128]{2,1,0:T(8,128)}), f32[16,72,128]{2,1,0:T(8,128)S(1)}, u32[]{:S(2)}, u32[]{:S(2)}) async-start(f32[16,72,128]{2,1,0:T(8,128)} %bitcast.12), calls=%async_computation | async-start | bytes 1179648 | tf_op jit(solution)/shard_map/all_to_all | solution.py:440
  15.4 0.0 copy-done.2
  15.4 0.0 copy-done.3
  15.4 7.2 %collective-permute-start.1 = (f32[72,128]{1,0:T(8,128)S(1)}, f32[72,128]{1,0:T(8,128)S(1)}, u32[]{:S(2)}, u32[]{:S(2)}) collective-permute-start(f32[72,128]{1,0:T(8,128)S(1)} %pad_maximum_fusion.2), channel_id=1, source_target_pairs={{0,0},{1,1},{64,2},{65,3},{2,4},{3,5},{66,6},{67,7},{4,8},{5,9},{6... | collective-permute-start | bytes 110600 | tf_op jit(solution)/shard_map/ppermute | solution.py:459
  22.6 3.3 %all-to-all-done = f32[16,72,128]{2,1,0:T(8,128)S(1)} async-done(((f32[16,72,128]{2,1,0:T(8,128)}), f32[16,72,128]{2,1,0:T(8,128)S(1)}, u32[]{:S(2)}, u32[]{:S(2)}) %all-to-all-start) | async-done | bytes 589856 | tf_op jit(solution)/shard_map/all_to_all | solution.py:440
  26.0 1.7 %collective-permute-done.1 = f32[72,128]{1,0:T(8,128)S(1)} collective-permute-done((f32[72,128]{1,0:T(8,128)S(1)}, f32[72,128]{1,0:T(8,128)S(1)}, u32[]{:S(2)}, u32[]{:S(2)}) %collective-permute-start.1) | collective-permute-done | bytes 36896 | tf_op jit(solution)/shard_map/ppermute | solution.py:459
  27.7 1.6 %collective-permute-start.2 = (f32[144,128]{1,0:T(8,128)S(1)}, f32[144,128]{1,0:T(8,128)S(1)}, u32[]{:S(2)}, u32[]{:S(2)}) collective-permute-start(f32[144,128]{1,0:T(8,128)S(1)} %pad_maximum_fusion.1), channel_id=1, source_target_pairs={{0,1},{1,2},{2,3},{3,0},{4,5},{5,6},{6,7},{7,4},{8,9},{9,10},{10,1... | collective-permute-start | bytes 221192 | tf_op jit(solution)/shard_map/ppermute | solution.py:432
  29.4 2.1 %collective-permute-start = (f32[72,128]{1,0:T(8,128)S(1)}, f32[72,128]{1,0:T(8,128)S(1)}, u32[]{:S(2)}, u32[]{:S(2)}) collective-permute-start(f32[72,128]{1,0:T(8,128)S(1)} %reduce_sum.18), channel_id=1, source_target_pairs={{0,2},{1,3},{2,0},{3,1},{4,6},{5,7},{6,4},{7,5},{8,10},{9,11},{10,... | collective-permute-start | bytes 110600 | tf_op jit(solution)/shard_map/ppermute | solution.py:432
  31.5 0.9 %collective-permute-start.3 = (f32[72,128]{1,0:T(8,128)S(1)}, f32[72,128]{1,0:T(8,128)S(1)}, u32[]{:S(2)}, u32[]{:S(2)}) collective-permute-start(f32[72,128]{1,0:T(8,128)S(1)} %reduce_sum.18), channel_id=1, source_target_pairs={{0,3},{1,0},{2,1},{3,2},{4,7},{5,4},{6,5},{7,6},{8,11},{9,8},{10,9... | collective-permute-start | bytes 110600 | tf_op jit(solution)/shard_map/ppermute | solution.py:432
  32.4 1.3 %collective-permute-done = f32[72,128]{1,0:T(8,128)S(1)} collective-permute-done((f32[72,128]{1,0:T(8,128)S(1)}, f32[72,128]{1,0:T(8,128)S(1)}, u32[]{:S(2)}, u32[]{:S(2)}) %collective-permute-start) | collective-permute-done | bytes 36896 | tf_op jit(solution)/shard_map/ppermute | solution.py:432
  33.7 0.9 %collective-permute-done.3 = f32[72,128]{1,0:T(8,128)S(1)} collective-permute-done((f32[72,128]{1,0:T(8,128)S(1)}, f32[72,128]{1,0:T(8,128)S(1)}, u32[]{:S(2)}, u32[]{:S(2)}) %collective-permute-start.3) | collective-permute-done | bytes 36896 | tf_op jit(solution)/shard_map/ppermute | solution.py:432
  34.6 0.0 collective-permute-done.2
  34.7 3.7 %collective-permute-start.4 = (f32[1,128]{1,0:T(1,128)S(1)}, f32[1,128]{1,0:T(1,128)S(1)}, u32[]{:S(2)}, u32[]{:S(2)}) collective-permute-start(f32[1,128]{1,0:T(1,128)S(1)} %bitcast.14), channel_id=1, source_target_pairs={{0,64},{64,0},{1,65},{65,1},{2,66},{66,2},{3,67},{67,3},{4,68},{68... | collective-permute-start | bytes 1544 | tf_op jit(solution)/shard_map/ppermute | solution.py:448
  38.3 0.8 collective-permute-done.4
  39.1 0.3 concatenate.14
  39.4 0.2 broadcast_in_dim.15
  39.6 0.0 copy-start
  39.6 30.3 %all_to_all.10.gathered = f32[16,224,128]{2,1,0:T(8,128)S(1)} all-to-all(f32[16,224,128]{2,1,0:T(8,128)S(1)} %broadcast_in_dim.15), channel_id=1, replica_groups={{0,4,8,12,16,20,24,28,32,36,40,44,48,52,56,60},{1,5,9,13,17,21,25,29,33..., dimensions={0} | all-to-all | bytes 3670016 | tf_op jit(solution)/shard_map/all_to_all | solution.py:440
  69.9 0.0 copy-done
  69.9 0.6 update.1.mine
  70.6 1.5 %collective-permute-start.5 = (f32[1152,128]{1,0:T(8,128)S(1)}, f32[1152,128]{1,0:T(8,128)S(1)}, u32[]{:S(2)}, u32[]{:S(2)}) collective-permute-start(f32[1152,128]{1,0:T(8,128)S(1)} %update.1.mine), channel_id=1, source_target_pairs={{0,64},{64,0},{1,65},{65,1},{2,66},{66,2},{3,67},{67,3},{4,68},{68... | collective-permute-start | bytes 1769480 | tf_op jit(solution)/shard_map/ppermute | solution.py:448
  72.0 0.0 copy-done.4
  72.0 1.6 %collective-permute-done.5.other = f32[1152,128]{1,0:T(8,128)S(1)} collective-permute-done((f32[1152,128]{1,0:T(8,128)S(1)}, f32[1152,128]{1,0:T(8,128)S(1)}, u32[]{:S(2)}, u32[]{:S(2)}) %collective-permute-start.5) | collective-permute-done | bytes 589856 | tf_op jit(solution)/shard_map/ppermute | solution.py:448
  73.7 0.0 copy-done.1
  73.7 5.5 %act.1 = f32[32,400]{1,0:T(8,128)S(1)} custom-call(s32[1]{0:T(128)} %bitcast.role, f32[1152,128]{1,0:T(8,128)S(1)} %update.1.mine, f32[1152,128]{1,0:T(8,128)S(1)} %collective-permute-done.5.other, bf16[10,10,64,128]{3,2,1,0:T(8,128)(2,1)S(1)} %bitcast.11, f32[4,128]{1,0:T(4,128)S(1)} %bitcast_convert_fusion.policy_t), custom_call_target="tpu_custom_call" | custom-call | flops 8000000000 | bytes 4000000 | tf_op jit(solution)/shard_map/act/pallas_call | solution.py:144
  79.2 0.5 collective-permute-start.6
  79.7 0.6 dynamic-slice_select_fusion
  80.3 0.3 collective-permute-done.6
  80.6 0.7 pad_maximum_fusion
  (11 shorter events, 0.1 us)
Async XLA Ops:
  1.3 14.1 %copy-start.2 = (f32[36,128]{1,0:T(8,128)S(1)}, f32[36,128]{1,0:T(8,128)}, u32[]{:S(2)}) copy-start(f32[36,128]{1,0:T(8,128)} %param.23) | copy-start | bytes 55300
  1.3 14.1 %copy-start.3 = (f32[36,128]{1,0:T(8,128)S(1)}, f32[36,128]{1,0:T(8,128)}, u32[]{:S(2)}) copy-start(f32[36,128]{1,0:T(8,128)} %param.22) | copy-start | bytes 55300
  7.8 18.2 %all-to-all-start = ((f32[16,72,128]{2,1,0:T(8,128)}), f32[16,72,128]{2,1,0:T(8,128)S(1)}, u32[]{:S(2)}, u32[]{:S(2)}) async-start(f32[16,72,128]{2,1,0:T(8,128)} %bitcast.12), calls=%async_computation | async-start | bytes 1179648 | tf_op jit(solution)/shard_map/all_to_all | solution.py:440
  15.4 12.3 %collective-permute-start.1 = (f32[72,128]{1,0:T(8,128)S(1)}, f32[72,128]{1,0:T(8,128)S(1)}, u32[]{:S(2)}, u32[]{:S(2)}) collective-permute-start(f32[72,128]{1,0:T(8,128)S(1)} %pad_maximum_fusion.2), channel_id=1, source_target_pairs={{0,0},{1,1},{64,2},{65,3},{2,4},{3,5},{66,6},{67,7},{4,8},{5,9},{6... | collective-permute-start | bytes 110600 | tf_op jit(solution)/shard_map/ppermute | solution.py:459
  27.7 6.9 %collective-permute-start.2 = (f32[144,128]{1,0:T(8,128)S(1)}, f32[144,128]{1,0:T(8,128)S(1)}, u32[]{:S(2)}, u32[]{:S(2)}) collective-permute-start(f32[144,128]{1,0:T(8,128)S(1)} %pad_maximum_fusion.1), channel_id=1, source_target_pairs={{0,1},{1,2},{2,3},{3,0},{4,5},{5,6},{6,7},{7,4},{8,9},{9,10},{10,1... | collective-permute-start | bytes 221192 | tf_op jit(solution)/shard_map/ppermute | solution.py:432
  29.4 4.3 %collective-permute-start = (f32[72,128]{1,0:T(8,128)S(1)}, f32[72,128]{1,0:T(8,128)S(1)}, u32[]{:S(2)}, u32[]{:S(2)}) collective-permute-start(f32[72,128]{1,0:T(8,128)S(1)} %reduce_sum.18), channel_id=1, source_target_pairs={{0,2},{1,3},{2,0},{3,1},{4,6},{5,7},{6,4},{7,5},{8,10},{9,11},{10,... | collective-permute-start | bytes 110600 | tf_op jit(solution)/shard_map/ppermute | solution.py:432
  31.5 3.1 %collective-permute-start.3 = (f32[72,128]{1,0:T(8,128)S(1)}, f32[72,128]{1,0:T(8,128)S(1)}, u32[]{:S(2)}, u32[]{:S(2)}) collective-permute-start(f32[72,128]{1,0:T(8,128)S(1)} %reduce_sum.18), channel_id=1, source_target_pairs={{0,3},{1,0},{2,1},{3,2},{4,7},{5,4},{6,5},{7,6},{8,11},{9,8},{10,9... | collective-permute-start | bytes 110600 | tf_op jit(solution)/shard_map/ppermute | solution.py:432
  34.7 4.5 %collective-permute-start.4 = (f32[1,128]{1,0:T(1,128)S(1)}, f32[1,128]{1,0:T(1,128)S(1)}, u32[]{:S(2)}, u32[]{:S(2)}) collective-permute-start(f32[1,128]{1,0:T(1,128)S(1)} %bitcast.14), channel_id=1, source_target_pairs={{0,64},{64,0},{1,65},{65,1},{2,66},{66,2},{3,67},{67,3},{4,68},{68... | collective-permute-start | bytes 1544 | tf_op jit(solution)/shard_map/ppermute | solution.py:448
  39.6 30.3 %copy-start = (f32[2304,128]{1,0:T(8,128)S(1)}, f32[2304,128]{1,0:T(8,128)}, u32[]{:S(2)}) copy-start(f32[2304,128]{1,0:T(8,128)} %torso_in.1) | copy-start | bytes 3538948
  69.9 2.1 %copy-start.4 = (bf16[128,4]{0,1:T(4,128)(2,1)S(1)}, bf16[128,4]{0,1:T(4,128)(2,1)}, u32[]{:S(2)}) copy-start(bf16[128,4]{0,1:T(4,128)(2,1)} %param.20) | copy-start | bytes 3076
  69.9 3.8 %copy-start.1 = (bf16[64,10,10,128]{3,0,2,1:T(8,128)(2,1)S(1)}, bf16[64,10,10,128]{3,0,2,1:T(8,128)(2,1)}, u32[]{:S(2)}) copy-start(bf16[64,10,10,128]{3,0,2,1:T(8,128)(2,1)} %param.12) | copy-start | bytes 4915204
  70.6 3.1 %collective-permute-start.5 = (f32[1152,128]{1,0:T(8,128)S(1)}, f32[1152,128]{1,0:T(8,128)S(1)}, u32[]{:S(2)}, u32[]{:S(2)}) collective-permute-start(f32[1152,128]{1,0:T(8,128)S(1)} %update.1.mine), channel_id=1, source_target_pairs={{0,64},{64,0},{1,65},{65,1},{2,66},{66,2},{3,67},{67,3},{4,68},{68... | collective-permute-start | bytes 1769480 | tf_op jit(solution)/shard_map/ppermute | solution.py:448
  79.2 1.4 %collective-permute-start.6 = (f32[32,400]{1,0:T(8,128)S(1)}, f32[32,400]{1,0:T(8,128)S(1)}, u32[]{:S(2)}, u32[]{:S(2)}) collective-permute-start(f32[32,400]{1,0:T(8,128)S(1)} %act.1), channel_id=1, source_target_pairs={{0,64},{64,0},{1,65},{65,1},{2,66},{66,2},{3,67},{67,3},{4,68},{68... | collective-permute-start | bytes 153608 | tf_op jit(solution)/shard_map/ppermute | solution.py:448

commit v6 on v5

--- a/solution.py
+++ b/solution.py
@@ -15,7 +15,8 @@
 NORM_EPS = 1e-12
 ROWS = 1152
 LINE = 4
-SHARE = ROWS // (LINE * LINE)
+SEGMENT = 2 * ROWS // (2 * LINE)
+PIECE = SEGMENT // 8
 
 
 def by_cell(boards):
@@ -24,6 +25,17 @@
 
 def inner_cells(ref):
     return ref.reshape((12, 12) + ref.shape[3:]).at[1:11, 1:11]
+
+
+def segment_parts(layer, offset):
+    start = layer * ROWS + offset * 128
+    at, parts = start, []
+    while at < start + 128:
+        segment = at // SEGMENT
+        end = min(start + 128, (segment + 1) * SEGMENT)
+        parts.append((segment, at - segment * SEGMENT, end - segment * SEGMENT, at - start))
+        at = end
+    return parts
 
 
 def clear_border(ref):
@@ -88,9 +100,12 @@
         heads[128 * j : 128 * j + 128, :] = by_column[:, 128 * j : 128 * j + 128].astype(jnp.bfloat16)
     for layer in range(2):
         def kernel_of(p, q, layer=layer):
-            at = (3 * p + q) * 128
-            block = jnp.where(role[0] == layer, mine[at : at + 128, :], other[at : at + 128, :])
-            return block.astype(jnp.bfloat16)
+            parts = []
+            for segment, first, last_row, _ in segment_parts(layer, 3 * p + q):
+                y, owner = segment // 2, segment % 2
+                rows = slice(first, last_row)
+                parts.append(jnp.where(role[0] == owner, mine[y, rows], other[y, rows]))
+            return jnp.concatenate(parts, axis=0).astype(jnp.bfloat16)
 
         def store(block, value, layer=layer):
             pairs[layer, block * 128 : (block + 1) * 128, :] = value
@@ -180,7 +195,7 @@
     count, role, length, boards_in, actions_in, behaviour_in, regular_in, rewards_in, weights_in,
     policy_in, value_in, grad,
     boards, weights, actions, behaviour, regular, rewards, policy_t, value_t, pairs, back_pairs,
-    middle, last, masks, slope, done,
+    middle, last, masks, slope, turned, done,
 ):
     slots = boards.shape[3]
     moves = [
@@ -307,43 +322,43 @@
     )
     act_grad = (out_grad * masks[1].reshape(-1, 128).astype(jnp.float32)).astype(jnp.bfloat16)
 
-    def kernel_gradients(source, act_grad):
-        turned = act_grad.T
-        windows = []
-        for p in range(3):
-            for q in range(3):
-                cols = [source[p : p + 10, (j + q) // 2, (j + q) % 2] for j in range(10)]
-                windows.append(jnp.stack(cols, axis=1).reshape(-1, 128))
-        for offset in range(9):
-            block = jnp.dot(turned, windows[offset], preferred_element_type=jnp.float32)
-            grad[offset * 128 : (offset + 1) * 128, :] = block.T
-
-    @pl.when(role[0] == 1)
-    def _():
-        kernel_gradients(middle, act_grad)
-
-    @pl.when(role[0] == 0)
-    def _():
-        def kernel_of(p, q):
-            at = ROWS + (8 - (3 * p + q)) * 128
-            return weights[at : at + 128, :].T.astype(jnp.bfloat16)
-
-        def store(block, value):
-            back_pairs[block * 128 : (block + 1) * 128, :] = value
-
-        pair_kernels(kernel_of, store)
-        act_cells = act_grad.reshape(10, 5, 2, slots, 128)
-        put_cells(slope, 0, 10, 0, act_cells[:, :, 0])
-        put_cells(slope, 0, 10, 1, act_cells[:, :, 1])
-        out_cells = out_grad.reshape(10, 5, 2, slots, 128)
-        for first in range(0, 10, count):
-            back = conv_pairs(slope, back_pairs[...], first, count)
-            for parity in range(2):
-                part = back[:, parity * 128 : (parity + 1) * 128].reshape(count, 5, slots, 128)
-                total = out_cells[first : first + count, :, parity] + part
-                gate = masks[0, first : first + count, :, parity].astype(jnp.float32)
-                last[pl.ds(first, count), :, parity] = (total * gate).astype(jnp.bfloat16)
-        kernel_gradients(boards, last[...].reshape(-1, 128))
+    def kernel_of(p, q):
+        at = ROWS + (8 - (3 * p + q)) * 128
+        return weights[at : at + 128, :].T.astype(jnp.bfloat16)
+
+    def store(block, value):
+        back_pairs[block * 128 : (block + 1) * 128, :] = value
+
+    pair_kernels(kernel_of, store)
+    act_cells = act_grad.reshape(10, 5, 2, slots, 128)
+    put_cells(slope, 0, 10, 0, act_cells[:, :, 0])
+    put_cells(slope, 0, 10, 1, act_cells[:, :, 1])
+    out_cells = out_grad.reshape(10, 5, 2, slots, 128)
+    for first in range(0, 10, count):
+        back = conv_pairs(slope, back_pairs[...], first, count)
+        for parity in range(2):
+            part = back[:, parity * 128 : (parity + 1) * 128].reshape(count, 5, slots, 128)
+            total = out_cells[first : first + count, :, parity] + part
+            gate = masks[0, first : first + count, :, parity].astype(jnp.float32)
+            last[pl.ds(first, count), :, parity] = (total * gate).astype(jnp.bfloat16)
+    turned[1] = act_grad.T
+    turned[0] = last[...].reshape(-1, 128).T
+
+    for core in range(2):
+
+        @pl.when(role[0] == core)
+        def _(core=core):
+            for layer, source in ((1, middle), (0, boards)):
+                across = turned[layer]
+                for offset in range(9):
+                    parts = [x for x in segment_parts(layer, offset) if x[0] % 2 == core]
+                    if parts:
+                        p, q = offset // 3, offset % 3
+                        cols = [source[p : p + 10, (j + q) // 2, (j + q) % 2] for j in range(10)]
+                        window = jnp.stack(cols, axis=1).reshape(-1, 128)
+                        block = jnp.dot(across, window, preferred_element_type=jnp.float32).T
+                        for segment, first, end, at in parts:
+                            grad[segment // 2, first:end] = block[at : at + end - first]
 
 
 def learn(
@@ -357,7 +372,7 @@
     around = (12, 6, 2, slots, 128)
     return pl.pallas_call(
         functools.partial(learner_kernel, count),
-        out_shape=jax.ShapeDtypeStruct((ROWS, 128), jnp.float32),
+        out_shape=jax.ShapeDtypeStruct((LINE, SEGMENT, 128), jnp.float32),
         in_specs=[smem, smem] + [anywhere] * 8,
         out_specs=vmem,
         scratch_shapes=[
@@ -375,6 +390,7 @@
             pltpu.VMEM(cells, jnp.bfloat16),
             pltpu.VMEM((2,) + cells, jnp.bfloat16),
             pltpu.VMEM(around, jnp.bfloat16),
+            pltpu.VMEM((2, 128, 100 * slots), jnp.bfloat16),
             pltpu.SemaphoreType.DMA((9,)),
         ],
         compiler_params=pltpu.CompilerParams(vmem_limit_bytes=60 * 1024 * 1024),
@@ -385,42 +401,39 @@
     )(role, length, boards, actions, behaviour, regular, rewards, weights, policy_t, value_t)
 
 
-def update_kernel(role, gathered, torso_in, mine, old, done):
-    fetch = pltpu.make_async_copy(
-        torso_in.at[pl.ds(pl.multiple_of(role[0] * ROWS, ROWS), ROWS)], old, done
-    )
+def update_kernel(place, summed, squares, moments, torso_in, fresh, old, first, second, done):
+    start = pl.multiple_of(place[1] * (2 * SEGMENT) + place[0] * SEGMENT, SEGMENT)
+    fetch = pltpu.make_async_copy(torso_in.at[pl.ds(start, SEGMENT)], old, done)
     fetch.start()
-    squares = jnp.sum(gathered[:, 3 * SHARE], axis=0, keepdims=True)
-    square_sum = jnp.sum(squares, axis=1, keepdims=True)
+    square_sum = jnp.sum(squares[...], axis=1, keepdims=True)
     factor = jnp.minimum(1.0, jnp.sqrt(256.0 * ROWS) / jnp.sqrt(square_sum + NORM_EPS))
+    for x in range(2):
+        for z in range(LINE):
+            rows = slice((LINE * x + z) * PIECE, (LINE * x + z + 1) * PIECE)
+            first[rows] = moments[z, x, 0:PIECE]
+            second[rows] = moments[z, x, PIECE : 2 * PIECE]
     fetch.wait()
-
-    for k in range(LINE * LINE):
-        clipped = gathered[k, 0:SHARE] * factor
-        first = gathered[k, SHARE : 2 * SHARE]
-        second = gathered[k, 2 * SHARE : 3 * SHARE]
-        first = BETA_ONE * first + (1.0 - BETA_ONE) * clipped
-        second = BETA_TWO * second + (1.0 - BETA_TWO) * clipped * clipped
-        rows = slice(k * SHARE, (k + 1) * SHARE)
-        mine[rows] = old[rows] - LEARN_RATE * first / (jnp.sqrt(second) + ADAM_EPS)
-
-
-def update(role, gathered, torso):
+    clipped = summed[...] * factor
+    moment_one = BETA_ONE * first[...] + (1.0 - BETA_ONE) * clipped
+    moment_two = BETA_TWO * second[...] + (1.0 - BETA_TWO) * clipped * clipped
+    fresh[...] = old[...] - LEARN_RATE * moment_one / (jnp.sqrt(moment_two) + ADAM_EPS)
+
+
+def update(place, summed, squares, moments, torso):
     vmem = pl.BlockSpec(memory_space=pltpu.VMEM)
+    rows = pltpu.VMEM((SEGMENT, 128), jnp.float32)
     return pl.pallas_call(
         update_kernel,
-        out_shape=jax.ShapeDtypeStruct((ROWS, 128), jnp.float32),
+        out_shape=jax.ShapeDtypeStruct((SEGMENT, 128), jnp.float32),
         in_specs=[
-            pl.BlockSpec(memory_space=pltpu.SMEM), vmem, pl.BlockSpec(memory_space=pltpu.HBM)
+            pl.BlockSpec(memory_space=pltpu.SMEM), vmem, vmem, vmem,
+            pl.BlockSpec(memory_space=pltpu.HBM),
         ],
         out_specs=vmem,
-        scratch_shapes=[pltpu.VMEM((ROWS, 128), jnp.float32), pltpu.SemaphoreType.DMA],
+        scratch_shapes=[rows, rows, rows, pltpu.SemaphoreType.DMA],
         compiler_params=pltpu.CompilerParams(vmem_limit_bytes=16 * 1024 * 1024),
         name="update",
-    )(role, gathered, torso)
-
-
-PLANES = [[LINE * k + z for k in range(LINE * LINE)] for z in range(LINE)]
+    )(place, summed, squares, moments, torso)
 
 
 def shifted(x, axis, step):
@@ -436,40 +449,36 @@
     return (x + shifted(x, axis, 2)) + (shifted(x, axis, 1) + shifted(x, axis, 3))
 
 
-def plane_exchange(x):
-    return lax.all_to_all(x, "dp", 0, 0, axis_index_groups=PLANES)
-
-
-def plane_gather(x):
-    return plane_exchange(jnp.broadcast_to(x, (LINE * LINE,) + x.shape))
+def line_scatter(chunks, axis, at):
+    def chunk(step):
+        return lax.dynamic_index_in_dim(chunks, (at + step) % LINE, 0, keepdims=False)
+
+    return (chunk(0) + shifted(chunk(2), axis, 2)) + (
+        shifted(chunk(1), axis, 1) + shifted(chunk(3), axis, 3)
+    )
+
+
+def line_place(pieces, at):
+    whole = jnp.zeros((LINE,) + pieces[0].shape, pieces[0].dtype)
+    for step, piece in enumerate(pieces):
+        whole = lax.dynamic_update_index_in_dim(whole, piece, (at - step) % LINE, 0)
+    return whole
+
+
+def line_gather(x, axis, at):
+    return line_place([x] + [shifted(x, axis, step) for step in range(1, LINE)], at)
+
+
+def line_exchange(summed, moments, axis, at):
+    rows = summed.shape[0]
+    both = jnp.concatenate([summed, moments])
+    got = [both] + [shifted(both, axis, step) for step in range(1, LINE)]
+    total = (got[0][:rows] + got[2][:rows]) + (got[1][:rows] + got[3][:rows])
+    return total, line_place([x[rows:] for x in got], at)
 
 
 def role_swap(x):
     return lax.ppermute(x, "role", [(0, 1), (1, 0)])
-
-
-def half_moments(first_moment, second_moment):
-    pairs = []
-    for role in range(2):
-        for d in range(LINE**3):
-            z = d % LINE
-            owner = 32 * role + 2 * (d // LINE) + z % 2
-            pairs.append(((z // 2) * LINE**3 + owner, role * LINE**3 + d))
-    both = jnp.concatenate([first_moment, second_moment])
-    return lax.ppermute(both, ("role", "dp"), pairs)
-
-
-def line_exchange(share, half, z):
-    near = shifted(jnp.concatenate([share, half]), "z", 1)
-    total = (share + shifted(share, "z", 2)) + (near[:SHARE] + shifted(share, "z", 3))
-    rows = SHARE // 2
-    low = jnp.where(z % 2 == 0, half, near[SHARE:])
-    high = jnp.where(z % 2 == 0, near[SHARE:], half)
-    return (
-        total,
-        jnp.concatenate([low[:rows], high[:rows]]),
-        jnp.concatenate([low[rows:], high[rows:]]),
-    )
 
 
 def body(
@@ -488,10 +497,10 @@
 ):
     role = lax.axis_index("role")
     dp = lax.axis_index("dp")
-    role_box = jnp.full((1,), role, jnp.int32)
-    half = half_moments(first_moment, second_moment)
+    y, x, z = dp // (LINE * LINE), dp // LINE % LINE, dp % LINE
+    place = jnp.stack([role, y]).astype(jnp.int32)
     gradient = learn(
-        role_box,
+        place,
         lengths,
         by_cell(traj_boards[0]),
         actions,
@@ -502,23 +511,22 @@
         policy_head.T,
         value_head[None],
     )
-    share = jnp.sum(plane_exchange(gradient.reshape(LINE * LINE, SHARE, 128)), axis=0)
-    share, first, second = line_exchange(share, half, dp % LINE)
-    squares = jnp.sum(share * share, axis=0, keepdims=True)
-    squares = squares + role_swap(squares)
-    squares = jnp.pad(squares, ((0, 7), (0, 0)))
-    gathered = plane_gather(jnp.concatenate([share, first, second, squares]))
-    mine = update(role_box, gathered, torso)
+    summed = line_scatter(gradient, "y", y)
+    summed, moments = line_exchange(summed, jnp.concatenate([first_moment, second_moment]), "x", x)
+    moments = lax.dynamic_slice_in_dim(moments, 2 * role, 2, 0)
+    summed, moments = line_exchange(summed, moments.reshape(-1, 128), "z", z)
+    squares = jnp.sum(summed * summed, axis=0, keepdims=True)
+    squares = line_total(squares + role_swap(squares), "y")
+    fresh = update(place, summed, squares, moments.reshape(LINE, 2, 2 * PIECE, 128), torso)
+    mine = line_gather(fresh, "y", y)
     other = role_swap(mine)
-    here = act(role_box, mine, other, by_cell(board_now), policy_head.T.astype(jnp.float32))
+    here = act(place, mine, other, by_cell(board_now), policy_head.T.astype(jnp.float32))
     there = role_swap(here)
-    out_rows = first_moment.shape[0]
-    layer = dp // (LINE**3 // 2)
-    at = dp % (LINE**3 // 2) * out_rows
+    at = (LINE * x + z) % (2 * LINE) * PIECE
     new_share = jnp.where(
-        role == layer,
-        lax.dynamic_slice_in_dim(mine, at, out_rows, 0),
-        lax.dynamic_slice_in_dim(other, at, out_rows, 0),
+        role == x // 2,
+        lax.dynamic_slice(mine, (y, at, 0), (1, PIECE, 128))[0],
+        lax.dynamic_slice(other, (y, at, 0), (1, PIECE, 128))[0],
     )
     move_logp = jnp.concatenate([jnp.where(role == 0, here, there), jnp.where(role == 0, there, here)])
     return (new_share, move_logp)

time: 81.6 us -> 80.1 us (0.982)
  blocking collectives: 30.3 us -> 0 us
  waiting for transfers between devices: 10 us -> 25.7 us
  starting transfers between devices: 25.1 us -> 33.2 us
  Pallas kernels: 12.6 us -> 15.2 us
  other arithmetic: 1.39 us -> 2.96 us
  local copies, waits for them, and re-layouts: 0.47 us -> 1.33 us
    all_to_all x1 -> x0, blocking collectives: 30.3 us -> none  [plane_exchange(): return lax.all_to_all(x, 'dp', 0, 0, axis_index_groups=PLANES)]
    ppermute x3 -> x15, starting transfers between devices: 4.65 us -> 26.6 us  [shifted(): return lax.ppermute(x, 'dp', pairs)]
    ppermute x3 -> x15, waiting for transfers between devices: 2.23 us -> 23 us  [shifted(): return lax.ppermute(x, 'dp', pairs)]
    all_to_all x1 -> x0, starting transfers between devices: 7.6 us -> none  [plane_exchange(): return lax.all_to_all(x, 'dp', 0, 0, axis_index_groups=PLANES)]
    ppermute x1 -> x0, starting transfers between devices: 7.23 us -> none  [half_moments(): return lax.ppermute(both, ('role', 'dp'), pairs)]
    all_to_all x1 -> x0, waiting for transfers between devices: 3.33 us -> none  [plane_exchange(): return lax.all_to_all(x, 'dp', 0, 0, axis_index_groups=PLANES)]
    ppermute x1 -> x0, waiting for transfers between devices: 1.71 us -> none  [half_moments(): return lax.ppermute(both, ('role', 'dp'), pairs)]
    pallas_call x1, Pallas kernels: 6.46 us -> 8.16 us  [learn(): pl.pallas_call(functools.partial(learner_kernel, count), out_shape=jax.Sh...]
  transfers between devices with their start and end apart: 8 -> 18, of which waited for: 7 -> 13; matrix products, arithmetic and copies ran while one was open for 1% -> 1% of each run, Pallas kernels for 0% -> 0%
where the time goes in v6:
time: 80.1 us; the launch traced here: 79.9 us
  starting transfers between devices  33.2 us (41%)
  waiting for transfers between devices  25.7 us (32%)
  Pallas kernels  15.2 us (19%)
  other arithmetic  2.96 us (4%)
  between operations  1.58 us (2%)
  local copies, waits for them, and re-layouts  1.33 us (2%)
    ppermute x15, starting transfers between devices, shifted(): return lax.ppermute(x, 'dp', pairs)  26.6 us
    ppermute x15, waiting for transfers between devices, shifted(): return lax.ppermute(x, 'dp', pairs)  23 us
    pallas_call x1, Pallas kernels, learn(): pl.pallas_call(functools.partial(learner_kernel, count), out_shape=jax.Sh...  8.16 us
    ppermute x3, starting transfers between devices, role_swap(): return lax.ppermute(x, 'role', [(0, 1), (1, 0)])  6.53 us
    pallas_call x1, Pallas kernels, act(): pl.pallas_call(functools.partial(actor_kernel, count, unroll), out_shape=...  6.14 us
    ppermute x3, waiting for transfers between devices, role_swap(): return lax.ppermute(x, 'role', [(0, 1), (1, 0)])  2.7 us
  transfers between devices with their start and end apart: 18, of which 13 were waited for; matrix products, arithmetic and copies ran while one was open for 1% of the time, Pallas kernels for 0%

profile of v6, /device:TPU:1, one launch (start us, length us, event | category | flops | bytes accessed | tf_op | source)
XLA Modules:
  0.0 79.9 jit_solution(3992651258769119690)
XLA Ops:
  1.9 8.2 %learn.1 = f32[4,288,128]{2,1,0:T(8,128)} custom-call(s32[2]{0:T(128)} %pad_add_fusion.role.place, s32[1]{0:T(128)S(6)} %copy.26.length, bf16[10,10,16,128]{3,2,1,0:T(8,128)(2,1)} %bitcast.70, s32[1,16]{1,0:T(1,128)} %actions_in.1, f32[1,16]{1,0:T(1,128)} %behaviour_in.1, f32[1,16]{1,0:T(1,128)} %regular_in.1, f32[1,16]{1,0:T(1,128)} %rewards_in.1, ...), custom_call_target="tpu_custom_call" | custom-call | flops 4000000000 | bytes 3000000 | tf_op jit(solution)/shard_map/learn/pallas_call | solution.py:373
  10.1 1.1 %dynamic-slice_bitcast_fusion = (f32[288,128]{1,0:T(8,128)S(1)}, f32[288,128]{1,0:T(8,128)S(1)}, f32[288,128]{1,0:T(8,128)S(1)}) fusion(f32[4,288,128]{2,1,0:T(8,128)} %learn.1, s32[]{:T(128)S(6)} %select_n.183, s32[]{:T(128)S(6)} %select_n.181, s32[]{:T(128)S(6)} %select_n.179), kind=kLoop, calls=%fused_computation.15 | loop fusion | bytes 884748 | tf_op jit(solution)/shard_map/jit(dynamic_index_in_dim)/squeeze | solution.py:454
  11.2 3.8 %collective-permute-start = (f32[288,128]{1,0:T(8,128)S(1)}, f32[288,128]{1,0:T(8,128)S(1)}, u32[]{:S(2)}, u32[]{:S(2)}) collective-permute-start(f32[288,128]{1,0:T(8,128)S(1)} %get-tuple-element.6), channel_id=1, source_target_pairs={{0,32},{1,33},{2,34},{3,35},{4,36},{5,37},{6,38},{7,39},{8,40},{9,... | collective-permute-start | bytes 442376 | tf_op jit(solution)/shard_map/ppermute | solution.py:445
  15.4 2.3 %collective-permute-start.2 = (f32[288,128]{1,0:T(8,128)S(1)}, f32[288,128]{1,0:T(8,128)S(1)}, u32[]{:S(2)}, u32[]{:S(2)}) collective-permute-start(f32[288,128]{1,0:T(8,128)S(1)} %get-tuple-element.4), channel_id=1, source_target_pairs={{0,48},{1,49},{2,50},{3,51},{4,52},{5,53},{6,54},{7,55},{8,56},{9,... | collective-permute-start | bytes 442376 | tf_op jit(solution)/shard_map/ppermute | solution.py:445
  17.7 0.7 collective-permute-done
  18.4 3.8 %collective-permute-done.1 = f32[288,128]{1,0:T(8,128)S(1)} collective-permute-done((f32[288,128]{1,0:T(8,128)S(1)}, f32[288,128]{1,0:T(8,128)S(1)}, u32[]{:S(2)}, u32[]{:S(2)}) %collective-permute-start.1) | collective-permute-done | bytes 147488 | tf_op jit(solution)/shard_map/ppermute | solution.py:445
  22.1 0.9 %fusion.2 = f32[288,128]{1,0:T(8,128)S(1)} fusion(f32[288,128]{1,0:T(8,128)S(1)} %collective-permute-done, f32[288,128]{1,0:T(8,128)S(1)} %collective-permute-done.1, f32[288,128]{1,0:T(8,128)S(1)} %collective-permute-done.2, f32[4,288,128]{2,1,0:T(8,128)} %learn.1, s32[]{:T(128)S(6)} %select_n.177), kind=kLoop, calls=%fused_computation.13 | loop fusion | flops 110592 | bytes 737284 | tf_op jit(solution)/shard_map/add | solution.py:456
  23.1 1.3 %collective-permute-start.4 = (f32[360,128]{1,0:T(8,128)S(1)}, f32[360,128]{1,0:T(8,128)S(1)}, u32[]{:S(2)}, u32[]{:S(2)}) collective-permute-start(f32[360,128]{1,0:T(8,128)S(1)} %pad_maximum_fusion.1), channel_id=1, source_target_pairs={{0,4},{1,5},{2,6},{3,7},{4,8},{5,9},{6,10},{7,11},{8,12},{9,13},{1... | collective-permute-start | bytes 552968 | tf_op jit(solution)/shard_map/ppermute | solution.py:445
  24.5 2.5 %collective-permute-start.3 = (f32[360,128]{1,0:T(8,128)S(1)}, f32[360,128]{1,0:T(8,128)S(1)}, u32[]{:S(2)}, u32[]{:S(2)}) collective-permute-start(f32[360,128]{1,0:T(8,128)S(1)} %pad_maximum_fusion.1), channel_id=1, source_target_pairs={{0,8},{1,9},{2,10},{3,11},{4,12},{5,13},{6,14},{7,15},{8,0},{9,1},... | collective-permute-start | bytes 552968 | tf_op jit(solution)/shard_map/ppermute | solution.py:445
  27.0 1.2 %collective-permute-start.5 = (f32[360,128]{1,0:T(8,128)S(1)}, f32[360,128]{1,0:T(8,128)S(1)}, u32[]{:S(2)}, u32[]{:S(2)}) collective-permute-start(f32[360,128]{1,0:T(8,128)S(1)} %pad_maximum_fusion.1), channel_id=1, source_target_pairs={{0,12},{1,13},{2,14},{3,15},{4,0},{5,1},{6,2},{7,3},{8,4},{9,5},{1... | collective-permute-start | bytes 552968 | tf_op jit(solution)/shard_map/ppermute | solution.py:445
  28.2 1.1 %collective-permute-done.4 = f32[360,128]{1,0:T(8,128)S(1)} collective-permute-done((f32[360,128]{1,0:T(8,128)S(1)}, f32[360,128]{1,0:T(8,128)S(1)}, u32[]{:S(2)}, u32[]{:S(2)}) %collective-permute-start.4) | collective-permute-done | bytes 184352 | tf_op jit(solution)/shard_map/ppermute | solution.py:445
  29.3 5.0 %collective-permute-done.3 = f32[360,128]{1,0:T(8,128)S(1)} collective-permute-done((f32[360,128]{1,0:T(8,128)S(1)}, f32[360,128]{1,0:T(8,128)S(1)}, u32[]{:S(2)}, u32[]{:S(2)}) %collective-permute-start.3) | collective-permute-done | bytes 184352 | tf_op jit(solution)/shard_map/ppermute | solution.py:445
  34.5 1.7 %collective-permute-start.7 = (f32[432,128]{1,0:T(8,128)S(1)}, f32[432,128]{1,0:T(8,128)S(1)}, u32[]{:S(2)}, u32[]{:S(2)}) collective-permute-start(f32[432,128]{1,0:T(8,128)S(1)} %pad_maximum_fusion), channel_id=1, source_target_pairs={{0,1},{1,2},{2,3},{3,0},{4,5},{5,6},{6,7},{7,4},{8,9},{9,10},{10,1... | collective-permute-start | bytes 663560 | tf_op jit(solution)/shard_map/ppermute | solution.py:445
  36.2 3.3 %collective-permute-start.6 = (f32[432,128]{1,0:T(8,128)S(1)}, f32[432,128]{1,0:T(8,128)S(1)}, u32[]{:S(2)}, u32[]{:S(2)}) collective-permute-start(f32[432,128]{1,0:T(8,128)S(1)} %pad_maximum_fusion), channel_id=1, source_target_pairs={{0,2},{1,3},{2,0},{3,1},{4,6},{5,7},{6,4},{7,5},{8,10},{9,11},{10,... | collective-permute-start | bytes 663560 | tf_op jit(solution)/shard_map/ppermute | solution.py:445
  39.5 0.7 collective-permute-start.8
  40.2 1.7 %collective-permute-done.7 = f32[432,128]{1,0:T(8,128)S(1)} collective-permute-done((f32[432,128]{1,0:T(8,128)S(1)}, f32[432,128]{1,0:T(8,128)S(1)}, u32[]{:S(2)}, u32[]{:S(2)}) %collective-permute-start.7) | collective-permute-done | bytes 221216 | tf_op jit(solution)/shard_map/ppermute | solution.py:445
  41.9 5.3 %collective-permute-done.6 = f32[432,128]{1,0:T(8,128)S(1)} collective-permute-done((f32[432,128]{1,0:T(8,128)S(1)}, f32[432,128]{1,0:T(8,128)S(1)}, u32[]{:S(2)}, u32[]{:S(2)}) %collective-permute-start.6) | collective-permute-done | bytes 221216 | tf_op jit(solution)/shard_map/ppermute | solution.py:445
  47.3 3.4 %collective-permute-start.9 = (f32[1,128]{1,0:T(1,128)S(1)}, f32[1,128]{1,0:T(1,128)S(1)}, u32[]{:S(2)}, u32[]{:S(2)}) collective-permute-start(f32[1,128]{1,0:T(1,128)S(1)} %bitcast.69), channel_id=1, source_target_pairs={{0,64},{64,0},{1,65},{65,1},{2,66},{66,2},{3,67},{67,3},{4,68},{68... | collective-permute-start | bytes 1544 | tf_op jit(solution)/shard_map/ppermute | solution.py:481
  50.8 0.8 collective-permute-done.9
  51.6 1.6 %collective-permute-start.10 = (f32[1,128]{1,0:T(1,128)S(1)}, f32[1,128]{1,0:T(1,128)S(1)}, u32[]{:S(2)}, u32[]{:S(2)}) collective-permute-start(f32[1,128]{1,0:T(1,128)S(1)} %bitcast_add_fusion.1), channel_id=1, source_target_pairs={{0,32},{1,33},{2,34},{3,35},{4,36},{5,37},{6,38},{7,39},{8,40},{9,... | collective-permute-start | bytes 1544 | tf_op jit(solution)/shard_map/ppermute | solution.py:445
  53.2 1.4 %collective-permute-start.11 = (f32[1,128]{1,0:T(1,128)S(1)}, f32[1,128]{1,0:T(1,128)S(1)}, u32[]{:S(2)}, u32[]{:S(2)}) collective-permute-start(f32[1,128]{1,0:T(1,128)S(1)} %bitcast_add_fusion.1), channel_id=1, source_target_pairs={{0,16},{1,17},{2,18},{3,19},{4,20},{5,21},{6,22},{7,23},{8,24},{9,... | collective-permute-start | bytes 1544 | tf_op jit(solution)/shard_map/ppermute | solution.py:445
  54.6 1.6 %collective-permute-start.12 = (f32[1,128]{1,0:T(1,128)S(1)}, f32[1,128]{1,0:T(1,128)S(1)}, u32[]{:S(2)}, u32[]{:S(2)}) collective-permute-start(f32[1,128]{1,0:T(1,128)S(1)} %bitcast_add_fusion.1), channel_id=1, source_target_pairs={{0,48},{1,49},{2,50},{3,51},{4,52},{5,53},{6,54},{7,55},{8,56},{9,... | collective-permute-start | bytes 1544 | tf_op jit(solution)/shard_map/ppermute | solution.py:445
  56.2 0.9 %collective-permute-done.11 = f32[1,128]{1,0:T(1,128)S(1)} collective-permute-done((f32[1,128]{1,0:T(1,128)S(1)}, f32[1,128]{1,0:T(1,128)S(1)}, u32[]{:S(2)}, u32[]{:S(2)}) %collective-permute-start.11) | collective-permute-done | bytes 544 | tf_op jit(solution)/shard_map/ppermute | solution.py:445
  57.2 0.9 %update.1 = f32[288,128]{1,0:T(8,128)S(1)} custom-call(s32[2]{0:T(128)S(1)} %copy-done.1, f32[288,128]{1,0:T(8,128)S(1)} %get-tuple-element.3.summed, f32[1,128]{1,0:T(1,128)S(1)} %add_add_fusion.squares, f32[4,2,72,128]{3,2,1,0:T(8,128)S(1)} %bitcast.64, f32[2304,128]{1,0:T(8,128)S(1)} %copy-done), custom_call_target="tpu_custom_call" | custom-call | tf_op jit(solution)/shard_map/update/pallas_call | solution.py:425
  58.1 0.9 %collective-permute-start.13 = (f32[288,128]{1,0:T(8,128)S(1)}, f32[288,128]{1,0:T(8,128)S(1)}, u32[]{:S(2)}, u32[]{:S(2)}) collective-permute-start(f32[288,128]{1,0:T(8,128)S(1)} %update.1), channel_id=1, source_target_pairs={{0,16},{1,17},{2,18},{3,19},{4,20},{5,21},{6,22},{7,23},{8,24},{9,... | collective-permute-start | bytes 442376 | tf_op jit(solution)/shard_map/ppermute | solution.py:445
  59.0 3.0 %collective-permute-start.14 = (f32[288,128]{1,0:T(8,128)S(1)}, f32[288,128]{1,0:T(8,128)S(1)}, u32[]{:S(2)}, u32[]{:S(2)}) collective-permute-start(f32[288,128]{1,0:T(8,128)S(1)} %update.1), channel_id=1, source_target_pairs={{0,32},{1,33},{2,34},{3,35},{4,36},{5,37},{6,38},{7,39},{8,40},{9,... | collective-permute-start | bytes 442376 | tf_op jit(solution)/shard_map/ppermute | solution.py:445
  62.0 0.9 %collective-permute-start.15 = (f32[288,128]{1,0:T(8,128)S(1)}, f32[288,128]{1,0:T(8,128)S(1)}, u32[]{:S(2)}, u32[]{:S(2)}) collective-permute-start(f32[288,128]{1,0:T(8,128)S(1)} %update.1), channel_id=1, source_target_pairs={{0,48},{1,49},{2,50},{3,51},{4,52},{5,53},{6,54},{7,55},{8,56},{9,... | collective-permute-start | bytes 442376 | tf_op jit(solution)/shard_map/ppermute | solution.py:445
  63.4 3.6 %collective-permute-done.14 = f32[288,128]{1,0:T(8,128)S(1)} collective-permute-done((f32[288,128]{1,0:T(8,128)S(1)}, f32[288,128]{1,0:T(8,128)S(1)}, u32[]{:S(2)}, u32[]{:S(2)}) %collective-permute-start.14) | collective-permute-done | bytes 147488 | tf_op jit(solution)/shard_map/ppermute | solution.py:445
  67.4 2.7 %collective-permute-start.16 = (f32[4,288,128]{2,1,0:T(8,128)S(1)}, f32[4,288,128]{2,1,0:T(8,128)S(1)}, u32[]{:S(2)}, u32[]{:S(2)}) collective-permute-start(f32[4,288,128]{2,1,0:T(8,128)S(1)} %bitcast_dynamic-update-slice_fusion.mine), channel_id=1, source_target_pairs={{0,64},{64,0},{1,65},{65,1},{2,66},{66,2},{3,67},{67,3},{4,68},{68... | collective-permute-start | bytes 1769480 | tf_op jit(solution)/shard_map/ppermute | solution.py:481
  70.1 1.6 %collective-permute-done.16.other = f32[4,288,128]{2,1,0:T(8,128)S(1)} collective-permute-done((f32[4,288,128]{2,1,0:T(8,128)S(1)}, f32[4,288,128]{2,1,0:T(8,128)S(1)}, u32[]{:S(2)}, u32[]{:S(2)}) %collective-permute-start.16) | collective-permute-done | bytes 589856 | tf_op jit(solution)/shard_map/ppermute | solution.py:481
  71.8 6.1 %act.1 = f32[32,400]{1,0:T(8,128)S(1)} custom-call(s32[2]{0:T(128)S(1)} %copy-done.1, f32[4,288,128]{2,1,0:T(8,128)S(1)} %bitcast_dynamic-update-slice_fusion.mine, f32[4,288,128]{2,1,0:T(8,128)S(1)} %collective-permute-done.16.other, bf16[10,10,64,128]{3,2,1,0:T(8,128)(2,1)S(1)} %bitcast.65, f32[4,128]{1,0:T(4,128)S(1)} %bitcast_convert_fusion.policy_t), custom_call_target="tpu_custom_call" | custom-call | flops 8000000000 | bytes 4000000 | tf_op jit(solution)/shard_map/act/pallas_call | solution.py:159
  79.3 0.7 pad_maximum_fusion.2
  (48 shorter events, 3.5 us)
Async XLA Ops:
  10.1 13.0 %copy-start.3 = (f32[36,128]{1,0:T(8,128)S(1)}, f32[36,128]{1,0:T(8,128)}, u32[]{:S(2)}) copy-start(f32[36,128]{1,0:T(8,128)} %param.23) | copy-start | bytes 55300
  10.1 13.0 %copy-start.4 = (f32[36,128]{1,0:T(8,128)S(1)}, f32[36,128]{1,0:T(8,128)}, u32[]{:S(2)}) copy-start(f32[36,128]{1,0:T(8,128)} %param.22) | copy-start | bytes 55300
  11.2 7.2 %collective-permute-start = (f32[288,128]{1,0:T(8,128)S(1)}, f32[288,128]{1,0:T(8,128)S(1)}, u32[]{:S(2)}, u32[]{:S(2)}) collective-permute-start(f32[288,128]{1,0:T(8,128)S(1)} %get-tuple-element.6), channel_id=1, source_target_pairs={{0,32},{1,33},{2,34},{3,35},{4,36},{5,37},{6,38},{7,39},{8,40},{9,... | collective-permute-start | bytes 442376 | tf_op jit(solution)/shard_map/ppermute | solution.py:445
  15.0 7.1 %collective-permute-start.1 = (f32[288,128]{1,0:T(8,128)S(1)}, f32[288,128]{1,0:T(8,128)S(1)}, u32[]{:S(2)}, u32[]{:S(2)}) collective-permute-start(f32[288,128]{1,0:T(8,128)S(1)} %get-tuple-element.5), channel_id=1, source_target_pairs={{0,16},{1,17},{2,18},{3,19},{4,20},{5,21},{6,22},{7,23},{8,24},{9,... | collective-permute-start | bytes 442376 | tf_op jit(solution)/shard_map/ppermute | solution.py:445
  15.4 6.7 %collective-permute-start.2 = (f32[288,128]{1,0:T(8,128)S(1)}, f32[288,128]{1,0:T(8,128)S(1)}, u32[]{:S(2)}, u32[]{:S(2)}) collective-permute-start(f32[288,128]{1,0:T(8,128)S(1)} %get-tuple-element.4), channel_id=1, source_target_pairs={{0,48},{1,49},{2,50},{3,51},{4,52},{5,53},{6,54},{7,55},{8,56},{9,... | collective-permute-start | bytes 442376 | tf_op jit(solution)/shard_map/ppermute | solution.py:445
  23.1 6.2 %collective-permute-start.4 = (f32[360,128]{1,0:T(8,128)S(1)}, f32[360,128]{1,0:T(8,128)S(1)}, u32[]{:S(2)}, u32[]{:S(2)}) collective-permute-start(f32[360,128]{1,0:T(8,128)S(1)} %pad_maximum_fusion.1), channel_id=1, source_target_pairs={{0,4},{1,5},{2,6},{3,7},{4,8},{5,9},{6,10},{7,11},{8,12},{9,13},{1... | collective-permute-start | bytes 552968 | tf_op jit(solution)/shard_map/ppermute | solution.py:445
  24.5 9.8 %collective-permute-start.3 = (f32[360,128]{1,0:T(8,128)S(1)}, f32[360,128]{1,0:T(8,128)S(1)}, u32[]{:S(2)}, u32[]{:S(2)}) collective-permute-start(f32[360,128]{1,0:T(8,128)S(1)} %pad_maximum_fusion.1), channel_id=1, source_target_pairs={{0,8},{1,9},{2,10},{3,11},{4,12},{5,13},{6,14},{7,15},{8,0},{9,1},... | collective-permute-start | bytes 552968 | tf_op jit(solution)/shard_map/ppermute | solution.py:445
  27.0 7.3 %collective-permute-start.5 = (f32[360,128]{1,0:T(8,128)S(1)}, f32[360,128]{1,0:T(8,128)S(1)}, u32[]{:S(2)}, u32[]{:S(2)}) collective-permute-start(f32[360,128]{1,0:T(8,128)S(1)} %pad_maximum_fusion.1), channel_id=1, source_target_pairs={{0,12},{1,13},{2,14},{3,15},{4,0},{5,1},{6,2},{7,3},{8,4},{9,5},{1... | collective-permute-start | bytes 552968 | tf_op jit(solution)/shard_map/ppermute | solution.py:445
  34.3 22.8 %copy-start = (f32[2304,128]{1,0:T(8,128)S(1)}, f32[2304,128]{1,0:T(8,128)}, u32[]{:S(2)}) copy-start(f32[2304,128]{1,0:T(8,128)} %torso_in.1) | copy-start | bytes 3538948
  34.3 22.8 %copy-start.1 = (s32[2]{0:T(128)S(1)}, s32[2]{0:T(128)}, u32[]{:S(2)}) copy-start(s32[2]{0:T(128)} %pad_add_fusion.role.place) | copy-start | bytes 28
  34.5 7.5 %collective-permute-start.7 = (f32[432,128]{1,0:T(8,128)S(1)}, f32[432,128]{1,0:T(8,128)S(1)}, u32[]{:S(2)}, u32[]{:S(2)}) collective-permute-start(f32[432,128]{1,0:T(8,128)S(1)} %pad_maximum_fusion), channel_id=1, source_target_pairs={{0,1},{1,2},{2,3},{3,0},{4,5},{5,6},{6,7},{7,4},{8,9},{9,10},{10,1... | collective-permute-start | bytes 663560 | tf_op jit(solution)/shard_map/ppermute | solution.py:445
  36.2 11.1 %collective-permute-start.6 = (f32[432,128]{1,0:T(8,128)S(1)}, f32[432,128]{1,0:T(8,128)S(1)}, u32[]{:S(2)}, u32[]{:S(2)}) collective-permute-start(f32[432,128]{1,0:T(8,128)S(1)} %pad_maximum_fusion), channel_id=1, source_target_pairs={{0,2},{1,3},{2,0},{3,1},{4,6},{5,7},{6,4},{7,5},{8,10},{9,11},{10,... | collective-permute-start | bytes 663560 | tf_op jit(solution)/shard_map/ppermute | solution.py:445
  39.5 7.8 %collective-permute-start.8 = (f32[432,128]{1,0:T(8,128)S(1)}, f32[432,128]{1,0:T(8,128)S(1)}, u32[]{:S(2)}, u32[]{:S(2)}) collective-permute-start(f32[432,128]{1,0:T(8,128)S(1)} %pad_maximum_fusion), channel_id=1, source_target_pairs={{0,3},{1,0},{2,1},{3,2},{4,7},{5,4},{6,5},{7,6},{8,11},{9,8},{10,9... | collective-permute-start | bytes 663560 | tf_op jit(solution)/shard_map/ppermute | solution.py:445
  47.3 4.2 %collective-permute-start.9 = (f32[1,128]{1,0:T(1,128)S(1)}, f32[1,128]{1,0:T(1,128)S(1)}, u32[]{:S(2)}, u32[]{:S(2)}) collective-permute-start(f32[1,128]{1,0:T(1,128)S(1)} %bitcast.69), channel_id=1, source_target_pairs={{0,64},{64,0},{1,65},{65,1},{2,66},{66,2},{3,67},{67,3},{4,68},{68... | collective-permute-start | bytes 1544 | tf_op jit(solution)/shard_map/ppermute | solution.py:481
  51.6 4.6 %collective-permute-start.10 = (f32[1,128]{1,0:T(1,128)S(1)}, f32[1,128]{1,0:T(1,128)S(1)}, u32[]{:S(2)}, u32[]{:S(2)}) collective-permute-start(f32[1,128]{1,0:T(1,128)S(1)} %bitcast_add_fusion.1), channel_id=1, source_target_pairs={{0,32},{1,33},{2,34},{3,35},{4,36},{5,37},{6,38},{7,39},{8,40},{9,... | collective-permute-start | bytes 1544 | tf_op jit(solution)/shard_map/ppermute | solution.py:445
  53.2 4.0 %collective-permute-start.11 = (f32[1,128]{1,0:T(1,128)S(1)}, f32[1,128]{1,0:T(1,128)S(1)}, u32[]{:S(2)}, u32[]{:S(2)}) collective-permute-start(f32[1,128]{1,0:T(1,128)S(1)} %bitcast_add_fusion.1), channel_id=1, source_target_pairs={{0,16},{1,17},{2,18},{3,19},{4,20},{5,21},{6,22},{7,23},{8,24},{9,... | collective-permute-start | bytes 1544 | tf_op jit(solution)/shard_map/ppermute | solution.py:445
  54.6 2.5 %collective-permute-start.12 = (f32[1,128]{1,0:T(1,128)S(1)}, f32[1,128]{1,0:T(1,128)S(1)}, u32[]{:S(2)}, u32[]{:S(2)}) collective-permute-start(f32[1,128]{1,0:T(1,128)S(1)} %bitcast_add_fusion.1), channel_id=1, source_target_pairs={{0,48},{1,49},{2,50},{3,51},{4,52},{5,53},{6,54},{7,55},{8,56},{9,... | collective-permute-start | bytes 1544 | tf_op jit(solution)/shard_map/ppermute | solution.py:445
  57.1 13.0 %copy-start.5 = (bf16[128,4]{0,1:T(4,128)(2,1)S(1)}, bf16[128,4]{0,1:T(4,128)(2,1)}, u32[]{:S(2)}) copy-start(bf16[128,4]{0,1:T(4,128)(2,1)} %param.20) | copy-start | bytes 3076
  57.2 14.6 %copy-start.2 = (bf16[64,10,10,128]{3,0,2,1:T(8,128)(2,1)S(1)}, bf16[64,10,10,128]{3,0,2,1:T(8,128)(2,1)}, u32[]{:S(2)}) copy-start(bf16[64,10,10,128]{3,0,2,1:T(8,128)(2,1)} %param.12) | copy-start | bytes 4915204
  58.1 5.3 %collective-permute-start.13 = (f32[288,128]{1,0:T(8,128)S(1)}, f32[288,128]{1,0:T(8,128)S(1)}, u32[]{:S(2)}, u32[]{:S(2)}) collective-permute-start(f32[288,128]{1,0:T(8,128)S(1)} %update.1), channel_id=1, source_target_pairs={{0,16},{1,17},{2,18},{3,19},{4,20},{5,21},{6,22},{7,23},{8,24},{9,... | collective-permute-start | bytes 442376 | tf_op jit(solution)/shard_map/ppermute | solution.py:445
  59.0 8.0 %collective-permute-start.14 = (f32[288,128]{1,0:T(8,128)S(1)}, f32[288,128]{1,0:T(8,128)S(1)}, u32[]{:S(2)}, u32[]{:S(2)}) collective-permute-start(f32[288,128]{1,0:T(8,128)S(1)} %update.1), channel_id=1, source_target_pairs={{0,32},{1,33},{2,34},{3,35},{4,36},{5,37},{6,38},{7,39},{8,40},{9,... | collective-permute-start | bytes 442376 | tf_op jit(solution)/shard_map/ppermute | solution.py:445
  62.0 5.4 %collective-permute-start.15 = (f32[288,128]{1,0:T(8,128)S(1)}, f32[288,128]{1,0:T(8,128)S(1)}, u32[]{:S(2)}, u32[]{:S(2)}) collective-permute-start(f32[288,128]{1,0:T(8,128)S(1)} %update.1), channel_id=1, source_target_pairs={{0,48},{1,49},{2,50},{3,51},{4,52},{5,53},{6,54},{7,55},{8,56},{9,... | collective-permute-start | bytes 442376 | tf_op jit(solution)/shard_map/ppermute | solution.py:445
  67.4 4.3 %collective-permute-start.16 = (f32[4,288,128]{2,1,0:T(8,128)S(1)}, f32[4,288,128]{2,1,0:T(8,128)S(1)}, u32[]{:S(2)}, u32[]{:S(2)}) collective-permute-start(f32[4,288,128]{2,1,0:T(8,128)S(1)} %bitcast_dynamic-update-slice_fusion.mine), channel_id=1, source_target_pairs={{0,64},{64,0},{1,65},{65,1},{2,66},{66,2},{3,67},{67,3},{4,68},{68... | collective-permute-start | bytes 1769480 | tf_op jit(solution)/shard_map/ppermute | solution.py:481
  77.9 1.4 %collective-permute-start.17 = (f32[32,400]{1,0:T(8,128)S(1)}, f32[32,400]{1,0:T(8,128)S(1)}, u32[]{:S(2)}, u32[]{:S(2)}) collective-permute-start(f32[32,400]{1,0:T(8,128)S(1)} %act.1), channel_id=1, source_target_pairs={{0,64},{64,0},{1,65},{65,1},{2,66},{66,2},{3,67},{67,3},{4,68},{68... | collective-permute-start | bytes 153608 | tf_op jit(solution)/shard_map/ppermute | solution.py:481

commit v7 on v6

--- a/solution.py
+++ b/solution.py
@@ -83,13 +83,12 @@
         target[pl.ds(first + 1, count), 1:6, 0] = value
 
 
-def actor_kernel(
-    count, unroll, role, mine, other, boards_in, policy_t, out, boards, pairs, middle, last, heads, done
-):
+def stage_kernel(mine, boards_in, policy_t, boards, heads, done):
     games = boards.shape[3]
-    half = pl.ds(pl.multiple_of(role[0] * games, games), games)
+    half = pl.ds(pl.multiple_of(lax.axis_index("role") * games, games), games)
     fetch = pltpu.make_async_copy(boards_in.at[:, :, half], inner_cells(boards), done)
     fetch.start()
+    clear_border(boards)
     spread = lax.broadcasted_iota(jnp.int32, (4, 1280), 1)
     row = lax.broadcasted_iota(jnp.int32, (4, 1280), 0)
     spread = (spread % 128 == 10 * row + spread // 128).astype(jnp.float32)
@@ -98,13 +97,40 @@
     )
     for j in range(10):
         heads[128 * j : 128 * j + 128, :] = by_column[:, 128 * j : 128 * j + 128].astype(jnp.bfloat16)
+    fetch.wait()
+
+
+def stage(mine, boards, policy_t):
+    games = boards.shape[2] // 2
+    vmem = pl.BlockSpec(memory_space=pltpu.VMEM)
+    anywhere = pl.BlockSpec(memory_space=pltpu.HBM)
+    return pl.pallas_call(
+        stage_kernel,
+        out_shape=[
+            jax.ShapeDtypeStruct((12, 6, 2, games, 128), jnp.bfloat16),
+            jax.ShapeDtypeStruct((1280, 128), jnp.bfloat16),
+        ],
+        in_specs=[anywhere, anywhere, vmem],
+        out_specs=[vmem, vmem],
+        scratch_shapes=[pltpu.SemaphoreType.DMA],
+        compiler_params=pltpu.CompilerParams(vmem_limit_bytes=16 * 1024 * 1024),
+        cost_estimate=pl.CostEstimate(
+            flops=10**9, bytes_accessed=4 * 10**6, transcendentals=0
+        ),
+        name="stage",
+    )(mine, boards, policy_t)
+
+
+def actor_kernel(count, unroll, mine, other, boards, heads, out, pairs, middle, last):
+    games = boards.shape[3]
+    role = lax.axis_index("role")
     for layer in range(2):
         def kernel_of(p, q, layer=layer):
             parts = []
             for segment, first, last_row, _ in segment_parts(layer, 3 * p + q):
                 y, owner = segment // 2, segment % 2
                 rows = slice(first, last_row)
-                parts.append(jnp.where(role[0] == owner, mine[y, rows], other[y, rows]))
+                parts.append(jnp.where(role == owner, mine[y, rows], other[y, rows]))
             return jnp.concatenate(parts, axis=0).astype(jnp.bfloat16)
 
         def store(block, value, layer=layer):
@@ -112,8 +138,6 @@
 
         pair_kernels(kernel_of, store)
     clear_border(middle)
-    clear_border(boards)
-    fetch.wait()
 
     def run_layer(layer, source, emit):
         def step(at, carry):
@@ -153,30 +177,25 @@
         out[:, 100 * d : 100 * d + 100] = (moves[d] - log_total)[:, :100]
 
 
-def act(role, mine, other, boards, policy_t, count=2, unroll=1):
-    games = boards.shape[2] // 2
+def act(mine, other, boards, heads, count=2, unroll=1):
+    games = boards.shape[3]
     vmem = pl.BlockSpec(memory_space=pltpu.VMEM)
     return pl.pallas_call(
         functools.partial(actor_kernel, count, unroll),
         out_shape=jax.ShapeDtypeStruct((games, 400), jnp.float32),
-        in_specs=[
-            pl.BlockSpec(memory_space=pltpu.SMEM), vmem, vmem, pl.BlockSpec(memory_space=pltpu.HBM), vmem
-        ],
+        in_specs=[vmem] * 4,
         out_specs=vmem,
         scratch_shapes=[
-            pltpu.VMEM((12, 6, 2, games, 128), jnp.bfloat16),
             pltpu.VMEM((2, 1536, 256), jnp.bfloat16),
             pltpu.VMEM((12, 6, 2, games, 128), jnp.bfloat16),
             pltpu.VMEM((10, 5, 2, games, 128), jnp.bfloat16),
-            pltpu.VMEM((1280, 128), jnp.bfloat16),
-            pltpu.SemaphoreType.DMA,
         ],
         compiler_params=pltpu.CompilerParams(vmem_limit_bytes=32 * 1024 * 1024),
         cost_estimate=pl.CostEstimate(
             flops=8 * 10**9, bytes_accessed=4 * 10**6, transcendentals=30000
         ),
         name="act",
-    )(role, mine, other, boards, policy_t)
+    )(mine, other, boards, heads)
 
 
 def column_of(row):
@@ -192,12 +211,14 @@
 
 
 def learner_kernel(
-    count, role, length, boards_in, actions_in, behaviour_in, regular_in, rewards_in, weights_in,
-    policy_in, value_in, grad,
-    boards, weights, actions, behaviour, regular, rewards, policy_t, value_t, pairs, back_pairs,
+    count, length, boards_in, actions_in, behaviour_in, regular_in, rewards_in, weights_in,
+    policy_in, value_in, own, next1, next2, next3,
+    grad, boards, weights, actions, behaviour, regular, rewards, policy_t, value_t, pairs, back_pairs,
     middle, last, masks, slope, turned, done,
 ):
     slots = boards.shape[3]
+    role = lax.axis_index("role")
+    y = lax.axis_index("dp") // (LINE * LINE)
     moves = [
         (weights_in.at[0:ROWS], weights.at[0:ROWS]),
         (boards_in, inner_cells(boards)),
@@ -346,7 +367,7 @@
 
     for core in range(2):
 
-        @pl.when(role[0] == core)
+        @pl.when(role == core)
         def _(core=core):
             for layer, source in ((1, middle), (0, boards)):
                 across = turned[layer]
@@ -360,22 +381,31 @@
                         for segment, first, end, at in parts:
                             grad[segment // 2, first:end] = block[at : at + end - first]
 
+    sends = [
+        pltpu.make_async_copy(grad.at[lax.rem(y + k, LINE)], out, done.at[k])
+        for k, out in enumerate((own, next1, next2, next3))
+    ]
+    for copy in sends:
+        copy.start()
+    for copy in sends:
+        copy.wait()
+
 
 def learn(
-    role, length, boards, actions, behaviour, regular, rewards, weights, policy_t, value_t, count=5
+    length, boards, actions, behaviour, regular, rewards, weights, policy_t, value_t, count=5
 ):
     slots = boards.shape[2]
     smem = pl.BlockSpec(memory_space=pltpu.SMEM)
-    vmem = pl.BlockSpec(memory_space=pltpu.VMEM)
     anywhere = pl.BlockSpec(memory_space=pltpu.HBM)
     cells = (10, 5, 2, slots, 128)
     around = (12, 6, 2, slots, 128)
     return pl.pallas_call(
         functools.partial(learner_kernel, count),
-        out_shape=jax.ShapeDtypeStruct((LINE, SEGMENT, 128), jnp.float32),
-        in_specs=[smem, smem] + [anywhere] * 8,
-        out_specs=vmem,
+        out_shape=[jax.ShapeDtypeStruct((SEGMENT, 128), jnp.float32)] * LINE,
+        in_specs=[smem] + [anywhere] * 8,
+        out_specs=[anywhere] * LINE,
         scratch_shapes=[
+            pltpu.VMEM((LINE, SEGMENT, 128), jnp.float32),
             pltpu.VMEM(around, jnp.bfloat16),
             pltpu.VMEM((2 * ROWS, 128), jnp.float32),
             pltpu.VMEM((1, slots), jnp.int32),
@@ -398,11 +428,12 @@
             flops=4 * 10**9, bytes_accessed=3 * 10**6, transcendentals=10000
         ),
         name="learn",
-    )(role, length, boards, actions, behaviour, regular, rewards, weights, policy_t, value_t)
-
-
-def update_kernel(place, summed, squares, moments, torso_in, fresh, old, first, second, done):
-    start = pl.multiple_of(place[1] * (2 * SEGMENT) + place[0] * SEGMENT, SEGMENT)
+    )(length, boards, actions, behaviour, regular, rewards, weights, policy_t, value_t)
+
+
+def update_kernel(summed, squares, moments, torso_in, fresh, old, first, second, done):
+    y = lax.axis_index("dp") // (LINE * LINE)
+    start = pl.multiple_of((2 * y + lax.axis_index("role")) * SEGMENT, SEGMENT)
     fetch = pltpu.make_async_copy(torso_in.at[pl.ds(start, SEGMENT)], old, done)
     fetch.start()
     square_sum = jnp.sum(squares[...], axis=1, keepdims=True)
@@ -419,21 +450,20 @@
     fresh[...] = old[...] - LEARN_RATE * moment_one / (jnp.sqrt(moment_two) + ADAM_EPS)
 
 
-def update(place, summed, squares, moments, torso):
+def update(summed, squares, moments, torso):
     vmem = pl.BlockSpec(memory_space=pltpu.VMEM)
     rows = pltpu.VMEM((SEGMENT, 128), jnp.float32)
     return pl.pallas_call(
         update_kernel,
         out_shape=jax.ShapeDtypeStruct((SEGMENT, 128), jnp.float32),
         in_specs=[
-            pl.BlockSpec(memory_space=pltpu.SMEM), vmem, vmem, vmem,
-            pl.BlockSpec(memory_space=pltpu.HBM),
+            vmem, vmem, vmem, pl.BlockSpec(memory_space=pltpu.HBM)
         ],
         out_specs=vmem,
         scratch_shapes=[rows, rows, rows, pltpu.SemaphoreType.DMA],
         compiler_params=pltpu.CompilerParams(vmem_limit_bytes=16 * 1024 * 1024),
         name="update",
-    )(place, summed, squares, moments, torso)
+    )(summed, squares, moments, torso)
 
 
 def shifted(x, axis, step):
@@ -449,12 +479,9 @@
     return (x + shifted(x, axis, 2)) + (shifted(x, axis, 1) + shifted(x, axis, 3))
 
 
-def line_scatter(chunks, axis, at):
-    def chunk(step):
-        return lax.dynamic_index_in_dim(chunks, (at + step) % LINE, 0, keepdims=False)
-
-    return (chunk(0) + shifted(chunk(2), axis, 2)) + (
-        shifted(chunk(1), axis, 1) + shifted(chunk(3), axis, 3)
+def line_scatter(chunks, axis):
+    return (chunks[0] + shifted(chunks[2], axis, 2)) + (
+        shifted(chunks[1], axis, 1) + shifted(chunks[3], axis, 3)
     )
 
 
@@ -467,14 +494,6 @@
 
 def line_gather(x, axis, at):
     return line_place([x] + [shifted(x, axis, step) for step in range(1, LINE)], at)
-
-
-def line_exchange(summed, moments, axis, at):
-    rows = summed.shape[0]
-    both = jnp.concatenate([summed, moments])
-    got = [both] + [shifted(both, axis, step) for step in range(1, LINE)]
-    total = (got[0][:rows] + got[2][:rows]) + (got[1][:rows] + got[3][:rows])
-    return total, line_place([x[rows:] for x in got], at)
 
 
 def role_swap(x):
@@ -498,9 +517,9 @@
     role = lax.axis_index("role")
     dp = lax.axis_index("dp")
     y, x, z = dp // (LINE * LINE), dp // LINE % LINE, dp % LINE
-    place = jnp.stack([role, y]).astype(jnp.int32)
-    gradient = learn(
-        place,
+    moments = line_gather(jnp.concatenate([first_moment, second_moment]), "x", x)
+    moments = lax.dynamic_slice_in_dim(moments, 2 * role, 2, 0).reshape(-1, 128)
+    chunks = learn(
         lengths,
         by_cell(traj_boards[0]),
         actions,
@@ -511,16 +530,16 @@
         policy_head.T,
         value_head[None],
     )
-    summed = line_scatter(gradient, "y", y)
-    summed, moments = line_exchange(summed, jnp.concatenate([first_moment, second_moment]), "x", x)
-    moments = lax.dynamic_slice_in_dim(moments, 2 * role, 2, 0)
-    summed, moments = line_exchange(summed, moments.reshape(-1, 128), "z", z)
+    chunks, moments = lax.optimization_barrier((chunks, moments))
+    moments = line_gather(moments, "z", z)
+    summed = line_total(line_total(line_scatter(chunks, "y"), "x"), "z")
     squares = jnp.sum(summed * summed, axis=0, keepdims=True)
     squares = line_total(squares + role_swap(squares), "y")
-    fresh = update(place, summed, squares, moments.reshape(LINE, 2, 2 * PIECE, 128), torso)
+    fresh = update(summed, squares, moments.reshape(LINE, 2, 2 * PIECE, 128), torso)
     mine = line_gather(fresh, "y", y)
     other = role_swap(mine)
-    here = act(place, mine, other, by_cell(board_now), policy_head.T.astype(jnp.float32))
+    boards, heads = stage(mine, by_cell(board_now), policy_head.T.astype(jnp.float32))
+    here = act(mine, other, boards, heads)
     there = role_swap(here)
     at = (LINE * x + z) % (2 * LINE) * PIECE
     new_share = jnp.where(

time: 80.1 us -> 77.8 us (0.971)
  starting transfers between devices: 33.2 us -> 42.1 us
  waiting for transfers between devices: 25.7 us -> 17 us
  Pallas kernels: 15.2 us -> 13.5 us
  local copies, waits for them, and re-layouts: 1.33 us -> 0.23 us
    ppermute x15 -> x21, starting transfers between devices: 26.6 us -> 35.4 us  [shifted(): return lax.ppermute(x, 'dp', pairs)]
    ppermute x15 -> x21, waiting for transfers between devices: 23 us -> 14.7 us  [shifted(): return lax.ppermute(x, 'dp', pairs)]
    squeeze x1 -> x0, local copies, waits for them, and re-layouts: 1.09 us -> none  [chunk(): lax.dynamic_index_in_dim(chunks, (at + step) % LINE, 0, keepdims=False)]
    pallas_call x1, Pallas kernels: 6.14 us -> 5.14 us  [act(): pl.pallas_call(functools.partial(actor_kernel, count, unroll), out_shape=...]
    pallas_call x1 -> x2, Pallas kernels: 8.16 us -> 7.91 us  [the longest x1 7.5 us: learn(): pl.pallas_call(functools.partial(learner_kernel, count), out_shape=[jax.S...]
  transfers between devices with their start and end apart: 18 -> 24, of which waited for: 13 -> 13; matrix products, arithmetic and copies ran while one was open for 1% -> 2% of each run, Pallas kernels for 0% -> 10%
where the time goes in v7:
time: 77.8 us; the launch traced here: 77.5 us
  starting transfers between devices  42.1 us (54%)
  waiting for transfers between devices  17 us (22%)
  Pallas kernels  13.5 us (17%)
  other arithmetic  3.11 us (4%)
  between operations  1.61 us (2%)
    ppermute x21, starting transfers between devices, shifted(): return lax.ppermute(x, 'dp', pairs)  35.4 us
    ppermute x21, waiting for transfers between devices, shifted(): return lax.ppermute(x, 'dp', pairs)  14.7 us
    pallas_call x1, Pallas kernels, learn(): pl.pallas_call(functools.partial(learner_kernel, count), out_shape=[jax.S...  7.5 us
    ppermute x3, starting transfers between devices, role_swap(): return lax.ppermute(x, 'role', [(0, 1), (1, 0)])  6.71 us
    pallas_call x1, Pallas kernels, act(): pl.pallas_call(functools.partial(actor_kernel, count, unroll), out_shape=...  5.14 us
    ppermute x3, waiting for transfers between devices, role_swap(): return lax.ppermute(x, 'role', [(0, 1), (1, 0)])  2.29 us
  transfers between devices with their start and end apart: 24, of which 13 were waited for; matrix products, arithmetic and copies ran while one was open for 2% of the time, Pallas kernels for 10%

profile of v7, /device:TPU:1, one launch (start us, length us, event | category | flops | bytes accessed | tf_op | source)
XLA Modules:
  0.0 77.5 jit_solution(16936776788068442136)
XLA Ops:
  0.7 0.8 bitcast_dynamic-update-slice_fusion.11
  1.5 2.0 %collective-permute-start = (f32[72,128]{1,0:T(8,128)S(1)}, f32[72,128]{1,0:T(8,128)S(1)}, u32[]{:S(2)}, u32[]{:S(2)}) collective-permute-start(f32[72,128]{1,0:T(8,128)S(1)} %get-tuple-element.27), channel_id=1, source_target_pairs={{0,4},{1,5},{2,6},{3,7},{4,8},{5,9},{6,10},{7,11},{8,12},{9,13},{1... | collective-permute-start | bytes 110600 | tf_op jit(solution)/shard_map/ppermute | solution.py:475
  3.5 2.5 %collective-permute-start.1 = (f32[72,128]{1,0:T(8,128)S(1)}, f32[72,128]{1,0:T(8,128)S(1)}, u32[]{:S(2)}, u32[]{:S(2)}) collective-permute-start(f32[72,128]{1,0:T(8,128)S(1)} %get-tuple-element.27), channel_id=1, source_target_pairs={{0,8},{1,9},{2,10},{3,11},{4,12},{5,13},{6,14},{7,15},{8,0},{9,1},... | collective-permute-start | bytes 110600 | tf_op jit(solution)/shard_map/ppermute | solution.py:475
  6.0 1.2 %collective-permute-start.2 = (f32[72,128]{1,0:T(8,128)S(1)}, f32[72,128]{1,0:T(8,128)S(1)}, u32[]{:S(2)}, u32[]{:S(2)}) collective-permute-start(f32[72,128]{1,0:T(8,128)S(1)} %get-tuple-element.27), channel_id=1, source_target_pairs={{0,12},{1,13},{2,14},{3,15},{4,0},{5,1},{6,2},{7,3},{8,4},{9,5},{1... | collective-permute-start | bytes 110600 | tf_op jit(solution)/shard_map/ppermute | solution.py:475
  7.8 7.5 %learn.1 = (f32[288,128]{1,0:T(8,128)}, f32[288,128]{1,0:T(8,128)}, f32[288,128]{1,0:T(8,128)}, f32[288,128]{1,0:T(8,128)}) custom-call(s32[1]{0:T(128)S(6)} %copy.26.length, bf16[10,10,16,128]{3,2,1,0:T(8,128)(2,1)} %bitcast.45, s32[1,16]{1,0:T(1,128)} %actions_in.1, f32[1,16]{1,0:T(1,128)} %behaviour_in.1, f32[1,16]{1,0:T(1,128)} %regular_in.1, ...), custom_call_target="tpu_custom_call" | custom-call | flops 4000000000 | bytes 3000000 | tf_op jit(solution)/shard_map/learn/pallas_call | solution.py:402
  15.4 3.0 %collective-permute-start.3 = (f32[288,128]{1,0:T(8,128)}, f32[288,128]{1,0:T(8,128)S(1)}, u32[]{:S(2)}, u32[]{:S(2)}) collective-permute-start(f32[288,128]{1,0:T(8,128)} %get-tuple-element.18), channel_id=1, source_target_pairs={{0,32},{1,33},{2,34},{3,35},{4,36},{5,37},{6,38},{7,39},{8,40},{9,... | collective-permute-start | bytes 442376 | tf_op jit(solution)/shard_map/ppermute | solution.py:475
  18.8 2.3 %collective-permute-start.5 = (f32[288,128]{1,0:T(8,128)}, f32[288,128]{1,0:T(8,128)S(1)}, u32[]{:S(2)}, u32[]{:S(2)}) collective-permute-start(f32[288,128]{1,0:T(8,128)} %get-tuple-element.20), channel_id=1, source_target_pairs={{0,48},{1,49},{2,50},{3,51},{4,52},{5,53},{6,54},{7,55},{8,56},{9,... | collective-permute-start | bytes 442376 | tf_op jit(solution)/shard_map/ppermute | solution.py:475
  21.1 1.6 %collective-permute-start.16 = (f32[144,128]{1,0:T(8,128)S(1)}, f32[144,128]{1,0:T(8,128)S(1)}, u32[]{:S(2)}, u32[]{:S(2)}) collective-permute-start(f32[144,128]{1,0:T(8,128)S(1)} %bitcast.39), channel_id=1, source_target_pairs={{0,1},{1,2},{2,3},{3,0},{4,5},{5,6},{6,7},{7,4},{8,9},{9,10},{10,1... | collective-permute-start | bytes 221192 | tf_op jit(solution)/shard_map/ppermute | solution.py:475
  22.8 3.3 %collective-permute-start.17 = (f32[144,128]{1,0:T(8,128)S(1)}, f32[144,128]{1,0:T(8,128)S(1)}, u32[]{:S(2)}, u32[]{:S(2)}) collective-permute-start(f32[144,128]{1,0:T(8,128)S(1)} %bitcast.40), channel_id=1, source_target_pairs={{0,2},{1,3},{2,0},{3,1},{4,6},{5,7},{6,4},{7,5},{8,10},{9,11},{10,... | collective-permute-start | bytes 221192 | tf_op jit(solution)/shard_map/ppermute | solution.py:475
  26.1 0.9 %add_add_fusion.2 = f32[288,128]{1,0:T(8,128)S(1)} fusion(f32[288,128]{1,0:T(8,128)S(1)} %collective-permute-done.4, f32[288,128]{1,0:T(8,128)S(1)} %collective-permute-done.5, f32[288,128]{1,0:T(8,128)} %get-tuple-element.17, f32[288,128]{1,0:T(8,128)S(1)} %collective-permute-done.3), kind=kLoop, calls=%fused_computation.7 | loop fusion | flops 110592 | bytes 737280 | tf_op jit(solution)/shard_map/add | solution.py:483
  27.7 2.3 %collective-permute-start.8 = (f32[288,128]{1,0:T(8,128)S(1)}, f32[288,128]{1,0:T(8,128)S(1)}, u32[]{:S(2)}, u32[]{:S(2)}) collective-permute-start(f32[288,128]{1,0:T(8,128)S(1)} %add_add_fusion.2), channel_id=1, source_target_pairs={{0,12},{1,13},{2,14},{3,15},{4,0},{5,1},{6,2},{7,3},{8,4},{9,5},{1... | collective-permute-start | bytes 442376 | tf_op jit(solution)/shard_map/ppermute | solution.py:475
  30.1 2.7 %collective-permute-done.6 = f32[288,128]{1,0:T(8,128)S(1)} collective-permute-done((f32[288,128]{1,0:T(8,128)S(1)}, f32[288,128]{1,0:T(8,128)S(1)}, u32[]{:S(2)}, u32[]{:S(2)}) %collective-permute-start.6) | collective-permute-done | bytes 147488 | tf_op jit(solution)/shard_map/ppermute | solution.py:475
  32.7 3.5 %collective-permute-start.18 = (f32[144,128]{1,0:T(8,128)S(1)}, f32[144,128]{1,0:T(8,128)S(1)}, u32[]{:S(2)}, u32[]{:S(2)}) collective-permute-start(f32[144,128]{1,0:T(8,128)S(1)} %bitcast.42), channel_id=1, source_target_pairs={{0,3},{1,0},{2,1},{3,2},{4,7},{5,4},{6,5},{7,6},{8,11},{9,8},{10,9... | collective-permute-start | bytes 221192 | tf_op jit(solution)/shard_map/ppermute | solution.py:475
  36.2 2.1 %collective-permute-start.10 = (f32[288,128]{1,0:T(8,128)S(1)}, f32[288,128]{1,0:T(8,128)S(1)}, u32[]{:S(2)}, u32[]{:S(2)}) collective-permute-start(f32[288,128]{1,0:T(8,128)S(1)} %add_add_fusion.1), channel_id=1, source_target_pairs={{0,1},{1,2},{2,3},{3,0},{4,5},{5,6},{6,7},{7,4},{8,9},{9,10},{10,1... | collective-permute-start | bytes 442376 | tf_op jit(solution)/shard_map/ppermute | solution.py:475
  38.3 2.2 %collective-permute-start.11 = (f32[288,128]{1,0:T(8,128)S(1)}, f32[288,128]{1,0:T(8,128)S(1)}, u32[]{:S(2)}, u32[]{:S(2)}) collective-permute-start(f32[288,128]{1,0:T(8,128)S(1)} %add_add_fusion.1), channel_id=1, source_target_pairs={{0,3},{1,0},{2,1},{3,2},{4,7},{5,4},{6,5},{7,6},{8,11},{9,8},{10,9... | collective-permute-start | bytes 442376 | tf_op jit(solution)/shard_map/ppermute | solution.py:475
  40.5 1.2 %collective-permute-start.9 = (f32[288,128]{1,0:T(8,128)S(1)}, f32[288,128]{1,0:T(8,128)S(1)}, u32[]{:S(2)}, u32[]{:S(2)}) collective-permute-start(f32[288,128]{1,0:T(8,128)S(1)} %add_add_fusion.1), channel_id=1, source_target_pairs={{0,2},{1,3},{2,0},{3,1},{4,6},{5,7},{6,4},{7,5},{8,10},{9,11},{10,... | collective-permute-start | bytes 442376 | tf_op jit(solution)/shard_map/ppermute | solution.py:475
  41.8 1.2 %collective-permute-done.10 = f32[288,128]{1,0:T(8,128)S(1)} collective-permute-done((f32[288,128]{1,0:T(8,128)S(1)}, f32[288,128]{1,0:T(8,128)S(1)}, u32[]{:S(2)}, u32[]{:S(2)}) %collective-permute-start.10) | collective-permute-done | bytes 147488 | tf_op jit(solution)/shard_map/ppermute | solution.py:475
  43.0 0.9 %collective-permute-done.11 = f32[288,128]{1,0:T(8,128)S(1)} collective-permute-done((f32[288,128]{1,0:T(8,128)S(1)}, f32[288,128]{1,0:T(8,128)S(1)}, u32[]{:S(2)}, u32[]{:S(2)}) %collective-permute-start.11) | collective-permute-done | bytes 147488 | tf_op jit(solution)/shard_map/ppermute | solution.py:475
  43.9 3.6 %collective-permute-done.9 = f32[288,128]{1,0:T(8,128)S(1)} collective-permute-done((f32[288,128]{1,0:T(8,128)S(1)}, f32[288,128]{1,0:T(8,128)S(1)}, u32[]{:S(2)}, u32[]{:S(2)}) %collective-permute-start.9) | collective-permute-done | bytes 147488 | tf_op jit(solution)/shard_map/ppermute | solution.py:475
  47.5 3.0 %collective-permute-start.12 = (f32[1,128]{1,0:T(1,128)S(1)}, f32[1,128]{1,0:T(1,128)S(1)}, u32[]{:S(2)}, u32[]{:S(2)}) collective-permute-start(f32[1,128]{1,0:T(1,128)S(1)} %bitcast.44), channel_id=1, source_target_pairs={{0,64},{64,0},{1,65},{65,1},{2,66},{66,2},{3,67},{67,3},{4,68},{68... | collective-permute-start | bytes 1544 | tf_op jit(solution)/shard_map/ppermute | solution.py:500
  50.5 0.8 %collective-permute-done.12 = f32[1,128]{1,0:T(1,128)S(1)} collective-permute-done((f32[1,128]{1,0:T(1,128)S(1)}, f32[1,128]{1,0:T(1,128)S(1)}, u32[]{:S(2)}, u32[]{:S(2)}) %collective-permute-start.12) | collective-permute-done | bytes 544 | tf_op jit(solution)/shard_map/ppermute | solution.py:500
  51.3 1.1 %collective-permute-start.13 = (f32[1,128]{1,0:T(1,128)S(1)}, f32[1,128]{1,0:T(1,128)S(1)}, u32[]{:S(2)}, u32[]{:S(2)}) collective-permute-start(f32[1,128]{1,0:T(1,128)S(1)} %bitcast_add_fusion), channel_id=1, source_target_pairs={{0,32},{1,33},{2,34},{3,35},{4,36},{5,37},{6,38},{7,39},{8,40},{9,... | collective-permute-start | bytes 1544 | tf_op jit(solution)/shard_map/ppermute | solution.py:475
  52.4 2.1 %collective-permute-start.14 = (f32[1,128]{1,0:T(1,128)S(1)}, f32[1,128]{1,0:T(1,128)S(1)}, u32[]{:S(2)}, u32[]{:S(2)}) collective-permute-start(f32[1,128]{1,0:T(1,128)S(1)} %bitcast_add_fusion), channel_id=1, source_target_pairs={{0,16},{1,17},{2,18},{3,19},{4,20},{5,21},{6,22},{7,23},{8,24},{9,... | collective-permute-start | bytes 1544 | tf_op jit(solution)/shard_map/ppermute | solution.py:475
  55.2 0.8 %collective-permute-done.14 = f32[1,128]{1,0:T(1,128)S(1)} collective-permute-done((f32[1,128]{1,0:T(1,128)S(1)}, f32[1,128]{1,0:T(1,128)S(1)}, u32[]{:S(2)}, u32[]{:S(2)}) %collective-permute-start.14) | collective-permute-done | bytes 544 | tf_op jit(solution)/shard_map/ppermute | solution.py:475
  56.0 0.9 %collective-permute-done.15 = f32[1,128]{1,0:T(1,128)S(1)} collective-permute-done((f32[1,128]{1,0:T(1,128)S(1)}, f32[1,128]{1,0:T(1,128)S(1)}, u32[]{:S(2)}, u32[]{:S(2)}) %collective-permute-start.15) | collective-permute-done | bytes 544 | tf_op jit(solution)/shard_map/ppermute | solution.py:475
  57.4 2.9 %collective-permute-start.20 = (f32[288,128]{1,0:T(8,128)S(1)}, f32[288,128]{1,0:T(8,128)S(1)}, u32[]{:S(2)}, u32[]{:S(2)}) collective-permute-start(f32[288,128]{1,0:T(8,128)S(1)} %update.1), channel_id=1, source_target_pairs={{0,32},{1,33},{2,34},{3,35},{4,36},{5,37},{6,38},{7,39},{8,40},{9,... | collective-permute-start | bytes 442376 | tf_op jit(solution)/shard_map/ppermute | solution.py:475
  60.8 1.8 %collective-permute-done.19 = f32[288,128]{1,0:T(8,128)S(1)} collective-permute-done((f32[288,128]{1,0:T(8,128)S(1)}, f32[288,128]{1,0:T(8,128)S(1)}, u32[]{:S(2)}, u32[]{:S(2)}) %collective-permute-start.19) | collective-permute-done | bytes 147488 | tf_op jit(solution)/shard_map/ppermute | solution.py:475
  62.6 2.4 %collective-permute-done.20 = f32[288,128]{1,0:T(8,128)S(1)} collective-permute-done((f32[288,128]{1,0:T(8,128)S(1)}, f32[288,128]{1,0:T(8,128)S(1)}, u32[]{:S(2)}, u32[]{:S(2)}) %collective-permute-start.20) | collective-permute-done | bytes 147488 | tf_op jit(solution)/shard_map/ppermute | solution.py:475
  65.4 3.3 %collective-permute-start.22 = (f32[4,288,128]{2,1,0:T(8,128)S(1)}, f32[4,288,128]{2,1,0:T(8,128)S(1)}, u32[]{:S(2)}, u32[]{:S(2)}) collective-permute-start(f32[4,288,128]{2,1,0:T(8,128)S(1)} %bitcast_dynamic-update-slice_fusion.mine), channel_id=1, source_target_pairs={{0,64},{64,0},{1,65},{65,1},{2,66},{66,2},{3,67},{67,3},{4,68},{68... | collective-permute-start | bytes 1769480 | tf_op jit(solution)/shard_map/ppermute | solution.py:500
  69.2 1.2 %collective-permute-done.22.other = f32[4,288,128]{2,1,0:T(8,128)S(1)} collective-permute-done((f32[4,288,128]{2,1,0:T(8,128)S(1)}, f32[4,288,128]{2,1,0:T(8,128)S(1)}, u32[]{:S(2)}, u32[]{:S(2)}) %collective-permute-start.22) | collective-permute-done | bytes 589856 | tf_op jit(solution)/shard_map/ppermute | solution.py:500
  70.4 5.1 %act.1 = f32[32,400]{1,0:T(8,128)S(1)} custom-call(f32[4,288,128]{2,1,0:T(8,128)S(1)} %bitcast_dynamic-update-slice_fusion.mine, f32[4,288,128]{2,1,0:T(8,128)S(1)} %collective-permute-done.22.other, bf16[12,6,2,32,128]{4,3,2,1,0:T(8,128)(2,1)S(1)} %get-tuple-element.22.boards, bf16[1280,128]{1,0:T(8,128)(2,1)S(1)} %get-tuple-element.23.heads), custom_call_target="tpu_custom_call" | custom-call | flops 8000000000 | bytes 4000000 | tf_op jit(solution)/shard_map/act/pallas_call | solution.py:183
  76.9 0.7 pad_maximum_fusion
  (51 shorter events, 5.1 us)
Async XLA Ops:
  1.5 13.9 %collective-permute-start = (f32[72,128]{1,0:T(8,128)S(1)}, f32[72,128]{1,0:T(8,128)S(1)}, u32[]{:S(2)}, u32[]{:S(2)}) collective-permute-start(f32[72,128]{1,0:T(8,128)S(1)} %get-tuple-element.27), channel_id=1, source_target_pairs={{0,4},{1,5},{2,6},{3,7},{4,8},{5,9},{6,10},{7,11},{8,12},{9,13},{1... | collective-permute-start | bytes 110600 | tf_op jit(solution)/shard_map/ppermute | solution.py:475
  3.5 11.9 %collective-permute-start.1 = (f32[72,128]{1,0:T(8,128)S(1)}, f32[72,128]{1,0:T(8,128)S(1)}, u32[]{:S(2)}, u32[]{:S(2)}) collective-permute-start(f32[72,128]{1,0:T(8,128)S(1)} %get-tuple-element.27), channel_id=1, source_target_pairs={{0,8},{1,9},{2,10},{3,11},{4,12},{5,13},{6,14},{7,15},{8,0},{9,1},... | collective-permute-start | bytes 110600 | tf_op jit(solution)/shard_map/ppermute | solution.py:475
  6.0 9.4 %collective-permute-start.2 = (f32[72,128]{1,0:T(8,128)S(1)}, f32[72,128]{1,0:T(8,128)S(1)}, u32[]{:S(2)}, u32[]{:S(2)}) collective-permute-start(f32[72,128]{1,0:T(8,128)S(1)} %get-tuple-element.27), channel_id=1, source_target_pairs={{0,12},{1,13},{2,14},{3,15},{4,0},{5,1},{6,2},{7,3},{8,4},{9,5},{1... | collective-permute-start | bytes 110600 | tf_op jit(solution)/shard_map/ppermute | solution.py:475
  15.4 10.6 %collective-permute-start.3 = (f32[288,128]{1,0:T(8,128)}, f32[288,128]{1,0:T(8,128)S(1)}, u32[]{:S(2)}, u32[]{:S(2)}) collective-permute-start(f32[288,128]{1,0:T(8,128)} %get-tuple-element.18), channel_id=1, source_target_pairs={{0,32},{1,33},{2,34},{3,35},{4,36},{5,37},{6,38},{7,39},{8,40},{9,... | collective-permute-start | bytes 442376 | tf_op jit(solution)/shard_map/ppermute | solution.py:475
  18.4 7.6 %collective-permute-start.4 = (f32[288,128]{1,0:T(8,128)}, f32[288,128]{1,0:T(8,128)S(1)}, u32[]{:S(2)}, u32[]{:S(2)}) collective-permute-start(f32[288,128]{1,0:T(8,128)} %get-tuple-element.19), channel_id=1, source_target_pairs={{0,16},{1,17},{2,18},{3,19},{4,20},{5,21},{6,22},{7,23},{8,24},{9,... | collective-permute-start | bytes 442376 | tf_op jit(solution)/shard_map/ppermute | solution.py:475
  18.8 7.2 %collective-permute-start.5 = (f32[288,128]{1,0:T(8,128)}, f32[288,128]{1,0:T(8,128)S(1)}, u32[]{:S(2)}, u32[]{:S(2)}) collective-permute-start(f32[288,128]{1,0:T(8,128)} %get-tuple-element.20), channel_id=1, source_target_pairs={{0,48},{1,49},{2,50},{3,51},{4,52},{5,53},{6,54},{7,55},{8,56},{9,... | collective-permute-start | bytes 442376 | tf_op jit(solution)/shard_map/ppermute | solution.py:475
  21.1 19.4 %collective-permute-start.16 = (f32[144,128]{1,0:T(8,128)S(1)}, f32[144,128]{1,0:T(8,128)S(1)}, u32[]{:S(2)}, u32[]{:S(2)}) collective-permute-start(f32[144,128]{1,0:T(8,128)S(1)} %bitcast.39), channel_id=1, source_target_pairs={{0,1},{1,2},{2,3},{3,0},{4,5},{5,6},{6,7},{7,4},{8,9},{9,10},{10,1... | collective-permute-start | bytes 221192 | tf_op jit(solution)/shard_map/ppermute | solution.py:475
  22.8 27.7 %collective-permute-start.17 = (f32[144,128]{1,0:T(8,128)S(1)}, f32[144,128]{1,0:T(8,128)S(1)}, u32[]{:S(2)}, u32[]{:S(2)}) collective-permute-start(f32[144,128]{1,0:T(8,128)S(1)} %bitcast.40), channel_id=1, source_target_pairs={{0,2},{1,3},{2,0},{3,1},{4,6},{5,7},{6,4},{7,5},{8,10},{9,11},{10,... | collective-permute-start | bytes 221192 | tf_op jit(solution)/shard_map/ppermute | solution.py:475
  27.0 29.9 %copy-start = (f32[2304,128]{1,0:T(8,128)S(1)}, f32[2304,128]{1,0:T(8,128)}, u32[]{:S(2)}) copy-start(f32[2304,128]{1,0:T(8,128)} %torso_in.1) | copy-start | bytes 3538948
  27.0 5.7 %collective-permute-start.6 = (f32[288,128]{1,0:T(8,128)S(1)}, f32[288,128]{1,0:T(8,128)S(1)}, u32[]{:S(2)}, u32[]{:S(2)}) collective-permute-start(f32[288,128]{1,0:T(8,128)S(1)} %add_add_fusion.2), channel_id=1, source_target_pairs={{0,8},{1,9},{2,10},{3,11},{4,12},{5,13},{6,14},{7,15},{8,0},{9,1},... | collective-permute-start | bytes 442376 | tf_op jit(solution)/shard_map/ppermute | solution.py:475
  27.3 8.9 %collective-permute-start.7 = (f32[288,128]{1,0:T(8,128)S(1)}, f32[288,128]{1,0:T(8,128)S(1)}, u32[]{:S(2)}, u32[]{:S(2)}) collective-permute-start(f32[288,128]{1,0:T(8,128)S(1)} %add_add_fusion.2), channel_id=1, source_target_pairs={{0,4},{1,5},{2,6},{3,7},{4,8},{5,9},{6,10},{7,11},{8,12},{9,13},{1... | collective-permute-start | bytes 442376 | tf_op jit(solution)/shard_map/ppermute | solution.py:475
  27.7 8.5 %collective-permute-start.8 = (f32[288,128]{1,0:T(8,128)S(1)}, f32[288,128]{1,0:T(8,128)S(1)}, u32[]{:S(2)}, u32[]{:S(2)}) collective-permute-start(f32[288,128]{1,0:T(8,128)S(1)} %add_add_fusion.2), channel_id=1, source_target_pairs={{0,12},{1,13},{2,14},{3,15},{4,0},{5,1},{6,2},{7,3},{8,4},{9,5},{1... | collective-permute-start | bytes 442376 | tf_op jit(solution)/shard_map/ppermute | solution.py:475
  32.7 22.3 %collective-permute-start.18 = (f32[144,128]{1,0:T(8,128)S(1)}, f32[144,128]{1,0:T(8,128)S(1)}, u32[]{:S(2)}, u32[]{:S(2)}) collective-permute-start(f32[144,128]{1,0:T(8,128)S(1)} %bitcast.42), channel_id=1, source_target_pairs={{0,3},{1,0},{2,1},{3,2},{4,7},{5,4},{6,5},{7,6},{8,11},{9,8},{10,9... | collective-permute-start | bytes 221192 | tf_op jit(solution)/shard_map/ppermute | solution.py:475
  36.2 6.7 %collective-permute-start.10 = (f32[288,128]{1,0:T(8,128)S(1)}, f32[288,128]{1,0:T(8,128)S(1)}, u32[]{:S(2)}, u32[]{:S(2)}) collective-permute-start(f32[288,128]{1,0:T(8,128)S(1)} %add_add_fusion.1), channel_id=1, source_target_pairs={{0,1},{1,2},{2,3},{3,0},{4,5},{5,6},{6,7},{7,4},{8,9},{9,10},{10,1... | collective-permute-start | bytes 442376 | tf_op jit(solution)/shard_map/ppermute | solution.py:475
  38.3 5.5 %collective-permute-start.11 = (f32[288,128]{1,0:T(8,128)S(1)}, f32[288,128]{1,0:T(8,128)S(1)}, u32[]{:S(2)}, u32[]{:S(2)}) collective-permute-start(f32[288,128]{1,0:T(8,128)S(1)} %add_add_fusion.1), channel_id=1, source_target_pairs={{0,3},{1,0},{2,1},{3,2},{4,7},{5,4},{6,5},{7,6},{8,11},{9,8},{10,9... | collective-permute-start | bytes 442376 | tf_op jit(solution)/shard_map/ppermute | solution.py:475
  40.5 6.9 %collective-permute-start.9 = (f32[288,128]{1,0:T(8,128)S(1)}, f32[288,128]{1,0:T(8,128)S(1)}, u32[]{:S(2)}, u32[]{:S(2)}) collective-permute-start(f32[288,128]{1,0:T(8,128)S(1)} %add_add_fusion.1), channel_id=1, source_target_pairs={{0,2},{1,3},{2,0},{3,1},{4,6},{5,7},{6,4},{7,5},{8,10},{9,11},{10,... | collective-permute-start | bytes 442376 | tf_op jit(solution)/shard_map/ppermute | solution.py:475
  47.5 3.8 %collective-permute-start.12 = (f32[1,128]{1,0:T(1,128)S(1)}, f32[1,128]{1,0:T(1,128)S(1)}, u32[]{:S(2)}, u32[]{:S(2)}) collective-permute-start(f32[1,128]{1,0:T(1,128)S(1)} %bitcast.44), channel_id=1, source_target_pairs={{0,64},{64,0},{1,65},{65,1},{2,66},{66,2},{3,67},{67,3},{4,68},{68... | collective-permute-start | bytes 1544 | tf_op jit(solution)/shard_map/ppermute | solution.py:500
  51.3 3.9 %collective-permute-start.13 = (f32[1,128]{1,0:T(1,128)S(1)}, f32[1,128]{1,0:T(1,128)S(1)}, u32[]{:S(2)}, u32[]{:S(2)}) collective-permute-start(f32[1,128]{1,0:T(1,128)S(1)} %bitcast_add_fusion), channel_id=1, source_target_pairs={{0,32},{1,33},{2,34},{3,35},{4,36},{5,37},{6,38},{7,39},{8,40},{9,... | collective-permute-start | bytes 1544 | tf_op jit(solution)/shard_map/ppermute | solution.py:475
  52.4 3.6 %collective-permute-start.14 = (f32[1,128]{1,0:T(1,128)S(1)}, f32[1,128]{1,0:T(1,128)S(1)}, u32[]{:S(2)}, u32[]{:S(2)}) collective-permute-start(f32[1,128]{1,0:T(1,128)S(1)} %bitcast_add_fusion), channel_id=1, source_target_pairs={{0,16},{1,17},{2,18},{3,19},{4,20},{5,21},{6,22},{7,23},{8,24},{9,... | collective-permute-start | bytes 1544 | tf_op jit(solution)/shard_map/ppermute | solution.py:475
  54.5 2.4 %collective-permute-start.15 = (f32[1,128]{1,0:T(1,128)S(1)}, f32[1,128]{1,0:T(1,128)S(1)}, u32[]{:S(2)}, u32[]{:S(2)}) collective-permute-start(f32[1,128]{1,0:T(1,128)S(1)} %bitcast_add_fusion), channel_id=1, source_target_pairs={{0,48},{1,49},{2,50},{3,51},{4,52},{5,53},{6,54},{7,55},{8,56},{9,... | collective-permute-start | bytes 1544 | tf_op jit(solution)/shard_map/ppermute | solution.py:475
  57.3 11.4 %copy-start.2 = (bf16[128,4]{0,1:T(4,128)(2,1)S(1)}, bf16[128,4]{0,1:T(4,128)(2,1)}, u32[]{:S(2)}) copy-start(bf16[128,4]{0,1:T(4,128)(2,1)} %param.20) | copy-start | bytes 3076
  57.3 11.4 %copy-start.1 = (bf16[64,10,10,128]{3,0,2,1:T(8,128)(2,1)S(1)}, bf16[64,10,10,128]{3,0,2,1:T(8,128)(2,1)}, u32[]{:S(2)}) copy-start(bf16[64,10,10,128]{3,0,2,1:T(8,128)(2,1)} %param.12) | copy-start | bytes 4915204
  57.3 5.3 %collective-permute-start.19 = (f32[288,128]{1,0:T(8,128)S(1)}, f32[288,128]{1,0:T(8,128)S(1)}, u32[]{:S(2)}, u32[]{:S(2)}) collective-permute-start(f32[288,128]{1,0:T(8,128)S(1)} %update.1), channel_id=1, source_target_pairs={{0,16},{1,17},{2,18},{3,19},{4,20},{5,21},{6,22},{7,23},{8,24},{9,... | collective-permute-start | bytes 442376 | tf_op jit(solution)/shard_map/ppermute | solution.py:475
  57.4 7.6 %collective-permute-start.20 = (f32[288,128]{1,0:T(8,128)S(1)}, f32[288,128]{1,0:T(8,128)S(1)}, u32[]{:S(2)}, u32[]{:S(2)}) collective-permute-start(f32[288,128]{1,0:T(8,128)S(1)} %update.1), channel_id=1, source_target_pairs={{0,32},{1,33},{2,34},{3,35},{4,36},{5,37},{6,38},{7,39},{8,40},{9,... | collective-permute-start | bytes 442376 | tf_op jit(solution)/shard_map/ppermute | solution.py:475
  60.4 5.1 %collective-permute-start.21 = (f32[288,128]{1,0:T(8,128)S(1)}, f32[288,128]{1,0:T(8,128)S(1)}, u32[]{:S(2)}, u32[]{:S(2)}) collective-permute-start(f32[288,128]{1,0:T(8,128)S(1)} %update.1), channel_id=1, source_target_pairs={{0,48},{1,49},{2,50},{3,51},{4,52},{5,53},{6,54},{7,55},{8,56},{9,... | collective-permute-start | bytes 442376 | tf_op jit(solution)/shard_map/ppermute | solution.py:475
  65.4 4.9 %collective-permute-start.22 = (f32[4,288,128]{2,1,0:T(8,128)S(1)}, f32[4,288,128]{2,1,0:T(8,128)S(1)}, u32[]{:S(2)}, u32[]{:S(2)}) collective-permute-start(f32[4,288,128]{2,1,0:T(8,128)S(1)} %bitcast_dynamic-update-slice_fusion.mine), channel_id=1, source_target_pairs={{0,64},{64,0},{1,65},{65,1},{2,66},{66,2},{3,67},{67,3},{4,68},{68... | collective-permute-start | bytes 1769480 | tf_op jit(solution)/shard_map/ppermute | solution.py:500
  75.5 1.4 %collective-permute-start.23 = (f32[32,400]{1,0:T(8,128)S(1)}, f32[32,400]{1,0:T(8,128)S(1)}, u32[]{:S(2)}, u32[]{:S(2)}) collective-permute-start(f32[32,400]{1,0:T(8,128)S(1)} %act.1), channel_id=1, source_target_pairs={{0,64},{64,0},{1,65},{65,1},{2,66},{66,2},{3,67},{67,3},{4,68},{68... | collective-permute-start | bytes 153608 | tf_op jit(solution)/shard_map/ppermute | solution.py:500

commit v8 on v7

--- a/solution.py
+++ b/solution.py
@@ -211,9 +211,9 @@
 
 
 def learner_kernel(
-    count, length, boards_in, actions_in, behaviour_in, regular_in, rewards_in, weights_in,
+    count, length_in, boards_in, actions_in, behaviour_in, regular_in, rewards_in, weights_in,
     policy_in, value_in, own, next1, next2, next3,
-    grad, boards, weights, actions, behaviour, regular, rewards, policy_t, value_t, pairs, back_pairs,
+    grad, length, boards, weights, actions, behaviour, regular, rewards, policy_t, value_t, pairs, back_pairs,
     middle, last, masks, slope, turned, done,
 ):
     slots = boards.shape[3]
@@ -229,6 +229,7 @@
         (rewards_in, rewards),
         (policy_in, policy_t),
         (value_in, value_t),
+        (length_in, length),
     ]
     copies = [pltpu.make_async_copy(a, b, done.at[k]) for k, (a, b) in enumerate(moves)]
     for copy in copies:
@@ -324,11 +325,7 @@
 
     value_cell = value_grad * (1.0 - value * value) / 100.0
     by_policy = policy_grad[None] * (taken.astype(jnp.float32) - jnp.exp(scores - log_total[None]))
-    in_policy = (lane % 8 < 4) & (lane < 24)
-    in_value = (lane % 8 == 4) & (lane < 24)
-    by_score = jnp.where(
-        in_policy[None], by_policy, jnp.where(in_value, value_cell, 0.0)[None]
-    )
+    by_score = jnp.where((lane % 8 == 4)[None], value_cell[None], by_policy)
     high = by_score.astype(jnp.bfloat16)
     rest = by_score - high.astype(jnp.float32)
     mid = rest.astype(jnp.bfloat16)
@@ -370,15 +367,25 @@
         @pl.when(role == core)
         def _(core=core):
             for layer, source in ((1, middle), (0, boards)):
-                across = turned[layer]
+                kept = []
                 for offset in range(9):
                     parts = [x for x in segment_parts(layer, offset) if x[0] % 2 == core]
                     if parts:
-                        p, q = offset // 3, offset % 3
-                        cols = [source[p : p + 10, (j + q) // 2, (j + q) % 2] for j in range(10)]
-                        window = jnp.stack(cols, axis=1).reshape(-1, 128)
-                        block = jnp.dot(across, window, preferred_element_type=jnp.float32).T
-                        for segment, first, end, at in parts:
+                        kept.append((offset, parts))
+                windows = []
+                for offset, _ in kept:
+                    p, q = offset // 3, offset % 3
+                    cols = [source[p : p + 10, (j + q) // 2, (j + q) % 2] for j in range(10)]
+                    windows.append(jnp.stack(cols, axis=1).reshape(-1, 128))
+                for pair in range(0, len(kept), 2):
+                    blocks = jnp.dot(
+                        turned[layer],
+                        jnp.concatenate(windows[pair : pair + 2], axis=1),
+                        preferred_element_type=jnp.float32,
+                    )
+                    for k in range(2):
+                        block = blocks[:, 128 * k : 128 * k + 128].T
+                        for segment, first, end, at in kept[pair + k][1]:
                             grad[segment // 2, first:end] = block[at : at + end - first]
 
     sends = [
@@ -395,17 +402,17 @@
     length, boards, actions, behaviour, regular, rewards, weights, policy_t, value_t, count=5
 ):
     slots = boards.shape[2]
-    smem = pl.BlockSpec(memory_space=pltpu.SMEM)
     anywhere = pl.BlockSpec(memory_space=pltpu.HBM)
     cells = (10, 5, 2, slots, 128)
     around = (12, 6, 2, slots, 128)
     return pl.pallas_call(
         functools.partial(learner_kernel, count),
         out_shape=[jax.ShapeDtypeStruct((SEGMENT, 128), jnp.float32)] * LINE,
-        in_specs=[smem] + [anywhere] * 8,
-        out_specs=[anywhere] * LINE,
+        in_specs=[anywhere] * 9,
+        out_specs=[pl.BlockSpec(memory_space=pl.ANY)] * LINE,
         scratch_shapes=[
             pltpu.VMEM((LINE, SEGMENT, 128), jnp.float32),
+            pltpu.SMEM((1,), jnp.int32),
             pltpu.VMEM(around, jnp.bfloat16),
             pltpu.VMEM((2 * ROWS, 128), jnp.float32),
             pltpu.VMEM((1, slots), jnp.int32),
@@ -421,7 +428,7 @@
             pltpu.VMEM((2,) + cells, jnp.bfloat16),
             pltpu.VMEM(around, jnp.bfloat16),
             pltpu.VMEM((2, 128, 100 * slots), jnp.bfloat16),
-            pltpu.SemaphoreType.DMA((9,)),
+            pltpu.SemaphoreType.DMA((10,)),
         ],
         compiler_params=pltpu.CompilerParams(vmem_limit_bytes=60 * 1024 * 1024),
         cost_estimate=pl.CostEstimate(
@@ -517,8 +524,6 @@
     role = lax.axis_index("role")
     dp = lax.axis_index("dp")
     y, x, z = dp // (LINE * LINE), dp // LINE % LINE, dp % LINE
-    moments = line_gather(jnp.concatenate([first_moment, second_moment]), "x", x)
-    moments = lax.dynamic_slice_in_dim(moments, 2 * role, 2, 0).reshape(-1, 128)
     chunks = learn(
         lengths,
         by_cell(traj_boards[0]),
@@ -530,7 +535,11 @@
         policy_head.T,
         value_head[None],
     )
-    chunks, moments = lax.optimization_barrier((chunks, moments))
+    chunks, moments = lax.optimization_barrier(
+        (chunks, jnp.concatenate([first_moment, second_moment]))
+    )
+    moments = line_gather(moments, "x", x)
+    moments = lax.dynamic_slice_in_dim(moments, 2 * role, 2, 0).reshape(-1, 128)
     moments = line_gather(moments, "z", z)
     summed = line_total(line_total(line_scatter(chunks, "y"), "x"), "z")
     squares = jnp.sum(summed * summed, axis=0, keepdims=True)

time: 77.8 us -> 76.2 us (0.979)
  starting transfers between devices: 42.1 us -> 40.6 us
    ppermute x3, starting transfers between devices: 6.71 us -> 5.14 us  [role_swap(): return lax.ppermute(x, 'role', [(0, 1), (1, 0)])]
  transfers between devices with their start and end apart: 24 -> 24, of which waited for: 13 -> 11; matrix products, arithmetic and copies ran while one was open for 2% -> 1% of each run, Pallas kernels for 10% -> 1%
where the time goes in v8:
time: 76.2 us; the launch traced here: 76 us
  starting transfers between devices  40.6 us (53%)
  waiting for transfers between devices  17.5 us (23%)
  Pallas kernels  12.9 us (17%)
  other arithmetic  3.11 us (4%)
  between operations  1.73 us (2%)
    ppermute x21, starting transfers between devices, shifted(): return lax.ppermute(x, 'dp', pairs)  35.4 us
    ppermute x21, waiting for transfers between devices, shifted(): return lax.ppermute(x, 'dp', pairs)  15.2 us
    pallas_call x1, Pallas kernels, learn(): pl.pallas_call(functools.partial(learner_kernel, count), out_shape=[jax.S...  6.95 us
    ppermute x3, starting transfers between devices, role_swap(): return lax.ppermute(x, 'role', [(0, 1), (1, 0)])  5.14 us
    pallas_call x1, Pallas kernels, act(): pl.pallas_call(functools.partial(actor_kernel, count, unroll), out_shape=...  5.14 us
    ppermute x3, waiting for transfers between devices, role_swap(): return lax.ppermute(x, 'role', [(0, 1), (1, 0)])  2.29 us
  transfers between devices with their start and end apart: 24, of which 11 were waited for; matrix products, arithmetic and copies ran while one was open for 1% of the time, Pallas kernels for 1%

profile of v8, /device:TPU:1, one launch (start us, length us, event | category | flops | bytes accessed | tf_op | source)
XLA Modules:
  0.0 76.0 jit_solution(1692310976328248172)
XLA Ops:
  1.3 0.8 pad_maximum_fusion.1
  2.0 7.0 %learn.1 = (f32[288,128]{1,0:T(8,128)}, f32[288,128]{1,0:T(8,128)}, f32[288,128]{1,0:T(8,128)}, f32[288,128]{1,0:T(8,128)}) custom-call(s32[1]{0:T(128)S(6)} %copy.26.length_in, bf16[10,10,16,128]{3,2,1,0:T(8,128)(2,1)} %bitcast.46, s32[1,16]{1,0:T(1,128)} %actions_in.1, f32[1,16]{1,0:T(1,128)} %behaviour_in.1, f32[1,16]{1,0:T(1,128)} %regular_in.1, ...), custom_call_target="tpu_custom_call" | custom-call | flops 4000000000 | bytes 3000000 | tf_op jit(solution)/shard_map/learn/pallas_call | solution.py:408
  9.0 2.1 %collective-permute-start.13 = (f32[72,128]{1,0:T(8,128)S(1)}, f32[72,128]{1,0:T(8,128)S(1)}, u32[]{:S(2)}, u32[]{:S(2)}) collective-permute-start(f32[72,128]{1,0:T(8,128)S(1)} %pad_maximum_fusion.1), channel_id=1, source_target_pairs={{0,4},{1,5},{2,6},{3,7},{4,8},{5,9},{6,10},{7,11},{8,12},{9,13},{1... | collective-permute-start | bytes 110600 | tf_op jit(solution)/shard_map/ppermute | solution.py:482
  11.1 2.4 %collective-permute-start.14 = (f32[72,128]{1,0:T(8,128)S(1)}, f32[72,128]{1,0:T(8,128)S(1)}, u32[]{:S(2)}, u32[]{:S(2)}) collective-permute-start(f32[72,128]{1,0:T(8,128)S(1)} %pad_maximum_fusion.1), channel_id=1, source_target_pairs={{0,8},{1,9},{2,10},{3,11},{4,12},{5,13},{6,14},{7,15},{8,0},{9,1},... | collective-permute-start | bytes 110600 | tf_op jit(solution)/shard_map/ppermute | solution.py:482
  13.5 1.2 %collective-permute-start.15 = (f32[72,128]{1,0:T(8,128)S(1)}, f32[72,128]{1,0:T(8,128)S(1)}, u32[]{:S(2)}, u32[]{:S(2)}) collective-permute-start(f32[72,128]{1,0:T(8,128)S(1)} %pad_maximum_fusion.1), channel_id=1, source_target_pairs={{0,12},{1,13},{2,14},{3,15},{4,0},{5,1},{6,2},{7,3},{8,4},{9,5},{1... | collective-permute-start | bytes 110600 | tf_op jit(solution)/shard_map/ppermute | solution.py:482
  14.7 2.9 %collective-permute-start = (f32[288,128]{1,0:T(8,128)}, f32[288,128]{1,0:T(8,128)S(1)}, u32[]{:S(2)}, u32[]{:S(2)}) collective-permute-start(f32[288,128]{1,0:T(8,128)} %get-tuple-element.18), channel_id=1, source_target_pairs={{0,32},{1,33},{2,34},{3,35},{4,36},{5,37},{6,38},{7,39},{8,40},{9,... | collective-permute-start | bytes 442376 | tf_op jit(solution)/shard_map/ppermute | solution.py:482
  18.3 2.3 %collective-permute-start.2 = (f32[288,128]{1,0:T(8,128)}, f32[288,128]{1,0:T(8,128)S(1)}, u32[]{:S(2)}, u32[]{:S(2)}) collective-permute-start(f32[288,128]{1,0:T(8,128)} %get-tuple-element.20), channel_id=1, source_target_pairs={{0,48},{1,49},{2,50},{3,51},{4,52},{5,53},{6,54},{7,55},{8,56},{9,... | collective-permute-start | bytes 442376 | tf_op jit(solution)/shard_map/ppermute | solution.py:482
  20.7 4.2 %collective-permute-done.1 = f32[288,128]{1,0:T(8,128)S(1)} collective-permute-done((f32[288,128]{1,0:T(8,128)}, f32[288,128]{1,0:T(8,128)S(1)}, u32[]{:S(2)}, u32[]{:S(2)}) %collective-permute-start.1) | collective-permute-done | bytes 147488 | tf_op jit(solution)/shard_map/ppermute | solution.py:482
  25.0 0.9 %add_add_fusion.2 = f32[288,128]{1,0:T(8,128)S(1)} fusion(f32[288,128]{1,0:T(8,128)S(1)} %collective-permute-done.1, f32[288,128]{1,0:T(8,128)S(1)} %collective-permute-done.2, f32[288,128]{1,0:T(8,128)} %get-tuple-element.17, f32[288,128]{1,0:T(8,128)S(1)} %collective-permute-done), kind=kLoop, calls=%fused_computation.7 | loop fusion | flops 110592 | bytes 737280 | tf_op jit(solution)/shard_map/add | solution.py:490
  26.5 2.4 %collective-permute-start.5 = (f32[288,128]{1,0:T(8,128)S(1)}, f32[288,128]{1,0:T(8,128)S(1)}, u32[]{:S(2)}, u32[]{:S(2)}) collective-permute-start(f32[288,128]{1,0:T(8,128)S(1)} %add_add_fusion.2), channel_id=1, source_target_pairs={{0,12},{1,13},{2,14},{3,15},{4,0},{5,1},{6,2},{7,3},{8,4},{9,5},{1... | collective-permute-start | bytes 442376 | tf_op jit(solution)/shard_map/ppermute | solution.py:482
  28.8 1.7 %collective-permute-start.16 = (f32[144,128]{1,0:T(8,128)S(1)}, f32[144,128]{1,0:T(8,128)S(1)}, u32[]{:S(2)}, u32[]{:S(2)}) collective-permute-start(f32[144,128]{1,0:T(8,128)S(1)} %bitcast.40), channel_id=1, source_target_pairs={{0,1},{1,2},{2,3},{3,0},{4,5},{5,6},{6,7},{7,4},{8,9},{9,10},{10,1... | collective-permute-start | bytes 221192 | tf_op jit(solution)/shard_map/ppermute | solution.py:482
  30.5 3.3 %collective-permute-start.17 = (f32[144,128]{1,0:T(8,128)S(1)}, f32[144,128]{1,0:T(8,128)S(1)}, u32[]{:S(2)}, u32[]{:S(2)}) collective-permute-start(f32[144,128]{1,0:T(8,128)S(1)} %bitcast.41), channel_id=1, source_target_pairs={{0,2},{1,3},{2,0},{3,1},{4,6},{5,7},{6,4},{7,5},{8,10},{9,11},{10,... | collective-permute-start | bytes 221192 | tf_op jit(solution)/shard_map/ppermute | solution.py:482
  33.9 1.5 %collective-permute-start.18 = (f32[144,128]{1,0:T(8,128)S(1)}, f32[144,128]{1,0:T(8,128)S(1)}, u32[]{:S(2)}, u32[]{:S(2)}) collective-permute-start(f32[144,128]{1,0:T(8,128)S(1)} %bitcast.43), channel_id=1, source_target_pairs={{0,3},{1,0},{2,1},{3,2},{4,7},{5,4},{6,5},{7,6},{8,11},{9,8},{10,9... | collective-permute-start | bytes 221192 | tf_op jit(solution)/shard_map/ppermute | solution.py:482
  35.7 3.8 %collective-permute-start.6 = (f32[288,128]{1,0:T(8,128)S(1)}, f32[288,128]{1,0:T(8,128)S(1)}, u32[]{:S(2)}, u32[]{:S(2)}) collective-permute-start(f32[288,128]{1,0:T(8,128)S(1)} %add_add_fusion.1), channel_id=1, source_target_pairs={{0,2},{1,3},{2,0},{3,1},{4,6},{5,7},{6,4},{7,5},{8,10},{9,11},{10,... | collective-permute-start | bytes 442376 | tf_op jit(solution)/shard_map/ppermute | solution.py:482
  39.5 0.7 collective-permute-start.7
  40.2 1.9 %collective-permute-start.8 = (f32[288,128]{1,0:T(8,128)S(1)}, f32[288,128]{1,0:T(8,128)S(1)}, u32[]{:S(2)}, u32[]{:S(2)}) collective-permute-start(f32[288,128]{1,0:T(8,128)S(1)} %add_add_fusion.1), channel_id=1, source_target_pairs={{0,3},{1,0},{2,1},{3,2},{4,7},{5,4},{6,5},{7,6},{8,11},{9,8},{10,9... | collective-permute-start | bytes 442376 | tf_op jit(solution)/shard_map/ppermute | solution.py:482
  42.2 4.9 %collective-permute-done.7 = f32[288,128]{1,0:T(8,128)S(1)} collective-permute-done((f32[288,128]{1,0:T(8,128)S(1)}, f32[288,128]{1,0:T(8,128)S(1)}, u32[]{:S(2)}, u32[]{:S(2)}) %collective-permute-start.7) | collective-permute-done | bytes 147488 | tf_op jit(solution)/shard_map/ppermute | solution.py:482
  47.1 1.5 %collective-permute-start.9 = (f32[1,128]{1,0:T(1,128)S(1)}, f32[1,128]{1,0:T(1,128)S(1)}, u32[]{:S(2)}, u32[]{:S(2)}) collective-permute-start(f32[1,128]{1,0:T(1,128)S(1)} %bitcast.45), channel_id=1, source_target_pairs={{0,64},{64,0},{1,65},{65,1},{2,66},{66,2},{3,67},{67,3},{4,68},{68... | collective-permute-start | bytes 1544 | tf_op jit(solution)/shard_map/ppermute | solution.py:507
  48.7 0.8 %collective-permute-done.9 = f32[1,128]{1,0:T(1,128)S(1)} collective-permute-done((f32[1,128]{1,0:T(1,128)S(1)}, f32[1,128]{1,0:T(1,128)S(1)}, u32[]{:S(2)}, u32[]{:S(2)}) %collective-permute-start.9) | collective-permute-done | bytes 544 | tf_op jit(solution)/shard_map/ppermute | solution.py:507
  49.5 1.4 %collective-permute-start.10 = (f32[1,128]{1,0:T(1,128)S(1)}, f32[1,128]{1,0:T(1,128)S(1)}, u32[]{:S(2)}, u32[]{:S(2)}) collective-permute-start(f32[1,128]{1,0:T(1,128)S(1)} %bitcast_add_fusion), channel_id=1, source_target_pairs={{0,32},{1,33},{2,34},{3,35},{4,36},{5,37},{6,38},{7,39},{8,40},{9,... | collective-permute-start | bytes 1544 | tf_op jit(solution)/shard_map/ppermute | solution.py:482
  50.9 1.5 %collective-permute-start.11 = (f32[1,128]{1,0:T(1,128)S(1)}, f32[1,128]{1,0:T(1,128)S(1)}, u32[]{:S(2)}, u32[]{:S(2)}) collective-permute-start(f32[1,128]{1,0:T(1,128)S(1)} %bitcast_add_fusion), channel_id=1, source_target_pairs={{0,16},{1,17},{2,18},{3,19},{4,20},{5,21},{6,22},{7,23},{8,24},{9,... | collective-permute-start | bytes 1544 | tf_op jit(solution)/shard_map/ppermute | solution.py:482
  52.3 1.2 %collective-permute-start.12 = (f32[1,128]{1,0:T(1,128)S(1)}, f32[1,128]{1,0:T(1,128)S(1)}, u32[]{:S(2)}, u32[]{:S(2)}) collective-permute-start(f32[1,128]{1,0:T(1,128)S(1)} %bitcast_add_fusion), channel_id=1, source_target_pairs={{0,48},{1,49},{2,50},{3,51},{4,52},{5,53},{6,54},{7,55},{8,56},{9,... | collective-permute-start | bytes 1544 | tf_op jit(solution)/shard_map/ppermute | solution.py:482
  53.6 0.9 %collective-permute-done.11 = f32[1,128]{1,0:T(1,128)S(1)} collective-permute-done((f32[1,128]{1,0:T(1,128)S(1)}, f32[1,128]{1,0:T(1,128)S(1)}, u32[]{:S(2)}, u32[]{:S(2)}) %collective-permute-start.11) | collective-permute-done | bytes 544 | tf_op jit(solution)/shard_map/ppermute | solution.py:482
  55.5 3.6 %collective-permute-start.20 = (f32[288,128]{1,0:T(8,128)S(1)}, f32[288,128]{1,0:T(8,128)S(1)}, u32[]{:S(2)}, u32[]{:S(2)}) collective-permute-start(f32[288,128]{1,0:T(8,128)S(1)} %update.1), channel_id=1, source_target_pairs={{0,32},{1,33},{2,34},{3,35},{4,36},{5,37},{6,38},{7,39},{8,40},{9,... | collective-permute-start | bytes 442376 | tf_op jit(solution)/shard_map/ppermute | solution.py:482
  59.4 1.2 %collective-permute-done.19 = f32[288,128]{1,0:T(8,128)S(1)} collective-permute-done((f32[288,128]{1,0:T(8,128)S(1)}, f32[288,128]{1,0:T(8,128)S(1)}, u32[]{:S(2)}, u32[]{:S(2)}) %collective-permute-start.19) | collective-permute-done | bytes 147488 | tf_op jit(solution)/shard_map/ppermute | solution.py:482
  60.6 3.2 %collective-permute-done.20 = f32[288,128]{1,0:T(8,128)S(1)} collective-permute-done((f32[288,128]{1,0:T(8,128)S(1)}, f32[288,128]{1,0:T(8,128)S(1)}, u32[]{:S(2)}, u32[]{:S(2)}) %collective-permute-start.20) | collective-permute-done | bytes 147488 | tf_op jit(solution)/shard_map/ppermute | solution.py:482
  64.0 3.2 %collective-permute-start.22 = (f32[4,288,128]{2,1,0:T(8,128)S(1)}, f32[4,288,128]{2,1,0:T(8,128)S(1)}, u32[]{:S(2)}, u32[]{:S(2)}) collective-permute-start(f32[4,288,128]{2,1,0:T(8,128)S(1)} %bitcast_dynamic-update-slice_fusion.mine), channel_id=1, source_target_pairs={{0,64},{64,0},{1,65},{65,1},{2,66},{66,2},{3,67},{67,3},{4,68},{68... | collective-permute-start | bytes 1769480 | tf_op jit(solution)/shard_map/ppermute | solution.py:507
  67.6 1.2 %collective-permute-done.22.other = f32[4,288,128]{2,1,0:T(8,128)S(1)} collective-permute-done((f32[4,288,128]{2,1,0:T(8,128)S(1)}, f32[4,288,128]{2,1,0:T(8,128)S(1)}, u32[]{:S(2)}, u32[]{:S(2)}) %collective-permute-start.22) | collective-permute-done | bytes 589856 | tf_op jit(solution)/shard_map/ppermute | solution.py:507
  68.8 5.1 %act.1 = f32[32,400]{1,0:T(8,128)S(1)} custom-call(f32[4,288,128]{2,1,0:T(8,128)S(1)} %bitcast_dynamic-update-slice_fusion.mine, f32[4,288,128]{2,1,0:T(8,128)S(1)} %collective-permute-done.22.other, bf16[12,6,2,32,128]{4,3,2,1,0:T(8,128)(2,1)S(1)} %get-tuple-element.22.boards, bf16[1280,128]{1,0:T(8,128)(2,1)S(1)} %get-tuple-element.23.heads), custom_call_target="tpu_custom_call" | custom-call | flops 8000000000 | bytes 4000000 | tf_op jit(solution)/shard_map/act/pallas_call | solution.py:183
  73.9 0.5 collective-permute-start.23
  74.4 0.6 select_bitcast_fusion
  75.3 0.7 pad_maximum_fusion
  (52 shorter events, 3.7 us)
Async XLA Ops:
  9.0 9.3 %collective-permute-start.13 = (f32[72,128]{1,0:T(8,128)S(1)}, f32[72,128]{1,0:T(8,128)S(1)}, u32[]{:S(2)}, u32[]{:S(2)}) collective-permute-start(f32[72,128]{1,0:T(8,128)S(1)} %pad_maximum_fusion.1), channel_id=1, source_target_pairs={{0,4},{1,5},{2,6},{3,7},{4,8},{5,9},{6,10},{7,11},{8,12},{9,13},{1... | collective-permute-start | bytes 110600 | tf_op jit(solution)/shard_map/ppermute | solution.py:482
  11.1 9.6 %collective-permute-start.14 = (f32[72,128]{1,0:T(8,128)S(1)}, f32[72,128]{1,0:T(8,128)S(1)}, u32[]{:S(2)}, u32[]{:S(2)}) collective-permute-start(f32[72,128]{1,0:T(8,128)S(1)} %pad_maximum_fusion.1), channel_id=1, source_target_pairs={{0,8},{1,9},{2,10},{3,11},{4,12},{5,13},{6,14},{7,15},{8,0},{9,1},... | collective-permute-start | bytes 110600 | tf_op jit(solution)/shard_map/ppermute | solution.py:482
  13.5 7.1 %collective-permute-start.15 = (f32[72,128]{1,0:T(8,128)S(1)}, f32[72,128]{1,0:T(8,128)S(1)}, u32[]{:S(2)}, u32[]{:S(2)}) collective-permute-start(f32[72,128]{1,0:T(8,128)S(1)} %pad_maximum_fusion.1), channel_id=1, source_target_pairs={{0,12},{1,13},{2,14},{3,15},{4,0},{5,1},{6,2},{7,3},{8,4},{9,5},{1... | collective-permute-start | bytes 110600 | tf_op jit(solution)/shard_map/ppermute | solution.py:482
  14.7 6.0 %collective-permute-start = (f32[288,128]{1,0:T(8,128)}, f32[288,128]{1,0:T(8,128)S(1)}, u32[]{:S(2)}, u32[]{:S(2)}) collective-permute-start(f32[288,128]{1,0:T(8,128)} %get-tuple-element.18), channel_id=1, source_target_pairs={{0,32},{1,33},{2,34},{3,35},{4,36},{5,37},{6,38},{7,39},{8,40},{9,... | collective-permute-start | bytes 442376 | tf_op jit(solution)/shard_map/ppermute | solution.py:482
  17.6 7.4 %collective-permute-start.1 = (f32[288,128]{1,0:T(8,128)}, f32[288,128]{1,0:T(8,128)S(1)}, u32[]{:S(2)}, u32[]{:S(2)}) collective-permute-start(f32[288,128]{1,0:T(8,128)} %get-tuple-element.19), channel_id=1, source_target_pairs={{0,16},{1,17},{2,18},{3,19},{4,20},{5,21},{6,22},{7,23},{8,24},{9,... | collective-permute-start | bytes 442376 | tf_op jit(solution)/shard_map/ppermute | solution.py:482
  18.3 6.7 %collective-permute-start.2 = (f32[288,128]{1,0:T(8,128)}, f32[288,128]{1,0:T(8,128)S(1)}, u32[]{:S(2)}, u32[]{:S(2)}) collective-permute-start(f32[288,128]{1,0:T(8,128)} %get-tuple-element.20), channel_id=1, source_target_pairs={{0,48},{1,49},{2,50},{3,51},{4,52},{5,53},{6,54},{7,55},{8,56},{9,... | collective-permute-start | bytes 442376 | tf_op jit(solution)/shard_map/ppermute | solution.py:482
  25.9 8.0 %collective-permute-start.3 = (f32[288,128]{1,0:T(8,128)S(1)}, f32[288,128]{1,0:T(8,128)S(1)}, u32[]{:S(2)}, u32[]{:S(2)}) collective-permute-start(f32[288,128]{1,0:T(8,128)S(1)} %add_add_fusion.2), channel_id=1, source_target_pairs={{0,8},{1,9},{2,10},{3,11},{4,12},{5,13},{6,14},{7,15},{8,0},{9,1},... | collective-permute-start | bytes 442376 | tf_op jit(solution)/shard_map/ppermute | solution.py:482
  26.2 9.5 %collective-permute-start.4 = (f32[288,128]{1,0:T(8,128)S(1)}, f32[288,128]{1,0:T(8,128)S(1)}, u32[]{:S(2)}, u32[]{:S(2)}) collective-permute-start(f32[288,128]{1,0:T(8,128)S(1)} %add_add_fusion.2), channel_id=1, source_target_pairs={{0,4},{1,5},{2,6},{3,7},{4,8},{5,9},{6,10},{7,11},{8,12},{9,13},{1... | collective-permute-start | bytes 442376 | tf_op jit(solution)/shard_map/ppermute | solution.py:482
  26.5 9.2 %collective-permute-start.5 = (f32[288,128]{1,0:T(8,128)S(1)}, f32[288,128]{1,0:T(8,128)S(1)}, u32[]{:S(2)}, u32[]{:S(2)}) collective-permute-start(f32[288,128]{1,0:T(8,128)S(1)} %add_add_fusion.2), channel_id=1, source_target_pairs={{0,12},{1,13},{2,14},{3,15},{4,0},{5,1},{6,2},{7,3},{8,4},{9,5},{1... | collective-permute-start | bytes 442376 | tf_op jit(solution)/shard_map/ppermute | solution.py:482
  28.8 11.3 %collective-permute-start.16 = (f32[144,128]{1,0:T(8,128)S(1)}, f32[144,128]{1,0:T(8,128)S(1)}, u32[]{:S(2)}, u32[]{:S(2)}) collective-permute-start(f32[144,128]{1,0:T(8,128)S(1)} %bitcast.40), channel_id=1, source_target_pairs={{0,1},{1,2},{2,3},{3,0},{4,5},{5,6},{6,7},{7,4},{8,9},{9,10},{10,1... | collective-permute-start | bytes 221192 | tf_op jit(solution)/shard_map/ppermute | solution.py:482
  30.5 18.1 %collective-permute-start.17 = (f32[144,128]{1,0:T(8,128)S(1)}, f32[144,128]{1,0:T(8,128)S(1)}, u32[]{:S(2)}, u32[]{:S(2)}) collective-permute-start(f32[144,128]{1,0:T(8,128)S(1)} %bitcast.41), channel_id=1, source_target_pairs={{0,2},{1,3},{2,0},{3,1},{4,6},{5,7},{6,4},{7,5},{8,10},{9,11},{10,... | collective-permute-start | bytes 221192 | tf_op jit(solution)/shard_map/ppermute | solution.py:482
  33.9 20.9 %copy-start = (f32[2304,128]{1,0:T(8,128)S(1)}, f32[2304,128]{1,0:T(8,128)}, u32[]{:S(2)}) copy-start(f32[2304,128]{1,0:T(8,128)} %torso_in.1) | copy-start | bytes 3538948
  33.9 19.6 %collective-permute-start.18 = (f32[144,128]{1,0:T(8,128)S(1)}, f32[144,128]{1,0:T(8,128)S(1)}, u32[]{:S(2)}, u32[]{:S(2)}) collective-permute-start(f32[144,128]{1,0:T(8,128)S(1)} %bitcast.43), channel_id=1, source_target_pairs={{0,3},{1,0},{2,1},{3,2},{4,7},{5,4},{6,5},{7,6},{8,11},{9,8},{10,9... | collective-permute-start | bytes 221192 | tf_op jit(solution)/shard_map/ppermute | solution.py:482
  35.7 6.5 %collective-permute-start.6 = (f32[288,128]{1,0:T(8,128)S(1)}, f32[288,128]{1,0:T(8,128)S(1)}, u32[]{:S(2)}, u32[]{:S(2)}) collective-permute-start(f32[288,128]{1,0:T(8,128)S(1)} %add_add_fusion.1), channel_id=1, source_target_pairs={{0,2},{1,3},{2,0},{3,1},{4,6},{5,7},{6,4},{7,5},{8,10},{9,11},{10,... | collective-permute-start | bytes 442376 | tf_op jit(solution)/shard_map/ppermute | solution.py:482
  39.5 7.6 %collective-permute-start.7 = (f32[288,128]{1,0:T(8,128)S(1)}, f32[288,128]{1,0:T(8,128)S(1)}, u32[]{:S(2)}, u32[]{:S(2)}) collective-permute-start(f32[288,128]{1,0:T(8,128)S(1)} %add_add_fusion.1), channel_id=1, source_target_pairs={{0,1},{1,2},{2,3},{3,0},{4,5},{5,6},{6,7},{7,4},{8,9},{9,10},{10,1... | collective-permute-start | bytes 442376 | tf_op jit(solution)/shard_map/ppermute | solution.py:482
  40.2 6.9 %collective-permute-start.8 = (f32[288,128]{1,0:T(8,128)S(1)}, f32[288,128]{1,0:T(8,128)S(1)}, u32[]{:S(2)}, u32[]{:S(2)}) collective-permute-start(f32[288,128]{1,0:T(8,128)S(1)} %add_add_fusion.1), channel_id=1, source_target_pairs={{0,3},{1,0},{2,1},{3,2},{4,7},{5,4},{6,5},{7,6},{8,11},{9,8},{10,9... | collective-permute-start | bytes 442376 | tf_op jit(solution)/shard_map/ppermute | solution.py:482
  47.1 2.4 %collective-permute-start.9 = (f32[1,128]{1,0:T(1,128)S(1)}, f32[1,128]{1,0:T(1,128)S(1)}, u32[]{:S(2)}, u32[]{:S(2)}) collective-permute-start(f32[1,128]{1,0:T(1,128)S(1)} %bitcast.45), channel_id=1, source_target_pairs={{0,64},{64,0},{1,65},{65,1},{2,66},{66,2},{3,67},{67,3},{4,68},{68... | collective-permute-start | bytes 1544 | tf_op jit(solution)/shard_map/ppermute | solution.py:507
  49.5 4.1 %collective-permute-start.10 = (f32[1,128]{1,0:T(1,128)S(1)}, f32[1,128]{1,0:T(1,128)S(1)}, u32[]{:S(2)}, u32[]{:S(2)}) collective-permute-start(f32[1,128]{1,0:T(1,128)S(1)} %bitcast_add_fusion), channel_id=1, source_target_pairs={{0,32},{1,33},{2,34},{3,35},{4,36},{5,37},{6,38},{7,39},{8,40},{9,... | collective-permute-start | bytes 1544 | tf_op jit(solution)/shard_map/ppermute | solution.py:482
  50.9 3.6 %collective-permute-start.11 = (f32[1,128]{1,0:T(1,128)S(1)}, f32[1,128]{1,0:T(1,128)S(1)}, u32[]{:S(2)}, u32[]{:S(2)}) collective-permute-start(f32[1,128]{1,0:T(1,128)S(1)} %bitcast_add_fusion), channel_id=1, source_target_pairs={{0,16},{1,17},{2,18},{3,19},{4,20},{5,21},{6,22},{7,23},{8,24},{9,... | collective-permute-start | bytes 1544 | tf_op jit(solution)/shard_map/ppermute | solution.py:482
  52.3 2.4 %collective-permute-start.12 = (f32[1,128]{1,0:T(1,128)S(1)}, f32[1,128]{1,0:T(1,128)S(1)}, u32[]{:S(2)}, u32[]{:S(2)}) collective-permute-start(f32[1,128]{1,0:T(1,128)S(1)} %bitcast_add_fusion), channel_id=1, source_target_pairs={{0,48},{1,49},{2,50},{3,51},{4,52},{5,53},{6,54},{7,55},{8,56},{9,... | collective-permute-start | bytes 1544 | tf_op jit(solution)/shard_map/ppermute | solution.py:482
  55.2 12.0 %copy-start.2 = (bf16[128,4]{0,1:T(4,128)(2,1)S(1)}, bf16[128,4]{0,1:T(4,128)(2,1)}, u32[]{:S(2)}) copy-start(bf16[128,4]{0,1:T(4,128)(2,1)} %param.20) | copy-start | bytes 3076
  55.2 12.0 %copy-start.1 = (bf16[64,10,10,128]{3,0,2,1:T(8,128)(2,1)S(1)}, bf16[64,10,10,128]{3,0,2,1:T(8,128)(2,1)}, u32[]{:S(2)}) copy-start(bf16[64,10,10,128]{3,0,2,1:T(8,128)(2,1)} %param.12) | copy-start | bytes 4915204
  55.2 5.5 %collective-permute-start.19 = (f32[288,128]{1,0:T(8,128)S(1)}, f32[288,128]{1,0:T(8,128)S(1)}, u32[]{:S(2)}, u32[]{:S(2)}) collective-permute-start(f32[288,128]{1,0:T(8,128)S(1)} %update.1), channel_id=1, source_target_pairs={{0,16},{1,17},{2,18},{3,19},{4,20},{5,21},{6,22},{7,23},{8,24},{9,... | collective-permute-start | bytes 442376 | tf_op jit(solution)/shard_map/ppermute | solution.py:482
  55.5 8.3 %collective-permute-start.20 = (f32[288,128]{1,0:T(8,128)S(1)}, f32[288,128]{1,0:T(8,128)S(1)}, u32[]{:S(2)}, u32[]{:S(2)}) collective-permute-start(f32[288,128]{1,0:T(8,128)S(1)} %update.1), channel_id=1, source_target_pairs={{0,32},{1,33},{2,34},{3,35},{4,36},{5,37},{6,38},{7,39},{8,40},{9,... | collective-permute-start | bytes 442376 | tf_op jit(solution)/shard_map/ppermute | solution.py:482
  59.0 5.0 %collective-permute-start.21 = (f32[288,128]{1,0:T(8,128)S(1)}, f32[288,128]{1,0:T(8,128)S(1)}, u32[]{:S(2)}, u32[]{:S(2)}) collective-permute-start(f32[288,128]{1,0:T(8,128)S(1)} %update.1), channel_id=1, source_target_pairs={{0,48},{1,49},{2,50},{3,51},{4,52},{5,53},{6,54},{7,55},{8,56},{9,... | collective-permute-start | bytes 442376 | tf_op jit(solution)/shard_map/ppermute | solution.py:482
  64.0 4.8 %collective-permute-start.22 = (f32[4,288,128]{2,1,0:T(8,128)S(1)}, f32[4,288,128]{2,1,0:T(8,128)S(1)}, u32[]{:S(2)}, u32[]{:S(2)}) collective-permute-start(f32[4,288,128]{2,1,0:T(8,128)S(1)} %bitcast_dynamic-update-slice_fusion.mine), channel_id=1, source_target_pairs={{0,64},{64,0},{1,65},{65,1},{2,66},{66,2},{3,67},{67,3},{4,68},{68... | collective-permute-start | bytes 1769480 | tf_op jit(solution)/shard_map/ppermute | solution.py:507
  73.9 1.4 %collective-permute-start.23 = (f32[32,400]{1,0:T(8,128)S(1)}, f32[32,400]{1,0:T(8,128)S(1)}, u32[]{:S(2)}, u32[]{:S(2)}) collective-permute-start(f32[32,400]{1,0:T(8,128)S(1)} %act.1), channel_id=1, source_target_pairs={{0,64},{64,0},{1,65},{65,1},{2,66},{66,2},{3,67},{67,3},{4,68},{68... | collective-permute-start | bytes 153608 | tf_op jit(solution)/shard_map/ppermute | solution.py:507

commit v9 on v8

--- a/solution.py
+++ b/solution.py
@@ -211,9 +211,9 @@
 
 
 def learner_kernel(
-    count, length_in, boards_in, actions_in, behaviour_in, regular_in, rewards_in, weights_in,
-    policy_in, value_in, own, next1, next2, next3,
-    grad, length, boards, weights, actions, behaviour, regular, rewards, policy_t, value_t, pairs, back_pairs,
+    count, first_in, second_in, length_in, boards_in, actions_in, behaviour_in, regular_in, rewards_in, weights_in,
+    policy_in, value_in, own, next1, next2, next3, both,
+    first, second, grad, length, boards, weights, actions, behaviour, regular, rewards, policy_t, value_t, pairs, back_pairs,
     middle, last, masks, slope, turned, done,
 ):
     slots = boards.shape[3]
@@ -230,6 +230,8 @@
         (policy_in, policy_t),
         (value_in, value_t),
         (length_in, length),
+        (first_in, first),
+        (second_in, second),
     ]
     copies = [pltpu.make_async_copy(a, b, done.at[k]) for k, (a, b) in enumerate(moves)]
     for copy in copies:
@@ -271,6 +273,8 @@
 
     for copy in copies[3:]:
         copy.wait()
+    both[0:PIECE] = first[...]
+    both[PIECE : 2 * PIECE] = second[...]
 
     eight = jnp.concatenate(
         [
@@ -390,27 +394,33 @@
 
     sends = [
         pltpu.make_async_copy(grad.at[lax.rem(y + k, LINE)], out, done.at[k])
-        for k, out in enumerate((own, next1, next2, next3))
+        for k, out in ((1, next1), (2, next2), (3, next3))
     ]
     for copy in sends:
         copy.start()
+    own[...] = grad[y]
     for copy in sends:
         copy.wait()
 
 
 def learn(
-    length, boards, actions, behaviour, regular, rewards, weights, policy_t, value_t, count=5
+    first, second, length, boards, actions, behaviour, regular, rewards, weights, policy_t, value_t,
+    count=5,
 ):
     slots = boards.shape[2]
+    vmem = pl.BlockSpec(memory_space=pltpu.VMEM)
     anywhere = pl.BlockSpec(memory_space=pltpu.HBM)
     cells = (10, 5, 2, slots, 128)
     around = (12, 6, 2, slots, 128)
     return pl.pallas_call(
         functools.partial(learner_kernel, count),
-        out_shape=[jax.ShapeDtypeStruct((SEGMENT, 128), jnp.float32)] * LINE,
-        in_specs=[anywhere] * 9,
-        out_specs=[pl.BlockSpec(memory_space=pl.ANY)] * LINE,
+        out_shape=[jax.ShapeDtypeStruct((SEGMENT, 128), jnp.float32)] * LINE
+        + [jax.ShapeDtypeStruct((2 * PIECE, 128), jnp.float32)],
+        in_specs=[anywhere] * 11,
+        out_specs=[vmem] + [anywhere] * (LINE - 1) + [vmem],
         scratch_shapes=[
+            pltpu.VMEM((PIECE, 128), jnp.float32),
+            pltpu.VMEM((PIECE, 128), jnp.float32),
             pltpu.VMEM((LINE, SEGMENT, 128), jnp.float32),
             pltpu.SMEM((1,), jnp.int32),
             pltpu.VMEM(around, jnp.bfloat16),
@@ -428,14 +438,14 @@
             pltpu.VMEM((2,) + cells, jnp.bfloat16),
             pltpu.VMEM(around, jnp.bfloat16),
             pltpu.VMEM((2, 128, 100 * slots), jnp.bfloat16),
-            pltpu.SemaphoreType.DMA((10,)),
+            pltpu.SemaphoreType.DMA((12,)),
         ],
         compiler_params=pltpu.CompilerParams(vmem_limit_bytes=60 * 1024 * 1024),
         cost_estimate=pl.CostEstimate(
             flops=4 * 10**9, bytes_accessed=3 * 10**6, transcendentals=10000
         ),
         name="learn",
-    )(length, boards, actions, behaviour, regular, rewards, weights, policy_t, value_t)
+    )(first, second, length, boards, actions, behaviour, regular, rewards, weights, policy_t, value_t)
 
 
 def update_kernel(summed, squares, moments, torso_in, fresh, old, first, second, done):
@@ -503,6 +513,25 @@
     return line_place([x] + [shifted(x, axis, step) for step in range(1, LINE)], at)
 
 
+def line_exchange(summed, moments, axis, at):
+    rows = summed.shape[0]
+    both = jnp.concatenate([summed, moments])
+    got = [both] + [shifted(both, axis, step) for step in range(1, LINE)]
+    total = (got[0][:rows] + got[2][:rows]) + (got[1][:rows] + got[3][:rows])
+    return total, line_place([x[rows:] for x in got], at)
+
+
+def swapped_z(x, bit):
+    return lax.ppermute(x, "dp", [(d, d ^ bit) for d in range(LINE**3)])
+
+
+def moments_along_z(x, z):
+    near = swapped_z(x, 1)
+    pair = jnp.where(z % 2 == 0, jnp.stack([x, near]), jnp.stack([near, x]))
+    far = swapped_z(pair, 2)
+    return jnp.where(z < 2, jnp.concatenate([pair, far]), jnp.concatenate([far, pair]))
+
+
 def role_swap(x):
     return lax.ppermute(x, "role", [(0, 1), (1, 0)])
 
@@ -524,7 +553,9 @@
     role = lax.axis_index("role")
     dp = lax.axis_index("dp")
     y, x, z = dp // (LINE * LINE), dp // LINE % LINE, dp % LINE
-    chunks = learn(
+    own, next1, next2, next3, moments = learn(
+        first_moment,
+        second_moment,
         lengths,
         by_cell(traj_boards[0]),
         actions,
@@ -535,13 +566,11 @@
         policy_head.T,
         value_head[None],
     )
-    chunks, moments = lax.optimization_barrier(
-        (chunks, jnp.concatenate([first_moment, second_moment]))
-    )
-    moments = line_gather(moments, "x", x)
+    summed = line_scatter((own, next1, next2, next3), "y")
+    summed, moments = line_exchange(summed, moments, "x", x)
     moments = lax.dynamic_slice_in_dim(moments, 2 * role, 2, 0).reshape(-1, 128)
-    moments = line_gather(moments, "z", z)
-    summed = line_total(line_total(line_scatter(chunks, "y"), "x"), "z")
+    moments = moments_along_z(moments, z)
+    summed = line_total(summed, "z")
     squares = jnp.sum(summed * summed, axis=0, keepdims=True)
     squares = line_total(squares + role_swap(squares), "y")
     fresh = update(summed, squares, moments.reshape(LINE, 2, 2 * PIECE, 128), torso)

time: 76.2 us -> 75.1 us (0.986)
  starting transfers between devices: 40.6 us -> 34.7 us
  waiting for transfers between devices: 17.5 us -> 21.7 us
    ppermute x21 -> x15, starting transfers between devices: 35.4 us -> 26.5 us  [shifted(): return lax.ppermute(x, 'dp', pairs)]
    ppermute x21 -> x15, waiting for transfers between devices: 15.2 us -> 20.2 us  [shifted(): return lax.ppermute(x, 'dp', pairs)]
    ppermute x0 -> x2, starting transfers between devices: none -> 1.71 us  [swapped_z(): return lax.ppermute(x, 'dp', [(d, d ^ bit) for d in range(LINE ** 3)])]
    ppermute x3, starting transfers between devices: 5.14 us -> 6.48 us  [role_swap(): return lax.ppermute(x, 'role', [(0, 1), (1, 0)])]
    ppermute x3, waiting for transfers between devices: 2.29 us -> 1.49 us  [role_swap(): return lax.ppermute(x, 'role', [(0, 1), (1, 0)])]
  transfers between devices with their start and end apart: 24 -> 20, of which waited for: 11 -> 12; matrix products, arithmetic and copies ran while one was open for 1% -> 1% of each run, Pallas kernels for 1% -> 1%
where the time goes in v9:
time: 75.1 us; the launch traced here: 74.9 us
  starting transfers between devices  34.7 us (46%)
  waiting for transfers between devices  21.7 us (29%)
  Pallas kernels  13.5 us (18%)
  other arithmetic  3.19 us (4%)
  between operations  1.48 us (2%)
    ppermute x15, starting transfers between devices, shifted(): return lax.ppermute(x, 'dp', pairs)  26.5 us
    ppermute x15, waiting for transfers between devices, shifted(): return lax.ppermute(x, 'dp', pairs)  20.2 us
    pallas_call x1, Pallas kernels, learn(): pl.pallas_call(functools.partial(learner_kernel, count), out_shape=[jax.S...  7.56 us
    ppermute x3, starting transfers between devices, role_swap(): return lax.ppermute(x, 'role', [(0, 1), (1, 0)])  6.48 us
    pallas_call x1, Pallas kernels, act(): pl.pallas_call(functools.partial(actor_kernel, count, unroll), out_shape=...  5.14 us
    ppermute x2, starting transfers between devices, swapped_z(): return lax.ppermute(x, 'dp', [(d, d ^ bit) for d in range(LINE ** 3)])  1.71 us
  transfers between devices with their start and end apart: 20, of which 12 were waited for; matrix products, arithmetic and copies ran while one was open for 1% of the time, Pallas kernels for 1%

profile of v9, /device:TPU:1, one launch (start us, length us, event | category | flops | bytes accessed | tf_op | source)
XLA Modules:
  0.0 74.9 jit_solution(9884466668285759266)
XLA Ops:
  1.3 7.6 %learn.1 = (f32[288,128]{1,0:T(8,128)}, f32[288,128]{1,0:T(8,128)}, f32[288,128]{1,0:T(8,128)}, f32[288,128]{1,0:T(8,128)}, f32[72,128]{1,0:T(8,128)}) custom-call(f32[36,128]{1,0:T(8,128)} %first_in.1, f32[36,128]{1,0:T(8,128)} %second_in.1, s32[1]{0:T(128)S(6)} %copy.22.length_in, bf16[10,10,16,128]{3,2,1,0:T(8,128)(2,1)} %bitcast.48, s32[1,16]{1,0:T(1,128)} %actions_in.1, ...), custom_call_target="tpu_custom_call" | custom-call | flops 4000000000 | bytes 3000000 | tf_op jit(solution)/shard_map/learn/pallas_call | solution.py:415
  8.9 3.8 %collective-permute-start = (f32[288,128]{1,0:T(8,128)}, f32[288,128]{1,0:T(8,128)S(1)}, u32[]{:S(2)}, u32[]{:S(2)}) collective-permute-start(f32[288,128]{1,0:T(8,128)} %get-tuple-element.10), channel_id=1, source_target_pairs={{0,32},{1,33},{2,34},{3,35},{4,36},{5,37},{6,38},{7,39},{8,40},{9,... | collective-permute-start | bytes 442376 | tf_op jit(solution)/shard_map/ppermute | solution.py:492
  13.1 2.3 %collective-permute-start.2 = (f32[288,128]{1,0:T(8,128)}, f32[288,128]{1,0:T(8,128)S(1)}, u32[]{:S(2)}, u32[]{:S(2)}) collective-permute-start(f32[288,128]{1,0:T(8,128)} %get-tuple-element.12), channel_id=1, source_target_pairs={{0,48},{1,49},{2,50},{3,51},{4,52},{5,53},{6,54},{7,55},{8,56},{9,... | collective-permute-start | bytes 442376 | tf_op jit(solution)/shard_map/ppermute | solution.py:492
  15.4 0.9 %collective-permute-done = f32[288,128]{1,0:T(8,128)S(1)} collective-permute-done((f32[288,128]{1,0:T(8,128)}, f32[288,128]{1,0:T(8,128)S(1)}, u32[]{:S(2)}, u32[]{:S(2)}) %collective-permute-start) | collective-permute-done | bytes 147488 | tf_op jit(solution)/shard_map/ppermute | solution.py:492
  16.2 3.8 %collective-permute-done.1 = f32[288,128]{1,0:T(8,128)S(1)} collective-permute-done((f32[288,128]{1,0:T(8,128)}, f32[288,128]{1,0:T(8,128)S(1)}, u32[]{:S(2)}, u32[]{:S(2)}) %collective-permute-start.1) | collective-permute-done | bytes 147488 | tf_op jit(solution)/shard_map/ppermute | solution.py:492
  20.0 0.9 %add_add_fusion.1 = f32[288,128]{1,0:T(8,128)S(1)} fusion(f32[288,128]{1,0:T(8,128)S(1)} %collective-permute-done.1, f32[288,128]{1,0:T(8,128)S(1)} %collective-permute-done.2, f32[288,128]{1,0:T(8,128)} %get-tuple-element.9, f32[288,128]{1,0:T(8,128)S(1)} %collective-permute-done), kind=kLoop, calls=%fused_computation.13 | loop fusion | flops 110592 | bytes 737280 | tf_op jit(solution)/shard_map/add | solution.py:500
  21.0 0.8 %pad_maximum_fusion = f32[360,128]{1,0:T(8,128)S(1)} fusion(f32[72,128]{1,0:T(8,128)} %get-tuple-element.13, f32[288,128]{1,0:T(8,128)S(1)} %add_add_fusion.1), kind=kLoop, calls=%fused_computation.1 | loop fusion | flops 46080 | bytes 368640 | tf_op jit(solution)/shard_map/concatenate | solution.py:518
  21.7 1.3 %collective-permute-start.4 = (f32[360,128]{1,0:T(8,128)S(1)}, f32[360,128]{1,0:T(8,128)S(1)}, u32[]{:S(2)}, u32[]{:S(2)}) collective-permute-start(f32[360,128]{1,0:T(8,128)S(1)} %pad_maximum_fusion), channel_id=1, source_target_pairs={{0,4},{1,5},{2,6},{3,7},{4,8},{5,9},{6,10},{7,11},{8,12},{9,13},{1... | collective-permute-start | bytes 552968 | tf_op jit(solution)/shard_map/ppermute | solution.py:492
  23.1 2.4 %collective-permute-start.3 = (f32[360,128]{1,0:T(8,128)S(1)}, f32[360,128]{1,0:T(8,128)S(1)}, u32[]{:S(2)}, u32[]{:S(2)}) collective-permute-start(f32[360,128]{1,0:T(8,128)S(1)} %pad_maximum_fusion), channel_id=1, source_target_pairs={{0,8},{1,9},{2,10},{3,11},{4,12},{5,13},{6,14},{7,15},{8,0},{9,1},... | collective-permute-start | bytes 552968 | tf_op jit(solution)/shard_map/ppermute | solution.py:492
  25.5 1.2 %collective-permute-start.5 = (f32[360,128]{1,0:T(8,128)S(1)}, f32[360,128]{1,0:T(8,128)S(1)}, u32[]{:S(2)}, u32[]{:S(2)}) collective-permute-start(f32[360,128]{1,0:T(8,128)S(1)} %pad_maximum_fusion), channel_id=1, source_target_pairs={{0,12},{1,13},{2,14},{3,15},{4,0},{5,1},{6,2},{7,3},{8,4},{9,5},{1... | collective-permute-start | bytes 552968 | tf_op jit(solution)/shard_map/ppermute | solution.py:492
  26.7 1.2 %collective-permute-done.4 = f32[360,128]{1,0:T(8,128)S(1)} collective-permute-done((f32[360,128]{1,0:T(8,128)S(1)}, f32[360,128]{1,0:T(8,128)S(1)}, u32[]{:S(2)}, u32[]{:S(2)}) %collective-permute-start.4) | collective-permute-done | bytes 184352 | tf_op jit(solution)/shard_map/ppermute | solution.py:492
  27.9 5.0 %collective-permute-done.3 = f32[360,128]{1,0:T(8,128)S(1)} collective-permute-done((f32[360,128]{1,0:T(8,128)S(1)}, f32[360,128]{1,0:T(8,128)S(1)}, u32[]{:S(2)}, u32[]{:S(2)}) %collective-permute-start.3) | collective-permute-done | bytes 184352 | tf_op jit(solution)/shard_map/ppermute | solution.py:492
  33.0 3.7 %collective-permute-start.6 = (f32[288,128]{1,0:T(8,128)S(1)}, f32[288,128]{1,0:T(8,128)S(1)}, u32[]{:S(2)}, u32[]{:S(2)}) collective-permute-start(f32[288,128]{1,0:T(8,128)S(1)} %fusion), channel_id=1, source_target_pairs={{0,2},{1,3},{2,0},{3,1},{4,6},{5,7},{6,4},{7,5},{8,10},{9,11},{10,... | collective-permute-start | bytes 442376 | tf_op jit(solution)/shard_map/ppermute | solution.py:492
  36.7 0.7 collective-permute-start.7
  37.4 1.9 %collective-permute-start.8 = (f32[288,128]{1,0:T(8,128)S(1)}, f32[288,128]{1,0:T(8,128)S(1)}, u32[]{:S(2)}, u32[]{:S(2)}) collective-permute-start(f32[288,128]{1,0:T(8,128)S(1)} %fusion), channel_id=1, source_target_pairs={{0,3},{1,0},{2,1},{3,2},{4,7},{5,4},{6,5},{7,6},{8,11},{9,8},{10,9... | collective-permute-start | bytes 442376 | tf_op jit(solution)/shard_map/ppermute | solution.py:492
  39.6 4.0 %collective-permute-done.7 = f32[288,128]{1,0:T(8,128)S(1)} collective-permute-done((f32[288,128]{1,0:T(8,128)S(1)}, f32[288,128]{1,0:T(8,128)S(1)}, u32[]{:S(2)}, u32[]{:S(2)}) %collective-permute-start.7) | collective-permute-done | bytes 147488 | tf_op jit(solution)/shard_map/ppermute | solution.py:492
  43.6 2.7 %collective-permute-start.9 = (f32[1,128]{1,0:T(1,128)S(1)}, f32[1,128]{1,0:T(1,128)S(1)}, u32[]{:S(2)}, u32[]{:S(2)}) collective-permute-start(f32[1,128]{1,0:T(1,128)S(1)} %bitcast.47), channel_id=1, source_target_pairs={{0,64},{64,0},{1,65},{65,1},{2,66},{66,2},{3,67},{67,3},{4,68},{68... | collective-permute-start | bytes 1544 | tf_op jit(solution)/shard_map/ppermute | solution.py:536
  46.3 1.6 %collective-permute-start.14 = (f32[2,144,128]{2,1,0:T(8,128)S(1)}, f32[2,144,128]{2,1,0:T(8,128)S(1)}, u32[]{:S(2)}, u32[]{:S(2)}) collective-permute-start(f32[2,144,128]{2,1,0:T(8,128)S(1)} %maximum_select_fusion.2), channel_id=1, source_target_pairs={{0,2},{1,3},{2,0},{3,1},{4,6},{5,7},{6,4},{7,5},{8,10},{9,11},{10,... | collective-permute-start | bytes 442376 | tf_op jit(solution)/shard_map/ppermute | solution.py:525
  48.0 1.6 %collective-permute-start.10 = (f32[1,128]{1,0:T(1,128)S(1)}, f32[1,128]{1,0:T(1,128)S(1)}, u32[]{:S(2)}, u32[]{:S(2)}) collective-permute-start(f32[1,128]{1,0:T(1,128)S(1)} %bitcast_add_fusion), channel_id=1, source_target_pairs={{0,32},{1,33},{2,34},{3,35},{4,36},{5,37},{6,38},{7,39},{8,40},{9,... | collective-permute-start | bytes 1544 | tf_op jit(solution)/shard_map/ppermute | solution.py:492
  49.5 1.4 %collective-permute-start.11 = (f32[1,128]{1,0:T(1,128)S(1)}, f32[1,128]{1,0:T(1,128)S(1)}, u32[]{:S(2)}, u32[]{:S(2)}) collective-permute-start(f32[1,128]{1,0:T(1,128)S(1)} %bitcast_add_fusion), channel_id=1, source_target_pairs={{0,16},{1,17},{2,18},{3,19},{4,20},{5,21},{6,22},{7,23},{8,24},{9,... | collective-permute-start | bytes 1544 | tf_op jit(solution)/shard_map/ppermute | solution.py:492
  51.0 1.4 %collective-permute-start.12 = (f32[1,128]{1,0:T(1,128)S(1)}, f32[1,128]{1,0:T(1,128)S(1)}, u32[]{:S(2)}, u32[]{:S(2)}) collective-permute-start(f32[1,128]{1,0:T(1,128)S(1)} %bitcast_add_fusion), channel_id=1, source_target_pairs={{0,48},{1,49},{2,50},{3,51},{4,52},{5,53},{6,54},{7,55},{8,56},{9,... | collective-permute-start | bytes 1544 | tf_op jit(solution)/shard_map/ppermute | solution.py:492
  52.3 1.2 %collective-permute-done.11 = f32[1,128]{1,0:T(1,128)S(1)} collective-permute-done((f32[1,128]{1,0:T(1,128)S(1)}, f32[1,128]{1,0:T(1,128)S(1)}, u32[]{:S(2)}, u32[]{:S(2)}) %collective-permute-start.11) | collective-permute-done | bytes 544 | tf_op jit(solution)/shard_map/ppermute | solution.py:492
  54.1 1.3 %collective-permute-start.15 = (f32[288,128]{1,0:T(8,128)S(1)}, f32[288,128]{1,0:T(8,128)S(1)}, u32[]{:S(2)}, u32[]{:S(2)}) collective-permute-start(f32[288,128]{1,0:T(8,128)S(1)} %update.1), channel_id=1, source_target_pairs={{0,16},{1,17},{2,18},{3,19},{4,20},{5,21},{6,22},{7,23},{8,24},{9,... | collective-permute-start | bytes 442376 | tf_op jit(solution)/shard_map/ppermute | solution.py:492
  55.4 2.5 %collective-permute-start.16 = (f32[288,128]{1,0:T(8,128)S(1)}, f32[288,128]{1,0:T(8,128)S(1)}, u32[]{:S(2)}, u32[]{:S(2)}) collective-permute-start(f32[288,128]{1,0:T(8,128)S(1)} %update.1), channel_id=1, source_target_pairs={{0,32},{1,33},{2,34},{3,35},{4,36},{5,37},{6,38},{7,39},{8,40},{9,... | collective-permute-start | bytes 442376 | tf_op jit(solution)/shard_map/ppermute | solution.py:492
  58.0 0.6 collective-permute-start.17
  58.6 0.8 %collective-permute-done.15 = f32[288,128]{1,0:T(8,128)S(1)} collective-permute-done((f32[288,128]{1,0:T(8,128)S(1)}, f32[288,128]{1,0:T(8,128)S(1)}, u32[]{:S(2)}, u32[]{:S(2)}) %collective-permute-start.15) | collective-permute-done | bytes 147488 | tf_op jit(solution)/shard_map/ppermute | solution.py:492
  59.4 3.0 %collective-permute-done.16 = f32[288,128]{1,0:T(8,128)S(1)} collective-permute-done((f32[288,128]{1,0:T(8,128)S(1)}, f32[288,128]{1,0:T(8,128)S(1)}, u32[]{:S(2)}, u32[]{:S(2)}) %collective-permute-start.16) | collective-permute-done | bytes 147488 | tf_op jit(solution)/shard_map/ppermute | solution.py:492
  62.7 3.4 %collective-permute-start.18 = (f32[4,288,128]{2,1,0:T(8,128)S(1)}, f32[4,288,128]{2,1,0:T(8,128)S(1)}, u32[]{:S(2)}, u32[]{:S(2)}) collective-permute-start(f32[4,288,128]{2,1,0:T(8,128)S(1)} %bitcast_dynamic-update-slice_fusion.mine), channel_id=1, source_target_pairs={{0,64},{64,0},{1,65},{65,1},{2,66},{66,2},{3,67},{67,3},{4,68},{68... | collective-permute-start | bytes 1769480 | tf_op jit(solution)/shard_map/ppermute | solution.py:536
  66.5 1.2 %collective-permute-done.18.other = f32[4,288,128]{2,1,0:T(8,128)S(1)} collective-permute-done((f32[4,288,128]{2,1,0:T(8,128)S(1)}, f32[4,288,128]{2,1,0:T(8,128)S(1)}, u32[]{:S(2)}, u32[]{:S(2)}) %collective-permute-start.18) | collective-permute-done | bytes 589856 | tf_op jit(solution)/shard_map/ppermute | solution.py:536
  67.7 5.1 %act.1 = f32[32,400]{1,0:T(8,128)S(1)} custom-call(f32[4,288,128]{2,1,0:T(8,128)S(1)} %bitcast_dynamic-update-slice_fusion.mine, f32[4,288,128]{2,1,0:T(8,128)S(1)} %collective-permute-done.18.other, bf16[12,6,2,32,128]{4,3,2,1,0:T(8,128)(2,1)S(1)} %get-tuple-element.14.boards, bf16[1280,128]{1,0:T(8,128)(2,1)S(1)} %get-tuple-element.15.heads), custom_call_target="tpu_custom_call" | custom-call | flops 8000000000 | bytes 4000000 | tf_op jit(solution)/shard_map/act/pallas_call | solution.py:183
  73.3 0.6 select_bitcast_fusion
  74.2 0.7 pad_maximum_fusion.1
  (45 shorter events, 2.8 us)
Async XLA Ops:
  8.8 17.9 %copy-start.2 = (f32[72,128]{1,0:T(8,128)S(1)}, f32[72,128]{1,0:T(8,128)}, u32[]{:S(2)}) copy-start(f32[72,128]{1,0:T(8,128)} %get-tuple-element.13) | copy-start | bytes 110596
  8.9 7.4 %collective-permute-start = (f32[288,128]{1,0:T(8,128)}, f32[288,128]{1,0:T(8,128)S(1)}, u32[]{:S(2)}, u32[]{:S(2)}) collective-permute-start(f32[288,128]{1,0:T(8,128)} %get-tuple-element.10), channel_id=1, source_target_pairs={{0,32},{1,33},{2,34},{3,35},{4,36},{5,37},{6,38},{7,39},{8,40},{9,... | collective-permute-start | bytes 442376 | tf_op jit(solution)/shard_map/ppermute | solution.py:492
  12.7 7.3 %collective-permute-start.1 = (f32[288,128]{1,0:T(8,128)}, f32[288,128]{1,0:T(8,128)S(1)}, u32[]{:S(2)}, u32[]{:S(2)}) collective-permute-start(f32[288,128]{1,0:T(8,128)} %get-tuple-element.11), channel_id=1, source_target_pairs={{0,16},{1,17},{2,18},{3,19},{4,20},{5,21},{6,22},{7,23},{8,24},{9,... | collective-permute-start | bytes 442376 | tf_op jit(solution)/shard_map/ppermute | solution.py:492
  13.1 6.9 %collective-permute-start.2 = (f32[288,128]{1,0:T(8,128)}, f32[288,128]{1,0:T(8,128)S(1)}, u32[]{:S(2)}, u32[]{:S(2)}) collective-permute-start(f32[288,128]{1,0:T(8,128)} %get-tuple-element.12), channel_id=1, source_target_pairs={{0,48},{1,49},{2,50},{3,51},{4,52},{5,53},{6,54},{7,55},{8,56},{9,... | collective-permute-start | bytes 442376 | tf_op jit(solution)/shard_map/ppermute | solution.py:492
  21.7 6.2 %collective-permute-start.4 = (f32[360,128]{1,0:T(8,128)S(1)}, f32[360,128]{1,0:T(8,128)S(1)}, u32[]{:S(2)}, u32[]{:S(2)}) collective-permute-start(f32[360,128]{1,0:T(8,128)S(1)} %pad_maximum_fusion), channel_id=1, source_target_pairs={{0,4},{1,5},{2,6},{3,7},{4,8},{5,9},{6,10},{7,11},{8,12},{9,13},{1... | collective-permute-start | bytes 552968 | tf_op jit(solution)/shard_map/ppermute | solution.py:492
  23.1 9.9 %collective-permute-start.3 = (f32[360,128]{1,0:T(8,128)S(1)}, f32[360,128]{1,0:T(8,128)S(1)}, u32[]{:S(2)}, u32[]{:S(2)}) collective-permute-start(f32[360,128]{1,0:T(8,128)S(1)} %pad_maximum_fusion), channel_id=1, source_target_pairs={{0,8},{1,9},{2,10},{3,11},{4,12},{5,13},{6,14},{7,15},{8,0},{9,1},... | collective-permute-start | bytes 552968 | tf_op jit(solution)/shard_map/ppermute | solution.py:492
  25.5 7.4 %collective-permute-start.5 = (f32[360,128]{1,0:T(8,128)S(1)}, f32[360,128]{1,0:T(8,128)S(1)}, u32[]{:S(2)}, u32[]{:S(2)}) collective-permute-start(f32[360,128]{1,0:T(8,128)S(1)} %pad_maximum_fusion), channel_id=1, source_target_pairs={{0,12},{1,13},{2,14},{3,15},{4,0},{5,1},{6,2},{7,3},{8,4},{9,5},{1... | collective-permute-start | bytes 552968 | tf_op jit(solution)/shard_map/ppermute | solution.py:492
  33.0 6.5 %collective-permute-start.6 = (f32[288,128]{1,0:T(8,128)S(1)}, f32[288,128]{1,0:T(8,128)S(1)}, u32[]{:S(2)}, u32[]{:S(2)}) collective-permute-start(f32[288,128]{1,0:T(8,128)S(1)} %fusion), channel_id=1, source_target_pairs={{0,2},{1,3},{2,0},{3,1},{4,6},{5,7},{6,4},{7,5},{8,10},{9,11},{10,... | collective-permute-start | bytes 442376 | tf_op jit(solution)/shard_map/ppermute | solution.py:492
  36.7 6.9 %collective-permute-start.7 = (f32[288,128]{1,0:T(8,128)S(1)}, f32[288,128]{1,0:T(8,128)S(1)}, u32[]{:S(2)}, u32[]{:S(2)}) collective-permute-start(f32[288,128]{1,0:T(8,128)S(1)} %fusion), channel_id=1, source_target_pairs={{0,1},{1,2},{2,3},{3,0},{4,5},{5,6},{6,7},{7,4},{8,9},{9,10},{10,1... | collective-permute-start | bytes 442376 | tf_op jit(solution)/shard_map/ppermute | solution.py:492
  37.4 6.2 %collective-permute-start.8 = (f32[288,128]{1,0:T(8,128)S(1)}, f32[288,128]{1,0:T(8,128)S(1)}, u32[]{:S(2)}, u32[]{:S(2)}) collective-permute-start(f32[288,128]{1,0:T(8,128)S(1)} %fusion), channel_id=1, source_target_pairs={{0,3},{1,0},{2,1},{3,2},{4,7},{5,4},{6,5},{7,6},{8,11},{9,8},{10,9... | collective-permute-start | bytes 442376 | tf_op jit(solution)/shard_map/ppermute | solution.py:492
  39.4 14.3 %copy-start = (f32[2304,128]{1,0:T(8,128)S(1)}, f32[2304,128]{1,0:T(8,128)}, u32[]{:S(2)}) copy-start(f32[2304,128]{1,0:T(8,128)} %torso_in.1) | copy-start | bytes 3538948
  39.4 6.9 %collective-permute-start.13 = (f32[144,128]{1,0:T(8,128)S(1)}, f32[144,128]{1,0:T(8,128)S(1)}, u32[]{:S(2)}, u32[]{:S(2)}) collective-permute-start(f32[144,128]{1,0:T(8,128)S(1)} %bitcast.41), channel_id=1, source_target_pairs={{0,1},{1,0},{2,3},{3,2},{4,5},{5,4},{6,7},{7,6},{8,9},{9,8},{10,11... | collective-permute-start | bytes 221192 | tf_op jit(solution)/shard_map/ppermute | solution.py:525
  43.6 4.3 %collective-permute-start.9 = (f32[1,128]{1,0:T(1,128)S(1)}, f32[1,128]{1,0:T(1,128)S(1)}, u32[]{:S(2)}, u32[]{:S(2)}) collective-permute-start(f32[1,128]{1,0:T(1,128)S(1)} %bitcast.47), channel_id=1, source_target_pairs={{0,64},{64,0},{1,65},{65,1},{2,66},{66,2},{3,67},{67,3},{4,68},{68... | collective-permute-start | bytes 1544 | tf_op jit(solution)/shard_map/ppermute | solution.py:536
  46.3 7.3 %collective-permute-start.14 = (f32[2,144,128]{2,1,0:T(8,128)S(1)}, f32[2,144,128]{2,1,0:T(8,128)S(1)}, u32[]{:S(2)}, u32[]{:S(2)}) collective-permute-start(f32[2,144,128]{2,1,0:T(8,128)S(1)} %maximum_select_fusion.2), channel_id=1, source_target_pairs={{0,2},{1,3},{2,0},{3,1},{4,6},{5,7},{6,4},{7,5},{8,10},{9,11},{10,... | collective-permute-start | bytes 442376 | tf_op jit(solution)/shard_map/ppermute | solution.py:525
  48.0 4.4 %collective-permute-start.10 = (f32[1,128]{1,0:T(1,128)S(1)}, f32[1,128]{1,0:T(1,128)S(1)}, u32[]{:S(2)}, u32[]{:S(2)}) collective-permute-start(f32[1,128]{1,0:T(1,128)S(1)} %bitcast_add_fusion), channel_id=1, source_target_pairs={{0,32},{1,33},{2,34},{3,35},{4,36},{5,37},{6,38},{7,39},{8,40},{9,... | collective-permute-start | bytes 1544 | tf_op jit(solution)/shard_map/ppermute | solution.py:492
  49.5 4.0 %collective-permute-start.11 = (f32[1,128]{1,0:T(1,128)S(1)}, f32[1,128]{1,0:T(1,128)S(1)}, u32[]{:S(2)}, u32[]{:S(2)}) collective-permute-start(f32[1,128]{1,0:T(1,128)S(1)} %bitcast_add_fusion), channel_id=1, source_target_pairs={{0,16},{1,17},{2,18},{3,19},{4,20},{5,21},{6,22},{7,23},{8,24},{9,... | collective-permute-start | bytes 1544 | tf_op jit(solution)/shard_map/ppermute | solution.py:492
  51.0 2.7 %collective-permute-start.12 = (f32[1,128]{1,0:T(1,128)S(1)}, f32[1,128]{1,0:T(1,128)S(1)}, u32[]{:S(2)}, u32[]{:S(2)}) collective-permute-start(f32[1,128]{1,0:T(1,128)S(1)} %bitcast_add_fusion), channel_id=1, source_target_pairs={{0,48},{1,49},{2,50},{3,51},{4,52},{5,53},{6,54},{7,55},{8,56},{9,... | collective-permute-start | bytes 1544 | tf_op jit(solution)/shard_map/ppermute | solution.py:492
  54.1 11.9 %copy-start.3 = (bf16[128,4]{0,1:T(4,128)(2,1)S(1)}, bf16[128,4]{0,1:T(4,128)(2,1)}, u32[]{:S(2)}) copy-start(bf16[128,4]{0,1:T(4,128)(2,1)} %param.20) | copy-start | bytes 3076
  54.1 11.9 %copy-start.1 = (bf16[64,10,10,128]{3,0,2,1:T(8,128)(2,1)S(1)}, bf16[64,10,10,128]{3,0,2,1:T(8,128)(2,1)}, u32[]{:S(2)}) copy-start(bf16[64,10,10,128]{3,0,2,1:T(8,128)(2,1)} %param.12) | copy-start | bytes 4915204
  54.1 5.3 %collective-permute-start.15 = (f32[288,128]{1,0:T(8,128)S(1)}, f32[288,128]{1,0:T(8,128)S(1)}, u32[]{:S(2)}, u32[]{:S(2)}) collective-permute-start(f32[288,128]{1,0:T(8,128)S(1)} %update.1), channel_id=1, source_target_pairs={{0,16},{1,17},{2,18},{3,19},{4,20},{5,21},{6,22},{7,23},{8,24},{9,... | collective-permute-start | bytes 442376 | tf_op jit(solution)/shard_map/ppermute | solution.py:492
  55.4 7.0 %collective-permute-start.16 = (f32[288,128]{1,0:T(8,128)S(1)}, f32[288,128]{1,0:T(8,128)S(1)}, u32[]{:S(2)}, u32[]{:S(2)}) collective-permute-start(f32[288,128]{1,0:T(8,128)S(1)} %update.1), channel_id=1, source_target_pairs={{0,32},{1,33},{2,34},{3,35},{4,36},{5,37},{6,38},{7,39},{8,40},{9,... | collective-permute-start | bytes 442376 | tf_op jit(solution)/shard_map/ppermute | solution.py:492
  58.0 4.7 %collective-permute-start.17 = (f32[288,128]{1,0:T(8,128)S(1)}, f32[288,128]{1,0:T(8,128)S(1)}, u32[]{:S(2)}, u32[]{:S(2)}) collective-permute-start(f32[288,128]{1,0:T(8,128)S(1)} %update.1), channel_id=1, source_target_pairs={{0,48},{1,49},{2,50},{3,51},{4,52},{5,53},{6,54},{7,55},{8,56},{9,... | collective-permute-start | bytes 442376 | tf_op jit(solution)/shard_map/ppermute | solution.py:492
  62.7 5.0 %collective-permute-start.18 = (f32[4,288,128]{2,1,0:T(8,128)S(1)}, f32[4,288,128]{2,1,0:T(8,128)S(1)}, u32[]{:S(2)}, u32[]{:S(2)}) collective-permute-start(f32[4,288,128]{2,1,0:T(8,128)S(1)} %bitcast_dynamic-update-slice_fusion.mine), channel_id=1, source_target_pairs={{0,64},{64,0},{1,65},{65,1},{2,66},{66,2},{3,67},{67,3},{4,68},{68... | collective-permute-start | bytes 1769480 | tf_op jit(solution)/shard_map/ppermute | solution.py:536
  72.8 1.4 %collective-permute-start.19 = (f32[32,400]{1,0:T(8,128)S(1)}, f32[32,400]{1,0:T(8,128)S(1)}, u32[]{:S(2)}, u32[]{:S(2)}) collective-permute-start(f32[32,400]{1,0:T(8,128)S(1)} %act.1), channel_id=1, source_target_pairs={{0,64},{64,0},{1,65},{65,1},{2,66},{66,2},{3,67},{67,3},{4,68},{68... | collective-permute-start | bytes 153608 | tf_op jit(solution)/shard_map/ppermute | solution.py:536

commit v10 on v8

--- a/solution.py
+++ b/solution.py
@@ -409,7 +409,7 @@
         functools.partial(learner_kernel, count),
         out_shape=[jax.ShapeDtypeStruct((SEGMENT, 128), jnp.float32)] * LINE,
         in_specs=[anywhere] * 9,
-        out_specs=[pl.BlockSpec(memory_space=pl.ANY)] * LINE,
+        out_specs=[anywhere] * LINE,
         scratch_shapes=[
             pltpu.VMEM((LINE, SEGMENT, 128), jnp.float32),
             pltpu.SMEM((1,), jnp.int32),
@@ -438,6 +438,34 @@
     )(length, boards, actions, behaviour, regular, rewards, weights, policy_t, value_t)
 
 
+def pull_kernel(own_in, first_in, second_in, own, both, first, second, done):
+    moves = [(own_in, own), (first_in, first), (second_in, second)]
+    copies = [pltpu.make_async_copy(a, b, done.at[k]) for k, (a, b) in enumerate(moves)]
+    for copy in copies:
+        copy.start()
+    for copy in copies:
+        copy.wait()
+    both[0:PIECE] = first[...]
+    both[PIECE : 2 * PIECE] = second[...]
+
+
+def pull(own, first, second):
+    vmem = pl.BlockSpec(memory_space=pltpu.VMEM)
+    rows = pltpu.VMEM((PIECE, 128), jnp.float32)
+    return pl.pallas_call(
+        pull_kernel,
+        out_shape=[
+            jax.ShapeDtypeStruct((SEGMENT, 128), jnp.float32),
+            jax.ShapeDtypeStruct((2 * PIECE, 128), jnp.float32),
+        ],
+        in_specs=[pl.BlockSpec(memory_space=pltpu.HBM)] * 3,
+        out_specs=[vmem, vmem],
+        scratch_shapes=[rows, rows, pltpu.SemaphoreType.DMA((3,))],
+        compiler_params=pltpu.CompilerParams(vmem_limit_bytes=16 * 1024 * 1024),
+        name="pull",
+    )(own, first, second)
+
+
 def update_kernel(summed, squares, moments, torso_in, fresh, old, first, second, done):
     y = lax.axis_index("dp") // (LINE * LINE)
     start = pl.multiple_of((2 * y + lax.axis_index("role")) * SEGMENT, SEGMENT)
@@ -503,6 +531,25 @@
     return line_place([x] + [shifted(x, axis, step) for step in range(1, LINE)], at)
 
 
+def line_exchange(summed, moments, axis, at):
+    rows = summed.shape[0]
+    both = jnp.concatenate([summed, moments])
+    got = [both] + [shifted(both, axis, step) for step in range(1, LINE)]
+    total = (got[0][:rows] + got[2][:rows]) + (got[1][:rows] + got[3][:rows])
+    return total, line_place([x[rows:] for x in got], at)
+
+
+def swapped_z(x, bit):
+    return lax.ppermute(x, "dp", [(d, d ^ bit) for d in range(LINE**3)])
+
+
+def moments_along_z(x, z):
+    near = swapped_z(x, 1)
+    pair = jnp.where(z % 2 == 0, jnp.stack([x, near]), jnp.stack([near, x]))
+    far = swapped_z(pair, 2)
+    return jnp.where(z < 2, jnp.concatenate([pair, far]), jnp.concatenate([far, pair]))
+
+
 def role_swap(x):
     return lax.ppermute(x, "role", [(0, 1), (1, 0)])
 
@@ -524,7 +571,7 @@
     role = lax.axis_index("role")
     dp = lax.axis_index("dp")
     y, x, z = dp // (LINE * LINE), dp // LINE % LINE, dp % LINE
-    chunks = learn(
+    own, next1, next2, next3 = learn(
         lengths,
         by_cell(traj_boards[0]),
         actions,
@@ -535,13 +582,12 @@
         policy_head.T,
         value_head[None],
     )
-    chunks, moments = lax.optimization_barrier(
-        (chunks, jnp.concatenate([first_moment, second_moment]))
-    )
-    moments = line_gather(moments, "x", x)
+    own, moments = pull(own, first_moment, second_moment)
+    summed = line_scatter((own, next1, next2, next3), "y")
+    summed, moments = line_exchange(summed, moments, "x", x)
     moments = lax.dynamic_slice_in_dim(moments, 2 * role, 2, 0).reshape(-1, 128)
-    moments = line_gather(moments, "z", z)
-    summed = line_total(line_total(line_scatter(chunks, "y"), "x"), "z")
+    moments = moments_along_z(moments, z)
+    summed = line_total(summed, "z")
     squares = jnp.sum(summed * summed, axis=0, keepdims=True)
     squares = line_total(squares + role_swap(squares), "y")
     fresh = update(summed, squares, moments.reshape(LINE, 2, 2 * PIECE, 128), torso)

time: 76.2 us -> 72.8 us (0.955)
  starting transfers between devices: 40.6 us -> 34.7 us
  waiting for transfers between devices: 17.5 us -> 20.6 us
  other arithmetic: 3.11 us -> 1.5 us
  local copies, waits for them, and re-layouts: 0.22 us -> 1.11 us
    ppermute x21 -> x15, starting transfers between devices: 35.4 us -> 26.5 us  [shifted(): return lax.ppermute(x, 'dp', pairs)]
    ppermute x21 -> x15, waiting for transfers between devices: 15.2 us -> 19.1 us  [shifted(): return lax.ppermute(x, 'dp', pairs)]
    ppermute x0 -> x2, starting transfers between devices: none -> 1.71 us  [swapped_z(): return lax.ppermute(x, 'dp', [(d, d ^ bit) for d in range(LINE ** 3)])]
    ppermute x3, starting transfers between devices: 5.14 us -> 6.5 us  [role_swap(): return lax.ppermute(x, 'role', [(0, 1), (1, 0)])]
    unnamed x6 -> x12, local copies, waits for them, and re-layouts: 0.02 us -> 0.94 us
    add x1, other arithmetic: 0.95 us -> 0.03 us  [line_scatter(): chunks[0] + shifted(chunks[2], axis, 2) + (shifted(chunks[1], axis, 1) +...]
    ppermute x3, waiting for transfers between devices: 2.29 us -> 1.49 us  [role_swap(): return lax.ppermute(x, 'role', [(0, 1), (1, 0)])]
  transfers between devices with their start and end apart: 24 -> 20, of which waited for: 11 -> 11; matrix products, arithmetic and copies ran while one was open for 1% -> 1% of each run, Pallas kernels for 1% -> 1%
where the time goes in v10:
time: 72.8 us; the launch traced here: 72.6 us
  starting transfers between devices  34.7 us (48%)
  waiting for transfers between devices  20.6 us (28%)
  Pallas kernels  13.2 us (18%)
  between operations  1.51 us (2%)
  other arithmetic  1.5 us (2%)
  local copies, waits for them, and re-layouts  1.11 us (2%)
    ppermute x15, starting transfers between devices, shifted(): return lax.ppermute(x, 'dp', pairs)  26.5 us
    ppermute x15, waiting for transfers between devices, shifted(): return lax.ppermute(x, 'dp', pairs)  19.1 us
    pallas_call x1, Pallas kernels, learn(): pl.pallas_call(functools.partial(learner_kernel, count), out_shape=[jax.S...  6.96 us
    ppermute x3, starting transfers between devices, role_swap(): return lax.ppermute(x, 'role', [(0, 1), (1, 0)])  6.5 us
    pallas_call x1, Pallas kernels, act(): pl.pallas_call(functools.partial(actor_kernel, count, unroll), out_shape=...  5.14 us
    ppermute x2, starting transfers between devices, swapped_z(): return lax.ppermute(x, 'dp', [(d, d ^ bit) for d in range(LINE ** 3)])  1.71 us
    ppermute x3, waiting for transfers between devices, role_swap(): return lax.ppermute(x, 'role', [(0, 1), (1, 0)])  1.49 us
  transfers between devices with their start and end apart: 20, of which 11 were waited for; matrix products, arithmetic and copies ran while one was open for 1% of the time, Pallas kernels for 1%

profile of v10, /device:TPU:1, one launch (start us, length us, event | category | flops | bytes accessed | tf_op | source)
XLA Modules:
  0.0 72.6 jit_solution(13922729199394074088)
XLA Ops:
  1.3 7.0 %learn.1 = (f32[288,128]{1,0:T(8,128)}, f32[288,128]{1,0:T(8,128)}, f32[288,128]{1,0:T(8,128)}, f32[288,128]{1,0:T(8,128)}) custom-call(s32[1]{0:T(128)S(6)} %copy.22.length_in, bf16[10,10,16,128]{3,2,1,0:T(8,128)(2,1)} %bitcast.48, s32[1,16]{1,0:T(1,128)} %actions_in.1, f32[1,16]{1,0:T(1,128)} %behaviour_in.1, f32[1,16]{1,0:T(1,128)} %regular_in.1, ...), custom_call_target="tpu_custom_call" | custom-call | flops 4000000000 | bytes 3000000 | tf_op jit(solution)/shard_map/learn/pallas_call | solution.py:408
  8.3 3.8 %collective-permute-start = (f32[288,128]{1,0:T(8,128)}, f32[288,128]{1,0:T(8,128)S(1)}, u32[]{:S(2)}, u32[]{:S(2)}) collective-permute-start(f32[288,128]{1,0:T(8,128)} %get-tuple-element.12), channel_id=1, source_target_pairs={{0,32},{1,33},{2,34},{3,35},{4,36},{5,37},{6,38},{7,39},{8,40},{9,... | collective-permute-start | bytes 442376 | tf_op jit(solution)/shard_map/ppermute | solution.py:510
  12.5 2.3 %collective-permute-start.2 = (f32[288,128]{1,0:T(8,128)}, f32[288,128]{1,0:T(8,128)S(1)}, u32[]{:S(2)}, u32[]{:S(2)}) collective-permute-start(f32[288,128]{1,0:T(8,128)} %get-tuple-element.14), channel_id=1, source_target_pairs={{0,48},{1,49},{2,50},{3,51},{4,52},{5,53},{6,54},{7,55},{8,56},{9,... | collective-permute-start | bytes 442376 | tf_op jit(solution)/shard_map/ppermute | solution.py:510
  14.8 0.9 %copy-done.1 = f32[288,128]{1,0:T(8,128)S(1)} copy-done((f32[288,128]{1,0:T(8,128)S(1)}, f32[288,128]{1,0:T(8,128)}, u32[]{:S(2)}) %copy-start.1) | copy-done | bytes 147480
  15.9 3.5 %collective-permute-done.1 = f32[288,128]{1,0:T(8,128)S(1)} collective-permute-done((f32[288,128]{1,0:T(8,128)}, f32[288,128]{1,0:T(8,128)S(1)}, u32[]{:S(2)}, u32[]{:S(2)}) %collective-permute-start.1) | collective-permute-done | bytes 147488 | tf_op jit(solution)/shard_map/ppermute | solution.py:510
  19.5 1.3 %collective-permute-start.4 = (f32[360,128]{1,0:T(8,128)S(1)}, f32[360,128]{1,0:T(8,128)S(1)}, u32[]{:S(2)}, u32[]{:S(2)}) collective-permute-start(f32[360,128]{1,0:T(8,128)S(1)} %pad_maximum_fusion), channel_id=1, source_target_pairs={{0,4},{1,5},{2,6},{3,7},{4,8},{5,9},{6,10},{7,11},{8,12},{9,13},{1... | collective-permute-start | bytes 552968 | tf_op jit(solution)/shard_map/ppermute | solution.py:510
  20.8 2.5 %collective-permute-start.3 = (f32[360,128]{1,0:T(8,128)S(1)}, f32[360,128]{1,0:T(8,128)S(1)}, u32[]{:S(2)}, u32[]{:S(2)}) collective-permute-start(f32[360,128]{1,0:T(8,128)S(1)} %pad_maximum_fusion), channel_id=1, source_target_pairs={{0,8},{1,9},{2,10},{3,11},{4,12},{5,13},{6,14},{7,15},{8,0},{9,1},... | collective-permute-start | bytes 552968 | tf_op jit(solution)/shard_map/ppermute | solution.py:510
  23.3 1.2 %collective-permute-start.5 = (f32[360,128]{1,0:T(8,128)S(1)}, f32[360,128]{1,0:T(8,128)S(1)}, u32[]{:S(2)}, u32[]{:S(2)}) collective-permute-start(f32[360,128]{1,0:T(8,128)S(1)} %pad_maximum_fusion), channel_id=1, source_target_pairs={{0,12},{1,13},{2,14},{3,15},{4,0},{5,1},{6,2},{7,3},{8,4},{9,5},{1... | collective-permute-start | bytes 552968 | tf_op jit(solution)/shard_map/ppermute | solution.py:510
  24.4 1.2 %collective-permute-done.4 = f32[360,128]{1,0:T(8,128)S(1)} collective-permute-done((f32[360,128]{1,0:T(8,128)S(1)}, f32[360,128]{1,0:T(8,128)S(1)}, u32[]{:S(2)}, u32[]{:S(2)}) %collective-permute-start.4) | collective-permute-done | bytes 184352 | tf_op jit(solution)/shard_map/ppermute | solution.py:510
  25.7 5.0 %collective-permute-done.3 = f32[360,128]{1,0:T(8,128)S(1)} collective-permute-done((f32[360,128]{1,0:T(8,128)S(1)}, f32[360,128]{1,0:T(8,128)S(1)}, u32[]{:S(2)}, u32[]{:S(2)}) %collective-permute-start.3) | collective-permute-done | bytes 184352 | tf_op jit(solution)/shard_map/ppermute | solution.py:510
  30.7 3.7 %collective-permute-start.6 = (f32[288,128]{1,0:T(8,128)S(1)}, f32[288,128]{1,0:T(8,128)S(1)}, u32[]{:S(2)}, u32[]{:S(2)}) collective-permute-start(f32[288,128]{1,0:T(8,128)S(1)} %fusion), channel_id=1, source_target_pairs={{0,2},{1,3},{2,0},{3,1},{4,6},{5,7},{6,4},{7,5},{8,10},{9,11},{10,... | collective-permute-start | bytes 442376 | tf_op jit(solution)/shard_map/ppermute | solution.py:510
  34.4 0.7 %collective-permute-start.7 = (f32[288,128]{1,0:T(8,128)S(1)}, f32[288,128]{1,0:T(8,128)S(1)}, u32[]{:S(2)}, u32[]{:S(2)}) collective-permute-start(f32[288,128]{1,0:T(8,128)S(1)} %fusion), channel_id=1, source_target_pairs={{0,1},{1,2},{2,3},{3,0},{4,5},{5,6},{6,7},{7,4},{8,9},{9,10},{10,1... | collective-permute-start | bytes 442376 | tf_op jit(solution)/shard_map/ppermute | solution.py:510
  35.1 1.9 %collective-permute-start.8 = (f32[288,128]{1,0:T(8,128)S(1)}, f32[288,128]{1,0:T(8,128)S(1)}, u32[]{:S(2)}, u32[]{:S(2)}) collective-permute-start(f32[288,128]{1,0:T(8,128)S(1)} %fusion), channel_id=1, source_target_pairs={{0,3},{1,0},{2,1},{3,2},{4,7},{5,4},{6,5},{7,6},{8,11},{9,8},{10,9... | collective-permute-start | bytes 442376 | tf_op jit(solution)/shard_map/ppermute | solution.py:510
  37.3 4.0 %collective-permute-done.7 = f32[288,128]{1,0:T(8,128)S(1)} collective-permute-done((f32[288,128]{1,0:T(8,128)S(1)}, f32[288,128]{1,0:T(8,128)S(1)}, u32[]{:S(2)}, u32[]{:S(2)}) %collective-permute-start.7) | collective-permute-done | bytes 147488 | tf_op jit(solution)/shard_map/ppermute | solution.py:510
  41.4 2.7 %collective-permute-start.9 = (f32[1,128]{1,0:T(1,128)S(1)}, f32[1,128]{1,0:T(1,128)S(1)}, u32[]{:S(2)}, u32[]{:S(2)}) collective-permute-start(f32[1,128]{1,0:T(1,128)S(1)} %bitcast.47), channel_id=1, source_target_pairs={{0,64},{64,0},{1,65},{65,1},{2,66},{66,2},{3,67},{67,3},{4,68},{68... | collective-permute-start | bytes 1544 | tf_op jit(solution)/shard_map/ppermute | solution.py:554
  44.0 1.6 %collective-permute-start.14 = (f32[2,144,128]{2,1,0:T(8,128)S(1)}, f32[2,144,128]{2,1,0:T(8,128)S(1)}, u32[]{:S(2)}, u32[]{:S(2)}) collective-permute-start(f32[2,144,128]{2,1,0:T(8,128)S(1)} %maximum_select_fusion.2), channel_id=1, source_target_pairs={{0,2},{1,3},{2,0},{3,1},{4,6},{5,7},{6,4},{7,5},{8,10},{9,11},{10,... | collective-permute-start | bytes 442376 | tf_op jit(solution)/shard_map/ppermute | solution.py:543
  45.7 1.6 %collective-permute-start.10 = (f32[1,128]{1,0:T(1,128)S(1)}, f32[1,128]{1,0:T(1,128)S(1)}, u32[]{:S(2)}, u32[]{:S(2)}) collective-permute-start(f32[1,128]{1,0:T(1,128)S(1)} %bitcast_add_fusion), channel_id=1, source_target_pairs={{0,32},{1,33},{2,34},{3,35},{4,36},{5,37},{6,38},{7,39},{8,40},{9,... | collective-permute-start | bytes 1544 | tf_op jit(solution)/shard_map/ppermute | solution.py:510
  47.3 1.4 %collective-permute-start.11 = (f32[1,128]{1,0:T(1,128)S(1)}, f32[1,128]{1,0:T(1,128)S(1)}, u32[]{:S(2)}, u32[]{:S(2)}) collective-permute-start(f32[1,128]{1,0:T(1,128)S(1)} %bitcast_add_fusion), channel_id=1, source_target_pairs={{0,16},{1,17},{2,18},{3,19},{4,20},{5,21},{6,22},{7,23},{8,24},{9,... | collective-permute-start | bytes 1544 | tf_op jit(solution)/shard_map/ppermute | solution.py:510
  48.7 1.3 %collective-permute-start.12 = (f32[1,128]{1,0:T(1,128)S(1)}, f32[1,128]{1,0:T(1,128)S(1)}, u32[]{:S(2)}, u32[]{:S(2)}) collective-permute-start(f32[1,128]{1,0:T(1,128)S(1)} %bitcast_add_fusion), channel_id=1, source_target_pairs={{0,48},{1,49},{2,50},{3,51},{4,52},{5,53},{6,54},{7,55},{8,56},{9,... | collective-permute-start | bytes 1544 | tf_op jit(solution)/shard_map/ppermute | solution.py:510
  50.1 1.2 %collective-permute-done.11 = f32[1,128]{1,0:T(1,128)S(1)} collective-permute-done((f32[1,128]{1,0:T(1,128)S(1)}, f32[1,128]{1,0:T(1,128)S(1)}, u32[]{:S(2)}, u32[]{:S(2)}) %collective-permute-start.11) | collective-permute-done | bytes 544 | tf_op jit(solution)/shard_map/ppermute | solution.py:510
  51.4 0.4 update.1
  51.9 1.3 %collective-permute-start.15 = (f32[288,128]{1,0:T(8,128)S(1)}, f32[288,128]{1,0:T(8,128)S(1)}, u32[]{:S(2)}, u32[]{:S(2)}) collective-permute-start(f32[288,128]{1,0:T(8,128)S(1)} %update.1), channel_id=1, source_target_pairs={{0,16},{1,17},{2,18},{3,19},{4,20},{5,21},{6,22},{7,23},{8,24},{9,... | collective-permute-start | bytes 442376 | tf_op jit(solution)/shard_map/ppermute | solution.py:510
  53.1 2.5 %collective-permute-start.16 = (f32[288,128]{1,0:T(8,128)S(1)}, f32[288,128]{1,0:T(8,128)S(1)}, u32[]{:S(2)}, u32[]{:S(2)}) collective-permute-start(f32[288,128]{1,0:T(8,128)S(1)} %update.1), channel_id=1, source_target_pairs={{0,32},{1,33},{2,34},{3,35},{4,36},{5,37},{6,38},{7,39},{8,40},{9,... | collective-permute-start | bytes 442376 | tf_op jit(solution)/shard_map/ppermute | solution.py:510
  55.7 0.6 collective-permute-start.17
  56.3 0.8 %collective-permute-done.15 = f32[288,128]{1,0:T(8,128)S(1)} collective-permute-done((f32[288,128]{1,0:T(8,128)S(1)}, f32[288,128]{1,0:T(8,128)S(1)}, u32[]{:S(2)}, u32[]{:S(2)}) %collective-permute-start.15) | collective-permute-done | bytes 147488 | tf_op jit(solution)/shard_map/ppermute | solution.py:510
  57.2 3.0 %collective-permute-done.16 = f32[288,128]{1,0:T(8,128)S(1)} collective-permute-done((f32[288,128]{1,0:T(8,128)S(1)}, f32[288,128]{1,0:T(8,128)S(1)}, u32[]{:S(2)}, u32[]{:S(2)}) %collective-permute-start.16) | collective-permute-done | bytes 147488 | tf_op jit(solution)/shard_map/ppermute | solution.py:510
  60.4 3.4 %collective-permute-start.18 = (f32[4,288,128]{2,1,0:T(8,128)S(1)}, f32[4,288,128]{2,1,0:T(8,128)S(1)}, u32[]{:S(2)}, u32[]{:S(2)}) collective-permute-start(f32[4,288,128]{2,1,0:T(8,128)S(1)} %bitcast_dynamic-update-slice_fusion.mine), channel_id=1, source_target_pairs={{0,64},{64,0},{1,65},{65,1},{2,66},{66,2},{3,67},{67,3},{4,68},{68... | collective-permute-start | bytes 1769480 | tf_op jit(solution)/shard_map/ppermute | solution.py:554
  64.2 1.2 %collective-permute-done.18.other = f32[4,288,128]{2,1,0:T(8,128)S(1)} collective-permute-done((f32[4,288,128]{2,1,0:T(8,128)S(1)}, f32[4,288,128]{2,1,0:T(8,128)S(1)}, u32[]{:S(2)}, u32[]{:S(2)}) %collective-permute-start.18) | collective-permute-done | bytes 589856 | tf_op jit(solution)/shard_map/ppermute | solution.py:554
  65.4 5.1 %act.1 = f32[32,400]{1,0:T(8,128)S(1)} custom-call(f32[4,288,128]{2,1,0:T(8,128)S(1)} %bitcast_dynamic-update-slice_fusion.mine, f32[4,288,128]{2,1,0:T(8,128)S(1)} %collective-permute-done.18.other, bf16[12,6,2,32,128]{4,3,2,1,0:T(8,128)(2,1)S(1)} %get-tuple-element.16.boards, bf16[1280,128]{1,0:T(8,128)(2,1)S(1)} %get-tuple-element.17.heads), custom_call_target="tpu_custom_call" | custom-call | flops 8000000000 | bytes 4000000 | tf_op jit(solution)/shard_map/act/pallas_call | solution.py:183
  70.6 0.5 collective-permute-start.19
  71.0 0.6 select_bitcast_fusion
  71.9 0.7 pad_maximum_fusion.1
  (50 shorter events, 2.2 us)
Async XLA Ops:
  1.3 13.5 %copy-start.2 = (f32[36,128]{1,0:T(8,128)S(1)}, f32[36,128]{1,0:T(8,128)}, u32[]{:S(2)}) copy-start(f32[36,128]{1,0:T(8,128)} %first_in.1) | copy-start | bytes 55300
  1.3 13.5 %copy-start.3 = (f32[36,128]{1,0:T(8,128)S(1)}, f32[36,128]{1,0:T(8,128)}, u32[]{:S(2)}) copy-start(f32[36,128]{1,0:T(8,128)} %second_in.1) | copy-start | bytes 55300
  8.3 7.7 %collective-permute-start = (f32[288,128]{1,0:T(8,128)}, f32[288,128]{1,0:T(8,128)S(1)}, u32[]{:S(2)}, u32[]{:S(2)}) collective-permute-start(f32[288,128]{1,0:T(8,128)} %get-tuple-element.12), channel_id=1, source_target_pairs={{0,32},{1,33},{2,34},{3,35},{4,36},{5,37},{6,38},{7,39},{8,40},{9,... | collective-permute-start | bytes 442376 | tf_op jit(solution)/shard_map/ppermute | solution.py:510
  12.1 7.3 %collective-permute-start.1 = (f32[288,128]{1,0:T(8,128)}, f32[288,128]{1,0:T(8,128)S(1)}, u32[]{:S(2)}, u32[]{:S(2)}) collective-permute-start(f32[288,128]{1,0:T(8,128)} %get-tuple-element.13), channel_id=1, source_target_pairs={{0,16},{1,17},{2,18},{3,19},{4,20},{5,21},{6,22},{7,23},{8,24},{9,... | collective-permute-start | bytes 442376 | tf_op jit(solution)/shard_map/ppermute | solution.py:510
  12.5 6.9 %collective-permute-start.2 = (f32[288,128]{1,0:T(8,128)}, f32[288,128]{1,0:T(8,128)S(1)}, u32[]{:S(2)}, u32[]{:S(2)}) collective-permute-start(f32[288,128]{1,0:T(8,128)} %get-tuple-element.14), channel_id=1, source_target_pairs={{0,48},{1,49},{2,50},{3,51},{4,52},{5,53},{6,54},{7,55},{8,56},{9,... | collective-permute-start | bytes 442376 | tf_op jit(solution)/shard_map/ppermute | solution.py:510
  14.8 0.9 %copy-start.1 = (f32[288,128]{1,0:T(8,128)S(1)}, f32[288,128]{1,0:T(8,128)}, u32[]{:S(2)}) copy-start(f32[288,128]{1,0:T(8,128)} %get-tuple-element.10.own_in) | copy-start | bytes 442372
  19.5 6.2 %collective-permute-start.4 = (f32[360,128]{1,0:T(8,128)S(1)}, f32[360,128]{1,0:T(8,128)S(1)}, u32[]{:S(2)}, u32[]{:S(2)}) collective-permute-start(f32[360,128]{1,0:T(8,128)S(1)} %pad_maximum_fusion), channel_id=1, source_target_pairs={{0,4},{1,5},{2,6},{3,7},{4,8},{5,9},{6,10},{7,11},{8,12},{9,13},{1... | collective-permute-start | bytes 552968 | tf_op jit(solution)/shard_map/ppermute | solution.py:510
  20.8 9.9 %collective-permute-start.3 = (f32[360,128]{1,0:T(8,128)S(1)}, f32[360,128]{1,0:T(8,128)S(1)}, u32[]{:S(2)}, u32[]{:S(2)}) collective-permute-start(f32[360,128]{1,0:T(8,128)S(1)} %pad_maximum_fusion), channel_id=1, source_target_pairs={{0,8},{1,9},{2,10},{3,11},{4,12},{5,13},{6,14},{7,15},{8,0},{9,1},... | collective-permute-start | bytes 552968 | tf_op jit(solution)/shard_map/ppermute | solution.py:510
  23.3 7.4 %collective-permute-start.5 = (f32[360,128]{1,0:T(8,128)S(1)}, f32[360,128]{1,0:T(8,128)S(1)}, u32[]{:S(2)}, u32[]{:S(2)}) collective-permute-start(f32[360,128]{1,0:T(8,128)S(1)} %pad_maximum_fusion), channel_id=1, source_target_pairs={{0,12},{1,13},{2,14},{3,15},{4,0},{5,1},{6,2},{7,3},{8,4},{9,5},{1... | collective-permute-start | bytes 552968 | tf_op jit(solution)/shard_map/ppermute | solution.py:510
  30.7 6.5 %collective-permute-start.6 = (f32[288,128]{1,0:T(8,128)S(1)}, f32[288,128]{1,0:T(8,128)S(1)}, u32[]{:S(2)}, u32[]{:S(2)}) collective-permute-start(f32[288,128]{1,0:T(8,128)S(1)} %fusion), channel_id=1, source_target_pairs={{0,2},{1,3},{2,0},{3,1},{4,6},{5,7},{6,4},{7,5},{8,10},{9,11},{10,... | collective-permute-start | bytes 442376 | tf_op jit(solution)/shard_map/ppermute | solution.py:510
  34.4 6.9 %collective-permute-start.7 = (f32[288,128]{1,0:T(8,128)S(1)}, f32[288,128]{1,0:T(8,128)S(1)}, u32[]{:S(2)}, u32[]{:S(2)}) collective-permute-start(f32[288,128]{1,0:T(8,128)S(1)} %fusion), channel_id=1, source_target_pairs={{0,1},{1,2},{2,3},{3,0},{4,5},{5,6},{6,7},{7,4},{8,9},{9,10},{10,1... | collective-permute-start | bytes 442376 | tf_op jit(solution)/shard_map/ppermute | solution.py:510
  35.1 6.2 %collective-permute-start.8 = (f32[288,128]{1,0:T(8,128)S(1)}, f32[288,128]{1,0:T(8,128)S(1)}, u32[]{:S(2)}, u32[]{:S(2)}) collective-permute-start(f32[288,128]{1,0:T(8,128)S(1)} %fusion), channel_id=1, source_target_pairs={{0,3},{1,0},{2,1},{3,2},{4,7},{5,4},{6,5},{7,6},{8,11},{9,8},{10,9... | collective-permute-start | bytes 442376 | tf_op jit(solution)/shard_map/ppermute | solution.py:510
  37.1 14.3 %copy-start = (f32[2304,128]{1,0:T(8,128)S(1)}, f32[2304,128]{1,0:T(8,128)}, u32[]{:S(2)}) copy-start(f32[2304,128]{1,0:T(8,128)} %torso_in.1) | copy-start | bytes 3538948
  37.1 6.9 %collective-permute-start.13 = (f32[144,128]{1,0:T(8,128)S(1)}, f32[144,128]{1,0:T(8,128)S(1)}, u32[]{:S(2)}, u32[]{:S(2)}) collective-permute-start(f32[144,128]{1,0:T(8,128)S(1)} %bitcast.41), channel_id=1, source_target_pairs={{0,1},{1,0},{2,3},{3,2},{4,5},{5,4},{6,7},{7,6},{8,9},{9,8},{10,11... | collective-permute-start | bytes 221192 | tf_op jit(solution)/shard_map/ppermute | solution.py:543
  41.4 4.3 %collective-permute-start.9 = (f32[1,128]{1,0:T(1,128)S(1)}, f32[1,128]{1,0:T(1,128)S(1)}, u32[]{:S(2)}, u32[]{:S(2)}) collective-permute-start(f32[1,128]{1,0:T(1,128)S(1)} %bitcast.47), channel_id=1, source_target_pairs={{0,64},{64,0},{1,65},{65,1},{2,66},{66,2},{3,67},{67,3},{4,68},{68... | collective-permute-start | bytes 1544 | tf_op jit(solution)/shard_map/ppermute | solution.py:554
  44.0 7.4 %collective-permute-start.14 = (f32[2,144,128]{2,1,0:T(8,128)S(1)}, f32[2,144,128]{2,1,0:T(8,128)S(1)}, u32[]{:S(2)}, u32[]{:S(2)}) collective-permute-start(f32[2,144,128]{2,1,0:T(8,128)S(1)} %maximum_select_fusion.2), channel_id=1, source_target_pairs={{0,2},{1,3},{2,0},{3,1},{4,6},{5,7},{6,4},{7,5},{8,10},{9,11},{10,... | collective-permute-start | bytes 442376 | tf_op jit(solution)/shard_map/ppermute | solution.py:543
  45.7 4.4 %collective-permute-start.10 = (f32[1,128]{1,0:T(1,128)S(1)}, f32[1,128]{1,0:T(1,128)S(1)}, u32[]{:S(2)}, u32[]{:S(2)}) collective-permute-start(f32[1,128]{1,0:T(1,128)S(1)} %bitcast_add_fusion), channel_id=1, source_target_pairs={{0,32},{1,33},{2,34},{3,35},{4,36},{5,37},{6,38},{7,39},{8,40},{9,... | collective-permute-start | bytes 1544 | tf_op jit(solution)/shard_map/ppermute | solution.py:510
  47.3 4.0 %collective-permute-start.11 = (f32[1,128]{1,0:T(1,128)S(1)}, f32[1,128]{1,0:T(1,128)S(1)}, u32[]{:S(2)}, u32[]{:S(2)}) collective-permute-start(f32[1,128]{1,0:T(1,128)S(1)} %bitcast_add_fusion), channel_id=1, source_target_pairs={{0,16},{1,17},{2,18},{3,19},{4,20},{5,21},{6,22},{7,23},{8,24},{9,... | collective-permute-start | bytes 1544 | tf_op jit(solution)/shard_map/ppermute | solution.py:510
  48.7 2.7 %collective-permute-start.12 = (f32[1,128]{1,0:T(1,128)S(1)}, f32[1,128]{1,0:T(1,128)S(1)}, u32[]{:S(2)}, u32[]{:S(2)}) collective-permute-start(f32[1,128]{1,0:T(1,128)S(1)} %bitcast_add_fusion), channel_id=1, source_target_pairs={{0,48},{1,49},{2,50},{3,51},{4,52},{5,53},{6,54},{7,55},{8,56},{9,... | collective-permute-start | bytes 1544 | tf_op jit(solution)/shard_map/ppermute | solution.py:510
  51.9 11.9 %copy-start.5 = (bf16[128,4]{0,1:T(4,128)(2,1)S(1)}, bf16[128,4]{0,1:T(4,128)(2,1)}, u32[]{:S(2)}) copy-start(bf16[128,4]{0,1:T(4,128)(2,1)} %param.20) | copy-start | bytes 3076
  51.9 11.9 %copy-start.4 = (bf16[64,10,10,128]{3,0,2,1:T(8,128)(2,1)S(1)}, bf16[64,10,10,128]{3,0,2,1:T(8,128)(2,1)}, u32[]{:S(2)}) copy-start(bf16[64,10,10,128]{3,0,2,1:T(8,128)(2,1)} %param.12) | copy-start | bytes 4915204
  51.9 5.3 %collective-permute-start.15 = (f32[288,128]{1,0:T(8,128)S(1)}, f32[288,128]{1,0:T(8,128)S(1)}, u32[]{:S(2)}, u32[]{:S(2)}) collective-permute-start(f32[288,128]{1,0:T(8,128)S(1)} %update.1), channel_id=1, source_target_pairs={{0,16},{1,17},{2,18},{3,19},{4,20},{5,21},{6,22},{7,23},{8,24},{9,... | collective-permute-start | bytes 442376 | tf_op jit(solution)/shard_map/ppermute | solution.py:510
  53.1 7.0 %collective-permute-start.16 = (f32[288,128]{1,0:T(8,128)S(1)}, f32[288,128]{1,0:T(8,128)S(1)}, u32[]{:S(2)}, u32[]{:S(2)}) collective-permute-start(f32[288,128]{1,0:T(8,128)S(1)} %update.1), channel_id=1, source_target_pairs={{0,32},{1,33},{2,34},{3,35},{4,36},{5,37},{6,38},{7,39},{8,40},{9,... | collective-permute-start | bytes 442376 | tf_op jit(solution)/shard_map/ppermute | solution.py:510
  55.7 4.7 %collective-permute-start.17 = (f32[288,128]{1,0:T(8,128)S(1)}, f32[288,128]{1,0:T(8,128)S(1)}, u32[]{:S(2)}, u32[]{:S(2)}) collective-permute-start(f32[288,128]{1,0:T(8,128)S(1)} %update.1), channel_id=1, source_target_pairs={{0,48},{1,49},{2,50},{3,51},{4,52},{5,53},{6,54},{7,55},{8,56},{9,... | collective-permute-start | bytes 442376 | tf_op jit(solution)/shard_map/ppermute | solution.py:510
  60.4 5.0 %collective-permute-start.18 = (f32[4,288,128]{2,1,0:T(8,128)S(1)}, f32[4,288,128]{2,1,0:T(8,128)S(1)}, u32[]{:S(2)}, u32[]{:S(2)}) collective-permute-start(f32[4,288,128]{2,1,0:T(8,128)S(1)} %bitcast_dynamic-update-slice_fusion.mine), channel_id=1, source_target_pairs={{0,64},{64,0},{1,65},{65,1},{2,66},{66,2},{3,67},{67,3},{4,68},{68... | collective-permute-start | bytes 1769480 | tf_op jit(solution)/shard_map/ppermute | solution.py:554
  70.6 1.4 %collective-permute-start.19 = (f32[32,400]{1,0:T(8,128)S(1)}, f32[32,400]{1,0:T(8,128)S(1)}, u32[]{:S(2)}, u32[]{:S(2)}) collective-permute-start(f32[32,400]{1,0:T(8,128)S(1)} %act.1), channel_id=1, source_target_pairs={{0,64},{64,0},{1,65},{65,1},{2,66},{66,2},{3,67},{67,3},{4,68},{68... | collective-permute-start | bytes 153608 | tf_op jit(solution)/shard_map/ppermute | solution.py:554

commit v11 on v10

--- a/solution.py
+++ b/solution.py
@@ -177,7 +177,7 @@
         out[:, 100 * d : 100 * d + 100] = (moves[d] - log_total)[:, :100]
 
 
-def act(mine, other, boards, heads, count=2, unroll=1):
+def act(mine, other, boards, heads, count=2, unroll=5):
     games = boards.shape[3]
     vmem = pl.BlockSpec(memory_space=pltpu.VMEM)
     return pl.pallas_call(
@@ -235,22 +235,21 @@
     for copy in copies:
         copy.start()
     clear_border(boards)
-    copies[0].wait()
-
-    for layer in range(2):
-        if layer == 1:
-            copies[2].wait()
-
-        def kernel_of(p, q, layer=layer):
+
+    def make_pairs(layer):
+        def kernel_of(p, q):
             at = layer * ROWS + (3 * p + q) * 128
             return weights[at : at + 128, :].astype(jnp.bfloat16)
 
-        def store(block, value, layer=layer):
+        def store(block, value):
             pairs[layer, block * 128 : (block + 1) * 128, :] = value
 
         pair_kernels(kernel_of, store)
+
     clear_border(middle)
     clear_border(slope)
+    copies[0].wait()
+    make_pairs(0)
     copies[1].wait()
 
     def run_layer(layer, source, emit):
@@ -263,6 +262,9 @@
                 masks[layer, first : first + count, :, parity] = (part > 0).astype(jnp.bfloat16)
 
     run_layer(0, boards, lambda first, parity, value: put_cells(middle, first, count, parity, value))
+
+    copies[2].wait()
+    make_pairs(1)
 
     def to_last(first, parity, value):
         last[pl.ds(first, count), :, parity] = value
@@ -362,40 +364,41 @@
     turned[1] = act_grad.T
     turned[0] = last[...].reshape(-1, 128).T
 
-    for core in range(2):
-
-        @pl.when(role == core)
-        def _(core=core):
-            for layer, source in ((1, middle), (0, boards)):
-                kept = []
-                for offset in range(9):
-                    parts = [x for x in segment_parts(layer, offset) if x[0] % 2 == core]
-                    if parts:
-                        kept.append((offset, parts))
-                windows = []
-                for offset, _ in kept:
-                    p, q = offset // 3, offset % 3
-                    cols = [source[p : p + 10, (j + q) // 2, (j + q) % 2] for j in range(10)]
-                    windows.append(jnp.stack(cols, axis=1).reshape(-1, 128))
-                for pair in range(0, len(kept), 2):
-                    blocks = jnp.dot(
-                        turned[layer],
-                        jnp.concatenate(windows[pair : pair + 2], axis=1),
-                        preferred_element_type=jnp.float32,
-                    )
-                    for k in range(2):
-                        block = blocks[:, 128 * k : 128 * k + 128].T
-                        for segment, first, end, at in kept[pair + k][1]:
-                            grad[segment // 2, first:end] = block[at : at + end - first]
-
-    sends = [
-        pltpu.make_async_copy(grad.at[lax.rem(y + k, LINE)], out, done.at[k])
-        for k, out in enumerate((own, next1, next2, next3))
-    ]
-    for copy in sends:
-        copy.start()
-    for copy in sends:
-        copy.wait()
+    def layer_gradient(layer, source, core):
+        kept = []
+        for offset in range(9):
+            parts = [x for x in segment_parts(layer, offset) if x[0] % 2 == core]
+            if parts:
+                kept.append((offset, parts))
+        windows = []
+        for offset, _ in kept:
+            p, q = offset // 3, offset % 3
+            cols = [source[p : p + 10, (j + q) // 2, (j + q) % 2] for j in range(10)]
+            windows.append(jnp.stack(cols, axis=1).reshape(-1, 128))
+        for pair in range(0, len(kept), 2):
+            blocks = jnp.dot(
+                turned[layer],
+                jnp.concatenate(windows[pair : pair + 2], axis=1),
+                preferred_element_type=jnp.float32,
+            )
+            for k in range(2):
+                block = blocks[:, 128 * k : 128 * k + 128].T
+                for segment, first, end, at in kept[pair + k][1]:
+                    grad[segment // 2, first:end] = block[at : at + end - first]
+
+    chunks = (own, next1, next2, next3)
+    for layer, source in ((1, middle), (0, boards)):
+        for core in range(2):
+            pl.when(role == core)(functools.partial(layer_gradient, layer, source, core))
+        for to_y in (2 * layer, 2 * layer + 1):
+            for k, out in enumerate(chunks):
+
+                @pl.when(lax.rem(y + k, LINE) == to_y)
+                def _(to_y=to_y, k=k, out=out):
+                    pltpu.make_async_copy(grad.at[to_y], out, done.at[k]).start()
+
+    for k, out in enumerate(chunks):
+        pltpu.make_async_copy(grad.at[0], out, done.at[k]).wait()
 
 
 def learn(
@@ -514,12 +517,6 @@
     return (x + shifted(x, axis, 2)) + (shifted(x, axis, 1) + shifted(x, axis, 3))
 
 
-def line_scatter(chunks, axis):
-    return (chunks[0] + shifted(chunks[2], axis, 2)) + (
-        shifted(chunks[1], axis, 1) + shifted(chunks[3], axis, 3)
-    )
-
-
 def line_place(pieces, at):
     whole = jnp.zeros((LINE,) + pieces[0].shape, pieces[0].dtype)
     for step, piece in enumerate(pieces):
@@ -531,12 +528,22 @@
     return line_place([x] + [shifted(x, axis, step) for step in range(1, LINE)], at)
 
 
-def line_exchange(summed, moments, axis, at):
-    rows = summed.shape[0]
-    both = jnp.concatenate([summed, moments])
-    got = [both] + [shifted(both, axis, step) for step in range(1, LINE)]
-    total = (got[0][:rows] + got[2][:rows]) + (got[1][:rows] + got[3][:rows])
-    return total, line_place([x[rows:] for x in got], at)
+def moments_along_x(own, role, x):
+    def device(role, x, rest):
+        return role * LINE**3 + rest // LINE * LINE * LINE + x * LINE + rest % LINE
+
+    same, next_to = [], []
+    for rest in range(LINE * LINE):
+        for to_role in range(2):
+            for to_x in range(LINE):
+                to = device(to_role, to_x, rest)
+                if to_x // 2 != to_role:
+                    same.append((device(to_role, to_x ^ 2, rest), to))
+                next_to.append((device(to_x // 2, 2 * to_role + 1 - to_x % 2, rest), to))
+    same = jnp.where(x // 2 == role, own, lax.ppermute(own, ("role", "dp"), same))
+    next_to = lax.ppermute(own, ("role", "dp"), next_to)
+    even = x % 2 == 0
+    return jnp.concatenate([jnp.where(even, same, next_to), jnp.where(even, next_to, same)])
 
 
 def swapped_z(x, bit):
@@ -583,11 +590,12 @@
         value_head[None],
     )
     own, moments = pull(own, first_moment, second_moment)
-    summed = line_scatter((own, next1, next2, next3), "y")
-    summed, moments = line_exchange(summed, moments, "x", x)
-    moments = lax.dynamic_slice_in_dim(moments, 2 * role, 2, 0).reshape(-1, 128)
+    next2 = shifted(next2, "y", 2)
+    next2, moments = lax.optimization_barrier((next2, moments))
+    moments = moments_along_x(moments, role, x)
     moments = moments_along_z(moments, z)
-    summed = line_total(summed, "z")
+    summed = (own + next2) + (shifted(next1, "y", 1) + shifted(next3, "y", 3))
+    summed = line_total(line_total(summed, "x"), "z")
     squares = jnp.sum(summed * summed, axis=0, keepdims=True)
     squares = line_total(squares + role_swap(squares), "y")
     fresh = update(summed, squares, moments.reshape(LINE, 2, 2 * PIECE, 128), torso)

time: 72.8 us -> 74.3 us (1.021)
  starting transfers between devices: 34.7 us -> 40.9 us
  waiting for transfers between devices: 20.6 us -> 17.5 us
  Pallas kernels: 13.2 us -> 11.6 us
    ppermute x0 -> x2, starting transfers between devices: none -> 6.05 us  [the longest x1 4.75 us: moments_along_x(): next_to = lax.ppermute(own, ('role', 'dp'), next_to)]
    ppermute x15, waiting for transfers between devices: 19.1 us -> 15.2 us  [shifted(): return lax.ppermute(x, 'dp', pairs)]
    pallas_call x1, Pallas kernels: 5.14 us -> 3.71 us  [act(): pl.pallas_call(functools.partial(actor_kernel, count, unroll), out_shape=...]
    ppermute x3, waiting for transfers between devices: 1.49 us -> 2.29 us  [role_swap(): return lax.ppermute(x, 'role', [(0, 1), (1, 0)])]
    ppermute x3, starting transfers between devices: 6.5 us -> 7.26 us  [role_swap(): return lax.ppermute(x, 'role', [(0, 1), (1, 0)])]
  transfers between devices with their start and end apart: 20 -> 22, of which waited for: 11 -> 11; matrix products, arithmetic and copies ran while one was open for 1% -> 1% of each run, Pallas kernels for 1% -> 1%
where the time goes in v11:
time: 74.3 us; the launch traced here: 74.1 us
  starting transfers between devices  40.9 us (55%)
  waiting for transfers between devices  17.5 us (24%)
  Pallas kernels  11.6 us (16%)
  other arithmetic  1.51 us (2%)
  between operations  1.5 us (2%)
  local copies, waits for them, and re-layouts  1.04 us (1%)
    ppermute x15, starting transfers between devices, shifted(): return lax.ppermute(x, 'dp', pairs)  25.8 us
    ppermute x15, waiting for transfers between devices, shifted(): return lax.ppermute(x, 'dp', pairs)  15.2 us
    ppermute x3, starting transfers between devices, role_swap(): return lax.ppermute(x, 'role', [(0, 1), (1, 0)])  7.26 us
    pallas_call x1, Pallas kernels, learn(): pl.pallas_call(functools.partial(learner_kernel, count), out_shape=[jax.S...  6.86 us
    ppermute x1, starting transfers between devices, moments_along_x(): next_to = lax.ppermute(own, ('role', 'dp'), next_to)  4.75 us
    pallas_call x1, Pallas kernels, act(): pl.pallas_call(functools.partial(actor_kernel, count, unroll), out_shape=...  3.71 us
    ppermute x3, waiting for transfers between devices, role_swap(): return lax.ppermute(x, 'role', [(0, 1), (1, 0)])  2.29 us
    ppermute x2, starting transfers between devices, swapped_z(): return lax.ppermute(x, 'dp', [(d, d ^ bit) for d in range(LINE ** 3)])  1.81 us
  transfers between devices with their start and end apart: 22, of which 11 were waited for; matrix products, arithmetic and copies ran while one was open for 1% of the time, Pallas kernels for 1%

profile of v11, /device:TPU:1, one launch (start us, length us, event | category | flops | bytes accessed | tf_op | source)
XLA Modules:
  0.0 74.1 jit_solution(1570356284682390145)
XLA Ops:
  1.3 6.9 %learn.1 = (f32[288,128]{1,0:T(8,128)}, f32[288,128]{1,0:T(8,128)}, f32[288,128]{1,0:T(8,128)}, f32[288,128]{1,0:T(8,128)}) custom-call(s32[1]{0:T(128)S(6)} %copy.18.length_in, bf16[10,10,16,128]{3,2,1,0:T(8,128)(2,1)} %bitcast.32, s32[1,16]{1,0:T(1,128)} %actions_in.1, f32[1,16]{1,0:T(1,128)} %behaviour_in.1, f32[1,16]{1,0:T(1,128)} %regular_in.1, ...), custom_call_target="tpu_custom_call" | custom-call | flops 4000000000 | bytes 3000000 | tf_op jit(solution)/shard_map/learn/pallas_call | solution.py:411
  8.2 3.8 %collective-permute-start = (f32[288,128]{1,0:T(8,128)}, f32[288,128]{1,0:T(8,128)S(1)}, u32[]{:S(2)}, u32[]{:S(2)}) collective-permute-start(f32[288,128]{1,0:T(8,128)} %get-tuple-element.14), channel_id=1, source_target_pairs={{0,32},{1,33},{2,34},{3,35},{4,36},{5,37},{6,38},{7,39},{8,40},{9,... | collective-permute-start | bytes 442376 | tf_op jit(solution)/shard_map/ppermute | solution.py:513
  12.4 2.3 %collective-permute-start.2 = (f32[288,128]{1,0:T(8,128)}, f32[288,128]{1,0:T(8,128)S(1)}, u32[]{:S(2)}, u32[]{:S(2)}) collective-permute-start(f32[288,128]{1,0:T(8,128)} %get-tuple-element.18), channel_id=1, source_target_pairs={{0,48},{1,49},{2,50},{3,51},{4,52},{5,53},{6,54},{7,55},{8,56},{9,... | collective-permute-start | bytes 442376 | tf_op jit(solution)/shard_map/ppermute | solution.py:513
  14.7 0.9 %copy-done.1 = f32[288,128]{1,0:T(8,128)S(1)} copy-done((f32[288,128]{1,0:T(8,128)S(1)}, f32[288,128]{1,0:T(8,128)}, u32[]{:S(2)}) %copy-start.1) | copy-done | bytes 147480
  15.8 1.3 %collective-permute-start.13 = (f32[72,128]{1,0:T(8,128)S(1)}, f32[72,128]{1,0:T(8,128)S(1)}, u32[]{:S(2)}, u32[]{:S(2)}) collective-permute-start(f32[72,128]{1,0:T(8,128)S(1)} %get-tuple-element.19), channel_id=1, source_target_pairs={{0,8},{4,12},{72,64},{76,68},{1,9},{5,13},{73,65},{77,69},{2,10},{... | collective-permute-start | bytes 110600 | tf_op jit(solution)/shard_map/ppermute | solution.py:543
  17.1 4.8 %collective-permute-start.14 = (f32[72,128]{1,0:T(8,128)S(1)}, f32[72,128]{1,0:T(8,128)S(1)}, u32[]{:S(2)}, u32[]{:S(2)}) collective-permute-start(f32[72,128]{1,0:T(8,128)S(1)} %get-tuple-element.19), channel_id=1, source_target_pairs={{4,0},{0,4},{68,8},{64,12},{12,64},{8,68},{76,72},{72,76},{5,1},{1... | collective-permute-start | bytes 110600 | tf_op jit(solution)/shard_map/ppermute | solution.py:544
  21.9 0.8 %collective-permute-start.3 = (f32[288,128]{1,0:T(8,128)S(1)}, f32[288,128]{1,0:T(8,128)S(1)}, u32[]{:S(2)}, u32[]{:S(2)}) collective-permute-start(f32[288,128]{1,0:T(8,128)S(1)} %add_add_fusion.2), channel_id=1, source_target_pairs={{0,8},{1,9},{2,10},{3,11},{4,12},{5,13},{6,14},{7,15},{8,0},{9,1},... | collective-permute-start | bytes 442376 | tf_op jit(solution)/shard_map/ppermute | solution.py:513
  22.7 2.7 %collective-permute-start.5 = (f32[288,128]{1,0:T(8,128)S(1)}, f32[288,128]{1,0:T(8,128)S(1)}, u32[]{:S(2)}, u32[]{:S(2)}) collective-permute-start(f32[288,128]{1,0:T(8,128)S(1)} %add_add_fusion.2), channel_id=1, source_target_pairs={{0,12},{1,13},{2,14},{3,15},{4,0},{5,1},{6,2},{7,3},{8,4},{9,5},{1... | collective-permute-start | bytes 442376 | tf_op jit(solution)/shard_map/ppermute | solution.py:513
  25.4 1.7 %collective-permute-start.15 = (f32[144,128]{1,0:T(8,128)S(1)}, f32[144,128]{1,0:T(8,128)S(1)}, u32[]{:S(2)}, u32[]{:S(2)}) collective-permute-start(f32[144,128]{1,0:T(8,128)S(1)} %get-tuple-element.29), channel_id=1, source_target_pairs={{0,1},{1,0},{2,3},{3,2},{4,5},{5,4},{6,7},{7,6},{8,9},{9,8},{10,11... | collective-permute-start | bytes 221192 | tf_op jit(solution)/shard_map/ppermute | solution.py:550
  27.2 0.4 collective-permute-done.3
  27.6 3.8 %collective-permute-done.4 = f32[288,128]{1,0:T(8,128)S(1)} collective-permute-done((f32[288,128]{1,0:T(8,128)S(1)}, f32[288,128]{1,0:T(8,128)S(1)}, u32[]{:S(2)}, u32[]{:S(2)}) %collective-permute-start.4) | collective-permute-done | bytes 147488 | tf_op jit(solution)/shard_map/ppermute | solution.py:513
  31.5 3.7 %collective-permute-start.6 = (f32[288,128]{1,0:T(8,128)S(1)}, f32[288,128]{1,0:T(8,128)S(1)}, u32[]{:S(2)}, u32[]{:S(2)}) collective-permute-start(f32[288,128]{1,0:T(8,128)S(1)} %add_add_fusion.1), channel_id=1, source_target_pairs={{0,2},{1,3},{2,0},{3,1},{4,6},{5,7},{6,4},{7,5},{8,10},{9,11},{10,... | collective-permute-start | bytes 442376 | tf_op jit(solution)/shard_map/ppermute | solution.py:513
  35.1 0.7 collective-permute-start.7
  35.9 1.9 %collective-permute-start.8 = (f32[288,128]{1,0:T(8,128)S(1)}, f32[288,128]{1,0:T(8,128)S(1)}, u32[]{:S(2)}, u32[]{:S(2)}) collective-permute-start(f32[288,128]{1,0:T(8,128)S(1)} %add_add_fusion.1), channel_id=1, source_target_pairs={{0,3},{1,0},{2,1},{3,2},{4,7},{5,4},{6,5},{7,6},{8,11},{9,8},{10,9... | collective-permute-start | bytes 442376 | tf_op jit(solution)/shard_map/ppermute | solution.py:513
  37.9 4.1 %collective-permute-done.7 = f32[288,128]{1,0:T(8,128)S(1)} collective-permute-done((f32[288,128]{1,0:T(8,128)S(1)}, f32[288,128]{1,0:T(8,128)S(1)}, u32[]{:S(2)}, u32[]{:S(2)}) %collective-permute-start.7) | collective-permute-done | bytes 147488 | tf_op jit(solution)/shard_map/ppermute | solution.py:513
  42.1 0.6 collective-permute-done.8
  42.8 3.9 %collective-permute-start.9 = (f32[1,128]{1,0:T(1,128)S(1)}, f32[1,128]{1,0:T(1,128)S(1)}, u32[]{:S(2)}, u32[]{:S(2)}) collective-permute-start(f32[1,128]{1,0:T(1,128)S(1)} %bitcast.31), channel_id=1, source_target_pairs={{0,64},{64,0},{1,65},{65,1},{2,66},{66,2},{3,67},{67,3},{4,68},{68... | collective-permute-start | bytes 1544 | tf_op jit(solution)/shard_map/ppermute | solution.py:561
  46.7 0.8 %collective-permute-done.9 = f32[1,128]{1,0:T(1,128)S(1)} collective-permute-done((f32[1,128]{1,0:T(1,128)S(1)}, f32[1,128]{1,0:T(1,128)S(1)}, u32[]{:S(2)}, u32[]{:S(2)}) %collective-permute-start.9) | collective-permute-done | bytes 544 | tf_op jit(solution)/shard_map/ppermute | solution.py:561
  47.5 2.9 %collective-permute-start.10 = (f32[1,128]{1,0:T(1,128)S(1)}, f32[1,128]{1,0:T(1,128)S(1)}, u32[]{:S(2)}, u32[]{:S(2)}) collective-permute-start(f32[1,128]{1,0:T(1,128)S(1)} %bitcast_add_fusion), channel_id=1, source_target_pairs={{0,32},{1,33},{2,34},{3,35},{4,36},{5,37},{6,38},{7,39},{8,40},{9,... | collective-permute-start | bytes 1544 | tf_op jit(solution)/shard_map/ppermute | solution.py:513
  50.8 2.3 %collective-permute-start.12 = (f32[1,128]{1,0:T(1,128)S(1)}, f32[1,128]{1,0:T(1,128)S(1)}, u32[]{:S(2)}, u32[]{:S(2)}) collective-permute-start(f32[1,128]{1,0:T(1,128)S(1)} %bitcast_add_fusion), channel_id=1, source_target_pairs={{0,48},{1,49},{2,50},{3,51},{4,52},{5,53},{6,54},{7,55},{8,56},{9,... | collective-permute-start | bytes 1544 | tf_op jit(solution)/shard_map/ppermute | solution.py:513
  53.2 0.9 %collective-permute-done.11 = f32[1,128]{1,0:T(1,128)S(1)} collective-permute-done((f32[1,128]{1,0:T(1,128)S(1)}, f32[1,128]{1,0:T(1,128)S(1)}, u32[]{:S(2)}, u32[]{:S(2)}) %collective-permute-start.11) | collective-permute-done | bytes 544 | tf_op jit(solution)/shard_map/ppermute | solution.py:513
  54.1 0.4 update.1
  54.6 3.8 %collective-permute-start.18 = (f32[288,128]{1,0:T(8,128)S(1)}, f32[288,128]{1,0:T(8,128)S(1)}, u32[]{:S(2)}, u32[]{:S(2)}) collective-permute-start(f32[288,128]{1,0:T(8,128)S(1)} %update.1), channel_id=1, source_target_pairs={{0,32},{1,33},{2,34},{3,35},{4,36},{5,37},{6,38},{7,39},{8,40},{9,... | collective-permute-start | bytes 442376 | tf_op jit(solution)/shard_map/ppermute | solution.py:513
  58.5 1.3 %collective-permute-done.17 = f32[288,128]{1,0:T(8,128)S(1)} collective-permute-done((f32[288,128]{1,0:T(8,128)S(1)}, f32[288,128]{1,0:T(8,128)S(1)}, u32[]{:S(2)}, u32[]{:S(2)}) %collective-permute-start.17) | collective-permute-done | bytes 147488 | tf_op jit(solution)/shard_map/ppermute | solution.py:513
  59.8 3.4 %collective-permute-done.18 = f32[288,128]{1,0:T(8,128)S(1)} collective-permute-done((f32[288,128]{1,0:T(8,128)S(1)}, f32[288,128]{1,0:T(8,128)S(1)}, u32[]{:S(2)}, u32[]{:S(2)}) %collective-permute-start.18) | collective-permute-done | bytes 147488 | tf_op jit(solution)/shard_map/ppermute | solution.py:513
  63.2 0.6 collective-permute-done.19
  63.9 2.9 %collective-permute-start.20 = (f32[4,288,128]{2,1,0:T(8,128)S(1)}, f32[4,288,128]{2,1,0:T(8,128)S(1)}, u32[]{:S(2)}, u32[]{:S(2)}) collective-permute-start(f32[4,288,128]{2,1,0:T(8,128)S(1)} %bitcast_dynamic-update-slice_fusion.mine), channel_id=1, source_target_pairs={{0,64},{64,0},{1,65},{65,1},{2,66},{66,2},{3,67},{67,3},{4,68},{68... | collective-permute-start | bytes 1769480 | tf_op jit(solution)/shard_map/ppermute | solution.py:561
  67.2 1.2 %collective-permute-done.20.other = f32[4,288,128]{2,1,0:T(8,128)S(1)} collective-permute-done((f32[4,288,128]{2,1,0:T(8,128)S(1)}, f32[4,288,128]{2,1,0:T(8,128)S(1)}, u32[]{:S(2)}, u32[]{:S(2)}) %collective-permute-start.20) | collective-permute-done | bytes 589856 | tf_op jit(solution)/shard_map/ppermute | solution.py:561
  68.4 3.7 %act.1 = f32[32,400]{1,0:T(8,128)S(1)} custom-call(f32[4,288,128]{2,1,0:T(8,128)S(1)} %bitcast_dynamic-update-slice_fusion.mine, f32[4,288,128]{2,1,0:T(8,128)S(1)} %collective-permute-done.20.other, bf16[12,6,2,32,128]{4,3,2,1,0:T(8,128)(2,1)S(1)} %get-tuple-element.20.boards, bf16[1280,128]{1,0:T(8,128)(2,1)S(1)} %get-tuple-element.21.heads), custom_call_target="tpu_custom_call" | custom-call | flops 8000000000 | bytes 4000000 | tf_op jit(solution)/shard_map/act/pallas_call | solution.py:183
  72.1 0.5 collective-permute-start.21
  72.5 0.6 select_bitcast_fusion
  73.5 0.7 pad_maximum_fusion
  (48 shorter events, 2.3 us)
Async XLA Ops:
  1.3 13.4 %copy-start.2 = (f32[36,128]{1,0:T(8,128)S(1)}, f32[36,128]{1,0:T(8,128)}, u32[]{:S(2)}) copy-start(f32[36,128]{1,0:T(8,128)} %first_in.1) | copy-start | bytes 55300
  1.3 13.4 %copy-start.3 = (f32[36,128]{1,0:T(8,128)S(1)}, f32[36,128]{1,0:T(8,128)}, u32[]{:S(2)}) copy-start(f32[36,128]{1,0:T(8,128)} %second_in.1) | copy-start | bytes 55300
  8.2 7.7 %collective-permute-start = (f32[288,128]{1,0:T(8,128)}, f32[288,128]{1,0:T(8,128)S(1)}, u32[]{:S(2)}, u32[]{:S(2)}) collective-permute-start(f32[288,128]{1,0:T(8,128)} %get-tuple-element.14), channel_id=1, source_target_pairs={{0,32},{1,33},{2,34},{3,35},{4,36},{5,37},{6,38},{7,39},{8,40},{9,... | collective-permute-start | bytes 442376 | tf_op jit(solution)/shard_map/ppermute | solution.py:513
  12.0 9.9 %collective-permute-start.1 = (f32[288,128]{1,0:T(8,128)}, f32[288,128]{1,0:T(8,128)S(1)}, u32[]{:S(2)}, u32[]{:S(2)}) collective-permute-start(f32[288,128]{1,0:T(8,128)} %get-tuple-element.17), channel_id=1, source_target_pairs={{0,16},{1,17},{2,18},{3,19},{4,20},{5,21},{6,22},{7,23},{8,24},{9,... | collective-permute-start | bytes 442376 | tf_op jit(solution)/shard_map/ppermute | solution.py:513
  12.4 9.5 %collective-permute-start.2 = (f32[288,128]{1,0:T(8,128)}, f32[288,128]{1,0:T(8,128)S(1)}, u32[]{:S(2)}, u32[]{:S(2)}) collective-permute-start(f32[288,128]{1,0:T(8,128)} %get-tuple-element.18), channel_id=1, source_target_pairs={{0,48},{1,49},{2,50},{3,51},{4,52},{5,53},{6,54},{7,55},{8,56},{9,... | collective-permute-start | bytes 442376 | tf_op jit(solution)/shard_map/ppermute | solution.py:513
  14.7 0.9 %copy-start.1 = (f32[288,128]{1,0:T(8,128)S(1)}, f32[288,128]{1,0:T(8,128)}, u32[]{:S(2)}) copy-start(f32[288,128]{1,0:T(8,128)} %get-tuple-element.12.own_in) | copy-start | bytes 442372
  15.8 9.6 %collective-permute-start.13 = (f32[72,128]{1,0:T(8,128)S(1)}, f32[72,128]{1,0:T(8,128)S(1)}, u32[]{:S(2)}, u32[]{:S(2)}) collective-permute-start(f32[72,128]{1,0:T(8,128)S(1)} %get-tuple-element.19), channel_id=1, source_target_pairs={{0,8},{4,12},{72,64},{76,68},{1,9},{5,13},{73,65},{77,69},{2,10},{... | collective-permute-start | bytes 110600 | tf_op jit(solution)/shard_map/ppermute | solution.py:543
  17.1 8.3 %collective-permute-start.14 = (f32[72,128]{1,0:T(8,128)S(1)}, f32[72,128]{1,0:T(8,128)S(1)}, u32[]{:S(2)}, u32[]{:S(2)}) collective-permute-start(f32[72,128]{1,0:T(8,128)S(1)} %get-tuple-element.19), channel_id=1, source_target_pairs={{4,0},{0,4},{68,8},{64,12},{12,64},{8,68},{76,72},{72,76},{5,1},{1... | collective-permute-start | bytes 110600 | tf_op jit(solution)/shard_map/ppermute | solution.py:544
  21.9 5.7 %collective-permute-start.3 = (f32[288,128]{1,0:T(8,128)S(1)}, f32[288,128]{1,0:T(8,128)S(1)}, u32[]{:S(2)}, u32[]{:S(2)}) collective-permute-start(f32[288,128]{1,0:T(8,128)S(1)} %add_add_fusion.2), channel_id=1, source_target_pairs={{0,8},{1,9},{2,10},{3,11},{4,12},{5,13},{6,14},{7,15},{8,0},{9,1},... | collective-permute-start | bytes 442376 | tf_op jit(solution)/shard_map/ppermute | solution.py:513
  22.7 8.7 %collective-permute-start.4 = (f32[288,128]{1,0:T(8,128)S(1)}, f32[288,128]{1,0:T(8,128)S(1)}, u32[]{:S(2)}, u32[]{:S(2)}) collective-permute-start(f32[288,128]{1,0:T(8,128)S(1)} %add_add_fusion.2), channel_id=1, source_target_pairs={{0,4},{1,5},{2,6},{3,7},{4,8},{5,9},{6,10},{7,11},{8,12},{9,13},{1... | collective-permute-start | bytes 442376 | tf_op jit(solution)/shard_map/ppermute | solution.py:513
  22.7 8.7 %collective-permute-start.5 = (f32[288,128]{1,0:T(8,128)S(1)}, f32[288,128]{1,0:T(8,128)S(1)}, u32[]{:S(2)}, u32[]{:S(2)}) collective-permute-start(f32[288,128]{1,0:T(8,128)S(1)} %add_add_fusion.2), channel_id=1, source_target_pairs={{0,12},{1,13},{2,14},{3,15},{4,0},{5,1},{6,2},{7,3},{8,4},{9,5},{1... | collective-permute-start | bytes 442376 | tf_op jit(solution)/shard_map/ppermute | solution.py:513
  25.4 12.4 %collective-permute-start.15 = (f32[144,128]{1,0:T(8,128)S(1)}, f32[144,128]{1,0:T(8,128)S(1)}, u32[]{:S(2)}, u32[]{:S(2)}) collective-permute-start(f32[144,128]{1,0:T(8,128)S(1)} %get-tuple-element.29), channel_id=1, source_target_pairs={{0,1},{1,0},{2,3},{3,2},{4,5},{5,4},{6,7},{7,6},{8,9},{9,8},{10,11... | collective-permute-start | bytes 221192 | tf_op jit(solution)/shard_map/ppermute | solution.py:550
  31.4 22.6 %copy-start = (f32[2304,128]{1,0:T(8,128)S(1)}, f32[2304,128]{1,0:T(8,128)}, u32[]{:S(2)}) copy-start(f32[2304,128]{1,0:T(8,128)} %torso_in.1) | copy-start | bytes 3538948
  31.5 6.5 %collective-permute-start.6 = (f32[288,128]{1,0:T(8,128)S(1)}, f32[288,128]{1,0:T(8,128)S(1)}, u32[]{:S(2)}, u32[]{:S(2)}) collective-permute-start(f32[288,128]{1,0:T(8,128)S(1)} %add_add_fusion.1), channel_id=1, source_target_pairs={{0,2},{1,3},{2,0},{3,1},{4,6},{5,7},{6,4},{7,5},{8,10},{9,11},{10,... | collective-permute-start | bytes 442376 | tf_op jit(solution)/shard_map/ppermute | solution.py:513
  35.1 6.9 %collective-permute-start.7 = (f32[288,128]{1,0:T(8,128)S(1)}, f32[288,128]{1,0:T(8,128)S(1)}, u32[]{:S(2)}, u32[]{:S(2)}) collective-permute-start(f32[288,128]{1,0:T(8,128)S(1)} %add_add_fusion.1), channel_id=1, source_target_pairs={{0,1},{1,2},{2,3},{3,0},{4,5},{5,6},{6,7},{7,4},{8,9},{9,10},{10,1... | collective-permute-start | bytes 442376 | tf_op jit(solution)/shard_map/ppermute | solution.py:513
  35.9 6.8 %collective-permute-start.8 = (f32[288,128]{1,0:T(8,128)S(1)}, f32[288,128]{1,0:T(8,128)S(1)}, u32[]{:S(2)}, u32[]{:S(2)}) collective-permute-start(f32[288,128]{1,0:T(8,128)S(1)} %add_add_fusion.1), channel_id=1, source_target_pairs={{0,3},{1,0},{2,1},{3,2},{4,7},{5,4},{6,5},{7,6},{8,11},{9,8},{10,9... | collective-permute-start | bytes 442376 | tf_op jit(solution)/shard_map/ppermute | solution.py:513
  37.8 15.3 %collective-permute-start.16 = (f32[2,144,128]{2,1,0:T(8,128)S(1)}, f32[2,144,128]{2,1,0:T(8,128)S(1)}, u32[]{:S(2)}, u32[]{:S(2)}) collective-permute-start(f32[2,144,128]{2,1,0:T(8,128)S(1)} %maximum_select_fusion.2), channel_id=1, source_target_pairs={{0,2},{1,3},{2,0},{3,1},{4,6},{5,7},{6,4},{7,5},{8,10},{9,11},{10,... | collective-permute-start | bytes 442376 | tf_op jit(solution)/shard_map/ppermute | solution.py:550
  42.8 4.8 %collective-permute-start.9 = (f32[1,128]{1,0:T(1,128)S(1)}, f32[1,128]{1,0:T(1,128)S(1)}, u32[]{:S(2)}, u32[]{:S(2)}) collective-permute-start(f32[1,128]{1,0:T(1,128)S(1)} %bitcast.31), channel_id=1, source_target_pairs={{0,64},{64,0},{1,65},{65,1},{2,66},{66,2},{3,67},{67,3},{4,68},{68... | collective-permute-start | bytes 1544 | tf_op jit(solution)/shard_map/ppermute | solution.py:561
  47.5 5.6 %collective-permute-start.10 = (f32[1,128]{1,0:T(1,128)S(1)}, f32[1,128]{1,0:T(1,128)S(1)}, u32[]{:S(2)}, u32[]{:S(2)}) collective-permute-start(f32[1,128]{1,0:T(1,128)S(1)} %bitcast_add_fusion), channel_id=1, source_target_pairs={{0,32},{1,33},{2,34},{3,35},{4,36},{5,37},{6,38},{7,39},{8,40},{9,... | collective-permute-start | bytes 1544 | tf_op jit(solution)/shard_map/ppermute | solution.py:513
  50.4 3.6 %collective-permute-start.11 = (f32[1,128]{1,0:T(1,128)S(1)}, f32[1,128]{1,0:T(1,128)S(1)}, u32[]{:S(2)}, u32[]{:S(2)}) collective-permute-start(f32[1,128]{1,0:T(1,128)S(1)} %bitcast_add_fusion), channel_id=1, source_target_pairs={{0,16},{1,17},{2,18},{3,19},{4,20},{5,21},{6,22},{7,23},{8,24},{9,... | collective-permute-start | bytes 1544 | tf_op jit(solution)/shard_map/ppermute | solution.py:513
  50.8 3.2 %collective-permute-start.12 = (f32[1,128]{1,0:T(1,128)S(1)}, f32[1,128]{1,0:T(1,128)S(1)}, u32[]{:S(2)}, u32[]{:S(2)}) collective-permute-start(f32[1,128]{1,0:T(1,128)S(1)} %bitcast_add_fusion), channel_id=1, source_target_pairs={{0,48},{1,49},{2,50},{3,51},{4,52},{5,53},{6,54},{7,55},{8,56},{9,... | collective-permute-start | bytes 1544 | tf_op jit(solution)/shard_map/ppermute | solution.py:513
  54.5 12.2 %copy-start.5 = (bf16[128,4]{0,1:T(4,128)(2,1)S(1)}, bf16[128,4]{0,1:T(4,128)(2,1)}, u32[]{:S(2)}) copy-start(bf16[128,4]{0,1:T(4,128)(2,1)} %param.20) | copy-start | bytes 3076
  54.5 12.2 %copy-start.4 = (bf16[64,10,10,128]{3,0,2,1:T(8,128)(2,1)S(1)}, bf16[64,10,10,128]{3,0,2,1:T(8,128)(2,1)}, u32[]{:S(2)}) copy-start(bf16[64,10,10,128]{3,0,2,1:T(8,128)(2,1)} %param.12) | copy-start | bytes 4915204
  54.5 5.3 %collective-permute-start.17 = (f32[288,128]{1,0:T(8,128)S(1)}, f32[288,128]{1,0:T(8,128)S(1)}, u32[]{:S(2)}, u32[]{:S(2)}) collective-permute-start(f32[288,128]{1,0:T(8,128)S(1)} %update.1), channel_id=1, source_target_pairs={{0,16},{1,17},{2,18},{3,19},{4,20},{5,21},{6,22},{7,23},{8,24},{9,... | collective-permute-start | bytes 442376 | tf_op jit(solution)/shard_map/ppermute | solution.py:513
  54.6 8.6 %collective-permute-start.18 = (f32[288,128]{1,0:T(8,128)S(1)}, f32[288,128]{1,0:T(8,128)S(1)}, u32[]{:S(2)}, u32[]{:S(2)}) collective-permute-start(f32[288,128]{1,0:T(8,128)S(1)} %update.1), channel_id=1, source_target_pairs={{0,32},{1,33},{2,34},{3,35},{4,36},{5,37},{6,38},{7,39},{8,40},{9,... | collective-permute-start | bytes 442376 | tf_op jit(solution)/shard_map/ppermute | solution.py:513
  58.4 5.4 %collective-permute-start.19 = (f32[288,128]{1,0:T(8,128)S(1)}, f32[288,128]{1,0:T(8,128)S(1)}, u32[]{:S(2)}, u32[]{:S(2)}) collective-permute-start(f32[288,128]{1,0:T(8,128)S(1)} %update.1), channel_id=1, source_target_pairs={{0,48},{1,49},{2,50},{3,51},{4,52},{5,53},{6,54},{7,55},{8,56},{9,... | collective-permute-start | bytes 442376 | tf_op jit(solution)/shard_map/ppermute | solution.py:513
  63.9 4.5 %collective-permute-start.20 = (f32[4,288,128]{2,1,0:T(8,128)S(1)}, f32[4,288,128]{2,1,0:T(8,128)S(1)}, u32[]{:S(2)}, u32[]{:S(2)}) collective-permute-start(f32[4,288,128]{2,1,0:T(8,128)S(1)} %bitcast_dynamic-update-slice_fusion.mine), channel_id=1, source_target_pairs={{0,64},{64,0},{1,65},{65,1},{2,66},{66,2},{3,67},{67,3},{4,68},{68... | collective-permute-start | bytes 1769480 | tf_op jit(solution)/shard_map/ppermute | solution.py:561
  72.1 1.4 %collective-permute-start.21 = (f32[32,400]{1,0:T(8,128)S(1)}, f32[32,400]{1,0:T(8,128)S(1)}, u32[]{:S(2)}, u32[]{:S(2)}) collective-permute-start(f32[32,400]{1,0:T(8,128)S(1)} %act.1), channel_id=1, source_target_pairs={{0,64},{64,0},{1,65},{65,1},{2,66},{66,2},{3,67},{67,3},{4,68},{68... | collective-permute-start | bytes 153608 | tf_op jit(solution)/shard_map/ppermute | solution.py:561

commit v12 on v11

--- a/solution.py
+++ b/solution.py
@@ -591,7 +591,6 @@
     )
     own, moments = pull(own, first_moment, second_moment)
     next2 = shifted(next2, "y", 2)
-    next2, moments = lax.optimization_barrier((next2, moments))
     moments = moments_along_x(moments, role, x)
     moments = moments_along_z(moments, z)
     summed = (own + next2) + (shifted(next1, "y", 1) + shifted(next3, "y", 3))

time: 74.3 us -> 71.1 us (0.957)
  waiting for transfers between devices: 17.5 us -> 15.6 us
  starting transfers between devices: 40.9 us -> 39.7 us
    ppermute x15, waiting for transfers between devices: 15.2 us -> 13.3 us  [shifted(): return lax.ppermute(x, 'dp', pairs)]
    ppermute x1, starting transfers between devices: 4.75 us -> 3.92 us  [moments_along_x(): next_to = lax.ppermute(own, ('role', 'dp'), next_to)]
    ppermute x15, starting transfers between devices: 25.8 us -> 25 us  [shifted(): return lax.ppermute(x, 'dp', pairs)]
  transfers between devices with their start and end apart: 22 -> 22, of which waited for: 11 -> 12; matrix products, arithmetic and copies ran while one was open for 1% -> 1% of each run, Pallas kernels for 1% -> 1%
where the time goes in v12:
time: 71.1 us; the launch traced here: 70.9 us
  starting transfers between devices  39.7 us (56%)
  waiting for transfers between devices  15.6 us (22%)
  Pallas kernels  11.6 us (16%)
  other arithmetic  1.52 us (2%)
  between operations  1.47 us (2%)
  local copies, waits for them, and re-layouts  1.04 us (1%)
    ppermute x15, starting transfers between devices, shifted(): return lax.ppermute(x, 'dp', pairs)  25 us
    ppermute x15, waiting for transfers between devices, shifted(): return lax.ppermute(x, 'dp', pairs)  13.3 us
    ppermute x3, starting transfers between devices, role_swap(): return lax.ppermute(x, 'role', [(0, 1), (1, 0)])  7.65 us
    pallas_call x1, Pallas kernels, learn(): pl.pallas_call(functools.partial(learner_kernel, count), out_shape=[jax.S...  6.86 us
    ppermute x1, starting transfers between devices, moments_along_x(): next_to = lax.ppermute(own, ('role', 'dp'), next_to)  3.92 us
    pallas_call x1, Pallas kernels, act(): pl.pallas_call(functools.partial(actor_kernel, count, unroll), out_shape=...  3.71 us
    ppermute x3, waiting for transfers between devices, role_swap(): return lax.ppermute(x, 'role', [(0, 1), (1, 0)])  2.29 us
    ppermute x2, starting transfers between devices, swapped_z(): return lax.ppermute(x, 'dp', [(d, d ^ bit) for d in range(LINE ** 3)])  1.81 us
  transfers between devices with their start and end apart: 22, of which 12 were waited for; matrix products, arithmetic and copies ran while one was open for 1% of the time, Pallas kernels for 1%

profile of v12, /device:TPU:1, one launch (start us, length us, event | category | flops | bytes accessed | tf_op | source)
XLA Modules:
  0.0 70.9 jit_solution(8233647286694588459)
XLA Ops:
  1.3 6.9 %learn.1 = (f32[288,128]{1,0:T(8,128)}, f32[288,128]{1,0:T(8,128)}, f32[288,128]{1,0:T(8,128)}, f32[288,128]{1,0:T(8,128)}) custom-call(s32[1]{0:T(128)S(6)} %copy.18.length_in, bf16[10,10,16,128]{3,2,1,0:T(8,128)(2,1)} %bitcast.32, s32[1,16]{1,0:T(1,128)} %actions_in.1, f32[1,16]{1,0:T(1,128)} %behaviour_in.1, f32[1,16]{1,0:T(1,128)} %regular_in.1, ...), custom_call_target="tpu_custom_call" | custom-call | flops 4000000000 | bytes 3000000 | tf_op jit(solution)/shard_map/learn/pallas_call | solution.py:411
  8.2 3.8 %collective-permute-start = (f32[288,128]{1,0:T(8,128)}, f32[288,128]{1,0:T(8,128)S(1)}, u32[]{:S(2)}, u32[]{:S(2)}) collective-permute-start(f32[288,128]{1,0:T(8,128)} %get-tuple-element.12), channel_id=1, source_target_pairs={{0,32},{1,33},{2,34},{3,35},{4,36},{5,37},{6,38},{7,39},{8,40},{9,... | collective-permute-start | bytes 442376 | tf_op jit(solution)/shard_map/ppermute | solution.py:513
  12.4 2.3 %collective-permute-start.2 = (f32[288,128]{1,0:T(8,128)}, f32[288,128]{1,0:T(8,128)S(1)}, u32[]{:S(2)}, u32[]{:S(2)}) collective-permute-start(f32[288,128]{1,0:T(8,128)} %get-tuple-element.14), channel_id=1, source_target_pairs={{0,48},{1,49},{2,50},{3,51},{4,52},{5,53},{6,54},{7,55},{8,56},{9,... | collective-permute-start | bytes 442376 | tf_op jit(solution)/shard_map/ppermute | solution.py:513
  14.7 0.9 %copy-done.1 = f32[288,128]{1,0:T(8,128)S(1)} copy-done((f32[288,128]{1,0:T(8,128)S(1)}, f32[288,128]{1,0:T(8,128)}, u32[]{:S(2)}) %copy-start.1) | copy-done | bytes 147480
  15.8 1.3 %collective-permute-start.13 = (f32[72,128]{1,0:T(8,128)S(1)}, f32[72,128]{1,0:T(8,128)S(1)}, u32[]{:S(2)}, u32[]{:S(2)}) collective-permute-start(f32[72,128]{1,0:T(8,128)S(1)} %get-tuple-element.15), channel_id=1, source_target_pairs={{0,8},{4,12},{72,64},{76,68},{1,9},{5,13},{73,65},{77,69},{2,10},{... | collective-permute-start | bytes 110600 | tf_op jit(solution)/shard_map/ppermute | solution.py:543
  17.1 3.9 %collective-permute-start.14 = (f32[72,128]{1,0:T(8,128)S(1)}, f32[72,128]{1,0:T(8,128)S(1)}, u32[]{:S(2)}, u32[]{:S(2)}) collective-permute-start(f32[72,128]{1,0:T(8,128)S(1)} %get-tuple-element.15), channel_id=1, source_target_pairs={{4,0},{0,4},{68,8},{64,12},{12,64},{8,68},{76,72},{72,76},{5,1},{1... | collective-permute-start | bytes 110600 | tf_op jit(solution)/shard_map/ppermute | solution.py:544
  21.1 1.6 %collective-permute-start.3 = (f32[288,128]{1,0:T(8,128)S(1)}, f32[288,128]{1,0:T(8,128)S(1)}, u32[]{:S(2)}, u32[]{:S(2)}) collective-permute-start(f32[288,128]{1,0:T(8,128)S(1)} %add_add_fusion.2), channel_id=1, source_target_pairs={{0,8},{1,9},{2,10},{3,11},{4,12},{5,13},{6,14},{7,15},{8,0},{9,1},... | collective-permute-start | bytes 442376 | tf_op jit(solution)/shard_map/ppermute | solution.py:513
  22.7 2.7 %collective-permute-start.5 = (f32[288,128]{1,0:T(8,128)S(1)}, f32[288,128]{1,0:T(8,128)S(1)}, u32[]{:S(2)}, u32[]{:S(2)}) collective-permute-start(f32[288,128]{1,0:T(8,128)S(1)} %add_add_fusion.2), channel_id=1, source_target_pairs={{0,12},{1,13},{2,14},{3,15},{4,0},{5,1},{6,2},{7,3},{8,4},{9,5},{1... | collective-permute-start | bytes 442376 | tf_op jit(solution)/shard_map/ppermute | solution.py:513
  25.4 1.7 %collective-permute-start.15 = (f32[144,128]{1,0:T(8,128)S(1)}, f32[144,128]{1,0:T(8,128)S(1)}, u32[]{:S(2)}, u32[]{:S(2)}) collective-permute-start(f32[144,128]{1,0:T(8,128)S(1)} %get-tuple-element.25), channel_id=1, source_target_pairs={{0,1},{1,0},{2,3},{3,2},{4,5},{5,4},{6,7},{7,6},{8,9},{9,8},{10,11... | collective-permute-start | bytes 221192 | tf_op jit(solution)/shard_map/ppermute | solution.py:550
  27.2 3.4 %collective-permute-done.4 = f32[288,128]{1,0:T(8,128)S(1)} collective-permute-done((f32[288,128]{1,0:T(8,128)S(1)}, f32[288,128]{1,0:T(8,128)S(1)}, u32[]{:S(2)}, u32[]{:S(2)}) %collective-permute-start.4) | collective-permute-done | bytes 147488 | tf_op jit(solution)/shard_map/ppermute | solution.py:513
  30.6 3.7 %collective-permute-start.6 = (f32[288,128]{1,0:T(8,128)S(1)}, f32[288,128]{1,0:T(8,128)S(1)}, u32[]{:S(2)}, u32[]{:S(2)}) collective-permute-start(f32[288,128]{1,0:T(8,128)S(1)} %add_add_fusion.1), channel_id=1, source_target_pairs={{0,2},{1,3},{2,0},{3,1},{4,6},{5,7},{6,4},{7,5},{8,10},{9,11},{10,... | collective-permute-start | bytes 442376 | tf_op jit(solution)/shard_map/ppermute | solution.py:513
  34.3 0.7 %collective-permute-start.7 = (f32[288,128]{1,0:T(8,128)S(1)}, f32[288,128]{1,0:T(8,128)S(1)}, u32[]{:S(2)}, u32[]{:S(2)}) collective-permute-start(f32[288,128]{1,0:T(8,128)S(1)} %add_add_fusion.1), channel_id=1, source_target_pairs={{0,1},{1,2},{2,3},{3,0},{4,5},{5,6},{6,7},{7,4},{8,9},{9,10},{10,1... | collective-permute-start | bytes 442376 | tf_op jit(solution)/shard_map/ppermute | solution.py:513
  35.0 1.9 %collective-permute-start.8 = (f32[288,128]{1,0:T(8,128)S(1)}, f32[288,128]{1,0:T(8,128)S(1)}, u32[]{:S(2)}, u32[]{:S(2)}) collective-permute-start(f32[288,128]{1,0:T(8,128)S(1)} %add_add_fusion.1), channel_id=1, source_target_pairs={{0,3},{1,0},{2,1},{3,2},{4,7},{5,4},{6,5},{7,6},{8,11},{9,8},{10,9... | collective-permute-start | bytes 442376 | tf_op jit(solution)/shard_map/ppermute | solution.py:513
  37.1 4.1 %collective-permute-done.7 = f32[288,128]{1,0:T(8,128)S(1)} collective-permute-done((f32[288,128]{1,0:T(8,128)S(1)}, f32[288,128]{1,0:T(8,128)S(1)}, u32[]{:S(2)}, u32[]{:S(2)}) %collective-permute-start.7) | collective-permute-done | bytes 147488 | tf_op jit(solution)/shard_map/ppermute | solution.py:513
  41.2 0.6 collective-permute-done.8
  41.9 4.0 %collective-permute-start.9 = (f32[1,128]{1,0:T(1,128)S(1)}, f32[1,128]{1,0:T(1,128)S(1)}, u32[]{:S(2)}, u32[]{:S(2)}) collective-permute-start(f32[1,128]{1,0:T(1,128)S(1)} %bitcast.31), channel_id=1, source_target_pairs={{0,64},{64,0},{1,65},{65,1},{2,66},{66,2},{3,67},{67,3},{4,68},{68... | collective-permute-start | bytes 1544 | tf_op jit(solution)/shard_map/ppermute | solution.py:561
  45.9 0.8 %collective-permute-done.9 = f32[1,128]{1,0:T(1,128)S(1)} collective-permute-done((f32[1,128]{1,0:T(1,128)S(1)}, f32[1,128]{1,0:T(1,128)S(1)}, u32[]{:S(2)}, u32[]{:S(2)}) %collective-permute-start.9) | collective-permute-done | bytes 544 | tf_op jit(solution)/shard_map/ppermute | solution.py:561
  46.7 0.5 collective-permute-start.10
  47.2 1.4 %collective-permute-start.11 = (f32[1,128]{1,0:T(1,128)S(1)}, f32[1,128]{1,0:T(1,128)S(1)}, u32[]{:S(2)}, u32[]{:S(2)}) collective-permute-start(f32[1,128]{1,0:T(1,128)S(1)} %bitcast_add_fusion), channel_id=1, source_target_pairs={{0,16},{1,17},{2,18},{3,19},{4,20},{5,21},{6,22},{7,23},{8,24},{9,... | collective-permute-start | bytes 1544 | tf_op jit(solution)/shard_map/ppermute | solution.py:513
  48.6 1.3 %collective-permute-start.12 = (f32[1,128]{1,0:T(1,128)S(1)}, f32[1,128]{1,0:T(1,128)S(1)}, u32[]{:S(2)}, u32[]{:S(2)}) collective-permute-start(f32[1,128]{1,0:T(1,128)S(1)} %bitcast_add_fusion), channel_id=1, source_target_pairs={{0,48},{1,49},{2,50},{3,51},{4,52},{5,53},{6,54},{7,55},{8,56},{9,... | collective-permute-start | bytes 1544 | tf_op jit(solution)/shard_map/ppermute | solution.py:513
  50.0 0.6 collective-permute-done.10
  51.5 0.8 %collective-permute-start.17 = (f32[288,128]{1,0:T(8,128)S(1)}, f32[288,128]{1,0:T(8,128)S(1)}, u32[]{:S(2)}, u32[]{:S(2)}) collective-permute-start(f32[288,128]{1,0:T(8,128)S(1)} %update.1), channel_id=1, source_target_pairs={{0,16},{1,17},{2,18},{3,19},{4,20},{5,21},{6,22},{7,23},{8,24},{9,... | collective-permute-start | bytes 442376 | tf_op jit(solution)/shard_map/ppermute | solution.py:513
  52.2 3.0 %collective-permute-start.18 = (f32[288,128]{1,0:T(8,128)S(1)}, f32[288,128]{1,0:T(8,128)S(1)}, u32[]{:S(2)}, u32[]{:S(2)}) collective-permute-start(f32[288,128]{1,0:T(8,128)S(1)} %update.1), channel_id=1, source_target_pairs={{0,32},{1,33},{2,34},{3,35},{4,36},{5,37},{6,38},{7,39},{8,40},{9,... | collective-permute-start | bytes 442376 | tf_op jit(solution)/shard_map/ppermute | solution.py:513
  55.2 0.9 %collective-permute-start.19 = (f32[288,128]{1,0:T(8,128)S(1)}, f32[288,128]{1,0:T(8,128)S(1)}, u32[]{:S(2)}, u32[]{:S(2)}) collective-permute-start(f32[288,128]{1,0:T(8,128)S(1)} %update.1), channel_id=1, source_target_pairs={{0,48},{1,49},{2,50},{3,51},{4,52},{5,53},{6,54},{7,55},{8,56},{9,... | collective-permute-start | bytes 442376 | tf_op jit(solution)/shard_map/ppermute | solution.py:513
  56.2 0.6 collective-permute-done.17
  56.8 3.2 %collective-permute-done.18 = f32[288,128]{1,0:T(8,128)S(1)} collective-permute-done((f32[288,128]{1,0:T(8,128)S(1)}, f32[288,128]{1,0:T(8,128)S(1)}, u32[]{:S(2)}, u32[]{:S(2)}) %collective-permute-start.18) | collective-permute-done | bytes 147488 | tf_op jit(solution)/shard_map/ppermute | solution.py:513
  60.3 3.2 %collective-permute-start.20 = (f32[4,288,128]{2,1,0:T(8,128)S(1)}, f32[4,288,128]{2,1,0:T(8,128)S(1)}, u32[]{:S(2)}, u32[]{:S(2)}) collective-permute-start(f32[4,288,128]{2,1,0:T(8,128)S(1)} %bitcast_dynamic-update-slice_fusion.mine), channel_id=1, source_target_pairs={{0,64},{64,0},{1,65},{65,1},{2,66},{66,2},{3,67},{67,3},{4,68},{68... | collective-permute-start | bytes 1769480 | tf_op jit(solution)/shard_map/ppermute | solution.py:561
  63.9 1.2 %collective-permute-done.20.other = f32[4,288,128]{2,1,0:T(8,128)S(1)} collective-permute-done((f32[4,288,128]{2,1,0:T(8,128)S(1)}, f32[4,288,128]{2,1,0:T(8,128)S(1)}, u32[]{:S(2)}, u32[]{:S(2)}) %collective-permute-start.20) | collective-permute-done | bytes 589856 | tf_op jit(solution)/shard_map/ppermute | solution.py:561
  65.1 3.7 %act.1 = f32[32,400]{1,0:T(8,128)S(1)} custom-call(f32[4,288,128]{2,1,0:T(8,128)S(1)} %bitcast_dynamic-update-slice_fusion.mine, f32[4,288,128]{2,1,0:T(8,128)S(1)} %collective-permute-done.20.other, bf16[12,6,2,32,128]{4,3,2,1,0:T(8,128)(2,1)S(1)} %get-tuple-element.16.boards, bf16[1280,128]{1,0:T(8,128)(2,1)S(1)} %get-tuple-element.17.heads), custom_call_target="tpu_custom_call" | custom-call | flops 8000000000 | bytes 4000000 | tf_op jit(solution)/shard_map/act/pallas_call | solution.py:183
  68.9 0.5 collective-permute-start.21
  69.3 0.6 select_bitcast_fusion
  70.2 0.7 pad_maximum_fusion
  (48 shorter events, 2.9 us)
Async XLA Ops:
  1.3 13.4 %copy-start.2 = (f32[36,128]{1,0:T(8,128)S(1)}, f32[36,128]{1,0:T(8,128)}, u32[]{:S(2)}) copy-start(f32[36,128]{1,0:T(8,128)} %first_in.1) | copy-start | bytes 55300
  1.3 13.4 %copy-start.3 = (f32[36,128]{1,0:T(8,128)S(1)}, f32[36,128]{1,0:T(8,128)}, u32[]{:S(2)}) copy-start(f32[36,128]{1,0:T(8,128)} %second_in.1) | copy-start | bytes 55300
  8.2 12.9 %collective-permute-start = (f32[288,128]{1,0:T(8,128)}, f32[288,128]{1,0:T(8,128)S(1)}, u32[]{:S(2)}, u32[]{:S(2)}) collective-permute-start(f32[288,128]{1,0:T(8,128)} %get-tuple-element.12), channel_id=1, source_target_pairs={{0,32},{1,33},{2,34},{3,35},{4,36},{5,37},{6,38},{7,39},{8,40},{9,... | collective-permute-start | bytes 442376 | tf_op jit(solution)/shard_map/ppermute | solution.py:513
  12.0 9.1 %collective-permute-start.1 = (f32[288,128]{1,0:T(8,128)}, f32[288,128]{1,0:T(8,128)S(1)}, u32[]{:S(2)}, u32[]{:S(2)}) collective-permute-start(f32[288,128]{1,0:T(8,128)} %get-tuple-element.13), channel_id=1, source_target_pairs={{0,16},{1,17},{2,18},{3,19},{4,20},{5,21},{6,22},{7,23},{8,24},{9,... | collective-permute-start | bytes 442376 | tf_op jit(solution)/shard_map/ppermute | solution.py:513
  12.4 8.7 %collective-permute-start.2 = (f32[288,128]{1,0:T(8,128)}, f32[288,128]{1,0:T(8,128)S(1)}, u32[]{:S(2)}, u32[]{:S(2)}) collective-permute-start(f32[288,128]{1,0:T(8,128)} %get-tuple-element.14), channel_id=1, source_target_pairs={{0,48},{1,49},{2,50},{3,51},{4,52},{5,53},{6,54},{7,55},{8,56},{9,... | collective-permute-start | bytes 442376 | tf_op jit(solution)/shard_map/ppermute | solution.py:513
  14.7 0.9 %copy-start.1 = (f32[288,128]{1,0:T(8,128)S(1)}, f32[288,128]{1,0:T(8,128)}, u32[]{:S(2)}) copy-start(f32[288,128]{1,0:T(8,128)} %get-tuple-element.10.own_in) | copy-start | bytes 442372
  15.8 9.6 %collective-permute-start.13 = (f32[72,128]{1,0:T(8,128)S(1)}, f32[72,128]{1,0:T(8,128)S(1)}, u32[]{:S(2)}, u32[]{:S(2)}) collective-permute-start(f32[72,128]{1,0:T(8,128)S(1)} %get-tuple-element.15), channel_id=1, source_target_pairs={{0,8},{4,12},{72,64},{76,68},{1,9},{5,13},{73,65},{77,69},{2,10},{... | collective-permute-start | bytes 110600 | tf_op jit(solution)/shard_map/ppermute | solution.py:543
  17.1 8.3 %collective-permute-start.14 = (f32[72,128]{1,0:T(8,128)S(1)}, f32[72,128]{1,0:T(8,128)S(1)}, u32[]{:S(2)}, u32[]{:S(2)}) collective-permute-start(f32[72,128]{1,0:T(8,128)S(1)} %get-tuple-element.15), channel_id=1, source_target_pairs={{4,0},{0,4},{68,8},{64,12},{12,64},{8,68},{76,72},{72,76},{5,1},{1... | collective-permute-start | bytes 110600 | tf_op jit(solution)/shard_map/ppermute | solution.py:544
  21.1 6.1 %collective-permute-start.3 = (f32[288,128]{1,0:T(8,128)S(1)}, f32[288,128]{1,0:T(8,128)S(1)}, u32[]{:S(2)}, u32[]{:S(2)}) collective-permute-start(f32[288,128]{1,0:T(8,128)S(1)} %add_add_fusion.2), channel_id=1, source_target_pairs={{0,8},{1,9},{2,10},{3,11},{4,12},{5,13},{6,14},{7,15},{8,0},{9,1},... | collective-permute-start | bytes 442376 | tf_op jit(solution)/shard_map/ppermute | solution.py:513
  22.7 7.8 %collective-permute-start.4 = (f32[288,128]{1,0:T(8,128)S(1)}, f32[288,128]{1,0:T(8,128)S(1)}, u32[]{:S(2)}, u32[]{:S(2)}) collective-permute-start(f32[288,128]{1,0:T(8,128)S(1)} %add_add_fusion.2), channel_id=1, source_target_pairs={{0,4},{1,5},{2,6},{3,7},{4,8},{5,9},{6,10},{7,11},{8,12},{9,13},{1... | collective-permute-start | bytes 442376 | tf_op jit(solution)/shard_map/ppermute | solution.py:513
  22.7 7.8 %collective-permute-start.5 = (f32[288,128]{1,0:T(8,128)S(1)}, f32[288,128]{1,0:T(8,128)S(1)}, u32[]{:S(2)}, u32[]{:S(2)}) collective-permute-start(f32[288,128]{1,0:T(8,128)S(1)} %add_add_fusion.2), channel_id=1, source_target_pairs={{0,12},{1,13},{2,14},{3,15},{4,0},{5,1},{6,2},{7,3},{8,4},{9,5},{1... | collective-permute-start | bytes 442376 | tf_op jit(solution)/shard_map/ppermute | solution.py:513
  25.4 11.5 %collective-permute-start.15 = (f32[144,128]{1,0:T(8,128)S(1)}, f32[144,128]{1,0:T(8,128)S(1)}, u32[]{:S(2)}, u32[]{:S(2)}) collective-permute-start(f32[144,128]{1,0:T(8,128)S(1)} %get-tuple-element.25), channel_id=1, source_target_pairs={{0,1},{1,0},{2,3},{3,2},{4,5},{5,4},{6,7},{7,6},{8,9},{9,8},{10,11... | collective-permute-start | bytes 221192 | tf_op jit(solution)/shard_map/ppermute | solution.py:550
  30.6 20.4 %copy-start = (f32[2304,128]{1,0:T(8,128)S(1)}, f32[2304,128]{1,0:T(8,128)}, u32[]{:S(2)}) copy-start(f32[2304,128]{1,0:T(8,128)} %torso_in.1) | copy-start | bytes 3538948
  30.6 6.5 %collective-permute-start.6 = (f32[288,128]{1,0:T(8,128)S(1)}, f32[288,128]{1,0:T(8,128)S(1)}, u32[]{:S(2)}, u32[]{:S(2)}) collective-permute-start(f32[288,128]{1,0:T(8,128)S(1)} %add_add_fusion.1), channel_id=1, source_target_pairs={{0,2},{1,3},{2,0},{3,1},{4,6},{5,7},{6,4},{7,5},{8,10},{9,11},{10,... | collective-permute-start | bytes 442376 | tf_op jit(solution)/shard_map/ppermute | solution.py:513
  34.3 6.9 %collective-permute-start.7 = (f32[288,128]{1,0:T(8,128)S(1)}, f32[288,128]{1,0:T(8,128)S(1)}, u32[]{:S(2)}, u32[]{:S(2)}) collective-permute-start(f32[288,128]{1,0:T(8,128)S(1)} %add_add_fusion.1), channel_id=1, source_target_pairs={{0,1},{1,2},{2,3},{3,0},{4,5},{5,6},{6,7},{7,4},{8,9},{9,10},{10,1... | collective-permute-start | bytes 442376 | tf_op jit(solution)/shard_map/ppermute | solution.py:513
  35.0 6.8 %collective-permute-start.8 = (f32[288,128]{1,0:T(8,128)S(1)}, f32[288,128]{1,0:T(8,128)S(1)}, u32[]{:S(2)}, u32[]{:S(2)}) collective-permute-start(f32[288,128]{1,0:T(8,128)S(1)} %add_add_fusion.1), channel_id=1, source_target_pairs={{0,3},{1,0},{2,1},{3,2},{4,7},{5,4},{6,5},{7,6},{8,11},{9,8},{10,9... | collective-permute-start | bytes 442376 | tf_op jit(solution)/shard_map/ppermute | solution.py:513
  37.0 12.9 %collective-permute-start.16 = (f32[2,144,128]{2,1,0:T(8,128)S(1)}, f32[2,144,128]{2,1,0:T(8,128)S(1)}, u32[]{:S(2)}, u32[]{:S(2)}) collective-permute-start(f32[2,144,128]{2,1,0:T(8,128)S(1)} %maximum_select_fusion.2), channel_id=1, source_target_pairs={{0,2},{1,3},{2,0},{3,1},{4,6},{5,7},{6,4},{7,5},{8,10},{9,11},{10,... | collective-permute-start | bytes 442376 | tf_op jit(solution)/shard_map/ppermute | solution.py:550
  41.9 4.8 %collective-permute-start.9 = (f32[1,128]{1,0:T(1,128)S(1)}, f32[1,128]{1,0:T(1,128)S(1)}, u32[]{:S(2)}, u32[]{:S(2)}) collective-permute-start(f32[1,128]{1,0:T(1,128)S(1)} %bitcast.31), channel_id=1, source_target_pairs={{0,64},{64,0},{1,65},{65,1},{2,66},{66,2},{3,67},{67,3},{4,68},{68... | collective-permute-start | bytes 1544 | tf_op jit(solution)/shard_map/ppermute | solution.py:561
  46.7 3.9 %collective-permute-start.10 = (f32[1,128]{1,0:T(1,128)S(1)}, f32[1,128]{1,0:T(1,128)S(1)}, u32[]{:S(2)}, u32[]{:S(2)}) collective-permute-start(f32[1,128]{1,0:T(1,128)S(1)} %bitcast_add_fusion), channel_id=1, source_target_pairs={{0,32},{1,33},{2,34},{3,35},{4,36},{5,37},{6,38},{7,39},{8,40},{9,... | collective-permute-start | bytes 1544 | tf_op jit(solution)/shard_map/ppermute | solution.py:513
  47.2 3.6 %collective-permute-start.11 = (f32[1,128]{1,0:T(1,128)S(1)}, f32[1,128]{1,0:T(1,128)S(1)}, u32[]{:S(2)}, u32[]{:S(2)}) collective-permute-start(f32[1,128]{1,0:T(1,128)S(1)} %bitcast_add_fusion), channel_id=1, source_target_pairs={{0,16},{1,17},{2,18},{3,19},{4,20},{5,21},{6,22},{7,23},{8,24},{9,... | collective-permute-start | bytes 1544 | tf_op jit(solution)/shard_map/ppermute | solution.py:513
  48.6 2.4 %collective-permute-start.12 = (f32[1,128]{1,0:T(1,128)S(1)}, f32[1,128]{1,0:T(1,128)S(1)}, u32[]{:S(2)}, u32[]{:S(2)}) collective-permute-start(f32[1,128]{1,0:T(1,128)S(1)} %bitcast_add_fusion), channel_id=1, source_target_pairs={{0,48},{1,49},{2,50},{3,51},{4,52},{5,53},{6,54},{7,55},{8,56},{9,... | collective-permute-start | bytes 1544 | tf_op jit(solution)/shard_map/ppermute | solution.py:513
  51.5 12.0 %copy-start.5 = (bf16[128,4]{0,1:T(4,128)(2,1)S(1)}, bf16[128,4]{0,1:T(4,128)(2,1)}, u32[]{:S(2)}) copy-start(bf16[128,4]{0,1:T(4,128)(2,1)} %param.20) | copy-start | bytes 3076
  51.5 12.0 %copy-start.4 = (bf16[64,10,10,128]{3,0,2,1:T(8,128)(2,1)S(1)}, bf16[64,10,10,128]{3,0,2,1:T(8,128)(2,1)}, u32[]{:S(2)}) copy-start(bf16[64,10,10,128]{3,0,2,1:T(8,128)(2,1)} %param.12) | copy-start | bytes 4915204
  51.5 5.3 %collective-permute-start.17 = (f32[288,128]{1,0:T(8,128)S(1)}, f32[288,128]{1,0:T(8,128)S(1)}, u32[]{:S(2)}, u32[]{:S(2)}) collective-permute-start(f32[288,128]{1,0:T(8,128)S(1)} %update.1), channel_id=1, source_target_pairs={{0,16},{1,17},{2,18},{3,19},{4,20},{5,21},{6,22},{7,23},{8,24},{9,... | collective-permute-start | bytes 442376 | tf_op jit(solution)/shard_map/ppermute | solution.py:513
  52.2 7.7 %collective-permute-start.18 = (f32[288,128]{1,0:T(8,128)S(1)}, f32[288,128]{1,0:T(8,128)S(1)}, u32[]{:S(2)}, u32[]{:S(2)}) collective-permute-start(f32[288,128]{1,0:T(8,128)S(1)} %update.1), channel_id=1, source_target_pairs={{0,32},{1,33},{2,34},{3,35},{4,36},{5,37},{6,38},{7,39},{8,40},{9,... | collective-permute-start | bytes 442376 | tf_op jit(solution)/shard_map/ppermute | solution.py:513
  55.2 5.0 %collective-permute-start.19 = (f32[288,128]{1,0:T(8,128)S(1)}, f32[288,128]{1,0:T(8,128)S(1)}, u32[]{:S(2)}, u32[]{:S(2)}) collective-permute-start(f32[288,128]{1,0:T(8,128)S(1)} %update.1), channel_id=1, source_target_pairs={{0,48},{1,49},{2,50},{3,51},{4,52},{5,53},{6,54},{7,55},{8,56},{9,... | collective-permute-start | bytes 442376 | tf_op jit(solution)/shard_map/ppermute | solution.py:513
  60.3 4.9 %collective-permute-start.20 = (f32[4,288,128]{2,1,0:T(8,128)S(1)}, f32[4,288,128]{2,1,0:T(8,128)S(1)}, u32[]{:S(2)}, u32[]{:S(2)}) collective-permute-start(f32[4,288,128]{2,1,0:T(8,128)S(1)} %bitcast_dynamic-update-slice_fusion.mine), channel_id=1, source_target_pairs={{0,64},{64,0},{1,65},{65,1},{2,66},{66,2},{3,67},{67,3},{4,68},{68... | collective-permute-start | bytes 1769480 | tf_op jit(solution)/shard_map/ppermute | solution.py:561
  68.9 1.4 %collective-permute-start.21 = (f32[32,400]{1,0:T(8,128)S(1)}, f32[32,400]{1,0:T(8,128)S(1)}, u32[]{:S(2)}, u32[]{:S(2)}) collective-permute-start(f32[32,400]{1,0:T(8,128)S(1)} %act.1), channel_id=1, source_target_pairs={{0,64},{64,0},{1,65},{65,1},{2,66},{66,2},{3,67},{67,3},{4,68},{68... | collective-permute-start | bytes 153608 | tf_op jit(solution)/shard_map/ppermute | solution.py:561

commit v13 on v12

--- a/solution.py
+++ b/solution.py
@@ -551,10 +551,19 @@
 
 
 def moments_along_z(x, z):
-    near = swapped_z(x, 1)
-    pair = jnp.where(z % 2 == 0, jnp.stack([x, near]), jnp.stack([near, x]))
-    far = swapped_z(pair, 2)
-    return jnp.where(z < 2, jnp.concatenate([pair, far]), jnp.concatenate([far, pair]))
+    far = swapped_z(x, 2)
+    pair = jnp.where(z < 2, jnp.stack([x, far]), jnp.stack([far, x]))
+    near = swapped_z(pair, 1)
+    even = z % 2 == 0
+    return jnp.stack([jnp.where(even, pair, near), jnp.where(even, near, pair)], axis=1)
+
+
+def pair_total_y(x):
+    for partner in ((1, 0, 3, 2), (3, 2, 1, 0)):
+        plane = LINE * LINE
+        pairs = [(d, partner[d // plane] * plane + d % plane) for d in range(LINE**3)]
+        x = x + lax.ppermute(x, "dp", pairs)
+    return x
 
 
 def role_swap(x):
@@ -596,7 +605,7 @@
     summed = (own + next2) + (shifted(next1, "y", 1) + shifted(next3, "y", 3))
     summed = line_total(line_total(summed, "x"), "z")
     squares = jnp.sum(summed * summed, axis=0, keepdims=True)
-    squares = line_total(squares + role_swap(squares), "y")
+    squares = pair_total_y(squares + role_swap(squares))
     fresh = update(summed, squares, moments.reshape(LINE, 2, 2 * PIECE, 128), torso)
     mine = line_gather(fresh, "y", y)
     other = role_swap(mine)

time: 71.1 us -> 72.1 us (1.014)
  waiting for transfers between devices: 15.6 us -> 18.4 us
  starting transfers between devices: 39.7 us -> 37.9 us
    ppermute x0 -> x2, starting transfers between devices: none -> 4.27 us  [pair_total_y(): x = x + lax.ppermute(x, 'dp', pairs)]
    ppermute x15 -> x12, starting transfers between devices: 25 us -> 22.3 us  [shifted(): return lax.ppermute(x, 'dp', pairs)]
    ppermute x1, starting transfers between devices: 3.92 us -> 1.72 us  [moments_along_x(): next_to = lax.ppermute(own, ('role', 'dp'), next_to)]
    ppermute x2, waiting for transfers between devices: 0.01 us -> 2.02 us  [swapped_z(): return lax.ppermute(x, 'dp', [(d, d ^ bit) for d in range(LINE ** 3)])]
    ppermute x2, starting transfers between devices: 1.81 us -> 0.58 us  [swapped_z(): return lax.ppermute(x, 'dp', [(d, d ^ bit) for d in range(LINE ** 3)])]
    ppermute x0 -> x2, waiting for transfers between devices: none -> 0.95 us  [pair_total_y(): x = x + lax.ppermute(x, 'dp', pairs)]
    ppermute x15 -> x12, waiting for transfers between devices: 13.3 us -> 13.6 us  [shifted(): return lax.ppermute(x, 'dp', pairs)]
  transfers between devices with their start and end apart: 22 -> 21, of which waited for: 12 -> 12; matrix products, arithmetic and copies ran while one was open for 1% -> 1% of each run, Pallas kernels for 1% -> 1%
where the time goes in v13:
time: 72.1 us; the launch traced here: 72 us
  starting transfers between devices  37.9 us (53%)
  waiting for transfers between devices  18.4 us (26%)
  Pallas kernels  11.6 us (16%)
  other arithmetic  1.52 us (2%)
  between operations  1.49 us (2%)
  local copies, waits for them, and re-layouts  1.05 us (1%)
    ppermute x12, starting transfers between devices, shifted(): return lax.ppermute(x, 'dp', pairs)  22.3 us
    ppermute x12, waiting for transfers between devices, shifted(): return lax.ppermute(x, 'dp', pairs)  13.6 us
    ppermute x3, starting transfers between devices, role_swap(): return lax.ppermute(x, 'role', [(0, 1), (1, 0)])  7.81 us
    pallas_call x1, Pallas kernels, learn(): pl.pallas_call(functools.partial(learner_kernel, count), out_shape=[jax.S...  6.86 us
    ppermute x2, starting transfers between devices, pair_total_y(): x = x + lax.ppermute(x, 'dp', pairs)  4.27 us
    pallas_call x1, Pallas kernels, act(): pl.pallas_call(functools.partial(actor_kernel, count, unroll), out_shape=...  3.72 us
    ppermute x2, waiting for transfers between devices, swapped_z(): return lax.ppermute(x, 'dp', [(d, d ^ bit) for d in range(LINE ** 3)])  2.02 us
    ppermute x3, waiting for transfers between devices, role_swap(): return lax.ppermute(x, 'role', [(0, 1), (1, 0)])  1.79 us
  transfers between devices with their start and end apart: 21, of which 12 were waited for; matrix products, arithmetic and copies ran while one was open for 1% of the time, Pallas kernels for 1%

profile of v13, /device:TPU:1, one launch (start us, length us, event | category | flops | bytes accessed | tf_op | source)
XLA Modules:
  0.0 72.0 jit_solution(6873345259830489384)
XLA Ops:
  1.3 6.9 %learn.1 = (f32[288,128]{1,0:T(8,128)}, f32[288,128]{1,0:T(8,128)}, f32[288,128]{1,0:T(8,128)}, f32[288,128]{1,0:T(8,128)}) custom-call(s32[1]{0:T(128)S(6)} %copy.19.length_in, bf16[10,10,16,128]{3,2,1,0:T(8,128)(2,1)} %bitcast.33, s32[1,16]{1,0:T(1,128)} %actions_in.1, f32[1,16]{1,0:T(1,128)} %behaviour_in.1, f32[1,16]{1,0:T(1,128)} %regular_in.1, ...), custom_call_target="tpu_custom_call" | custom-call | flops 4000000000 | bytes 3000000 | tf_op jit(solution)/shard_map/learn/pallas_call | solution.py:411
  8.2 3.8 %collective-permute-start = (f32[288,128]{1,0:T(8,128)}, f32[288,128]{1,0:T(8,128)S(1)}, u32[]{:S(2)}, u32[]{:S(2)}) collective-permute-start(f32[288,128]{1,0:T(8,128)} %get-tuple-element.12), channel_id=1, source_target_pairs={{0,32},{1,33},{2,34},{3,35},{4,36},{5,37},{6,38},{7,39},{8,40},{9,... | collective-permute-start | bytes 442376 | tf_op jit(solution)/shard_map/ppermute | solution.py:513
  12.0 0.4 collective-permute-start.1
  12.4 2.3 %collective-permute-start.2 = (f32[288,128]{1,0:T(8,128)}, f32[288,128]{1,0:T(8,128)S(1)}, u32[]{:S(2)}, u32[]{:S(2)}) collective-permute-start(f32[288,128]{1,0:T(8,128)} %get-tuple-element.14), channel_id=1, source_target_pairs={{0,48},{1,49},{2,50},{3,51},{4,52},{5,53},{6,54},{7,55},{8,56},{9,... | collective-permute-start | bytes 442376 | tf_op jit(solution)/shard_map/ppermute | solution.py:513
  14.7 0.9 %copy-done.1 = f32[288,128]{1,0:T(8,128)S(1)} copy-done((f32[288,128]{1,0:T(8,128)S(1)}, f32[288,128]{1,0:T(8,128)}, u32[]{:S(2)}) %copy-start.1) | copy-done | bytes 147480
  15.8 3.5 %collective-permute-done.1 = f32[288,128]{1,0:T(8,128)S(1)} collective-permute-done((f32[288,128]{1,0:T(8,128)}, f32[288,128]{1,0:T(8,128)S(1)}, u32[]{:S(2)}, u32[]{:S(2)}) %collective-permute-start.1) | collective-permute-done | bytes 147488 | tf_op jit(solution)/shard_map/ppermute | solution.py:513
  19.4 2.9 %collective-permute-start.3 = (f32[288,128]{1,0:T(8,128)S(1)}, f32[288,128]{1,0:T(8,128)S(1)}, u32[]{:S(2)}, u32[]{:S(2)}) collective-permute-start(f32[288,128]{1,0:T(8,128)S(1)} %add_add_fusion.2), channel_id=1, source_target_pairs={{0,8},{1,9},{2,10},{3,11},{4,12},{5,13},{6,14},{7,15},{8,0},{9,1},... | collective-permute-start | bytes 442376 | tf_op jit(solution)/shard_map/ppermute | solution.py:513
  22.5 2.4 %collective-permute-start.5 = (f32[288,128]{1,0:T(8,128)S(1)}, f32[288,128]{1,0:T(8,128)S(1)}, u32[]{:S(2)}, u32[]{:S(2)}) collective-permute-start(f32[288,128]{1,0:T(8,128)S(1)} %add_add_fusion.2), channel_id=1, source_target_pairs={{0,12},{1,13},{2,14},{3,15},{4,0},{5,1},{6,2},{7,3},{8,4},{9,5},{1... | collective-permute-start | bytes 442376 | tf_op jit(solution)/shard_map/ppermute | solution.py:513
  24.9 1.3 %collective-permute-start.12 = (f32[72,128]{1,0:T(8,128)S(1)}, f32[72,128]{1,0:T(8,128)S(1)}, u32[]{:S(2)}, u32[]{:S(2)}) collective-permute-start(f32[72,128]{1,0:T(8,128)S(1)} %get-tuple-element.15), channel_id=1, source_target_pairs={{0,8},{4,12},{72,64},{76,68},{1,9},{5,13},{73,65},{77,69},{2,10},{... | collective-permute-start | bytes 110600 | tf_op jit(solution)/shard_map/ppermute | solution.py:543
  26.2 1.7 %collective-permute-start.13 = (f32[72,128]{1,0:T(8,128)S(1)}, f32[72,128]{1,0:T(8,128)S(1)}, u32[]{:S(2)}, u32[]{:S(2)}) collective-permute-start(f32[72,128]{1,0:T(8,128)S(1)} %get-tuple-element.15), channel_id=1, source_target_pairs={{4,0},{0,4},{68,8},{64,12},{12,64},{8,68},{76,72},{72,76},{5,1},{1... | collective-permute-start | bytes 110600 | tf_op jit(solution)/shard_map/ppermute | solution.py:544
  27.9 1.5 %collective-permute-done.4 = f32[288,128]{1,0:T(8,128)S(1)} collective-permute-done((f32[288,128]{1,0:T(8,128)S(1)}, f32[288,128]{1,0:T(8,128)S(1)}, u32[]{:S(2)}, u32[]{:S(2)}) %collective-permute-start.4) | collective-permute-done | bytes 147488 | tf_op jit(solution)/shard_map/ppermute | solution.py:513
  29.4 3.7 %collective-permute-start.6 = (f32[288,128]{1,0:T(8,128)S(1)}, f32[288,128]{1,0:T(8,128)S(1)}, u32[]{:S(2)}, u32[]{:S(2)}) collective-permute-start(f32[288,128]{1,0:T(8,128)S(1)} %add_add_fusion.1), channel_id=1, source_target_pairs={{0,2},{1,3},{2,0},{3,1},{4,6},{5,7},{6,4},{7,5},{8,10},{9,11},{10,... | collective-permute-start | bytes 442376 | tf_op jit(solution)/shard_map/ppermute | solution.py:513
  33.1 0.7 %collective-permute-start.7 = (f32[288,128]{1,0:T(8,128)S(1)}, f32[288,128]{1,0:T(8,128)S(1)}, u32[]{:S(2)}, u32[]{:S(2)}) collective-permute-start(f32[288,128]{1,0:T(8,128)S(1)} %add_add_fusion.1), channel_id=1, source_target_pairs={{0,1},{1,2},{2,3},{3,0},{4,5},{5,6},{6,7},{7,4},{8,9},{9,10},{10,1... | collective-permute-start | bytes 442376 | tf_op jit(solution)/shard_map/ppermute | solution.py:513
  33.8 1.9 %collective-permute-start.8 = (f32[288,128]{1,0:T(8,128)S(1)}, f32[288,128]{1,0:T(8,128)S(1)}, u32[]{:S(2)}, u32[]{:S(2)}) collective-permute-start(f32[288,128]{1,0:T(8,128)S(1)} %add_add_fusion.1), channel_id=1, source_target_pairs={{0,3},{1,0},{2,1},{3,2},{4,7},{5,4},{6,5},{7,6},{8,11},{9,8},{10,9... | collective-permute-start | bytes 442376 | tf_op jit(solution)/shard_map/ppermute | solution.py:513
  35.9 4.1 %collective-permute-done.7 = f32[288,128]{1,0:T(8,128)S(1)} collective-permute-done((f32[288,128]{1,0:T(8,128)S(1)}, f32[288,128]{1,0:T(8,128)S(1)}, u32[]{:S(2)}, u32[]{:S(2)}) %collective-permute-start.7) | collective-permute-done | bytes 147488 | tf_op jit(solution)/shard_map/ppermute | solution.py:513
  40.5 2.6 %collective-permute-start.9 = (f32[1,128]{1,0:T(1,128)S(1)}, f32[1,128]{1,0:T(1,128)S(1)}, u32[]{:S(2)}, u32[]{:S(2)}) collective-permute-start(f32[1,128]{1,0:T(1,128)S(1)} %bitcast.32), channel_id=1, source_target_pairs={{0,64},{64,0},{1,65},{65,1},{2,66},{66,2},{3,67},{67,3},{4,68},{68... | collective-permute-start | bytes 1544 | tf_op jit(solution)/shard_map/ppermute | solution.py:570
  43.1 0.5 collective-permute-start.15
  43.9 1.6 %collective-permute-start.10 = (f32[1,128]{1,0:T(1,128)S(1)}, f32[1,128]{1,0:T(1,128)S(1)}, u32[]{:S(2)}, u32[]{:S(2)}) collective-permute-start(f32[1,128]{1,0:T(1,128)S(1)} %bitcast_add_fusion), channel_id=1, source_target_pairs={{0,16},{1,17},{2,18},{3,19},{4,20},{5,21},{6,22},{7,23},{8,24},{9,... | collective-permute-start | bytes 1544 | tf_op jit(solution)/shard_map/ppermute | solution.py:565
  45.5 2.0 %collective-permute-done.15 = f32[2,144,128]{2,1,0:T(8,128)S(1)} collective-permute-done((f32[2,144,128]{2,1,0:T(8,128)S(1)}, f32[2,144,128]{2,1,0:T(8,128)S(1)}, u32[]{:S(2)}, u32[]{:S(2)}) %collective-permute-start.15) | collective-permute-done | bytes 147488 | tf_op jit(solution)/shard_map/ppermute | solution.py:550
  47.6 2.7 %collective-permute-start.11 = (f32[1,128]{1,0:T(1,128)S(1)}, f32[1,128]{1,0:T(1,128)S(1)}, u32[]{:S(2)}, u32[]{:S(2)}) collective-permute-start(f32[1,128]{1,0:T(1,128)S(1)} %add.105), channel_id=1, source_target_pairs={{0,48},{1,49},{2,50},{3,51},{4,52},{5,53},{6,54},{7,55},{8,56},{9,... | collective-permute-start | bytes 1544 | tf_op jit(solution)/shard_map/ppermute | solution.py:565
  50.3 0.9 %collective-permute-done.11 = f32[1,128]{1,0:T(1,128)S(1)} collective-permute-done((f32[1,128]{1,0:T(1,128)S(1)}, f32[1,128]{1,0:T(1,128)S(1)}, u32[]{:S(2)}, u32[]{:S(2)}) %collective-permute-start.11) | collective-permute-done | bytes 544 | tf_op jit(solution)/shard_map/ppermute | solution.py:565
  51.7 0.7 collective-permute-start.16
  52.3 3.2 %collective-permute-start.17 = (f32[288,128]{1,0:T(8,128)S(1)}, f32[288,128]{1,0:T(8,128)S(1)}, u32[]{:S(2)}, u32[]{:S(2)}) collective-permute-start(f32[288,128]{1,0:T(8,128)S(1)} %update.1), channel_id=1, source_target_pairs={{0,32},{1,33},{2,34},{3,35},{4,36},{5,37},{6,38},{7,39},{8,40},{9,... | collective-permute-start | bytes 442376 | tf_op jit(solution)/shard_map/ppermute | solution.py:513
  55.6 1.3 %collective-permute-done.16 = f32[288,128]{1,0:T(8,128)S(1)} collective-permute-done((f32[288,128]{1,0:T(8,128)S(1)}, f32[288,128]{1,0:T(8,128)S(1)}, u32[]{:S(2)}, u32[]{:S(2)}) %collective-permute-start.16) | collective-permute-done | bytes 147488 | tf_op jit(solution)/shard_map/ppermute | solution.py:513
  57.0 2.7 %collective-permute-done.17 = f32[288,128]{1,0:T(8,128)S(1)} collective-permute-done((f32[288,128]{1,0:T(8,128)S(1)}, f32[288,128]{1,0:T(8,128)S(1)}, u32[]{:S(2)}, u32[]{:S(2)}) %collective-permute-start.17) | collective-permute-done | bytes 147488 | tf_op jit(solution)/shard_map/ppermute | solution.py:513
  59.8 4.7 %collective-permute-start.19 = (f32[4,288,128]{2,1,0:T(8,128)S(1)}, f32[4,288,128]{2,1,0:T(8,128)S(1)}, u32[]{:S(2)}, u32[]{:S(2)}) collective-permute-start(f32[4,288,128]{2,1,0:T(8,128)S(1)} %bitcast_dynamic-update-slice_fusion.mine), channel_id=1, source_target_pairs={{0,64},{64,0},{1,65},{65,1},{2,66},{66,2},{3,67},{67,3},{4,68},{68... | collective-permute-start | bytes 1769480 | tf_op jit(solution)/shard_map/ppermute | solution.py:570
  64.6 0.4 stage.1
  65.0 1.2 %collective-permute-done.19.other = f32[4,288,128]{2,1,0:T(8,128)S(1)} collective-permute-done((f32[4,288,128]{2,1,0:T(8,128)S(1)}, f32[4,288,128]{2,1,0:T(8,128)S(1)}, u32[]{:S(2)}, u32[]{:S(2)}) %collective-permute-start.19) | collective-permute-done | bytes 589856 | tf_op jit(solution)/shard_map/ppermute | solution.py:570
  66.2 3.7 %act.1 = f32[32,400]{1,0:T(8,128)S(1)} custom-call(f32[4,288,128]{2,1,0:T(8,128)S(1)} %bitcast_dynamic-update-slice_fusion.mine, f32[4,288,128]{2,1,0:T(8,128)S(1)} %collective-permute-done.19.other, bf16[12,6,2,32,128]{4,3,2,1,0:T(8,128)(2,1)S(1)} %get-tuple-element.16.boards, bf16[1280,128]{1,0:T(8,128)(2,1)S(1)} %get-tuple-element.17.heads), custom_call_target="tpu_custom_call" | custom-call | flops 8000000000 | bytes 4000000 | tf_op jit(solution)/shard_map/act/pallas_call | solution.py:183
  69.9 0.5 collective-permute-start.20
  70.4 0.6 select_bitcast_fusion.2
  71.3 0.7 pad_maximum_fusion.1
  (48 shorter events, 2.5 us)
Async XLA Ops:
  1.3 13.4 %copy-start.2 = (f32[36,128]{1,0:T(8,128)S(1)}, f32[36,128]{1,0:T(8,128)}, u32[]{:S(2)}) copy-start(f32[36,128]{1,0:T(8,128)} %first_in.1) | copy-start | bytes 55300
  1.3 13.4 %copy-start.3 = (f32[36,128]{1,0:T(8,128)S(1)}, f32[36,128]{1,0:T(8,128)}, u32[]{:S(2)}) copy-start(f32[36,128]{1,0:T(8,128)} %second_in.1) | copy-start | bytes 55300
  8.2 7.7 %collective-permute-start = (f32[288,128]{1,0:T(8,128)}, f32[288,128]{1,0:T(8,128)S(1)}, u32[]{:S(2)}, u32[]{:S(2)}) collective-permute-start(f32[288,128]{1,0:T(8,128)} %get-tuple-element.12), channel_id=1, source_target_pairs={{0,32},{1,33},{2,34},{3,35},{4,36},{5,37},{6,38},{7,39},{8,40},{9,... | collective-permute-start | bytes 442376 | tf_op jit(solution)/shard_map/ppermute | solution.py:513
  12.0 7.3 %collective-permute-start.1 = (f32[288,128]{1,0:T(8,128)}, f32[288,128]{1,0:T(8,128)S(1)}, u32[]{:S(2)}, u32[]{:S(2)}) collective-permute-start(f32[288,128]{1,0:T(8,128)} %get-tuple-element.13), channel_id=1, source_target_pairs={{0,16},{1,17},{2,18},{3,19},{4,20},{5,21},{6,22},{7,23},{8,24},{9,... | collective-permute-start | bytes 442376 | tf_op jit(solution)/shard_map/ppermute | solution.py:513
  12.4 6.9 %collective-permute-start.2 = (f32[288,128]{1,0:T(8,128)}, f32[288,128]{1,0:T(8,128)S(1)}, u32[]{:S(2)}, u32[]{:S(2)}) collective-permute-start(f32[288,128]{1,0:T(8,128)} %get-tuple-element.14), channel_id=1, source_target_pairs={{0,48},{1,49},{2,50},{3,51},{4,52},{5,53},{6,54},{7,55},{8,56},{9,... | collective-permute-start | bytes 442376 | tf_op jit(solution)/shard_map/ppermute | solution.py:513
  14.7 0.9 %copy-start.1 = (f32[288,128]{1,0:T(8,128)S(1)}, f32[288,128]{1,0:T(8,128)}, u32[]{:S(2)}) copy-start(f32[288,128]{1,0:T(8,128)} %get-tuple-element.10.own_in) | copy-start | bytes 442372
  19.4 8.6 %collective-permute-start.3 = (f32[288,128]{1,0:T(8,128)S(1)}, f32[288,128]{1,0:T(8,128)S(1)}, u32[]{:S(2)}, u32[]{:S(2)}) collective-permute-start(f32[288,128]{1,0:T(8,128)S(1)} %add_add_fusion.2), channel_id=1, source_target_pairs={{0,8},{1,9},{2,10},{3,11},{4,12},{5,13},{6,14},{7,15},{8,0},{9,1},... | collective-permute-start | bytes 442376 | tf_op jit(solution)/shard_map/ppermute | solution.py:513
  22.2 7.1 %collective-permute-start.4 = (f32[288,128]{1,0:T(8,128)S(1)}, f32[288,128]{1,0:T(8,128)S(1)}, u32[]{:S(2)}, u32[]{:S(2)}) collective-permute-start(f32[288,128]{1,0:T(8,128)S(1)} %add_add_fusion.2), channel_id=1, source_target_pairs={{0,4},{1,5},{2,6},{3,7},{4,8},{5,9},{6,10},{7,11},{8,12},{9,13},{1... | collective-permute-start | bytes 442376 | tf_op jit(solution)/shard_map/ppermute | solution.py:513
  22.5 6.8 %collective-permute-start.5 = (f32[288,128]{1,0:T(8,128)S(1)}, f32[288,128]{1,0:T(8,128)S(1)}, u32[]{:S(2)}, u32[]{:S(2)}) collective-permute-start(f32[288,128]{1,0:T(8,128)S(1)} %add_add_fusion.2), channel_id=1, source_target_pairs={{0,12},{1,13},{2,14},{3,15},{4,0},{5,1},{6,2},{7,3},{8,4},{9,5},{1... | collective-permute-start | bytes 442376 | tf_op jit(solution)/shard_map/ppermute | solution.py:513
  24.9 10.9 %collective-permute-start.12 = (f32[72,128]{1,0:T(8,128)S(1)}, f32[72,128]{1,0:T(8,128)S(1)}, u32[]{:S(2)}, u32[]{:S(2)}) collective-permute-start(f32[72,128]{1,0:T(8,128)S(1)} %get-tuple-element.15), channel_id=1, source_target_pairs={{0,8},{4,12},{72,64},{76,68},{1,9},{5,13},{73,65},{77,69},{2,10},{... | collective-permute-start | bytes 110600 | tf_op jit(solution)/shard_map/ppermute | solution.py:543
  26.2 9.6 %collective-permute-start.13 = (f32[72,128]{1,0:T(8,128)S(1)}, f32[72,128]{1,0:T(8,128)S(1)}, u32[]{:S(2)}, u32[]{:S(2)}) collective-permute-start(f32[72,128]{1,0:T(8,128)S(1)} %get-tuple-element.15), channel_id=1, source_target_pairs={{4,0},{0,4},{68,8},{64,12},{12,64},{8,68},{76,72},{72,76},{5,1},{1... | collective-permute-start | bytes 110600 | tf_op jit(solution)/shard_map/ppermute | solution.py:544
  29.4 6.5 %collective-permute-start.6 = (f32[288,128]{1,0:T(8,128)S(1)}, f32[288,128]{1,0:T(8,128)S(1)}, u32[]{:S(2)}, u32[]{:S(2)}) collective-permute-start(f32[288,128]{1,0:T(8,128)S(1)} %add_add_fusion.1), channel_id=1, source_target_pairs={{0,2},{1,3},{2,0},{3,1},{4,6},{5,7},{6,4},{7,5},{8,10},{9,11},{10,... | collective-permute-start | bytes 442376 | tf_op jit(solution)/shard_map/ppermute | solution.py:513
  33.1 6.9 %collective-permute-start.7 = (f32[288,128]{1,0:T(8,128)S(1)}, f32[288,128]{1,0:T(8,128)S(1)}, u32[]{:S(2)}, u32[]{:S(2)}) collective-permute-start(f32[288,128]{1,0:T(8,128)S(1)} %add_add_fusion.1), channel_id=1, source_target_pairs={{0,1},{1,2},{2,3},{3,0},{4,5},{5,6},{6,7},{7,4},{8,9},{9,10},{10,1... | collective-permute-start | bytes 442376 | tf_op jit(solution)/shard_map/ppermute | solution.py:513
  33.8 6.6 %collective-permute-start.8 = (f32[288,128]{1,0:T(8,128)S(1)}, f32[288,128]{1,0:T(8,128)S(1)}, u32[]{:S(2)}, u32[]{:S(2)}) collective-permute-start(f32[288,128]{1,0:T(8,128)S(1)} %add_add_fusion.1), channel_id=1, source_target_pairs={{0,3},{1,0},{2,1},{3,2},{4,7},{5,4},{6,5},{7,6},{8,11},{9,8},{10,9... | collective-permute-start | bytes 442376 | tf_op jit(solution)/shard_map/ppermute | solution.py:513
  35.8 7.3 %collective-permute-start.14 = (f32[144,128]{1,0:T(8,128)S(1)}, f32[144,128]{1,0:T(8,128)S(1)}, u32[]{:S(2)}, u32[]{:S(2)}) collective-permute-start(f32[144,128]{1,0:T(8,128)S(1)} %get-tuple-element.27), channel_id=1, source_target_pairs={{0,2},{1,3},{2,0},{3,1},{4,6},{5,7},{6,4},{7,5},{8,10},{9,11},{10,... | collective-permute-start | bytes 221192 | tf_op jit(solution)/shard_map/ppermute | solution.py:550
  40.4 10.8 %copy-start = (f32[2304,128]{1,0:T(8,128)S(1)}, f32[2304,128]{1,0:T(8,128)}, u32[]{:S(2)}) copy-start(f32[2304,128]{1,0:T(8,128)} %torso_in.1) | copy-start | bytes 3538948
  40.5 3.4 %collective-permute-start.9 = (f32[1,128]{1,0:T(1,128)S(1)}, f32[1,128]{1,0:T(1,128)S(1)}, u32[]{:S(2)}, u32[]{:S(2)}) collective-permute-start(f32[1,128]{1,0:T(1,128)S(1)} %bitcast.32), channel_id=1, source_target_pairs={{0,64},{64,0},{1,65},{65,1},{2,66},{66,2},{3,67},{67,3},{4,68},{68... | collective-permute-start | bytes 1544 | tf_op jit(solution)/shard_map/ppermute | solution.py:570
  43.1 4.4 %collective-permute-start.15 = (f32[2,144,128]{2,1,0:T(8,128)S(1)}, f32[2,144,128]{2,1,0:T(8,128)S(1)}, u32[]{:S(2)}, u32[]{:S(2)}) collective-permute-start(f32[2,144,128]{2,1,0:T(8,128)S(1)} %maximum_select_fusion), channel_id=1, source_target_pairs={{0,1},{1,0},{2,3},{3,2},{4,5},{5,4},{6,7},{7,6},{8,9},{9,8},{10,11... | collective-permute-start | bytes 442376 | tf_op jit(solution)/shard_map/ppermute | solution.py:550
  43.9 3.6 %collective-permute-start.10 = (f32[1,128]{1,0:T(1,128)S(1)}, f32[1,128]{1,0:T(1,128)S(1)}, u32[]{:S(2)}, u32[]{:S(2)}) collective-permute-start(f32[1,128]{1,0:T(1,128)S(1)} %bitcast_add_fusion), channel_id=1, source_target_pairs={{0,16},{1,17},{2,18},{3,19},{4,20},{5,21},{6,22},{7,23},{8,24},{9,... | collective-permute-start | bytes 1544 | tf_op jit(solution)/shard_map/ppermute | solution.py:565
  47.6 3.7 %collective-permute-start.11 = (f32[1,128]{1,0:T(1,128)S(1)}, f32[1,128]{1,0:T(1,128)S(1)}, u32[]{:S(2)}, u32[]{:S(2)}) collective-permute-start(f32[1,128]{1,0:T(1,128)S(1)} %add.105), channel_id=1, source_target_pairs={{0,48},{1,49},{2,50},{3,51},{4,52},{5,53},{6,54},{7,55},{8,56},{9,... | collective-permute-start | bytes 1544 | tf_op jit(solution)/shard_map/ppermute | solution.py:565
  51.6 12.9 %copy-start.5 = (bf16[128,4]{0,1:T(4,128)(2,1)S(1)}, bf16[128,4]{0,1:T(4,128)(2,1)}, u32[]{:S(2)}) copy-start(bf16[128,4]{0,1:T(4,128)(2,1)} %param.20) | copy-start | bytes 3076
  51.7 12.9 %copy-start.4 = (bf16[64,10,10,128]{3,0,2,1:T(8,128)(2,1)S(1)}, bf16[64,10,10,128]{3,0,2,1:T(8,128)(2,1)}, u32[]{:S(2)}) copy-start(bf16[64,10,10,128]{3,0,2,1:T(8,128)(2,1)} %param.12) | copy-start | bytes 4915204
  51.7 5.3 %collective-permute-start.16 = (f32[288,128]{1,0:T(8,128)S(1)}, f32[288,128]{1,0:T(8,128)S(1)}, u32[]{:S(2)}, u32[]{:S(2)}) collective-permute-start(f32[288,128]{1,0:T(8,128)S(1)} %update.1), channel_id=1, source_target_pairs={{0,16},{1,17},{2,18},{3,19},{4,20},{5,21},{6,22},{7,23},{8,24},{9,... | collective-permute-start | bytes 442376 | tf_op jit(solution)/shard_map/ppermute | solution.py:513
  52.3 7.4 %collective-permute-start.17 = (f32[288,128]{1,0:T(8,128)S(1)}, f32[288,128]{1,0:T(8,128)S(1)}, u32[]{:S(2)}, u32[]{:S(2)}) collective-permute-start(f32[288,128]{1,0:T(8,128)S(1)} %update.1), channel_id=1, source_target_pairs={{0,32},{1,33},{2,34},{3,35},{4,36},{5,37},{6,38},{7,39},{8,40},{9,... | collective-permute-start | bytes 442376 | tf_op jit(solution)/shard_map/ppermute | solution.py:513
  55.5 4.3 %collective-permute-start.18 = (f32[288,128]{1,0:T(8,128)S(1)}, f32[288,128]{1,0:T(8,128)S(1)}, u32[]{:S(2)}, u32[]{:S(2)}) collective-permute-start(f32[288,128]{1,0:T(8,128)S(1)} %update.1), channel_id=1, source_target_pairs={{0,48},{1,49},{2,50},{3,51},{4,52},{5,53},{6,54},{7,55},{8,56},{9,... | collective-permute-start | bytes 442376 | tf_op jit(solution)/shard_map/ppermute | solution.py:513
  59.8 6.4 %collective-permute-start.19 = (f32[4,288,128]{2,1,0:T(8,128)S(1)}, f32[4,288,128]{2,1,0:T(8,128)S(1)}, u32[]{:S(2)}, u32[]{:S(2)}) collective-permute-start(f32[4,288,128]{2,1,0:T(8,128)S(1)} %bitcast_dynamic-update-slice_fusion.mine), channel_id=1, source_target_pairs={{0,64},{64,0},{1,65},{65,1},{2,66},{66,2},{3,67},{67,3},{4,68},{68... | collective-permute-start | bytes 1769480 | tf_op jit(solution)/shard_map/ppermute | solution.py:570
  69.9 1.4 %collective-permute-start.20 = (f32[32,400]{1,0:T(8,128)S(1)}, f32[32,400]{1,0:T(8,128)S(1)}, u32[]{:S(2)}, u32[]{:S(2)}) collective-permute-start(f32[32,400]{1,0:T(8,128)S(1)} %act.1), channel_id=1, source_target_pairs={{0,64},{64,0},{1,65},{65,1},{2,66},{66,2},{3,67},{67,3},{4,68},{68... | collective-permute-start | bytes 153608 | tf_op jit(solution)/shard_map/ppermute | solution.py:570

commit v14 on v13

--- a/solution.py
+++ b/solution.py
@@ -469,39 +469,55 @@
     )(own, first, second)
 
 
-def update_kernel(summed, squares, moments, torso_in, fresh, old, first, second, done):
+def arrange_kernel(moments, first, second):
+    for x in range(2):
+        for z in range(LINE):
+            rows = slice((LINE * x + z) * PIECE, (LINE * x + z + 1) * PIECE)
+            first[rows] = BETA_ONE * moments[z, x, 0:PIECE]
+            second[rows] = BETA_TWO * moments[z, x, PIECE : 2 * PIECE]
+
+
+def arrange(moments):
+    vmem = pl.BlockSpec(memory_space=pltpu.VMEM)
+    return pl.pallas_call(
+        arrange_kernel,
+        out_shape=[jax.ShapeDtypeStruct((SEGMENT, 128), jnp.float32)] * 2,
+        in_specs=[vmem],
+        out_specs=[vmem, vmem],
+        compiler_params=pltpu.CompilerParams(vmem_limit_bytes=16 * 1024 * 1024),
+        cost_estimate=pl.CostEstimate(
+            flops=4 * 10**9, bytes_accessed=10**6, transcendentals=0
+        ),
+        name="arrange",
+    )(moments)
+
+
+def update_kernel(summed, squares, first, second, torso_in, fresh, old, done):
     y = lax.axis_index("dp") // (LINE * LINE)
     start = pl.multiple_of((2 * y + lax.axis_index("role")) * SEGMENT, SEGMENT)
     fetch = pltpu.make_async_copy(torso_in.at[pl.ds(start, SEGMENT)], old, done)
     fetch.start()
     square_sum = jnp.sum(squares[...], axis=1, keepdims=True)
     factor = jnp.minimum(1.0, jnp.sqrt(256.0 * ROWS) / jnp.sqrt(square_sum + NORM_EPS))
-    for x in range(2):
-        for z in range(LINE):
-            rows = slice((LINE * x + z) * PIECE, (LINE * x + z + 1) * PIECE)
-            first[rows] = moments[z, x, 0:PIECE]
-            second[rows] = moments[z, x, PIECE : 2 * PIECE]
+    clipped = summed[...] * factor
+    moment_one = first[...] + (1.0 - BETA_ONE) * clipped
+    moment_two = second[...] + (1.0 - BETA_TWO) * clipped * clipped
+    step = LEARN_RATE * moment_one / (jnp.sqrt(moment_two) + ADAM_EPS)
     fetch.wait()
-    clipped = summed[...] * factor
-    moment_one = BETA_ONE * first[...] + (1.0 - BETA_ONE) * clipped
-    moment_two = BETA_TWO * second[...] + (1.0 - BETA_TWO) * clipped * clipped
-    fresh[...] = old[...] - LEARN_RATE * moment_one / (jnp.sqrt(moment_two) + ADAM_EPS)
-
-
-def update(summed, squares, moments, torso):
+    fresh[...] = old[...] - step
+
+
+def update(summed, squares, first, second, torso):
     vmem = pl.BlockSpec(memory_space=pltpu.VMEM)
-    rows = pltpu.VMEM((SEGMENT, 128), jnp.float32)
     return pl.pallas_call(
         update_kernel,
         out_shape=jax.ShapeDtypeStruct((SEGMENT, 128), jnp.float32),
-        in_specs=[
-            vmem, vmem, vmem, pl.BlockSpec(memory_space=pltpu.HBM)
-        ],
+        in_specs=[vmem] * 4 + [pl.BlockSpec(memory_space=pltpu.HBM)],
         out_specs=vmem,
-        scratch_shapes=[rows, rows, rows, pltpu.SemaphoreType.DMA],
+        scratch_shapes=[pltpu.VMEM((SEGMENT, 128), jnp.float32), pltpu.SemaphoreType.DMA],
         compiler_params=pltpu.CompilerParams(vmem_limit_bytes=16 * 1024 * 1024),
         name="update",
-    )(summed, squares, moments, torso)
+    )(summed, squares, first, second, torso)
 
 
 def shifted(x, axis, step):
@@ -601,12 +617,12 @@
     own, moments = pull(own, first_moment, second_moment)
     next2 = shifted(next2, "y", 2)
     moments = moments_along_x(moments, role, x)
-    moments = moments_along_z(moments, z)
+    first, second = arrange(moments_along_z(moments, z).reshape(LINE, 2, 2 * PIECE, 128))
     summed = (own + next2) + (shifted(next1, "y", 1) + shifted(next3, "y", 3))
     summed = line_total(line_total(summed, "x"), "z")
     squares = jnp.sum(summed * summed, axis=0, keepdims=True)
     squares = pair_total_y(squares + role_swap(squares))
-    fresh = update(summed, squares, moments.reshape(LINE, 2, 2 * PIECE, 128), torso)
+    fresh = update(summed, squares, first, second, torso)
     mine = line_gather(fresh, "y", y)
     other = role_swap(mine)
     boards, heads = stage(mine, by_cell(board_now), policy_head.T.astype(jnp.float32))

time: 72.1 us -> 71.7 us (level)
  waiting for transfers between devices: 18.4 us -> 16.6 us
  starting transfers between devices: 37.9 us -> 39.2 us
    ppermute x2, starting transfers between devices: 0.58 us -> 3.77 us  [swapped_z(): return lax.ppermute(x, 'dp', [(d, d ^ bit) for d in range(LINE ** 3)])]
    ppermute x12, waiting for transfers between devices: 13.6 us -> 10.5 us  [shifted(): return lax.ppermute(x, 'dp', pairs)]
    ppermute x2, waiting for transfers between devices: 0.95 us -> 3.82 us  [pair_total_y(): x = x + lax.ppermute(x, 'dp', pairs)]
    ppermute x12, starting transfers between devices: 22.3 us -> 19.9 us  [shifted(): return lax.ppermute(x, 'dp', pairs)]
    ppermute x1, starting transfers between devices: 1.72 us -> 3.92 us  [moments_along_x(): next_to = lax.ppermute(own, ('role', 'dp'), next_to)]
    ppermute x2, starting transfers between devices: 4.27 us -> 2.08 us  [pair_total_y(): x = x + lax.ppermute(x, 'dp', pairs)]
    ppermute x2, waiting for transfers between devices: 2.02 us -> 0.01 us  [swapped_z(): return lax.ppermute(x, 'dp', [(d, d ^ bit) for d in range(LINE ** 3)])]
  transfers between devices with their start and end apart: 21 -> 21, of which waited for: 12 -> 10; matrix products, arithmetic and copies ran while one was open for 1% -> 1% of each run, Pallas kernels for 1% -> 1%
where the time goes in v14:
time: 71.7 us; the launch traced here: 71.6 us
  starting transfers between devices  39.2 us (55%)
  waiting for transfers between devices  16.6 us (23%)
  Pallas kernels  11.6 us (16%)
  other arithmetic  1.53 us (2%)
  between operations  1.47 us (2%)
  local copies, waits for them, and re-layouts  1.05 us (1%)
    ppermute x12, starting transfers between devices, shifted(): return lax.ppermute(x, 'dp', pairs)  19.9 us
    ppermute x12, waiting for transfers between devices, shifted(): return lax.ppermute(x, 'dp', pairs)  10.5 us
    ppermute x3, starting transfers between devices, role_swap(): return lax.ppermute(x, 'role', [(0, 1), (1, 0)])  8.29 us
    pallas_call x1, Pallas kernels, learn(): pl.pallas_call(functools.partial(learner_kernel, count), out_shape=[jax.S...  6.86 us
    ppermute x1, starting transfers between devices, moments_along_x(): next_to = lax.ppermute(own, ('role', 'dp'), next_to)  3.92 us
    ppermute x2, waiting for transfers between devices, pair_total_y(): x = x + lax.ppermute(x, 'dp', pairs)  3.82 us
    ppermute x2, starting transfers between devices, swapped_z(): return lax.ppermute(x, 'dp', [(d, d ^ bit) for d in range(LINE ** 3)])  3.77 us
    pallas_call x1, Pallas kernels, act(): pl.pallas_call(functools.partial(actor_kernel, count, unroll), out_shape=...  3.72 us
  transfers between devices with their start and end apart: 21, of which 10 were waited for; matrix products, arithmetic and copies ran while one was open for 1% of the time, Pallas kernels for 1%

profile of v14, /device:TPU:1, one launch (start us, length us, event | category | flops | bytes accessed | tf_op | source)
XLA Modules:
  0.0 71.6 jit_solution(10127741924116396867)
XLA Ops:
  1.3 6.9 %learn.1 = (f32[288,128]{1,0:T(8,128)}, f32[288,128]{1,0:T(8,128)}, f32[288,128]{1,0:T(8,128)}, f32[288,128]{1,0:T(8,128)}) custom-call(s32[1]{0:T(128)S(6)} %copy.19.length_in, bf16[10,10,16,128]{3,2,1,0:T(8,128)(2,1)} %bitcast.33, s32[1,16]{1,0:T(1,128)} %actions_in.1, f32[1,16]{1,0:T(1,128)} %behaviour_in.1, f32[1,16]{1,0:T(1,128)} %regular_in.1, ...), custom_call_target="tpu_custom_call" | custom-call | flops 4000000000 | bytes 3000000 | tf_op jit(solution)/shard_map/learn/pallas_call | solution.py:411
  8.2 3.8 %collective-permute-start = (f32[288,128]{1,0:T(8,128)}, f32[288,128]{1,0:T(8,128)S(1)}, u32[]{:S(2)}, u32[]{:S(2)}) collective-permute-start(f32[288,128]{1,0:T(8,128)} %get-tuple-element.14), channel_id=1, source_target_pairs={{0,32},{1,33},{2,34},{3,35},{4,36},{5,37},{6,38},{7,39},{8,40},{9,... | collective-permute-start | bytes 442376 | tf_op jit(solution)/shard_map/ppermute | solution.py:529
  12.0 0.4 collective-permute-start.1
  12.4 2.3 %collective-permute-start.2 = (f32[288,128]{1,0:T(8,128)}, f32[288,128]{1,0:T(8,128)S(1)}, u32[]{:S(2)}, u32[]{:S(2)}) collective-permute-start(f32[288,128]{1,0:T(8,128)} %get-tuple-element.16), channel_id=1, source_target_pairs={{0,48},{1,49},{2,50},{3,51},{4,52},{5,53},{6,54},{7,55},{8,56},{9,... | collective-permute-start | bytes 442376 | tf_op jit(solution)/shard_map/ppermute | solution.py:529
  14.7 0.9 %copy-done.1 = f32[288,128]{1,0:T(8,128)S(1)} copy-done((f32[288,128]{1,0:T(8,128)S(1)}, f32[288,128]{1,0:T(8,128)}, u32[]{:S(2)}) %copy-start.1) | copy-done | bytes 147480
  15.8 1.3 %collective-permute-start.12 = (f32[72,128]{1,0:T(8,128)S(1)}, f32[72,128]{1,0:T(8,128)S(1)}, u32[]{:S(2)}, u32[]{:S(2)}) collective-permute-start(f32[72,128]{1,0:T(8,128)S(1)} %get-tuple-element.17), channel_id=1, source_target_pairs={{0,8},{4,12},{72,64},{76,68},{1,9},{5,13},{73,65},{77,69},{2,10},{... | collective-permute-start | bytes 110600 | tf_op jit(solution)/shard_map/ppermute | solution.py:559
  17.1 3.9 %collective-permute-start.13 = (f32[72,128]{1,0:T(8,128)S(1)}, f32[72,128]{1,0:T(8,128)S(1)}, u32[]{:S(2)}, u32[]{:S(2)}) collective-permute-start(f32[72,128]{1,0:T(8,128)S(1)} %get-tuple-element.17), channel_id=1, source_target_pairs={{4,0},{0,4},{68,8},{64,12},{12,64},{8,68},{76,72},{72,76},{5,1},{1... | collective-permute-start | bytes 110600 | tf_op jit(solution)/shard_map/ppermute | solution.py:560
  21.1 1.6 %collective-permute-start.3 = (f32[288,128]{1,0:T(8,128)S(1)}, f32[288,128]{1,0:T(8,128)S(1)}, u32[]{:S(2)}, u32[]{:S(2)}) collective-permute-start(f32[288,128]{1,0:T(8,128)S(1)} %add_add_fusion.2), channel_id=1, source_target_pairs={{0,8},{1,9},{2,10},{3,11},{4,12},{5,13},{6,14},{7,15},{8,0},{9,1},... | collective-permute-start | bytes 442376 | tf_op jit(solution)/shard_map/ppermute | solution.py:529
  22.7 2.7 %collective-permute-start.5 = (f32[288,128]{1,0:T(8,128)S(1)}, f32[288,128]{1,0:T(8,128)S(1)}, u32[]{:S(2)}, u32[]{:S(2)}) collective-permute-start(f32[288,128]{1,0:T(8,128)S(1)} %add_add_fusion.2), channel_id=1, source_target_pairs={{0,12},{1,13},{2,14},{3,15},{4,0},{5,1},{6,2},{7,3},{8,4},{9,5},{1... | collective-permute-start | bytes 442376 | tf_op jit(solution)/shard_map/ppermute | solution.py:529
  25.5 3.7 %collective-permute-start.14 = (f32[144,128]{1,0:T(8,128)S(1)}, f32[144,128]{1,0:T(8,128)S(1)}, u32[]{:S(2)}, u32[]{:S(2)}) collective-permute-start(f32[144,128]{1,0:T(8,128)S(1)} %get-tuple-element.31), channel_id=1, source_target_pairs={{0,2},{1,3},{2,0},{3,1},{4,6},{5,7},{6,4},{7,5},{8,10},{9,11},{10,... | collective-permute-start | bytes 221192 | tf_op jit(solution)/shard_map/ppermute | solution.py:566
  29.1 1.4 %collective-permute-done.4 = f32[288,128]{1,0:T(8,128)S(1)} collective-permute-done((f32[288,128]{1,0:T(8,128)S(1)}, f32[288,128]{1,0:T(8,128)S(1)}, u32[]{:S(2)}, u32[]{:S(2)}) %collective-permute-start.4) | collective-permute-done | bytes 147488 | tf_op jit(solution)/shard_map/ppermute | solution.py:529
  30.6 3.7 %collective-permute-start.6 = (f32[288,128]{1,0:T(8,128)S(1)}, f32[288,128]{1,0:T(8,128)S(1)}, u32[]{:S(2)}, u32[]{:S(2)}) collective-permute-start(f32[288,128]{1,0:T(8,128)S(1)} %add_add_fusion.1), channel_id=1, source_target_pairs={{0,2},{1,3},{2,0},{3,1},{4,6},{5,7},{6,4},{7,5},{8,10},{9,11},{10,... | collective-permute-start | bytes 442376 | tf_op jit(solution)/shard_map/ppermute | solution.py:529
  34.3 0.7 %collective-permute-start.7 = (f32[288,128]{1,0:T(8,128)S(1)}, f32[288,128]{1,0:T(8,128)S(1)}, u32[]{:S(2)}, u32[]{:S(2)}) collective-permute-start(f32[288,128]{1,0:T(8,128)S(1)} %add_add_fusion.1), channel_id=1, source_target_pairs={{0,1},{1,2},{2,3},{3,0},{4,5},{5,6},{6,7},{7,4},{8,9},{9,10},{10,1... | collective-permute-start | bytes 442376 | tf_op jit(solution)/shard_map/ppermute | solution.py:529
  35.0 1.9 %collective-permute-start.8 = (f32[288,128]{1,0:T(8,128)S(1)}, f32[288,128]{1,0:T(8,128)S(1)}, u32[]{:S(2)}, u32[]{:S(2)}) collective-permute-start(f32[288,128]{1,0:T(8,128)S(1)} %add_add_fusion.1), channel_id=1, source_target_pairs={{0,3},{1,0},{2,1},{3,2},{4,7},{5,4},{6,5},{7,6},{8,11},{9,8},{10,9... | collective-permute-start | bytes 442376 | tf_op jit(solution)/shard_map/ppermute | solution.py:529
  37.1 4.1 %collective-permute-done.7 = f32[288,128]{1,0:T(8,128)S(1)} collective-permute-done((f32[288,128]{1,0:T(8,128)S(1)}, f32[288,128]{1,0:T(8,128)S(1)}, u32[]{:S(2)}, u32[]{:S(2)}) %collective-permute-start.7) | collective-permute-done | bytes 147488 | tf_op jit(solution)/shard_map/ppermute | solution.py:529
  41.3 3.4 %collective-permute-start.9 = (f32[1,128]{1,0:T(1,128)S(1)}, f32[1,128]{1,0:T(1,128)S(1)}, u32[]{:S(2)}, u32[]{:S(2)}) collective-permute-start(f32[1,128]{1,0:T(1,128)S(1)} %bitcast.32), channel_id=1, source_target_pairs={{0,64},{64,0},{1,65},{65,1},{2,66},{66,2},{3,67},{67,3},{4,68},{68... | collective-permute-start | bytes 1544 | tf_op jit(solution)/shard_map/ppermute | solution.py:586
  44.7 0.8 %collective-permute-done.9 = f32[1,128]{1,0:T(1,128)S(1)} collective-permute-done((f32[1,128]{1,0:T(1,128)S(1)}, f32[1,128]{1,0:T(1,128)S(1)}, u32[]{:S(2)}, u32[]{:S(2)}) %collective-permute-start.9) | collective-permute-done | bytes 544 | tf_op jit(solution)/shard_map/ppermute | solution.py:586
  45.5 0.7 collective-permute-start.10
  46.3 1.7 %collective-permute-done.10 = f32[1,128]{1,0:T(1,128)S(1)} collective-permute-done((f32[1,128]{1,0:T(1,128)S(1)}, f32[1,128]{1,0:T(1,128)S(1)}, u32[]{:S(2)}, u32[]{:S(2)}) %collective-permute-start.10) | collective-permute-done | bytes 544 | tf_op jit(solution)/shard_map/ppermute | solution.py:581
  47.9 1.4 %collective-permute-start.11 = (f32[1,128]{1,0:T(1,128)S(1)}, f32[1,128]{1,0:T(1,128)S(1)}, u32[]{:S(2)}, u32[]{:S(2)}) collective-permute-start(f32[1,128]{1,0:T(1,128)S(1)} %add.105), channel_id=1, source_target_pairs={{0,48},{1,49},{2,50},{3,51},{4,52},{5,53},{6,54},{7,55},{8,56},{9,... | collective-permute-start | bytes 1544 | tf_op jit(solution)/shard_map/ppermute | solution.py:581
  49.4 2.2 %collective-permute-done.11 = f32[1,128]{1,0:T(1,128)S(1)} collective-permute-done((f32[1,128]{1,0:T(1,128)S(1)}, f32[1,128]{1,0:T(1,128)S(1)}, u32[]{:S(2)}, u32[]{:S(2)}) %collective-permute-start.11) | collective-permute-done | bytes 544 | tf_op jit(solution)/shard_map/ppermute | solution.py:581
  52.0 2.6 %collective-permute-start.17 = (f32[288,128]{1,0:T(8,128)S(1)}, f32[288,128]{1,0:T(8,128)S(1)}, u32[]{:S(2)}, u32[]{:S(2)}) collective-permute-start(f32[288,128]{1,0:T(8,128)S(1)} %update.1), channel_id=1, source_target_pairs={{0,32},{1,33},{2,34},{3,35},{4,36},{5,37},{6,38},{7,39},{8,40},{9,... | collective-permute-start | bytes 442376 | tf_op jit(solution)/shard_map/ppermute | solution.py:529
  54.8 2.5 %collective-permute-done.16 = f32[288,128]{1,0:T(8,128)S(1)} collective-permute-done((f32[288,128]{1,0:T(8,128)S(1)}, f32[288,128]{1,0:T(8,128)S(1)}, u32[]{:S(2)}, u32[]{:S(2)}) %collective-permute-start.16) | collective-permute-done | bytes 147488 | tf_op jit(solution)/shard_map/ppermute | solution.py:529
  57.2 1.6 %collective-permute-done.17 = f32[288,128]{1,0:T(8,128)S(1)} collective-permute-done((f32[288,128]{1,0:T(8,128)S(1)}, f32[288,128]{1,0:T(8,128)S(1)}, u32[]{:S(2)}, u32[]{:S(2)}) %collective-permute-start.17) | collective-permute-done | bytes 147488 | tf_op jit(solution)/shard_map/ppermute | solution.py:529
  58.8 0.9 %collective-permute-done.18 = f32[288,128]{1,0:T(8,128)S(1)} collective-permute-done((f32[288,128]{1,0:T(8,128)S(1)}, f32[288,128]{1,0:T(8,128)S(1)}, u32[]{:S(2)}, u32[]{:S(2)}) %collective-permute-start.18) | collective-permute-done | bytes 147488 | tf_op jit(solution)/shard_map/ppermute | solution.py:529
  59.7 4.4 %collective-permute-start.19 = (f32[4,288,128]{2,1,0:T(8,128)S(1)}, f32[4,288,128]{2,1,0:T(8,128)S(1)}, u32[]{:S(2)}, u32[]{:S(2)}) collective-permute-start(f32[4,288,128]{2,1,0:T(8,128)S(1)} %bitcast_dynamic-update-slice_fusion.mine), channel_id=1, source_target_pairs={{0,64},{64,0},{1,65},{65,1},{2,66},{66,2},{3,67},{67,3},{4,68},{68... | collective-permute-start | bytes 1769480 | tf_op jit(solution)/shard_map/ppermute | solution.py:586
  64.2 0.4 stage.1
  64.6 1.2 %collective-permute-done.19.other = f32[4,288,128]{2,1,0:T(8,128)S(1)} collective-permute-done((f32[4,288,128]{2,1,0:T(8,128)S(1)}, f32[4,288,128]{2,1,0:T(8,128)S(1)}, u32[]{:S(2)}, u32[]{:S(2)}) %collective-permute-start.19) | collective-permute-done | bytes 589856 | tf_op jit(solution)/shard_map/ppermute | solution.py:586
  65.8 3.7 %act.1 = f32[32,400]{1,0:T(8,128)S(1)} custom-call(f32[4,288,128]{2,1,0:T(8,128)S(1)} %bitcast_dynamic-update-slice_fusion.mine, f32[4,288,128]{2,1,0:T(8,128)S(1)} %collective-permute-done.19.other, bf16[12,6,2,32,128]{4,3,2,1,0:T(8,128)(2,1)S(1)} %get-tuple-element.20.boards, bf16[1280,128]{1,0:T(8,128)(2,1)S(1)} %get-tuple-element.21.heads), custom_call_target="tpu_custom_call" | custom-call | flops 8000000000 | bytes 4000000 | tf_op jit(solution)/shard_map/act/pallas_call | solution.py:183
  69.5 0.4 collective-permute-start.20
  70.0 0.6 select_bitcast_fusion.2
  70.9 0.7 pad_maximum_fusion.1
  (49 shorter events, 1.6 us)
Async XLA Ops:
  1.3 13.4 %copy-start.2 = (f32[36,128]{1,0:T(8,128)S(1)}, f32[36,128]{1,0:T(8,128)}, u32[]{:S(2)}) copy-start(f32[36,128]{1,0:T(8,128)} %first_in.1) | copy-start | bytes 55300
  1.3 13.4 %copy-start.3 = (f32[36,128]{1,0:T(8,128)S(1)}, f32[36,128]{1,0:T(8,128)}, u32[]{:S(2)}) copy-start(f32[36,128]{1,0:T(8,128)} %second_in.1) | copy-start | bytes 55300
  8.2 12.9 %collective-permute-start = (f32[288,128]{1,0:T(8,128)}, f32[288,128]{1,0:T(8,128)S(1)}, u32[]{:S(2)}, u32[]{:S(2)}) collective-permute-start(f32[288,128]{1,0:T(8,128)} %get-tuple-element.14), channel_id=1, source_target_pairs={{0,32},{1,33},{2,34},{3,35},{4,36},{5,37},{6,38},{7,39},{8,40},{9,... | collective-permute-start | bytes 442376 | tf_op jit(solution)/shard_map/ppermute | solution.py:529
  12.0 9.1 %collective-permute-start.1 = (f32[288,128]{1,0:T(8,128)}, f32[288,128]{1,0:T(8,128)S(1)}, u32[]{:S(2)}, u32[]{:S(2)}) collective-permute-start(f32[288,128]{1,0:T(8,128)} %get-tuple-element.15), channel_id=1, source_target_pairs={{0,16},{1,17},{2,18},{3,19},{4,20},{5,21},{6,22},{7,23},{8,24},{9,... | collective-permute-start | bytes 442376 | tf_op jit(solution)/shard_map/ppermute | solution.py:529
  12.4 8.7 %collective-permute-start.2 = (f32[288,128]{1,0:T(8,128)}, f32[288,128]{1,0:T(8,128)S(1)}, u32[]{:S(2)}, u32[]{:S(2)}) collective-permute-start(f32[288,128]{1,0:T(8,128)} %get-tuple-element.16), channel_id=1, source_target_pairs={{0,48},{1,49},{2,50},{3,51},{4,52},{5,53},{6,54},{7,55},{8,56},{9,... | collective-permute-start | bytes 442376 | tf_op jit(solution)/shard_map/ppermute | solution.py:529
  14.7 0.9 %copy-start.1 = (f32[288,128]{1,0:T(8,128)S(1)}, f32[288,128]{1,0:T(8,128)}, u32[]{:S(2)}) copy-start(f32[288,128]{1,0:T(8,128)} %get-tuple-element.12.own_in) | copy-start | bytes 442372
  15.8 9.6 %collective-permute-start.12 = (f32[72,128]{1,0:T(8,128)S(1)}, f32[72,128]{1,0:T(8,128)S(1)}, u32[]{:S(2)}, u32[]{:S(2)}) collective-permute-start(f32[72,128]{1,0:T(8,128)S(1)} %get-tuple-element.17), channel_id=1, source_target_pairs={{0,8},{4,12},{72,64},{76,68},{1,9},{5,13},{73,65},{77,69},{2,10},{... | collective-permute-start | bytes 110600 | tf_op jit(solution)/shard_map/ppermute | solution.py:559
  17.1 8.3 %collective-permute-start.13 = (f32[72,128]{1,0:T(8,128)S(1)}, f32[72,128]{1,0:T(8,128)S(1)}, u32[]{:S(2)}, u32[]{:S(2)}) collective-permute-start(f32[72,128]{1,0:T(8,128)S(1)} %get-tuple-element.17), channel_id=1, source_target_pairs={{4,0},{0,4},{68,8},{64,12},{12,64},{8,68},{76,72},{72,76},{5,1},{1... | collective-permute-start | bytes 110600 | tf_op jit(solution)/shard_map/ppermute | solution.py:560
  21.1 8.0 %collective-permute-start.3 = (f32[288,128]{1,0:T(8,128)S(1)}, f32[288,128]{1,0:T(8,128)S(1)}, u32[]{:S(2)}, u32[]{:S(2)}) collective-permute-start(f32[288,128]{1,0:T(8,128)S(1)} %add_add_fusion.2), channel_id=1, source_target_pairs={{0,8},{1,9},{2,10},{3,11},{4,12},{5,13},{6,14},{7,15},{8,0},{9,1},... | collective-permute-start | bytes 442376 | tf_op jit(solution)/shard_map/ppermute | solution.py:529
  22.7 7.8 %collective-permute-start.4 = (f32[288,128]{1,0:T(8,128)S(1)}, f32[288,128]{1,0:T(8,128)S(1)}, u32[]{:S(2)}, u32[]{:S(2)}) collective-permute-start(f32[288,128]{1,0:T(8,128)S(1)} %add_add_fusion.2), channel_id=1, source_target_pairs={{0,4},{1,5},{2,6},{3,7},{4,8},{5,9},{6,10},{7,11},{8,12},{9,13},{1... | collective-permute-start | bytes 442376 | tf_op jit(solution)/shard_map/ppermute | solution.py:529
  22.7 7.8 %collective-permute-start.5 = (f32[288,128]{1,0:T(8,128)S(1)}, f32[288,128]{1,0:T(8,128)S(1)}, u32[]{:S(2)}, u32[]{:S(2)}) collective-permute-start(f32[288,128]{1,0:T(8,128)S(1)} %add_add_fusion.2), channel_id=1, source_target_pairs={{0,12},{1,13},{2,14},{3,15},{4,0},{5,1},{6,2},{7,3},{8,4},{9,5},{1... | collective-permute-start | bytes 442376 | tf_op jit(solution)/shard_map/ppermute | solution.py:529
  25.5 11.5 %collective-permute-start.14 = (f32[144,128]{1,0:T(8,128)S(1)}, f32[144,128]{1,0:T(8,128)S(1)}, u32[]{:S(2)}, u32[]{:S(2)}) collective-permute-start(f32[144,128]{1,0:T(8,128)S(1)} %get-tuple-element.31), channel_id=1, source_target_pairs={{0,2},{1,3},{2,0},{3,1},{4,6},{5,7},{6,4},{7,5},{8,10},{9,11},{10,... | collective-permute-start | bytes 221192 | tf_op jit(solution)/shard_map/ppermute | solution.py:566
  30.6 6.5 %collective-permute-start.6 = (f32[288,128]{1,0:T(8,128)S(1)}, f32[288,128]{1,0:T(8,128)S(1)}, u32[]{:S(2)}, u32[]{:S(2)}) collective-permute-start(f32[288,128]{1,0:T(8,128)S(1)} %add_add_fusion.1), channel_id=1, source_target_pairs={{0,2},{1,3},{2,0},{3,1},{4,6},{5,7},{6,4},{7,5},{8,10},{9,11},{10,... | collective-permute-start | bytes 442376 | tf_op jit(solution)/shard_map/ppermute | solution.py:529
  34.3 6.9 %collective-permute-start.7 = (f32[288,128]{1,0:T(8,128)S(1)}, f32[288,128]{1,0:T(8,128)S(1)}, u32[]{:S(2)}, u32[]{:S(2)}) collective-permute-start(f32[288,128]{1,0:T(8,128)S(1)} %add_add_fusion.1), channel_id=1, source_target_pairs={{0,1},{1,2},{2,3},{3,0},{4,5},{5,6},{6,7},{7,4},{8,9},{9,10},{10,1... | collective-permute-start | bytes 442376 | tf_op jit(solution)/shard_map/ppermute | solution.py:529
  35.0 6.2 %collective-permute-start.8 = (f32[288,128]{1,0:T(8,128)S(1)}, f32[288,128]{1,0:T(8,128)S(1)}, u32[]{:S(2)}, u32[]{:S(2)}) collective-permute-start(f32[288,128]{1,0:T(8,128)S(1)} %add_add_fusion.1), channel_id=1, source_target_pairs={{0,3},{1,0},{2,1},{3,2},{4,7},{5,4},{6,5},{7,6},{8,11},{9,8},{10,9... | collective-permute-start | bytes 442376 | tf_op jit(solution)/shard_map/ppermute | solution.py:529
  37.0 7.7 %collective-permute-start.15 = (f32[2,144,128]{2,1,0:T(8,128)S(1)}, f32[2,144,128]{2,1,0:T(8,128)S(1)}, u32[]{:S(2)}, u32[]{:S(2)}) collective-permute-start(f32[2,144,128]{2,1,0:T(8,128)S(1)} %maximum_select_fusion), channel_id=1, source_target_pairs={{0,1},{1,0},{2,3},{3,2},{4,5},{5,4},{6,7},{7,6},{8,9},{9,8},{10,11... | collective-permute-start | bytes 442376 | tf_op jit(solution)/shard_map/ppermute | solution.py:566
  41.3 4.2 %collective-permute-start.9 = (f32[1,128]{1,0:T(1,128)S(1)}, f32[1,128]{1,0:T(1,128)S(1)}, u32[]{:S(2)}, u32[]{:S(2)}) collective-permute-start(f32[1,128]{1,0:T(1,128)S(1)} %bitcast.32), channel_id=1, source_target_pairs={{0,64},{64,0},{1,65},{65,1},{2,66},{66,2},{3,67},{67,3},{4,68},{68... | collective-permute-start | bytes 1544 | tf_op jit(solution)/shard_map/ppermute | solution.py:586
  45.5 2.4 %collective-permute-start.10 = (f32[1,128]{1,0:T(1,128)S(1)}, f32[1,128]{1,0:T(1,128)S(1)}, u32[]{:S(2)}, u32[]{:S(2)}) collective-permute-start(f32[1,128]{1,0:T(1,128)S(1)} %bitcast_add_fusion), channel_id=1, source_target_pairs={{0,16},{1,17},{2,18},{3,19},{4,20},{5,21},{6,22},{7,23},{8,24},{9,... | collective-permute-start | bytes 1544 | tf_op jit(solution)/shard_map/ppermute | solution.py:581
  47.9 3.6 %collective-permute-start.11 = (f32[1,128]{1,0:T(1,128)S(1)}, f32[1,128]{1,0:T(1,128)S(1)}, u32[]{:S(2)}, u32[]{:S(2)}) collective-permute-start(f32[1,128]{1,0:T(1,128)S(1)} %add.105), channel_id=1, source_target_pairs={{0,48},{1,49},{2,50},{3,51},{4,52},{5,53},{6,54},{7,55},{8,56},{9,... | collective-permute-start | bytes 1544 | tf_op jit(solution)/shard_map/ppermute | solution.py:581
  49.3 2.2 %copy-start = (f32[2304,128]{1,0:T(8,128)S(1)}, f32[2304,128]{1,0:T(8,128)}, u32[]{:S(2)}) copy-start(f32[2304,128]{1,0:T(8,128)} %torso_in.1) | copy-start | bytes 3538948
  51.9 12.3 %copy-start.5 = (bf16[128,4]{0,1:T(4,128)(2,1)S(1)}, bf16[128,4]{0,1:T(4,128)(2,1)}, u32[]{:S(2)}) copy-start(bf16[128,4]{0,1:T(4,128)(2,1)} %param.20) | copy-start | bytes 3076
  51.9 12.2 %copy-start.4 = (bf16[64,10,10,128]{3,0,2,1:T(8,128)(2,1)S(1)}, bf16[64,10,10,128]{3,0,2,1:T(8,128)(2,1)}, u32[]{:S(2)}) copy-start(bf16[64,10,10,128]{3,0,2,1:T(8,128)(2,1)} %param.12) | copy-start | bytes 4915204
  51.9 5.3 %collective-permute-start.16 = (f32[288,128]{1,0:T(8,128)S(1)}, f32[288,128]{1,0:T(8,128)S(1)}, u32[]{:S(2)}, u32[]{:S(2)}) collective-permute-start(f32[288,128]{1,0:T(8,128)S(1)} %update.1), channel_id=1, source_target_pairs={{0,16},{1,17},{2,18},{3,19},{4,20},{5,21},{6,22},{7,23},{8,24},{9,... | collective-permute-start | bytes 442376 | tf_op jit(solution)/shard_map/ppermute | solution.py:529
  52.0 6.8 %collective-permute-start.17 = (f32[288,128]{1,0:T(8,128)S(1)}, f32[288,128]{1,0:T(8,128)S(1)}, u32[]{:S(2)}, u32[]{:S(2)}) collective-permute-start(f32[288,128]{1,0:T(8,128)S(1)} %update.1), channel_id=1, source_target_pairs={{0,32},{1,33},{2,34},{3,35},{4,36},{5,37},{6,38},{7,39},{8,40},{9,... | collective-permute-start | bytes 442376 | tf_op jit(solution)/shard_map/ppermute | solution.py:529
  54.6 5.1 %collective-permute-start.18 = (f32[288,128]{1,0:T(8,128)S(1)}, f32[288,128]{1,0:T(8,128)S(1)}, u32[]{:S(2)}, u32[]{:S(2)}) collective-permute-start(f32[288,128]{1,0:T(8,128)S(1)} %update.1), channel_id=1, source_target_pairs={{0,48},{1,49},{2,50},{3,51},{4,52},{5,53},{6,54},{7,55},{8,56},{9,... | collective-permute-start | bytes 442376 | tf_op jit(solution)/shard_map/ppermute | solution.py:529
  59.7 6.1 %collective-permute-start.19 = (f32[4,288,128]{2,1,0:T(8,128)S(1)}, f32[4,288,128]{2,1,0:T(8,128)S(1)}, u32[]{:S(2)}, u32[]{:S(2)}) collective-permute-start(f32[4,288,128]{2,1,0:T(8,128)S(1)} %bitcast_dynamic-update-slice_fusion.mine), channel_id=1, source_target_pairs={{0,64},{64,0},{1,65},{65,1},{2,66},{66,2},{3,67},{67,3},{4,68},{68... | collective-permute-start | bytes 1769480 | tf_op jit(solution)/shard_map/ppermute | solution.py:586
  69.5 1.3 %collective-permute-start.20 = (f32[32,400]{1,0:T(8,128)S(1)}, f32[32,400]{1,0:T(8,128)S(1)}, u32[]{:S(2)}, u32[]{:S(2)}) collective-permute-start(f32[32,400]{1,0:T(8,128)S(1)} %act.1), channel_id=1, source_target_pairs={{0,64},{64,0},{1,65},{65,1},{2,66},{66,2},{3,67},{67,3},{4,68},{68... | collective-permute-start | bytes 153608 | tf_op jit(solution)/shard_map/ppermute | solution.py:586

commit v15 on v14

--- a/solution.py
+++ b/solution.py
@@ -177,7 +177,7 @@
         out[:, 100 * d : 100 * d + 100] = (moves[d] - log_total)[:, :100]
 
 
-def act(mine, other, boards, heads, count=2, unroll=5):
+def act(mine, other, boards, heads, count=1, unroll=10):
     games = boards.shape[3]
     vmem = pl.BlockSpec(memory_space=pltpu.VMEM)
     return pl.pallas_call(
@@ -533,15 +533,12 @@
     return (x + shifted(x, axis, 2)) + (shifted(x, axis, 1) + shifted(x, axis, 3))
 
 
-def line_place(pieces, at):
-    whole = jnp.zeros((LINE,) + pieces[0].shape, pieces[0].dtype)
-    for step, piece in enumerate(pieces):
+def line_gather(x, axis, at):
+    whole = jnp.zeros((LINE,) + x.shape, x.dtype)
+    for step in (0, 2, 1, 3):
+        piece = shifted(x, axis, step) if step else x
         whole = lax.dynamic_update_index_in_dim(whole, piece, (at - step) % LINE, 0)
     return whole
-
-
-def line_gather(x, axis, at):
-    return line_place([x] + [shifted(x, axis, step) for step in range(1, LINE)], at)
 
 
 def moments_along_x(own, role, x):

time: 71.7 us -> 70.7 us (0.986)
  waiting for transfers between devices: 16.6 us -> 15.7 us
    ppermute x12, waiting for transfers between devices: 10.5 us -> 9.62 us  [shifted(): return lax.ppermute(x, 'dp', pairs)]
  transfers between devices with their start and end apart: 21 -> 21, of which waited for: 10 -> 9; matrix products, arithmetic and copies ran while one was open for 1% -> 1% of each run, Pallas kernels for 1% -> 1%
where the time goes in v15:
time: 70.7 us; the launch traced here: 70.5 us
  starting transfers between devices  39.4 us (56%)
  waiting for transfers between devices  15.7 us (22%)
  Pallas kernels  11.3 us (16%)
  other arithmetic  1.53 us (2%)
  between operations  1.48 us (2%)
  local copies, waits for them, and re-layouts  1.06 us (1%)
    ppermute x12, starting transfers between devices, shifted(): return lax.ppermute(x, 'dp', pairs)  20 us
    ppermute x12, waiting for transfers between devices, shifted(): return lax.ppermute(x, 'dp', pairs)  9.62 us
    ppermute x3, starting transfers between devices, role_swap(): return lax.ppermute(x, 'role', [(0, 1), (1, 0)])  8.28 us
    pallas_call x1, Pallas kernels, learn(): pl.pallas_call(functools.partial(learner_kernel, count), out_shape=[jax.S...  6.86 us
    ppermute x1, starting transfers between devices, moments_along_x(): next_to = lax.ppermute(own, ('role', 'dp'), next_to)  3.92 us
    ppermute x2, waiting for transfers between devices, pair_total_y(): x = x + lax.ppermute(x, 'dp', pairs)  3.82 us
    ppermute x2, starting transfers between devices, swapped_z(): return lax.ppermute(x, 'dp', [(d, d ^ bit) for d in range(LINE ** 3)])  3.77 us
    pallas_call x1, Pallas kernels, act(): pl.pallas_call(functools.partial(actor_kernel, count, unroll), out_shape=...  3.42 us
  transfers between devices with their start and end apart: 21, of which 9 were waited for; matrix products, arithmetic and copies ran while one was open for 1% of the time, Pallas kernels for 1%

profile of v15, /device:TPU:1, one launch (start us, length us, event | category | flops | bytes accessed | tf_op | source)
XLA Modules:
  0.0 70.5 jit_solution(13283222195671543762)
XLA Ops:
  1.3 6.9 %learn.1 = (f32[288,128]{1,0:T(8,128)}, f32[288,128]{1,0:T(8,128)}, f32[288,128]{1,0:T(8,128)}, f32[288,128]{1,0:T(8,128)}) custom-call(s32[1]{0:T(128)S(6)} %copy.19.length_in, bf16[10,10,16,128]{3,2,1,0:T(8,128)(2,1)} %bitcast.33, s32[1,16]{1,0:T(1,128)} %actions_in.1, f32[1,16]{1,0:T(1,128)} %behaviour_in.1, f32[1,16]{1,0:T(1,128)} %regular_in.1, ...), custom_call_target="tpu_custom_call" | custom-call | flops 4000000000 | bytes 3000000 | tf_op jit(solution)/shard_map/learn/pallas_call | solution.py:411
  8.2 3.8 %collective-permute-start = (f32[288,128]{1,0:T(8,128)}, f32[288,128]{1,0:T(8,128)S(1)}, u32[]{:S(2)}, u32[]{:S(2)}) collective-permute-start(f32[288,128]{1,0:T(8,128)} %get-tuple-element.14), channel_id=1, source_target_pairs={{0,32},{1,33},{2,34},{3,35},{4,36},{5,37},{6,38},{7,39},{8,40},{9,... | collective-permute-start | bytes 442376 | tf_op jit(solution)/shard_map/ppermute | solution.py:529
  12.0 0.4 collective-permute-start.1
  12.4 2.3 %collective-permute-start.2 = (f32[288,128]{1,0:T(8,128)}, f32[288,128]{1,0:T(8,128)S(1)}, u32[]{:S(2)}, u32[]{:S(2)}) collective-permute-start(f32[288,128]{1,0:T(8,128)} %get-tuple-element.16), channel_id=1, source_target_pairs={{0,48},{1,49},{2,50},{3,51},{4,52},{5,53},{6,54},{7,55},{8,56},{9,... | collective-permute-start | bytes 442376 | tf_op jit(solution)/shard_map/ppermute | solution.py:529
  14.7 0.9 %copy-done.1 = f32[288,128]{1,0:T(8,128)S(1)} copy-done((f32[288,128]{1,0:T(8,128)S(1)}, f32[288,128]{1,0:T(8,128)}, u32[]{:S(2)}) %copy-start.1) | copy-done | bytes 147480
  15.8 1.3 %collective-permute-start.12 = (f32[72,128]{1,0:T(8,128)S(1)}, f32[72,128]{1,0:T(8,128)S(1)}, u32[]{:S(2)}, u32[]{:S(2)}) collective-permute-start(f32[72,128]{1,0:T(8,128)S(1)} %get-tuple-element.17), channel_id=1, source_target_pairs={{0,8},{4,12},{72,64},{76,68},{1,9},{5,13},{73,65},{77,69},{2,10},{... | collective-permute-start | bytes 110600 | tf_op jit(solution)/shard_map/ppermute | solution.py:556
  17.1 3.9 %collective-permute-start.13 = (f32[72,128]{1,0:T(8,128)S(1)}, f32[72,128]{1,0:T(8,128)S(1)}, u32[]{:S(2)}, u32[]{:S(2)}) collective-permute-start(f32[72,128]{1,0:T(8,128)S(1)} %get-tuple-element.17), channel_id=1, source_target_pairs={{4,0},{0,4},{68,8},{64,12},{12,64},{8,68},{76,72},{72,76},{5,1},{1... | collective-permute-start | bytes 110600 | tf_op jit(solution)/shard_map/ppermute | solution.py:557
  21.1 1.6 %collective-permute-start.3 = (f32[288,128]{1,0:T(8,128)S(1)}, f32[288,128]{1,0:T(8,128)S(1)}, u32[]{:S(2)}, u32[]{:S(2)}) collective-permute-start(f32[288,128]{1,0:T(8,128)S(1)} %add_add_fusion.2), channel_id=1, source_target_pairs={{0,8},{1,9},{2,10},{3,11},{4,12},{5,13},{6,14},{7,15},{8,0},{9,1},... | collective-permute-start | bytes 442376 | tf_op jit(solution)/shard_map/ppermute | solution.py:529
  22.7 2.7 %collective-permute-start.5 = (f32[288,128]{1,0:T(8,128)S(1)}, f32[288,128]{1,0:T(8,128)S(1)}, u32[]{:S(2)}, u32[]{:S(2)}) collective-permute-start(f32[288,128]{1,0:T(8,128)S(1)} %add_add_fusion.2), channel_id=1, source_target_pairs={{0,12},{1,13},{2,14},{3,15},{4,0},{5,1},{6,2},{7,3},{8,4},{9,5},{1... | collective-permute-start | bytes 442376 | tf_op jit(solution)/shard_map/ppermute | solution.py:529
  25.5 3.7 %collective-permute-start.14 = (f32[144,128]{1,0:T(8,128)S(1)}, f32[144,128]{1,0:T(8,128)S(1)}, u32[]{:S(2)}, u32[]{:S(2)}) collective-permute-start(f32[144,128]{1,0:T(8,128)S(1)} %get-tuple-element.31), channel_id=1, source_target_pairs={{0,2},{1,3},{2,0},{3,1},{4,6},{5,7},{6,4},{7,5},{8,10},{9,11},{10,... | collective-permute-start | bytes 221192 | tf_op jit(solution)/shard_map/ppermute | solution.py:563
  29.1 1.4 %collective-permute-done.4 = f32[288,128]{1,0:T(8,128)S(1)} collective-permute-done((f32[288,128]{1,0:T(8,128)S(1)}, f32[288,128]{1,0:T(8,128)S(1)}, u32[]{:S(2)}, u32[]{:S(2)}) %collective-permute-start.4) | collective-permute-done | bytes 147488 | tf_op jit(solution)/shard_map/ppermute | solution.py:529
  30.6 3.7 %collective-permute-start.6 = (f32[288,128]{1,0:T(8,128)S(1)}, f32[288,128]{1,0:T(8,128)S(1)}, u32[]{:S(2)}, u32[]{:S(2)}) collective-permute-start(f32[288,128]{1,0:T(8,128)S(1)} %add_add_fusion.1), channel_id=1, source_target_pairs={{0,2},{1,3},{2,0},{3,1},{4,6},{5,7},{6,4},{7,5},{8,10},{9,11},{10,... | collective-permute-start | bytes 442376 | tf_op jit(solution)/shard_map/ppermute | solution.py:529
  34.3 0.7 %collective-permute-start.7 = (f32[288,128]{1,0:T(8,128)S(1)}, f32[288,128]{1,0:T(8,128)S(1)}, u32[]{:S(2)}, u32[]{:S(2)}) collective-permute-start(f32[288,128]{1,0:T(8,128)S(1)} %add_add_fusion.1), channel_id=1, source_target_pairs={{0,1},{1,2},{2,3},{3,0},{4,5},{5,6},{6,7},{7,4},{8,9},{9,10},{10,1... | collective-permute-start | bytes 442376 | tf_op jit(solution)/shard_map/ppermute | solution.py:529
  35.0 1.9 %collective-permute-start.8 = (f32[288,128]{1,0:T(8,128)S(1)}, f32[288,128]{1,0:T(8,128)S(1)}, u32[]{:S(2)}, u32[]{:S(2)}) collective-permute-start(f32[288,128]{1,0:T(8,128)S(1)} %add_add_fusion.1), channel_id=1, source_target_pairs={{0,3},{1,0},{2,1},{3,2},{4,7},{5,4},{6,5},{7,6},{8,11},{9,8},{10,9... | collective-permute-start | bytes 442376 | tf_op jit(solution)/shard_map/ppermute | solution.py:529
  37.1 4.1 %collective-permute-done.7 = f32[288,128]{1,0:T(8,128)S(1)} collective-permute-done((f32[288,128]{1,0:T(8,128)S(1)}, f32[288,128]{1,0:T(8,128)S(1)}, u32[]{:S(2)}, u32[]{:S(2)}) %collective-permute-start.7) | collective-permute-done | bytes 147488 | tf_op jit(solution)/shard_map/ppermute | solution.py:529
  41.3 3.4 %collective-permute-start.9 = (f32[1,128]{1,0:T(1,128)S(1)}, f32[1,128]{1,0:T(1,128)S(1)}, u32[]{:S(2)}, u32[]{:S(2)}) collective-permute-start(f32[1,128]{1,0:T(1,128)S(1)} %bitcast.32), channel_id=1, source_target_pairs={{0,64},{64,0},{1,65},{65,1},{2,66},{66,2},{3,67},{67,3},{4,68},{68... | collective-permute-start | bytes 1544 | tf_op jit(solution)/shard_map/ppermute | solution.py:583
  44.7 0.8 %collective-permute-done.9 = f32[1,128]{1,0:T(1,128)S(1)} collective-permute-done((f32[1,128]{1,0:T(1,128)S(1)}, f32[1,128]{1,0:T(1,128)S(1)}, u32[]{:S(2)}, u32[]{:S(2)}) %collective-permute-start.9) | collective-permute-done | bytes 544 | tf_op jit(solution)/shard_map/ppermute | solution.py:583
  45.5 0.7 collective-permute-start.10
  46.3 1.7 %collective-permute-done.10 = f32[1,128]{1,0:T(1,128)S(1)} collective-permute-done((f32[1,128]{1,0:T(1,128)S(1)}, f32[1,128]{1,0:T(1,128)S(1)}, u32[]{:S(2)}, u32[]{:S(2)}) %collective-permute-start.10) | collective-permute-done | bytes 544 | tf_op jit(solution)/shard_map/ppermute | solution.py:578
  47.9 1.4 %collective-permute-start.11 = (f32[1,128]{1,0:T(1,128)S(1)}, f32[1,128]{1,0:T(1,128)S(1)}, u32[]{:S(2)}, u32[]{:S(2)}) collective-permute-start(f32[1,128]{1,0:T(1,128)S(1)} %add.105), channel_id=1, source_target_pairs={{0,48},{1,49},{2,50},{3,51},{4,52},{5,53},{6,54},{7,55},{8,56},{9,... | collective-permute-start | bytes 1544 | tf_op jit(solution)/shard_map/ppermute | solution.py:578
  49.4 2.2 %collective-permute-done.11 = f32[1,128]{1,0:T(1,128)S(1)} collective-permute-done((f32[1,128]{1,0:T(1,128)S(1)}, f32[1,128]{1,0:T(1,128)S(1)}, u32[]{:S(2)}, u32[]{:S(2)}) %collective-permute-start.11) | collective-permute-done | bytes 544 | tf_op jit(solution)/shard_map/ppermute | solution.py:578
  52.1 1.9 %collective-permute-start.17 = (f32[288,128]{1,0:T(8,128)S(1)}, f32[288,128]{1,0:T(8,128)S(1)}, u32[]{:S(2)}, u32[]{:S(2)}) collective-permute-start(f32[288,128]{1,0:T(8,128)S(1)} %update.1), channel_id=1, source_target_pairs={{0,16},{1,17},{2,18},{3,19},{4,20},{5,21},{6,22},{7,23},{8,24},{9,... | collective-permute-start | bytes 442376 | tf_op jit(solution)/shard_map/ppermute | solution.py:529
  54.0 0.8 %collective-permute-start.18 = (f32[288,128]{1,0:T(8,128)S(1)}, f32[288,128]{1,0:T(8,128)S(1)}, u32[]{:S(2)}, u32[]{:S(2)}) collective-permute-start(f32[288,128]{1,0:T(8,128)S(1)} %update.1), channel_id=1, source_target_pairs={{0,48},{1,49},{2,50},{3,51},{4,52},{5,53},{6,54},{7,55},{8,56},{9,... | collective-permute-start | bytes 442376 | tf_op jit(solution)/shard_map/ppermute | solution.py:529
  54.9 2.8 %collective-permute-done.16 = f32[288,128]{1,0:T(8,128)S(1)} collective-permute-done((f32[288,128]{1,0:T(8,128)S(1)}, f32[288,128]{1,0:T(8,128)S(1)}, u32[]{:S(2)}, u32[]{:S(2)}) %collective-permute-start.16) | collective-permute-done | bytes 147488 | tf_op jit(solution)/shard_map/ppermute | solution.py:529
  57.6 1.3 %collective-permute-done.17 = f32[288,128]{1,0:T(8,128)S(1)} collective-permute-done((f32[288,128]{1,0:T(8,128)S(1)}, f32[288,128]{1,0:T(8,128)S(1)}, u32[]{:S(2)}, u32[]{:S(2)}) %collective-permute-start.17) | collective-permute-done | bytes 147488 | tf_op jit(solution)/shard_map/ppermute | solution.py:529
  59.0 4.4 %collective-permute-start.19 = (f32[4,288,128]{2,1,0:T(8,128)S(1)}, f32[4,288,128]{2,1,0:T(8,128)S(1)}, u32[]{:S(2)}, u32[]{:S(2)}) collective-permute-start(f32[4,288,128]{2,1,0:T(8,128)S(1)} %bitcast_dynamic-update-slice_fusion.mine), channel_id=1, source_target_pairs={{0,64},{64,0},{1,65},{65,1},{2,66},{66,2},{3,67},{67,3},{4,68},{68... | collective-permute-start | bytes 1769480 | tf_op jit(solution)/shard_map/ppermute | solution.py:583
  63.4 0.4 stage.1
  63.8 1.2 %collective-permute-done.19.other = f32[4,288,128]{2,1,0:T(8,128)S(1)} collective-permute-done((f32[4,288,128]{2,1,0:T(8,128)S(1)}, f32[4,288,128]{2,1,0:T(8,128)S(1)}, u32[]{:S(2)}, u32[]{:S(2)}) %collective-permute-start.19) | collective-permute-done | bytes 589856 | tf_op jit(solution)/shard_map/ppermute | solution.py:583
  65.0 3.4 %act.1 = f32[32,400]{1,0:T(8,128)S(1)} custom-call(f32[4,288,128]{2,1,0:T(8,128)S(1)} %bitcast_dynamic-update-slice_fusion.mine, f32[4,288,128]{2,1,0:T(8,128)S(1)} %collective-permute-done.19.other, bf16[12,6,2,32,128]{4,3,2,1,0:T(8,128)(2,1)S(1)} %get-tuple-element.20.boards, bf16[1280,128]{1,0:T(8,128)(2,1)S(1)} %get-tuple-element.21.heads), custom_call_target="tpu_custom_call" | custom-call | flops 8000000000 | bytes 4000000 | tf_op jit(solution)/shard_map/act/pallas_call | solution.py:183
  68.5 0.5 collective-permute-start.20
  68.9 0.6 select_bitcast_fusion.2
  69.8 0.7 pad_maximum_fusion.1
  (49 shorter events, 1.6 us)
Async XLA Ops:
  1.3 13.4 %copy-start.2 = (f32[36,128]{1,0:T(8,128)S(1)}, f32[36,128]{1,0:T(8,128)}, u32[]{:S(2)}) copy-start(f32[36,128]{1,0:T(8,128)} %first_in.1) | copy-start | bytes 55300
  1.3 13.4 %copy-start.3 = (f32[36,128]{1,0:T(8,128)S(1)}, f32[36,128]{1,0:T(8,128)}, u32[]{:S(2)}) copy-start(f32[36,128]{1,0:T(8,128)} %second_in.1) | copy-start | bytes 55300
  8.2 12.9 %collective-permute-start = (f32[288,128]{1,0:T(8,128)}, f32[288,128]{1,0:T(8,128)S(1)}, u32[]{:S(2)}, u32[]{:S(2)}) collective-permute-start(f32[288,128]{1,0:T(8,128)} %get-tuple-element.14), channel_id=1, source_target_pairs={{0,32},{1,33},{2,34},{3,35},{4,36},{5,37},{6,38},{7,39},{8,40},{9,... | collective-permute-start | bytes 442376 | tf_op jit(solution)/shard_map/ppermute | solution.py:529
  12.0 9.1 %collective-permute-start.1 = (f32[288,128]{1,0:T(8,128)}, f32[288,128]{1,0:T(8,128)S(1)}, u32[]{:S(2)}, u32[]{:S(2)}) collective-permute-start(f32[288,128]{1,0:T(8,128)} %get-tuple-element.15), channel_id=1, source_target_pairs={{0,16},{1,17},{2,18},{3,19},{4,20},{5,21},{6,22},{7,23},{8,24},{9,... | collective-permute-start | bytes 442376 | tf_op jit(solution)/shard_map/ppermute | solution.py:529
  12.4 8.7 %collective-permute-start.2 = (f32[288,128]{1,0:T(8,128)}, f32[288,128]{1,0:T(8,128)S(1)}, u32[]{:S(2)}, u32[]{:S(2)}) collective-permute-start(f32[288,128]{1,0:T(8,128)} %get-tuple-element.16), channel_id=1, source_target_pairs={{0,48},{1,49},{2,50},{3,51},{4,52},{5,53},{6,54},{7,55},{8,56},{9,... | collective-permute-start | bytes 442376 | tf_op jit(solution)/shard_map/ppermute | solution.py:529
  14.7 0.9 %copy-start.1 = (f32[288,128]{1,0:T(8,128)S(1)}, f32[288,128]{1,0:T(8,128)}, u32[]{:S(2)}) copy-start(f32[288,128]{1,0:T(8,128)} %get-tuple-element.12.own_in) | copy-start | bytes 442372
  15.8 9.6 %collective-permute-start.12 = (f32[72,128]{1,0:T(8,128)S(1)}, f32[72,128]{1,0:T(8,128)S(1)}, u32[]{:S(2)}, u32[]{:S(2)}) collective-permute-start(f32[72,128]{1,0:T(8,128)S(1)} %get-tuple-element.17), channel_id=1, source_target_pairs={{0,8},{4,12},{72,64},{76,68},{1,9},{5,13},{73,65},{77,69},{2,10},{... | collective-permute-start | bytes 110600 | tf_op jit(solution)/shard_map/ppermute | solution.py:556
  17.1 8.3 %collective-permute-start.13 = (f32[72,128]{1,0:T(8,128)S(1)}, f32[72,128]{1,0:T(8,128)S(1)}, u32[]{:S(2)}, u32[]{:S(2)}) collective-permute-start(f32[72,128]{1,0:T(8,128)S(1)} %get-tuple-element.17), channel_id=1, source_target_pairs={{4,0},{0,4},{68,8},{64,12},{12,64},{8,68},{76,72},{72,76},{5,1},{1... | collective-permute-start | bytes 110600 | tf_op jit(solution)/shard_map/ppermute | solution.py:557
  21.1 8.0 %collective-permute-start.3 = (f32[288,128]{1,0:T(8,128)S(1)}, f32[288,128]{1,0:T(8,128)S(1)}, u32[]{:S(2)}, u32[]{:S(2)}) collective-permute-start(f32[288,128]{1,0:T(8,128)S(1)} %add_add_fusion.2), channel_id=1, source_target_pairs={{0,8},{1,9},{2,10},{3,11},{4,12},{5,13},{6,14},{7,15},{8,0},{9,1},... | collective-permute-start | bytes 442376 | tf_op jit(solution)/shard_map/ppermute | solution.py:529
  22.7 7.8 %collective-permute-start.4 = (f32[288,128]{1,0:T(8,128)S(1)}, f32[288,128]{1,0:T(8,128)S(1)}, u32[]{:S(2)}, u32[]{:S(2)}) collective-permute-start(f32[288,128]{1,0:T(8,128)S(1)} %add_add_fusion.2), channel_id=1, source_target_pairs={{0,4},{1,5},{2,6},{3,7},{4,8},{5,9},{6,10},{7,11},{8,12},{9,13},{1... | collective-permute-start | bytes 442376 | tf_op jit(solution)/shard_map/ppermute | solution.py:529
  22.7 7.8 %collective-permute-start.5 = (f32[288,128]{1,0:T(8,128)S(1)}, f32[288,128]{1,0:T(8,128)S(1)}, u32[]{:S(2)}, u32[]{:S(2)}) collective-permute-start(f32[288,128]{1,0:T(8,128)S(1)} %add_add_fusion.2), channel_id=1, source_target_pairs={{0,12},{1,13},{2,14},{3,15},{4,0},{5,1},{6,2},{7,3},{8,4},{9,5},{1... | collective-permute-start | bytes 442376 | tf_op jit(solution)/shard_map/ppermute | solution.py:529
  25.5 11.5 %collective-permute-start.14 = (f32[144,128]{1,0:T(8,128)S(1)}, f32[144,128]{1,0:T(8,128)S(1)}, u32[]{:S(2)}, u32[]{:S(2)}) collective-permute-start(f32[144,128]{1,0:T(8,128)S(1)} %get-tuple-element.31), channel_id=1, source_target_pairs={{0,2},{1,3},{2,0},{3,1},{4,6},{5,7},{6,4},{7,5},{8,10},{9,11},{10,... | collective-permute-start | bytes 221192 | tf_op jit(solution)/shard_map/ppermute | solution.py:563
  30.6 6.5 %collective-permute-start.6 = (f32[288,128]{1,0:T(8,128)S(1)}, f32[288,128]{1,0:T(8,128)S(1)}, u32[]{:S(2)}, u32[]{:S(2)}) collective-permute-start(f32[288,128]{1,0:T(8,128)S(1)} %add_add_fusion.1), channel_id=1, source_target_pairs={{0,2},{1,3},{2,0},{3,1},{4,6},{5,7},{6,4},{7,5},{8,10},{9,11},{10,... | collective-permute-start | bytes 442376 | tf_op jit(solution)/shard_map/ppermute | solution.py:529
  34.3 6.9 %collective-permute-start.7 = (f32[288,128]{1,0:T(8,128)S(1)}, f32[288,128]{1,0:T(8,128)S(1)}, u32[]{:S(2)}, u32[]{:S(2)}) collective-permute-start(f32[288,128]{1,0:T(8,128)S(1)} %add_add_fusion.1), channel_id=1, source_target_pairs={{0,1},{1,2},{2,3},{3,0},{4,5},{5,6},{6,7},{7,4},{8,9},{9,10},{10,1... | collective-permute-start | bytes 442376 | tf_op jit(solution)/shard_map/ppermute | solution.py:529
  35.0 6.2 %collective-permute-start.8 = (f32[288,128]{1,0:T(8,128)S(1)}, f32[288,128]{1,0:T(8,128)S(1)}, u32[]{:S(2)}, u32[]{:S(2)}) collective-permute-start(f32[288,128]{1,0:T(8,128)S(1)} %add_add_fusion.1), channel_id=1, source_target_pairs={{0,3},{1,0},{2,1},{3,2},{4,7},{5,4},{6,5},{7,6},{8,11},{9,8},{10,9... | collective-permute-start | bytes 442376 | tf_op jit(solution)/shard_map/ppermute | solution.py:529
  37.0 7.7 %collective-permute-start.15 = (f32[2,144,128]{2,1,0:T(8,128)S(1)}, f32[2,144,128]{2,1,0:T(8,128)S(1)}, u32[]{:S(2)}, u32[]{:S(2)}) collective-permute-start(f32[2,144,128]{2,1,0:T(8,128)S(1)} %maximum_select_fusion), channel_id=1, source_target_pairs={{0,1},{1,0},{2,3},{3,2},{4,5},{5,4},{6,7},{7,6},{8,9},{9,8},{10,11... | collective-permute-start | bytes 442376 | tf_op jit(solution)/shard_map/ppermute | solution.py:563
  41.3 4.2 %collective-permute-start.9 = (f32[1,128]{1,0:T(1,128)S(1)}, f32[1,128]{1,0:T(1,128)S(1)}, u32[]{:S(2)}, u32[]{:S(2)}) collective-permute-start(f32[1,128]{1,0:T(1,128)S(1)} %bitcast.32), channel_id=1, source_target_pairs={{0,64},{64,0},{1,65},{65,1},{2,66},{66,2},{3,67},{67,3},{4,68},{68... | collective-permute-start | bytes 1544 | tf_op jit(solution)/shard_map/ppermute | solution.py:583
  45.5 2.4 %collective-permute-start.10 = (f32[1,128]{1,0:T(1,128)S(1)}, f32[1,128]{1,0:T(1,128)S(1)}, u32[]{:S(2)}, u32[]{:S(2)}) collective-permute-start(f32[1,128]{1,0:T(1,128)S(1)} %bitcast_add_fusion), channel_id=1, source_target_pairs={{0,16},{1,17},{2,18},{3,19},{4,20},{5,21},{6,22},{7,23},{8,24},{9,... | collective-permute-start | bytes 1544 | tf_op jit(solution)/shard_map/ppermute | solution.py:578
  47.9 3.6 %collective-permute-start.11 = (f32[1,128]{1,0:T(1,128)S(1)}, f32[1,128]{1,0:T(1,128)S(1)}, u32[]{:S(2)}, u32[]{:S(2)}) collective-permute-start(f32[1,128]{1,0:T(1,128)S(1)} %add.105), channel_id=1, source_target_pairs={{0,48},{1,49},{2,50},{3,51},{4,52},{5,53},{6,54},{7,55},{8,56},{9,... | collective-permute-start | bytes 1544 | tf_op jit(solution)/shard_map/ppermute | solution.py:578
  49.3 2.2 %copy-start = (f32[2304,128]{1,0:T(8,128)S(1)}, f32[2304,128]{1,0:T(8,128)}, u32[]{:S(2)}) copy-start(f32[2304,128]{1,0:T(8,128)} %torso_in.1) | copy-start | bytes 3538948
  51.9 11.5 %copy-start.5 = (bf16[128,4]{0,1:T(4,128)(2,1)S(1)}, bf16[128,4]{0,1:T(4,128)(2,1)}, u32[]{:S(2)}) copy-start(bf16[128,4]{0,1:T(4,128)(2,1)} %param.20) | copy-start | bytes 3076
  51.9 11.5 %copy-start.4 = (bf16[64,10,10,128]{3,0,2,1:T(8,128)(2,1)S(1)}, bf16[64,10,10,128]{3,0,2,1:T(8,128)(2,1)}, u32[]{:S(2)}) copy-start(bf16[64,10,10,128]{3,0,2,1:T(8,128)(2,1)} %param.12) | copy-start | bytes 4915204
  51.9 5.7 %collective-permute-start.16 = (f32[288,128]{1,0:T(8,128)S(1)}, f32[288,128]{1,0:T(8,128)S(1)}, u32[]{:S(2)}, u32[]{:S(2)}) collective-permute-start(f32[288,128]{1,0:T(8,128)S(1)} %update.1), channel_id=1, source_target_pairs={{0,32},{1,33},{2,34},{3,35},{4,36},{5,37},{6,38},{7,39},{8,40},{9,... | collective-permute-start | bytes 442376 | tf_op jit(solution)/shard_map/ppermute | solution.py:529
  52.1 6.8 %collective-permute-start.17 = (f32[288,128]{1,0:T(8,128)S(1)}, f32[288,128]{1,0:T(8,128)S(1)}, u32[]{:S(2)}, u32[]{:S(2)}) collective-permute-start(f32[288,128]{1,0:T(8,128)S(1)} %update.1), channel_id=1, source_target_pairs={{0,16},{1,17},{2,18},{3,19},{4,20},{5,21},{6,22},{7,23},{8,24},{9,... | collective-permute-start | bytes 442376 | tf_op jit(solution)/shard_map/ppermute | solution.py:529
  54.0 4.9 %collective-permute-start.18 = (f32[288,128]{1,0:T(8,128)S(1)}, f32[288,128]{1,0:T(8,128)S(1)}, u32[]{:S(2)}, u32[]{:S(2)}) collective-permute-start(f32[288,128]{1,0:T(8,128)S(1)} %update.1), channel_id=1, source_target_pairs={{0,48},{1,49},{2,50},{3,51},{4,52},{5,53},{6,54},{7,55},{8,56},{9,... | collective-permute-start | bytes 442376 | tf_op jit(solution)/shard_map/ppermute | solution.py:529
  59.0 6.1 %collective-permute-start.19 = (f32[4,288,128]{2,1,0:T(8,128)S(1)}, f32[4,288,128]{2,1,0:T(8,128)S(1)}, u32[]{:S(2)}, u32[]{:S(2)}) collective-permute-start(f32[4,288,128]{2,1,0:T(8,128)S(1)} %bitcast_dynamic-update-slice_fusion.mine), channel_id=1, source_target_pairs={{0,64},{64,0},{1,65},{65,1},{2,66},{66,2},{3,67},{67,3},{4,68},{68... | collective-permute-start | bytes 1769480 | tf_op jit(solution)/shard_map/ppermute | solution.py:583
  68.5 1.4 %collective-permute-start.20 = (f32[32,400]{1,0:T(8,128)S(1)}, f32[32,400]{1,0:T(8,128)S(1)}, u32[]{:S(2)}, u32[]{:S(2)}) collective-permute-start(f32[32,400]{1,0:T(8,128)S(1)} %act.1), channel_id=1, source_target_pairs={{0,64},{64,0},{1,65},{65,1},{2,66},{66,2},{3,67},{67,3},{4,68},{68... | collective-permute-start | bytes 153608 | tf_op jit(solution)/shard_map/ppermute | solution.py:583

commit v16 on v15

--- a/solution.py
+++ b/solution.py
@@ -534,11 +534,14 @@
 
 
 def line_gather(x, axis, at):
-    whole = jnp.zeros((LINE,) + x.shape, x.dtype)
+    mine = jnp.zeros((LINE,) + x.shape, x.dtype)
+    other = jnp.zeros((LINE,) + x.shape, x.dtype)
     for step in (0, 2, 1, 3):
         piece = shifted(x, axis, step) if step else x
-        whole = lax.dynamic_update_index_in_dim(whole, piece, (at - step) % LINE, 0)
-    return whole
+        place = (at - step) % LINE
+        mine = lax.dynamic_update_index_in_dim(mine, piece, place, 0)
+        other = lax.dynamic_update_index_in_dim(other, role_swap(piece), place, 0)
+    return mine, other
 
 
 def moments_along_x(own, role, x):
@@ -620,8 +623,7 @@
     squares = jnp.sum(summed * summed, axis=0, keepdims=True)
     squares = pair_total_y(squares + role_swap(squares))
     fresh = update(summed, squares, first, second, torso)
-    mine = line_gather(fresh, "y", y)
-    other = role_swap(mine)
+    mine, other = line_gather(fresh, "y", y)
     boards, heads = stage(mine, by_cell(board_now), policy_head.T.astype(jnp.float32))
     here = act(mine, other, boards, heads)
     there = role_swap(here)

time: 70.7 us -> 76.1 us (1.076)
  waiting for transfers between devices: 15.7 us -> 23.8 us
  starting transfers between devices: 39.4 us -> 36.5 us
    ppermute x12, waiting for transfers between devices: 9.62 us -> 15.9 us  [shifted(): return lax.ppermute(x, 'dp', pairs)]
    ppermute x2, starting transfers between devices: 2.08 us -> 0.01 us  [pair_total_y(): x = x + lax.ppermute(x, 'dp', pairs)]
    ppermute x2, waiting for transfers between devices: 3.82 us -> 5.89 us  [pair_total_y(): x = x + lax.ppermute(x, 'dp', pairs)]
    ppermute x2, starting transfers between devices: 3.77 us -> 5.7 us  [swapped_z(): return lax.ppermute(x, 'dp', [(d, d ^ bit) for d in range(LINE ** 3)])]
    ppermute x12, starting transfers between devices: 20 us -> 18.2 us  [shifted(): return lax.ppermute(x, 'dp', pairs)]
    ppermute x3 -> x6, starting transfers between devices: 8.28 us -> 7.34 us  [role_swap(): return lax.ppermute(x, 'role', [(0, 1), (1, 0)])]
    ppermute x3 -> x6, waiting for transfers between devices: 2.27 us -> 1.99 us  [role_swap(): return lax.ppermute(x, 'role', [(0, 1), (1, 0)])]
  transfers between devices with their start and end apart: 21 -> 24, of which waited for: 9 -> 9; matrix products, arithmetic and copies ran while one was open for 1% -> 1% of each run, Pallas kernels for 1% -> 1%
where the time goes in v16:
time: 76.1 us; the launch traced here: 75.9 us
  starting transfers between devices  36.5 us (48%)
  waiting for transfers between devices  23.8 us (31%)
  Pallas kernels  11.4 us (15%)
  between operations  1.62 us (2%)
  other arithmetic  1.54 us (2%)
  local copies, waits for them, and re-layouts  1.17 us (2%)
    ppermute x12, starting transfers between devices, shifted(): return lax.ppermute(x, 'dp', pairs)  18.2 us
    ppermute x12, waiting for transfers between devices, shifted(): return lax.ppermute(x, 'dp', pairs)  15.9 us
    ppermute x6, starting transfers between devices, role_swap(): return lax.ppermute(x, 'role', [(0, 1), (1, 0)])  7.34 us
    pallas_call x1, Pallas kernels, learn(): pl.pallas_call(functools.partial(learner_kernel, count), out_shape=[jax.S...  6.88 us
    ppermute x2, waiting for transfers between devices, pair_total_y(): x = x + lax.ppermute(x, 'dp', pairs)  5.89 us
    ppermute x2, starting transfers between devices, swapped_z(): return lax.ppermute(x, 'dp', [(d, d ^ bit) for d in range(LINE ** 3)])  5.7 us
    ppermute x1, starting transfers between devices, moments_along_x(): next_to = lax.ppermute(own, ('role', 'dp'), next_to)  3.92 us
    pallas_call x1, Pallas kernels, act(): pl.pallas_call(functools.partial(actor_kernel, count, unroll), out_shape=...  3.42 us
  transfers between devices with their start and end apart: 24, of which 9 were waited for; matrix products, arithmetic and copies ran while one was open for 1% of the time, Pallas kernels for 1%

profile of v16, /device:TPU:1, one launch (start us, length us, event | category | flops | bytes accessed | tf_op | source)
XLA Modules:
  0.0 75.9 jit_solution(731645788625109894)
XLA Ops:
  1.3 6.9 %learn.1 = (f32[288,128]{1,0:T(8,128)}, f32[288,128]{1,0:T(8,128)}, f32[288,128]{1,0:T(8,128)}, f32[288,128]{1,0:T(8,128)}) custom-call(s32[1]{0:T(128)S(6)} %copy.23.length_in, bf16[10,10,16,128]{3,2,1,0:T(8,128)(2,1)} %bitcast.41, s32[1,16]{1,0:T(1,128)} %actions_in.1, f32[1,16]{1,0:T(1,128)} %behaviour_in.1, f32[1,16]{1,0:T(1,128)} %regular_in.1, ...), custom_call_target="tpu_custom_call" | custom-call | flops 4000000000 | bytes 3000000 | tf_op jit(solution)/shard_map/learn/pallas_call | solution.py:411
  8.2 3.8 %collective-permute-start = (f32[288,128]{1,0:T(8,128)}, f32[288,128]{1,0:T(8,128)S(1)}, u32[]{:S(2)}, u32[]{:S(2)}) collective-permute-start(f32[288,128]{1,0:T(8,128)} %get-tuple-element.14), channel_id=1, source_target_pairs={{0,32},{1,33},{2,34},{3,35},{4,36},{5,37},{6,38},{7,39},{8,40},{9,... | collective-permute-start | bytes 442376 | tf_op jit(solution)/shard_map/ppermute | solution.py:529
  12.0 0.4 collective-permute-start.1
  12.4 2.3 %collective-permute-start.2 = (f32[288,128]{1,0:T(8,128)}, f32[288,128]{1,0:T(8,128)S(1)}, u32[]{:S(2)}, u32[]{:S(2)}) collective-permute-start(f32[288,128]{1,0:T(8,128)} %get-tuple-element.16), channel_id=1, source_target_pairs={{0,48},{1,49},{2,50},{3,51},{4,52},{5,53},{6,54},{7,55},{8,56},{9,... | collective-permute-start | bytes 442376 | tf_op jit(solution)/shard_map/ppermute | solution.py:529
  14.7 0.9 %copy-done.1 = f32[288,128]{1,0:T(8,128)S(1)} copy-done((f32[288,128]{1,0:T(8,128)S(1)}, f32[288,128]{1,0:T(8,128)}, u32[]{:S(2)}) %copy-start.1) | copy-done | bytes 147480
  15.8 3.9 %collective-permute-start.13 = (f32[72,128]{1,0:T(8,128)S(1)}, f32[72,128]{1,0:T(8,128)S(1)}, u32[]{:S(2)}, u32[]{:S(2)}) collective-permute-start(f32[72,128]{1,0:T(8,128)S(1)} %get-tuple-element.17), channel_id=1, source_target_pairs={{4,0},{0,4},{68,8},{64,12},{12,64},{8,68},{76,72},{72,76},{5,1},{1... | collective-permute-start | bytes 110600 | tf_op jit(solution)/shard_map/ppermute | solution.py:560
  19.8 1.3 %collective-permute-start.12 = (f32[72,128]{1,0:T(8,128)S(1)}, f32[72,128]{1,0:T(8,128)S(1)}, u32[]{:S(2)}, u32[]{:S(2)}) collective-permute-start(f32[72,128]{1,0:T(8,128)S(1)} %get-tuple-element.17), channel_id=1, source_target_pairs={{0,8},{4,12},{72,64},{76,68},{1,9},{5,13},{73,65},{77,69},{2,10},{... | collective-permute-start | bytes 110600 | tf_op jit(solution)/shard_map/ppermute | solution.py:559
  21.2 3.0 %collective-permute-start.5 = (f32[288,128]{1,0:T(8,128)S(1)}, f32[288,128]{1,0:T(8,128)S(1)}, u32[]{:S(2)}, u32[]{:S(2)}) collective-permute-start(f32[288,128]{1,0:T(8,128)S(1)} %add_add_fusion.2), channel_id=1, source_target_pairs={{0,12},{1,13},{2,14},{3,15},{4,0},{5,1},{6,2},{7,3},{8,4},{9,5},{1... | collective-permute-start | bytes 442376 | tf_op jit(solution)/shard_map/ppermute | solution.py:529
  24.2 2.1 %collective-permute-start.3 = (f32[288,128]{1,0:T(8,128)S(1)}, f32[288,128]{1,0:T(8,128)S(1)}, u32[]{:S(2)}, u32[]{:S(2)}) collective-permute-start(f32[288,128]{1,0:T(8,128)S(1)} %add_add_fusion.2), channel_id=1, source_target_pairs={{0,8},{1,9},{2,10},{3,11},{4,12},{5,13},{6,14},{7,15},{8,0},{9,1},... | collective-permute-start | bytes 442376 | tf_op jit(solution)/shard_map/ppermute | solution.py:529
  26.3 3.7 %collective-permute-start.14 = (f32[144,128]{1,0:T(8,128)S(1)}, f32[144,128]{1,0:T(8,128)S(1)}, u32[]{:S(2)}, u32[]{:S(2)}) collective-permute-start(f32[144,128]{1,0:T(8,128)S(1)} %get-tuple-element.31), channel_id=1, source_target_pairs={{0,2},{1,3},{2,0},{3,1},{4,6},{5,7},{6,4},{7,5},{8,10},{9,11},{10,... | collective-permute-start | bytes 221192 | tf_op jit(solution)/shard_map/ppermute | solution.py:566
  30.0 3.8 %collective-permute-done.4 = f32[288,128]{1,0:T(8,128)S(1)} collective-permute-done((f32[288,128]{1,0:T(8,128)S(1)}, f32[288,128]{1,0:T(8,128)S(1)}, u32[]{:S(2)}, u32[]{:S(2)}) %collective-permute-start.4) | collective-permute-done | bytes 147488 | tf_op jit(solution)/shard_map/ppermute | solution.py:529
  33.9 3.8 %collective-permute-start.8 = (f32[288,128]{1,0:T(8,128)S(1)}, f32[288,128]{1,0:T(8,128)S(1)}, u32[]{:S(2)}, u32[]{:S(2)}) collective-permute-start(f32[288,128]{1,0:T(8,128)S(1)} %add_add_fusion.1), channel_id=1, source_target_pairs={{0,3},{1,0},{2,1},{3,2},{4,7},{5,4},{6,5},{7,6},{8,11},{9,8},{10,9... | collective-permute-start | bytes 442376 | tf_op jit(solution)/shard_map/ppermute | solution.py:529
  37.7 1.3 %collective-permute-start.6 = (f32[288,128]{1,0:T(8,128)S(1)}, f32[288,128]{1,0:T(8,128)S(1)}, u32[]{:S(2)}, u32[]{:S(2)}) collective-permute-start(f32[288,128]{1,0:T(8,128)S(1)} %add_add_fusion.1), channel_id=1, source_target_pairs={{0,2},{1,3},{2,0},{3,1},{4,6},{5,7},{6,4},{7,5},{8,10},{9,11},{10,... | collective-permute-start | bytes 442376 | tf_op jit(solution)/shard_map/ppermute | solution.py:529
  39.1 2.0 %collective-permute-start.15 = (f32[2,144,128]{2,1,0:T(8,128)S(1)}, f32[2,144,128]{2,1,0:T(8,128)S(1)}, u32[]{:S(2)}, u32[]{:S(2)}) collective-permute-start(f32[2,144,128]{2,1,0:T(8,128)S(1)} %maximum_select_fusion), channel_id=1, source_target_pairs={{0,1},{1,0},{2,3},{3,2},{4,5},{5,4},{6,7},{7,6},{8,9},{9,8},{10,11... | collective-permute-start | bytes 442376 | tf_op jit(solution)/shard_map/ppermute | solution.py:566
  41.1 5.3 %collective-permute-done.7 = f32[288,128]{1,0:T(8,128)S(1)} collective-permute-done((f32[288,128]{1,0:T(8,128)S(1)}, f32[288,128]{1,0:T(8,128)S(1)}, u32[]{:S(2)}, u32[]{:S(2)}) %collective-permute-start.7) | collective-permute-done | bytes 147488 | tf_op jit(solution)/shard_map/ppermute | solution.py:529
  46.4 2.1 %collective-permute-start.9 = (f32[1,128]{1,0:T(1,128)S(1)}, f32[1,128]{1,0:T(1,128)S(1)}, u32[]{:S(2)}, u32[]{:S(2)}) collective-permute-start(f32[1,128]{1,0:T(1,128)S(1)} %bitcast.40), channel_id=1, source_target_pairs={{0,64},{64,0},{1,65},{65,1},{2,66},{66,2},{3,67},{67,3},{4,68},{68... | collective-permute-start | bytes 1544 | tf_op jit(solution)/shard_map/ppermute | solution.py:586
  48.5 0.8 %collective-permute-done.9 = f32[1,128]{1,0:T(1,128)S(1)} collective-permute-done((f32[1,128]{1,0:T(1,128)S(1)}, f32[1,128]{1,0:T(1,128)S(1)}, u32[]{:S(2)}, u32[]{:S(2)}) %collective-permute-start.9) | collective-permute-done | bytes 544 | tf_op jit(solution)/shard_map/ppermute | solution.py:586
  49.4 2.3 %collective-permute-done.10 = f32[1,128]{1,0:T(1,128)S(1)} collective-permute-done((f32[1,128]{1,0:T(1,128)S(1)}, f32[1,128]{1,0:T(1,128)S(1)}, u32[]{:S(2)}, u32[]{:S(2)}) %collective-permute-start.10) | collective-permute-done | bytes 544 | tf_op jit(solution)/shard_map/ppermute | solution.py:581
  51.8 3.6 %collective-permute-done.11 = f32[1,128]{1,0:T(1,128)S(1)} collective-permute-done((f32[1,128]{1,0:T(1,128)S(1)}, f32[1,128]{1,0:T(1,128)S(1)}, u32[]{:S(2)}, u32[]{:S(2)}) %collective-permute-start.11) | collective-permute-done | bytes 544 | tf_op jit(solution)/shard_map/ppermute | solution.py:581
  55.3 0.4 update.1
  55.7 2.7 %collective-permute-start.19 = (f32[288,128]{1,0:T(8,128)S(1)}, f32[288,128]{1,0:T(8,128)S(1)}, u32[]{:S(2)}, u32[]{:S(2)}) collective-permute-start(f32[288,128]{1,0:T(8,128)S(1)} %update.1), channel_id=1, source_target_pairs={{0,64},{64,0},{1,65},{65,1},{2,66},{66,2},{3,67},{67,3},{4,68},{68... | collective-permute-start | bytes 442376 | tf_op jit(solution)/shard_map/ppermute | solution.py:586
  58.4 1.5 %collective-permute-start.17 = (f32[288,128]{1,0:T(8,128)S(1)}, f32[288,128]{1,0:T(8,128)S(1)}, u32[]{:S(2)}, u32[]{:S(2)}) collective-permute-start(f32[288,128]{1,0:T(8,128)S(1)} %update.1), channel_id=1, source_target_pairs={{0,16},{1,17},{2,18},{3,19},{4,20},{5,21},{6,22},{7,23},{8,24},{9,... | collective-permute-start | bytes 442376 | tf_op jit(solution)/shard_map/ppermute | solution.py:529
  60.0 3.9 %collective-permute-done.18 = f32[288,128]{1,0:T(8,128)S(1)} collective-permute-done((f32[288,128]{1,0:T(8,128)S(1)}, f32[288,128]{1,0:T(8,128)S(1)}, u32[]{:S(2)}, u32[]{:S(2)}) %collective-permute-start.18) | collective-permute-done | bytes 147488 | tf_op jit(solution)/shard_map/ppermute | solution.py:529
  63.8 1.3 %collective-permute-start.22 = (f32[288,128]{1,0:T(8,128)S(1)}, f32[288,128]{1,0:T(8,128)S(1)}, u32[]{:S(2)}, u32[]{:S(2)}) collective-permute-start(f32[288,128]{1,0:T(8,128)S(1)} %collective-permute-done.18), channel_id=1, source_target_pairs={{0,64},{64,0},{1,65},{65,1},{2,66},{66,2},{3,67},{67,3},{4,68},{68... | collective-permute-start | bytes 442376 | tf_op jit(solution)/shard_map/ppermute | solution.py:586
  65.1 2.9 %collective-permute-done.17 = f32[288,128]{1,0:T(8,128)S(1)} collective-permute-done((f32[288,128]{1,0:T(8,128)S(1)}, f32[288,128]{1,0:T(8,128)S(1)}, u32[]{:S(2)}, u32[]{:S(2)}) %collective-permute-start.17) | collective-permute-done | bytes 147488 | tf_op jit(solution)/shard_map/ppermute | solution.py:529
  68.1 1.0 %collective-permute-start.21 = (f32[288,128]{1,0:T(8,128)S(1)}, f32[288,128]{1,0:T(8,128)S(1)}, u32[]{:S(2)}, u32[]{:S(2)}) collective-permute-start(f32[288,128]{1,0:T(8,128)S(1)} %collective-permute-done.17), channel_id=1, source_target_pairs={{0,64},{64,0},{1,65},{65,1},{2,66},{66,2},{3,67},{67,3},{4,68},{68... | collective-permute-start | bytes 442376 | tf_op jit(solution)/shard_map/ppermute | solution.py:586
  69.2 0.4 stage.1
  69.6 0.8 %collective-permute-done.20 = f32[288,128]{1,0:T(8,128)S(1)} collective-permute-done((f32[288,128]{1,0:T(8,128)S(1)}, f32[288,128]{1,0:T(8,128)S(1)}, u32[]{:S(2)}, u32[]{:S(2)}) %collective-permute-start.20) | collective-permute-done | bytes 147488 | tf_op jit(solution)/shard_map/ppermute | solution.py:586
  70.5 3.4 %act.1 = f32[32,400]{1,0:T(8,128)S(1)} custom-call(f32[4,288,128]{2,1,0:T(8,128)S(1)} %bitcast_dynamic-update-slice_fusion.4.mine, f32[4,288,128]{2,1,0:T(8,128)S(1)} %bitcast_dynamic-update-slice_fusion.other, bf16[12,6,2,32,128]{4,3,2,1,0:T(8,128)(2,1)S(1)} %get-tuple-element.20.boards, bf16[1280,128]{1,0:T(8,128)(2,1)S(1)} %get-tuple-element.21.heads), custom_call_target="tpu_custom_call" | custom-call | flops 8000000000 | bytes 4000000 | tf_op jit(solution)/shard_map/act/pallas_call | solution.py:183
  74.2 0.6 select_bitcast_fusion.2
  74.8 0.4 collective-permute-done.23
  75.3 0.7 pad_maximum_fusion.1
  (60 shorter events, 1.1 us)
Async XLA Ops:
  1.3 13.4 %copy-start.2 = (f32[36,128]{1,0:T(8,128)S(1)}, f32[36,128]{1,0:T(8,128)}, u32[]{:S(2)}) copy-start(f32[36,128]{1,0:T(8,128)} %first_in.1) | copy-start | bytes 55300
  1.3 13.4 %copy-start.3 = (f32[36,128]{1,0:T(8,128)S(1)}, f32[36,128]{1,0:T(8,128)}, u32[]{:S(2)}) copy-start(f32[36,128]{1,0:T(8,128)} %second_in.1) | copy-start | bytes 55300
  8.2 30.8 %copy-start.5 = (bf16[128,4]{0,1:T(4,128)(2,1)S(1)}, bf16[128,4]{0,1:T(4,128)(2,1)}, u32[]{:S(2)}) copy-start(bf16[128,4]{0,1:T(4,128)(2,1)} %param.20) | copy-start | bytes 3076
  8.2 12.9 %collective-permute-start = (f32[288,128]{1,0:T(8,128)}, f32[288,128]{1,0:T(8,128)S(1)}, u32[]{:S(2)}, u32[]{:S(2)}) collective-permute-start(f32[288,128]{1,0:T(8,128)} %get-tuple-element.14), channel_id=1, source_target_pairs={{0,32},{1,33},{2,34},{3,35},{4,36},{5,37},{6,38},{7,39},{8,40},{9,... | collective-permute-start | bytes 442376 | tf_op jit(solution)/shard_map/ppermute | solution.py:529
  12.0 9.1 %collective-permute-start.1 = (f32[288,128]{1,0:T(8,128)}, f32[288,128]{1,0:T(8,128)S(1)}, u32[]{:S(2)}, u32[]{:S(2)}) collective-permute-start(f32[288,128]{1,0:T(8,128)} %get-tuple-element.15), channel_id=1, source_target_pairs={{0,16},{1,17},{2,18},{3,19},{4,20},{5,21},{6,22},{7,23},{8,24},{9,... | collective-permute-start | bytes 442376 | tf_op jit(solution)/shard_map/ppermute | solution.py:529
  12.4 8.7 %collective-permute-start.2 = (f32[288,128]{1,0:T(8,128)}, f32[288,128]{1,0:T(8,128)S(1)}, u32[]{:S(2)}, u32[]{:S(2)}) collective-permute-start(f32[288,128]{1,0:T(8,128)} %get-tuple-element.16), channel_id=1, source_target_pairs={{0,48},{1,49},{2,50},{3,51},{4,52},{5,53},{6,54},{7,55},{8,56},{9,... | collective-permute-start | bytes 442376 | tf_op jit(solution)/shard_map/ppermute | solution.py:529
  14.7 0.9 %copy-start.1 = (f32[288,128]{1,0:T(8,128)S(1)}, f32[288,128]{1,0:T(8,128)}, u32[]{:S(2)}) copy-start(f32[288,128]{1,0:T(8,128)} %get-tuple-element.12.own_in) | copy-start | bytes 442372
  15.8 10.5 %collective-permute-start.13 = (f32[72,128]{1,0:T(8,128)S(1)}, f32[72,128]{1,0:T(8,128)S(1)}, u32[]{:S(2)}, u32[]{:S(2)}) collective-permute-start(f32[72,128]{1,0:T(8,128)S(1)} %get-tuple-element.17), channel_id=1, source_target_pairs={{4,0},{0,4},{68,8},{64,12},{12,64},{8,68},{76,72},{72,76},{5,1},{1... | collective-permute-start | bytes 110600 | tf_op jit(solution)/shard_map/ppermute | solution.py:560
  19.8 6.6 %collective-permute-start.12 = (f32[72,128]{1,0:T(8,128)S(1)}, f32[72,128]{1,0:T(8,128)S(1)}, u32[]{:S(2)}, u32[]{:S(2)}) collective-permute-start(f32[72,128]{1,0:T(8,128)S(1)} %get-tuple-element.17), channel_id=1, source_target_pairs={{0,8},{4,12},{72,64},{76,68},{1,9},{5,13},{73,65},{77,69},{2,10},{... | collective-permute-start | bytes 110600 | tf_op jit(solution)/shard_map/ppermute | solution.py:559
  21.2 8.8 %collective-permute-start.5 = (f32[288,128]{1,0:T(8,128)S(1)}, f32[288,128]{1,0:T(8,128)S(1)}, u32[]{:S(2)}, u32[]{:S(2)}) collective-permute-start(f32[288,128]{1,0:T(8,128)S(1)} %add_add_fusion.2), channel_id=1, source_target_pairs={{0,12},{1,13},{2,14},{3,15},{4,0},{5,1},{6,2},{7,3},{8,4},{9,5},{1... | collective-permute-start | bytes 442376 | tf_op jit(solution)/shard_map/ppermute | solution.py:529
  24.2 9.7 %collective-permute-start.4 = (f32[288,128]{1,0:T(8,128)S(1)}, f32[288,128]{1,0:T(8,128)S(1)}, u32[]{:S(2)}, u32[]{:S(2)}) collective-permute-start(f32[288,128]{1,0:T(8,128)S(1)} %add_add_fusion.2), channel_id=1, source_target_pairs={{0,4},{1,5},{2,6},{3,7},{4,8},{5,9},{6,10},{7,11},{8,12},{9,13},{1... | collective-permute-start | bytes 442376 | tf_op jit(solution)/shard_map/ppermute | solution.py:529
  24.2 9.7 %collective-permute-start.3 = (f32[288,128]{1,0:T(8,128)S(1)}, f32[288,128]{1,0:T(8,128)S(1)}, u32[]{:S(2)}, u32[]{:S(2)}) collective-permute-start(f32[288,128]{1,0:T(8,128)S(1)} %add_add_fusion.2), channel_id=1, source_target_pairs={{0,8},{1,9},{2,10},{3,11},{4,12},{5,13},{6,14},{7,15},{8,0},{9,1},... | collective-permute-start | bytes 442376 | tf_op jit(solution)/shard_map/ppermute | solution.py:529
  26.3 12.7 %collective-permute-start.14 = (f32[144,128]{1,0:T(8,128)S(1)}, f32[144,128]{1,0:T(8,128)S(1)}, u32[]{:S(2)}, u32[]{:S(2)}) collective-permute-start(f32[144,128]{1,0:T(8,128)S(1)} %get-tuple-element.31), channel_id=1, source_target_pairs={{0,2},{1,3},{2,0},{3,1},{4,6},{5,7},{6,4},{7,5},{8,10},{9,11},{10,... | collective-permute-start | bytes 221192 | tf_op jit(solution)/shard_map/ppermute | solution.py:566
  33.9 7.2 %collective-permute-start.8 = (f32[288,128]{1,0:T(8,128)S(1)}, f32[288,128]{1,0:T(8,128)S(1)}, u32[]{:S(2)}, u32[]{:S(2)}) collective-permute-start(f32[288,128]{1,0:T(8,128)S(1)} %add_add_fusion.1), channel_id=1, source_target_pairs={{0,3},{1,0},{2,1},{3,2},{4,7},{5,4},{6,5},{7,6},{8,11},{9,8},{10,9... | collective-permute-start | bytes 442376 | tf_op jit(solution)/shard_map/ppermute | solution.py:529
  37.7 8.6 %collective-permute-start.7 = (f32[288,128]{1,0:T(8,128)S(1)}, f32[288,128]{1,0:T(8,128)S(1)}, u32[]{:S(2)}, u32[]{:S(2)}) collective-permute-start(f32[288,128]{1,0:T(8,128)S(1)} %add_add_fusion.1), channel_id=1, source_target_pairs={{0,1},{1,2},{2,3},{3,0},{4,5},{5,6},{6,7},{7,4},{8,9},{9,10},{10,1... | collective-permute-start | bytes 442376 | tf_op jit(solution)/shard_map/ppermute | solution.py:529
  37.7 8.6 %collective-permute-start.6 = (f32[288,128]{1,0:T(8,128)S(1)}, f32[288,128]{1,0:T(8,128)S(1)}, u32[]{:S(2)}, u32[]{:S(2)}) collective-permute-start(f32[288,128]{1,0:T(8,128)S(1)} %add_add_fusion.1), channel_id=1, source_target_pairs={{0,2},{1,3},{2,0},{3,1},{4,6},{5,7},{6,4},{7,5},{8,10},{9,11},{10,... | collective-permute-start | bytes 442376 | tf_op jit(solution)/shard_map/ppermute | solution.py:529
  39.1 9.4 %collective-permute-start.15 = (f32[2,144,128]{2,1,0:T(8,128)S(1)}, f32[2,144,128]{2,1,0:T(8,128)S(1)}, u32[]{:S(2)}, u32[]{:S(2)}) collective-permute-start(f32[2,144,128]{2,1,0:T(8,128)S(1)} %maximum_select_fusion), channel_id=1, source_target_pairs={{0,1},{1,0},{2,3},{3,2},{4,5},{5,4},{6,7},{7,6},{8,9},{9,8},{10,11... | collective-permute-start | bytes 442376 | tf_op jit(solution)/shard_map/ppermute | solution.py:566
  46.4 2.9 %collective-permute-start.9 = (f32[1,128]{1,0:T(1,128)S(1)}, f32[1,128]{1,0:T(1,128)S(1)}, u32[]{:S(2)}, u32[]{:S(2)}) collective-permute-start(f32[1,128]{1,0:T(1,128)S(1)} %bitcast.40), channel_id=1, source_target_pairs={{0,64},{64,0},{1,65},{65,1},{2,66},{66,2},{3,67},{67,3},{4,68},{68... | collective-permute-start | bytes 1544 | tf_op jit(solution)/shard_map/ppermute | solution.py:586
  49.3 2.4 %collective-permute-start.10 = (f32[1,128]{1,0:T(1,128)S(1)}, f32[1,128]{1,0:T(1,128)S(1)}, u32[]{:S(2)}, u32[]{:S(2)}) collective-permute-start(f32[1,128]{1,0:T(1,128)S(1)} %bitcast_add_fusion), channel_id=1, source_target_pairs={{0,16},{1,17},{2,18},{3,19},{4,20},{5,21},{6,22},{7,23},{8,24},{9,... | collective-permute-start | bytes 1544 | tf_op jit(solution)/shard_map/ppermute | solution.py:581
  51.7 3.6 %collective-permute-start.11 = (f32[1,128]{1,0:T(1,128)S(1)}, f32[1,128]{1,0:T(1,128)S(1)}, u32[]{:S(2)}, u32[]{:S(2)}) collective-permute-start(f32[1,128]{1,0:T(1,128)S(1)} %add.109), channel_id=1, source_target_pairs={{0,48},{1,49},{2,50},{3,51},{4,52},{5,53},{6,54},{7,55},{8,56},{9,... | collective-permute-start | bytes 1544 | tf_op jit(solution)/shard_map/ppermute | solution.py:581
  51.7 3.6 %copy-start = (f32[2304,128]{1,0:T(8,128)S(1)}, f32[2304,128]{1,0:T(8,128)}, u32[]{:S(2)}) copy-start(f32[2304,128]{1,0:T(8,128)} %torso_in.1) | copy-start | bytes 3538948
  55.7 13.3 %collective-permute-start.19 = (f32[288,128]{1,0:T(8,128)S(1)}, f32[288,128]{1,0:T(8,128)S(1)}, u32[]{:S(2)}, u32[]{:S(2)}) collective-permute-start(f32[288,128]{1,0:T(8,128)S(1)} %update.1), channel_id=1, source_target_pairs={{0,64},{64,0},{1,65},{65,1},{2,66},{66,2},{3,67},{67,3},{4,68},{68... | collective-permute-start | bytes 442376 | tf_op jit(solution)/shard_map/ppermute | solution.py:586
  58.4 5.4 %collective-permute-start.18 = (f32[288,128]{1,0:T(8,128)S(1)}, f32[288,128]{1,0:T(8,128)S(1)}, u32[]{:S(2)}, u32[]{:S(2)}) collective-permute-start(f32[288,128]{1,0:T(8,128)S(1)} %update.1), channel_id=1, source_target_pairs={{0,48},{1,49},{2,50},{3,51},{4,52},{5,53},{6,54},{7,55},{8,56},{9,... | collective-permute-start | bytes 442376 | tf_op jit(solution)/shard_map/ppermute | solution.py:529
  58.4 9.7 %collective-permute-start.17 = (f32[288,128]{1,0:T(8,128)S(1)}, f32[288,128]{1,0:T(8,128)S(1)}, u32[]{:S(2)}, u32[]{:S(2)}) collective-permute-start(f32[288,128]{1,0:T(8,128)S(1)} %update.1), channel_id=1, source_target_pairs={{0,16},{1,17},{2,18},{3,19},{4,20},{5,21},{6,22},{7,23},{8,24},{9,... | collective-permute-start | bytes 442376 | tf_op jit(solution)/shard_map/ppermute | solution.py:529
  59.9 9.2 %collective-permute-start.16 = (f32[288,128]{1,0:T(8,128)S(1)}, f32[288,128]{1,0:T(8,128)S(1)}, u32[]{:S(2)}, u32[]{:S(2)}) collective-permute-start(f32[288,128]{1,0:T(8,128)S(1)} %update.1), channel_id=1, source_target_pairs={{0,32},{1,33},{2,34},{3,35},{4,36},{5,37},{6,38},{7,39},{8,40},{9,... | collective-permute-start | bytes 442376 | tf_op jit(solution)/shard_map/ppermute | solution.py:529
  59.9 9.3 %copy-start.4 = (bf16[64,10,10,128]{3,0,2,1:T(8,128)(2,1)S(1)}, bf16[64,10,10,128]{3,0,2,1:T(8,128)(2,1)}, u32[]{:S(2)}) copy-start(bf16[64,10,10,128]{3,0,2,1:T(8,128)(2,1)} %param.12) | copy-start | bytes 4915204
  63.8 6.7 %collective-permute-start.22 = (f32[288,128]{1,0:T(8,128)S(1)}, f32[288,128]{1,0:T(8,128)S(1)}, u32[]{:S(2)}, u32[]{:S(2)}) collective-permute-start(f32[288,128]{1,0:T(8,128)S(1)} %collective-permute-done.18), channel_id=1, source_target_pairs={{0,64},{64,0},{1,65},{65,1},{2,66},{66,2},{3,67},{67,3},{4,68},{68... | collective-permute-start | bytes 442376 | tf_op jit(solution)/shard_map/ppermute | solution.py:586
  68.1 2.4 %collective-permute-start.21 = (f32[288,128]{1,0:T(8,128)S(1)}, f32[288,128]{1,0:T(8,128)S(1)}, u32[]{:S(2)}, u32[]{:S(2)}) collective-permute-start(f32[288,128]{1,0:T(8,128)S(1)} %collective-permute-done.17), channel_id=1, source_target_pairs={{0,64},{64,0},{1,65},{65,1},{2,66},{66,2},{3,67},{67,3},{4,68},{68... | collective-permute-start | bytes 442376 | tf_op jit(solution)/shard_map/ppermute | solution.py:586
  69.0 1.4 %collective-permute-start.20 = (f32[288,128]{1,0:T(8,128)S(1)}, f32[288,128]{1,0:T(8,128)S(1)}, u32[]{:S(2)}, u32[]{:S(2)}) collective-permute-start(f32[288,128]{1,0:T(8,128)S(1)} %collective-permute-done.16), channel_id=1, source_target_pairs={{0,64},{64,0},{1,65},{65,1},{2,66},{66,2},{3,67},{67,3},{4,68},{68... | collective-permute-start | bytes 442376 | tf_op jit(solution)/shard_map/ppermute | solution.py:586
  73.9 1.3 %collective-permute-start.23 = (f32[32,400]{1,0:T(8,128)S(1)}, f32[32,400]{1,0:T(8,128)S(1)}, u32[]{:S(2)}, u32[]{:S(2)}) collective-permute-start(f32[32,400]{1,0:T(8,128)S(1)} %act.1), channel_id=1, source_target_pairs={{0,64},{64,0},{1,65},{65,1},{2,66},{66,2},{3,67},{67,3},{4,68},{68... | collective-permute-start | bytes 153608 | tf_op jit(solution)/shard_map/ppermute | solution.py:586
